TPU v7x, 32 devices: a whole 2x2x4 slice. The times are simulated.
32 devices in a mesh: groups: 2 (over y), expert: 4 (over x, core), dp: 4 (over z).
Axes of the slice: x: 2, y: 2, z: 4, core: 2. Of those that a mesh axis runs over, the one named last changes fastest.
Arguments:
- tokens: bfloat16 [512, 2048], P(('groups', 'expert', 'dp')), parts along dimension 0, may hold values from -6 to 6
- expert_ids: int32 [512, 8], P(('groups', 'expert', 'dp')), parts along dimension 0, may hold values from 0 to 15, as said below
- slot_index: int32 [512, 8], P(('groups', 'expert', 'dp')), parts along dimension 0, may hold values from 0 to 15, as said below
- route_weights: bfloat16 [512, 8], P(('groups', 'expert', 'dp')), parts along dimension 0, may hold values from 0.099609375 to 1
- w_gate: bfloat16 [16, 2048, 768], P('expert'), may hold values from -0.125 to 0.125
- w_up: bfloat16 [16, 2048, 768], P('expert'), may hold values from -0.125 to 0.125
- w_down: bfloat16 [16, 768, 2048], P('expert'), may hold values from -0.21875 to 0.21875
- block_masks: int32 [16, 6], P('expert'), may hold values from 0 to 1, as said below
- cotangent: bfloat16 [512, 2048], P(('groups', 'expert', 'dp')), parts along dimension 0, may hold values from -6 to 6
Outputs:
- mixed: bfloat16 [512, 2048], P(('groups', 'expert', 'dp')), parts along dimension 0
- token_grad: bfloat16 [512, 2048], P(('groups', 'expert', 'dp')), parts along dimension 0
- route_grad: float32 [512, 8], P(('groups', 'expert', 'dp')), parts along dimension 0
- grad_gate: float32 [32, 2048, 768], P(('groups', 'expert'), 'dp'), parts along dimension 0
- grad_up: float32 [32, 2048, 768], P(('groups', 'expert'), 'dp'), parts along dimension 0
- grad_down: float32 [32, 768, 2048], P(('groups', 'expert'), None, 'dp'), parts along dimension 0
There are 2 independent parts, one for each index of `groups`. A program takes and returns all parts, laid end to end along the dimension named above; an argument that names none is the same for every part. Nothing has to cross between parts.
Inputs may be any that keep to these rules, and one draw needn't show every extreme that they name: `expert_ids`: each token names 8 different experts. The tokens of one device name any one expert at most 16 times. slot_index[t, k] counts the routes of the same device's tokens to the same expert that come before (t, k) in row-major order of tokens and routes. `block_masks`: each expert keeps 3 to 6 of its 6 blocks.
All inputs are finite; a program needn't handle non-finite values.
Results may differ from a plain program's by a relative error of at most 0.012.
Values may be sent and summed in bfloat16 or wider, within the bound.
No kernel may reach another device: no remote copies, remote signals or barrier semaphores. Data moves between devices by JAX's collectives and lax.ppermute only.
A program may use at most 256 MiB of HBM per device.

v0:
```python
import jax
import jax.numpy as jnp
from jax import lax
from jax.sharding import PartitionSpec as P

BLK = 128


def expand_mask(block_masks):
    return jnp.repeat(block_masks.astype(jnp.float32), BLK, axis=1)


def dense_forward(inbox, w_gate, w_up, w_down, block_masks):
    keep = expand_mask(block_masks)[:, None, :]
    gate_pre = jnp.einsum("erd,edf->erf", inbox, w_gate, preferred_element_type=jnp.float32)
    up_proj = jnp.einsum("erd,edf->erf", inbox, w_up, preferred_element_type=jnp.float32)
    sigma = jax.nn.sigmoid(gate_pre)
    hidden = (gate_pre * sigma * up_proj * keep).astype(jnp.bfloat16)
    outbox = jnp.einsum("erf,efd->erd", hidden, w_down, preferred_element_type=jnp.float32).astype(
        jnp.bfloat16
    )
    return (gate_pre, up_proj, hidden, outbox)


def dense_backward(grad_box, gate_pre, up_proj, w_gate, w_up, w_down, block_masks):
    keep = expand_mask(block_masks)[:, None, :]
    d_hidden = (
        jnp.einsum("erd,efd->erf", grad_box, w_down, preferred_element_type=jnp.float32) * keep
    )
    sigma = jax.nn.sigmoid(gate_pre)
    d_up = (d_hidden * (gate_pre * sigma)).astype(jnp.bfloat16)
    d_gate = (d_hidden * up_proj * sigma * (1.0 + gate_pre * (1.0 - sigma))).astype(jnp.bfloat16)
    d_inbox = (
        jnp.einsum("erf,edf->erd", d_gate, w_gate, preferred_element_type=jnp.float32)
        + jnp.einsum("erf,edf->erd", d_up, w_up, preferred_element_type=jnp.float32)
    ).astype(jnp.bfloat16)
    return (d_gate, d_up, d_inbox)


def expert_forward(inbox, w_gate, w_up, w_down, block_masks):
    return dense_forward(inbox, w_gate, w_up, w_down, block_masks)


def expert_backward(grad_box, gate_pre, up_proj, w_gate, w_up, w_down, block_masks):
    return dense_backward(grad_box, gate_pre, up_proj, w_gate, w_up, w_down, block_masks)


def rounded_term(product):
    rounded = lax.optimization_barrier(product.astype(jnp.bfloat16))
    return rounded.astype(jnp.float32)


def per_device(
    tokens, expert_ids, slot_index, route_weights, w_gate, w_up, w_down, block_masks, cotangent
):
    tok_rows, width = tokens.shape
    top_count = expert_ids.shape[1]
    local_experts = w_gate.shape[0]
    sources = lax.axis_size("expert")
    slot_count = local_experts * sources * tok_rows
    target = (expert_ids * tok_rows + slot_index).reshape(-1)
    hits = (target[None, :] == jnp.arange(slot_count, dtype=jnp.int32)[:, None]).astype(
        jnp.bfloat16
    )
    per_token = jnp.sum(hits.reshape(slot_count, tok_rows, top_count), axis=2)
    sendbox = jnp.dot(per_token, tokens, preferred_element_type=jnp.float32).astype(jnp.bfloat16)
    inbox = lax.all_to_all(
        sendbox.reshape(slot_count // tok_rows, tok_rows, width),
        "expert",
        split_axis=0,
        concat_axis=1,
        tiled=True,
    )
    gate_pre, up_proj, hidden, outbox = expert_forward(inbox, w_gate, w_up, w_down, block_masks)
    returned = lax.all_to_all(outbox, "expert", split_axis=1, concat_axis=0, tiled=True).reshape(
        slot_count, width
    )
    routed = (
        jnp.take(returned, target, axis=0).reshape(tok_rows, top_count, width).astype(jnp.float32)
    )
    weights_f = route_weights.astype(jnp.float32)
    cot_f = cotangent.astype(jnp.float32)
    mixed = jnp.sum(weights_f[:, :, None] * routed, axis=1).astype(jnp.bfloat16)
    route_grad = jnp.sum(cot_f[:, None, :] * routed, axis=2)
    scaled = (weights_f[:, :, None] * cot_f[:, None, :]).astype(jnp.bfloat16).reshape(-1, width)
    grad_send = jnp.dot(hits, scaled, preferred_element_type=jnp.float32).astype(jnp.bfloat16)
    grad_box = lax.all_to_all(
        grad_send.reshape(slot_count // tok_rows, tok_rows, width),
        "expert",
        split_axis=0,
        concat_axis=1,
        tiled=True,
    )
    d_gate, d_up, d_inbox = expert_backward(
        grad_box, gate_pre, up_proj, w_gate, w_up, w_down, block_masks
    )
    d_back = lax.all_to_all(d_inbox, "expert", split_axis=1, concat_axis=0, tiled=True).reshape(
        slot_count, width
    )
    d_routed = (
        jnp.take(d_back, target, axis=0).reshape(tok_rows, top_count, width).astype(jnp.float32)
    )
    token_grad = jnp.sum(d_routed, axis=1).astype(jnp.bfloat16)
    part_gate = rounded_term(
        jnp.einsum("erd,erf->edf", inbox, d_gate, preferred_element_type=jnp.float32)
    )
    part_up = rounded_term(
        jnp.einsum("erd,erf->edf", inbox, d_up, preferred_element_type=jnp.float32)
    )
    part_down = rounded_term(
        jnp.einsum("erf,erd->efd", hidden, grad_box, preferred_element_type=jnp.float32)
    )
    grad_gate, grad_up, grad_down = (
        lax.psum_scatter(
            part_gate.astype(jnp.bfloat16), "dp", scatter_dimension=1, tiled=True
        ).astype(jnp.float32),
        lax.psum_scatter(
            part_up.astype(jnp.bfloat16), "dp", scatter_dimension=1, tiled=True
        ).astype(jnp.float32),
        lax.psum_scatter(
            part_down.astype(jnp.bfloat16), "dp", scatter_dimension=2, tiled=True
        ).astype(jnp.float32),
    )
    return (mixed, token_grad, route_grad, grad_gate, grad_up, grad_down)


def solution(mesh):
    return jax.shard_map(
        per_device,
        mesh=mesh,
        in_specs=(
            P(("groups", "expert", "dp"), None),
            P(("groups", "expert", "dp"), None),
            P(("groups", "expert", "dp"), None),
            P(("groups", "expert", "dp"), None),
            P("expert", None, None),
            P("expert", None, None),
            P("expert", None, None),
            P("expert", None),
            P(("groups", "expert", "dp"), None),
        ),
        out_specs=(
            P(("groups", "expert", "dp"), None),
            P(("groups", "expert", "dp"), None),
            P(("groups", "expert", "dp"), None),
            P(("groups", "expert"), "dp", None),
            P(("groups", "expert"), "dp", None),
            P(("groups", "expert"), None, "dp"),
        ),
        check_vma=False,
    )
```

profile of v0, /device:TPU:0, one launch (start us, length us, event | category | flops | bytes accessed | tf_op | source)
XLA Modules:
  0.0 718.8 jit_solution(2610612757672057709)
XLA Ops:
  7.2 0.7 multiply_add_fusion
  7.9 0.1 copy.45
  8.0 0.1 fusion.10
  8.1 1.4 convolution_convert_fusion.5
  9.6 4.2 all-to-all-start
  13.8 0.1 reshape.60
  13.8 0.7 convert_element_type.82
  14.5 0.8 copy.44
  15.3 0.1 mul.86
  15.4 0.1 broadcast_bitcast_fusion
  15.5 0.9 convert_element_type.88
  16.3 1.5 convolution_convert_fusion.3
  17.8 10.4 %all-to-all-done = bf16[16,16,2048]{2,1,0:T(8,128)(2,1)S(1)} async-done(((bf16[16,16,2048]{2,1,0:T(8,128)(2,1)}), bf16[16,16,2048]{2,1,0:T(8,128)(2,1)S(1)}, u32[]{:S(2)}, u32[]{:S(2)}) %all-to-all-start) | async-done | bytes 1048608 | tf_op jit(solution)/shard_map/all_to_all | solution.py:67
  28.2 4.2 all-to-all-start.2
  32.5 0.1 copy.47
  32.6 6.8 fusion.13
  39.4 1.2 copy-done.2
  40.7 3.0 fusion.12
  43.6 3.4 all-to-all-done.2
  47.0 1.3 copy.51
  48.3 8.8 %multiply_convert_fusion = (bf16[4,64,768]{2,1,0:T(8,128)(2,1)S(1)}, bf16[4,64,768]{2,1,0:T(8,128)(2,1)S(1)}, bf16[4,64,768]{2,1,0:T(8,128)(2,1)S(1)}) fusion(f32[4,64,768]{2,1,0:T(8,128)} %fusion.12, f32[4,64,768]{2,1,0:T(8,128)S(1)} %fusion.13, f32[4,768]{1,0:T(4,128)S(1)} %bitcast.70, bf16[4,64,2048]{2,1,0:T(8,128)(2,1)S(1)} %bitcast.65, ...), kind=kOutput, calls=%fused_computation.18 | convolution fusion | flops 808648704 | bytes 16396288 | tf_op jit(solution)/shard_map/erd,efd->erf/dot_general | solution.py:28
  57.1 6.4 convolution_convert_fusion
  63.6 6.3 convolution_convert_fusion.1
  70.0 0.2 reduce-scatter.4.cloned.1.call-start
  70.2 6.4 convolution_convert_fusion.2
  76.6 6.9 convolution_convert_fusion.4
  83.5 1.8 copy.48
  85.3 3.5 all-to-all-start.1
  88.8 8.6 %fusion.14 = f32[4,64,2048]{2,1,0:T(8,128)S(1)} fusion(bf16[4,64,768]{2,1,0:T(8,128)(2,1)S(1)} %get-tuple-element.32, bf16[4,2048,768]{2,1,0:T(8,128)(2,1)} %param.15), kind=kOutput, calls=%fused_computation.40 | convolution fusion | flops 805306368 | bytes 15073280 | tf_op jit(solution)/shard_map/erf,edf->erd/dot_general | solution.py:34
  97.4 8.6 %fusion = bf16[4,64,2048]{2,1,0:T(8,128)(2,1)S(1)} fusion(f32[4,64,2048]{2,1,0:T(8,128)S(1)} %fusion.14, bf16[4,64,768]{2,1,0:T(8,128)(2,1)S(1)} %get-tuple-element.31, bf16[4,2048,768]{2,1,0:T(8,128)(2,1)} %param.16), kind=kOutput, calls=%fused_computation.7 | convolution fusion | flops 806354944 | bytes 16121856 | tf_op jit(solution)/shard_map/erf,edf->erd/dot_general | solution.py:35
  106.0 1.8 copy.52
  107.8 3.7 all-to-all-start.3
  111.6 0.6 copy.49
  112.2 0.9 gather_fusion
  113.1 0.3 fusion.4
  113.4 0.1 reduce_sum.48
  113.5 0.7 copy.54
  114.1 11.8 %all-to-all-done.3 = bf16[4,64,2048]{2,0,1:T(4,128)(2,1)S(1)} async-done(((bf16[4,64,2048]{2,0,1:T(4,128)(2,1)}), bf16[4,64,2048]{2,0,1:T(4,128)(2,1)S(1)}, u32[]{:S(2)}, u32[]{:S(2)}) %all-to-all-start.3) | async-done | bytes 1048608 | tf_op jit(solution)/shard_map/all_to_all | solution.py:97
  125.9 0.6 copy.53
  126.5 0.9 gather_fusion.1
  127.4 0.9 bitcast_reduce_fusion
  128.4 1.7 fusion.2
  130.1 146.5 %reduce-scatter.8.cloned.1.call-done = bf16[4,768,512]{2,1,0:T(8,128)(2,1)} async-done(((bf16[4,768,2048]{2,1,0:T(8,128)(2,1)}), bf16[4,768,512]{2,1,0:T(8,128)(2,1)}) %reduce-scatter.8.cloned.1.call-update) | async-done | bytes 3145744 | tf_op jit(solution)/shard_map/reduce_scatter | solution.py:120
  276.6 5.5 convert_element_type.100
  282.1 209.8 %reduce-scatter.6.cloned.1.call-done = bf16[4,512,768]{2,1,0:T(8,128)(2,1)} async-done(((bf16[4,2048,768]{2,1,0:T(8,128)(2,1)}), bf16[4,512,768]{2,1,0:T(8,128)(2,1)}) %reduce-scatter.6.cloned.1.call-update) | async-done | bytes 3145744 | tf_op jit(solution)/shard_map/reduce_scatter | solution.py:117
  491.9 5.1 convert_element_type.98
  497.0 210.2 %reduce-scatter.4.cloned.1.call-done = bf16[4,512,768]{2,1,0:T(8,128)(2,1)} async-done(((bf16[4,2048,768]{2,1,0:T(8,128)(2,1)}), bf16[4,512,768]{2,1,0:T(8,128)(2,1)}) %reduce-scatter.4.cloned.1.call-update) | async-done | bytes 3145744 | tf_op jit(solution)/shard_map/reduce_scatter | solution.py:114
  707.2 5.1 convert_element_type.96
  (15 shorter events, 0.2 us)
Async XLA Ops:
  7.2 1.0 copy-start
  9.6 18.7 %all-to-all-start = ((bf16[16,16,2048]{2,1,0:T(8,128)(2,1)}), bf16[16,16,2048]{2,1,0:T(8,128)(2,1)S(1)}, u32[]{:S(2)}, u32[]{:S(2)}) async-start(bf16[16,16,2048]{2,1,0:T(8,128)(2,1)} %bitcast), calls=%async_computation | async-start | bytes 2097152 | tf_op jit(solution)/shard_map/all_to_all | solution.py:67
  28.2 18.8 %all-to-all-start.2 = ((bf16[16,16,2048]{2,1,0:T(8,128)(2,1)}), bf16[16,16,2048]{2,1,0:T(8,128)(2,1)}, u32[]{:S(2)}, u32[]{:S(2)}) async-start(bf16[16,16,2048]{2,1,0:T(8,128)(2,1)} %bitcast.10), calls=%async_computation.2 | async-start | bytes 2097152 | tf_op jit(solution)/shard_map/all_to_all | solution.py:87
  32.5 244.1 %reduce-scatter.8.cloned.1.call-start = ((), (), s32[]{:S(2)}) async-start(), calls=%async_computation.9 | async-start | bytes 15728640 | tf_op jit(solution)/shard_map/reduce_scatter | solution.py:120
  32.5 8.2 %copy-start.2 = (bf16[4,2048,768]{2,1,0:T(8,128)(2,1)S(1)}, bf16[4,2048,768]{2,1,0:T(8,128)(2,1)}, u32[]{:S(2)}) copy-start(bf16[4,2048,768]{2,1,0:T(8,128)(2,1)} %param.15) | copy-start | bytes 37748740
  63.5 428.3 %reduce-scatter.6.cloned.1.call-start = ((), (), s32[]{:S(2)}) async-start(), calls=%async_computation.8 | async-start | bytes 15728640 | tf_op jit(solution)/shard_map/reduce_scatter | solution.py:117
  70.0 637.2 %reduce-scatter.4.cloned.1.call-start = ((), (), s32[]{:S(2)}) async-start(), calls=%async_computation.7 | async-start | bytes 15728640 | tf_op jit(solution)/shard_map/reduce_scatter | solution.py:114
  85.3 22.5 %all-to-all-start.1 = ((bf16[4,64,2048]{2,0,1:T(4,128)(2,1)}), bf16[4,64,2048]{2,0,1:T(4,128)(2,1)S(1)}, u32[]{:S(2)}, u32[]{:S(2)}) async-start(bf16[4,64,2048]{2,0,1:T(4,128)(2,1)} %copy.48), calls=%async_computation.1 | async-start | bytes 2097152 | tf_op jit(solution)/shard_map/all_to_all | solution.py:75
  107.8 18.1 %all-to-all-start.3 = ((bf16[4,64,2048]{2,0,1:T(4,128)(2,1)}), bf16[4,64,2048]{2,0,1:T(4,128)(2,1)S(1)}, u32[]{:S(2)}, u32[]{:S(2)}) async-start(bf16[4,64,2048]{2,0,1:T(4,128)(2,1)} %copy.52), calls=%async_computation.3 | async-start | bytes 2097152 | tf_op jit(solution)/shard_map/all_to_all | solution.py:97
  128.4 583.9 %copy-start.1 = (bf16[16,2048]{1,0:T(8,128)(2,1)S(1)}, bf16[16,2048]{1,0:T(8,128)(2,1)}, u32[]{:S(2)}) copy-start(bf16[16,2048]{1,0:T(8,128)(2,1)} %param.11) | copy-start | bytes 196612
Sparse Core Ops, SparseCore 0:
  63.7 212.8 reduce-scatter.7
  279.0 212.8 reduce-scatter.5
  494.2 212.8 reduce-scatter.3
where the time goes:
time: 720 us; the launch traced here: 719 us
  waiting for transfers between devices  592 us (82%)
  matrix products  64.6 us (9%)
  other arithmetic  21.1 us (3%)
  starting transfers between devices  16 us (2%)
  between operations  13.9 us (2%)
  local copies, waits for them, and re-layouts  11.1 us (2%)
    reduce_scatter x1, waiting for transfers between devices, per_device(): lax.psum_scatter(part_gate.astype(jnp.bfloat16), 'dp', scatter_dimension=...  210 us
    reduce_scatter x1, waiting for transfers between devices, per_device(): lax.psum_scatter(part_up.astype(jnp.bfloat16), 'dp', scatter_dimension=1,...  210 us
    reduce_scatter x1, waiting for transfers between devices, per_device(): lax.psum_scatter(part_down.astype(jnp.bfloat16), 'dp', scatter_dimension=...  147 us
    convert_element_type x3, other arithmetic, per_device(): grad_gate, grad_up, grad_down = (lax.psum_scatter(part_gate.astype(jnp.bf...  15.7 us
  transfers between devices with their start and end apart: 7, of which 6 were waited for; matrix products, arithmetic and copies ran while one was open for 10% of the time, Pallas kernels for 0%

commit v1 on v0

v1 whole, which is shorter than its diff:
```python
import jax
import jax.numpy as jnp
from jax import lax
from jax.sharding import PartitionSpec as P

BLK = 128
LANES = 128


def round_up(value, unit):
    return -(-value // unit) * unit


def per_device(
    tokens, expert_ids, slot_index, route_weights, w_gate, w_up, w_down, block_masks, cotangent
):
    rows, width = tokens.shape
    local_experts, _, hidden_units = w_gate.shape
    experts = local_experts * lax.axis_size("expert")
    here, column = lax.axis_index("expert"), lax.axis_index("dp")
    chosen = expert_ids[:, :, None] == jnp.arange(experts, dtype=jnp.int32)
    dense = jnp.sum(jnp.where(chosen, route_weights[:, :, None].astype(jnp.float32), 0.0), axis=1)
    pad = round_up(experts, LANES) - experts
    dense = jnp.pad(dense, ((0, 0), (0, pad))).astype(jnp.bfloat16)
    packet = jnp.concatenate([tokens, cotangent, dense], axis=1)
    everyone = lax.all_gather(packet, ("dp", "expert"), axis=0, tiled=True)
    x, cot = everyone[:, :width], everyone[:, width : 2 * width]
    weights = lax.dynamic_slice_in_dim(
        everyone, 2 * width + here * local_experts, local_experts, axis=1
    ).astype(jnp.float32)
    weights = weights.T[:, :, None]
    keep = jnp.repeat(block_masks.astype(jnp.float32), BLK, axis=1)[:, None, :]

    gate_pre = jnp.einsum("td,edf->etf", x, w_gate, preferred_element_type=jnp.float32)
    up_proj = jnp.einsum("td,edf->etf", x, w_up, preferred_element_type=jnp.float32)
    back = jnp.einsum("td,efd->etf", cot, w_down, preferred_element_type=jnp.float32) * keep
    sigma = jax.nn.sigmoid(gate_pre)
    silu = gate_pre * sigma
    hidden = silu * up_proj * keep
    own = lax.axis_size("expert") * rows
    inner = lax.dynamic_slice_in_dim(jnp.sum(hidden * back, axis=2), column * own, own, axis=1)
    hidden = (hidden * weights).astype(jnp.bfloat16)
    d_hidden = back * weights
    d_up = (d_hidden * silu).astype(jnp.bfloat16)
    d_gate = (d_hidden * up_proj * sigma * (1.0 + gate_pre * (1.0 - sigma))).astype(jnp.bfloat16)

    def mine(array):
        return lax.dynamic_slice_in_dim(array, column * own, own, axis=1)

    mixed = jnp.einsum("etf,efd->td", mine(hidden), w_down, preferred_element_type=jnp.float32)
    token_grad = jnp.einsum(
        "etf,edf->td", mine(d_gate), w_gate, preferred_element_type=jnp.float32
    ) + jnp.einsum("etf,edf->td", mine(d_up), w_up, preferred_element_type=jnp.float32)
    inner = jnp.pad(inner.T, ((0, 0), (0, LANES // 2 - local_experts)))
    high = inner.astype(jnp.bfloat16)
    low = (inner - high.astype(jnp.float32)).astype(jnp.bfloat16)
    back_packet = jnp.concatenate(
        [mixed.astype(jnp.bfloat16), token_grad.astype(jnp.bfloat16), high, low], axis=1
    )
    arrived = lax.all_to_all(back_packet, "expert", split_axis=0, concat_axis=0, tiled=True)
    arrived = arrived.reshape(-1, rows, 2 * width + LANES).astype(jnp.float32)
    total = jnp.sum(arrived[:, :, : 2 * width], axis=0).astype(jnp.bfloat16)
    tail = arrived[:, :, 2 * width :]
    inner = tail[:, :, :local_experts] + tail[:, :, LANES // 2 : LANES // 2 + local_experts]
    inner = inner.transpose(1, 0, 2).reshape(rows, experts)
    route_grad = jnp.sum(jnp.where(chosen, inner[:, None, :], 0.0), axis=2)

    part = width // lax.axis_size("dp")
    x_part = lax.dynamic_slice_in_dim(x, column * part, part, axis=1)
    cot_part = lax.dynamic_slice_in_dim(cot, column * part, part, axis=1)
    grad_gate = jnp.einsum("td,etf->edf", x_part, d_gate, preferred_element_type=jnp.float32)
    grad_up = jnp.einsum("td,etf->edf", x_part, d_up, preferred_element_type=jnp.float32)
    grad_down = jnp.einsum("etf,td->efd", hidden, cot_part, preferred_element_type=jnp.float32)
    return (total[:, :width], total[:, width:], route_grad, grad_gate, grad_up, grad_down)


def solution(mesh):
    rows = P(("groups", "expert", "dp"), None)
    experts = P("expert", None, None)
    return jax.shard_map(
        per_device,
        mesh=mesh,
        in_specs=(rows, rows, rows, rows, experts, experts, experts, P("expert", None), rows),
        out_specs=(
            rows,
            rows,
            rows,
            P(("groups", "expert"), "dp", None),
            P(("groups", "expert"), "dp", None),
            P(("groups", "expert"), None, "dp"),
        ),
        check_vma=False,
    )
```

time: 720 us -> 151 us (0.21)
  waiting for transfers between devices: 592 us -> 43.9 us
  other arithmetic: 21.1 us -> 3.64 us
  starting transfers between devices: 16 us -> 3.73 us
  local copies, waits for them, and re-layouts: 11.1 us -> 21.3 us
    reduce_scatter x3 -> x0, waiting for transfers between devices: 566 us -> none  [the longest x1 210 us: per_device(): lax.psum_scatter(part_gate.astype(jnp.bfloat16), 'dp', scatter_dimension=...]
    all_gather x0 -> x1, waiting for transfers between devices: none -> 43.9 us  [per_device(): everyone = lax.all_gather(packet, ('dp', 'expert'), axis=0, tiled=True)]
    all_to_all x4 -> x1, waiting for transfers between devices: 25.6 us -> 0.01 us  [per_device(): lax.all_to_all(back_packet, 'expert', split_axis=0, concat_axis=0, tiled=...]
    convert_element_type x5 -> x3, other arithmetic: 17.3 us -> 0.77 us  [the longest x1 0.69 us: per_device(): keep = jnp.repeat(block_masks.astype(jnp.float32), BLK, axis=1)[:, None, :]]
    unnamed x9 -> x26, local copies, waits for them, and re-layouts: 2.02 us -> 18.1 us
    all_to_all x4 -> x1, starting transfers between devices: 15.7 us -> 3.69 us  [per_device(): lax.all_to_all(back_packet, 'expert', split_axis=0, concat_axis=0, tiled=...]
    dot_general x11 -> x9, matrix products: 64.6 us -> 63.3 us  [the longest x1 10.1 us: per_device(): jnp.einsum('td,edf->etf', x, w_up, preferred_element_type=jnp.float32)]
  transfers between devices with their start and end apart: 7 -> 2, of which waited for: 6 -> 1; matrix products, arithmetic and copies ran while one was open for 10% -> 12% of each run, Pallas kernels for 0% -> 0%
where the time goes in v1:
time: 151 us; the launch traced here: 150 us
  matrix products  63.3 us (42%)
  waiting for transfers between devices  43.9 us (29%)
  local copies, waits for them, and re-layouts  21.3 us (14%)
  between operations  14.1 us (9%)
  starting transfers between devices  3.73 us (2%)
  other arithmetic  3.64 us (2%)
    all_gather x1, waiting for transfers between devices, per_device(): everyone = lax.all_gather(packet, ('dp', 'expert'), axis=0, tiled=True)  43.9 us
    unnamed x26, local copies, waits for them, and re-layouts  18.1 us
    dot_general x1, matrix products, per_device(): jnp.einsum('td,edf->etf', x, w_up, preferred_element_type=jnp.float32)  10.1 us
    dot_general x1, matrix products, per_device(): jnp.einsum('td,edf->etf', x, w_gate, preferred_element_type=jnp.float32)  10.1 us
    dot_general x1, matrix products, per_device(): jnp.einsum('etf,edf->td', mine(d_gate), w_gate, preferred_element_type=jn...  9.52 us
    dot_general x1, matrix products, per_device(): jnp.einsum('td,efd->etf', cot, w_down, preferred_element_type=jnp.float32)  8.89 us
    dot_general x1, matrix products, per_device(): jnp.einsum('etf,efd->td', mine(hidden), w_down, preferred_element_type=jn...  6.87 us
    dot_general x1, matrix products, per_device(): jnp.einsum('etf,edf->td', mine(d_up), w_up, preferred_element_type=jnp.fl...  4.92 us
  transfers between devices with their start and end apart: 2, of which 1 were waited for; matrix products, arithmetic and copies ran while one was open for 12% of the time, Pallas kernels for 0%

profile of v1, /device:TPU:0, one launch (start us, length us, event | category | flops | bytes accessed | tf_op | source)
XLA Modules:
  0.0 150.0 jit_solution(14067634362220081191)
XLA Ops:
  7.2 0.0 all-gather.2.cloned.1.call-start
  7.2 0.8 copy.46
  8.0 0.8 copy.47
  8.7 0.1 select_reduce_fusion.1
  8.8 1.5 %fusion.29 = bf16[16,4224]{1,0:T(8,128)(2,1)} fusion(bf16[16,16]{1,0:T(8,128)(2,1)S(1)} %select_reduce_fusion.1, bf16[16,2048]{1,0:T(8,128)(2,1)} %param.16, bf16[16,2048]{1,0:T(8,128)(2,1)} %param.9), kind=kLoop, calls=%fused_computation.45 | loop fusion | flops 540672 | bytes 266752 | tf_op jit(solution)/shard_map/concatenate | solution.py:25
  10.4 0.0 all-gather.2.cloned.1.call-update
  10.4 0.7 convert_element_type.44
  11.1 0.1 broadcast_bitcast_fusion
  11.2 43.9 %all-gather.2.cloned.1.call-done = bf16[256,4224]{1,0:T(8,128)(2,1)} async-done(((bf16[16,4224]{1,0:T(8,128)(2,1)}), bf16[256,4224]{1,0:T(8,128)(2,1)}) %all-gather.2.cloned.1.call-update) | async-done | bytes 2162704 | tf_op jit(solution)/shard_map/all_gather | solution.py:26
  55.1 0.9 convert_bitcast_fusion
  56.0 0.1 copy.48
  56.1 10.1 %fusion.14 = f32[256,4,768]{2,0,1:T(8,128)} fusion(bf16[4,2048,768]{2,1,0:T(8,128)(2,1)} %param.13, bf16[256,4224]{1,0:T(8,128)(2,1)} %all-gather.2.cloned.1.call-done), kind=kOutput, calls=%fused_computation.29 | convolution fusion | flops 3221225472 | bytes 16777216 | tf_op jit(solution)/shard_map/td,edf->etf/dot_general | solution.py:35
  66.2 10.1 %fusion.16 = f32[256,4,768]{2,0,1:T(8,128)} fusion(bf16[4,2048,768]{2,1,0:T(8,128)(2,1)} %param.12, bf16[256,4224]{1,0:T(8,128)(2,1)} %all-gather.2.cloned.1.call-done), kind=kOutput, calls=%fused_computation.31 | convolution fusion | flops 3221225472 | bytes 16777216 | tf_op jit(solution)/shard_map/td,edf->etf/dot_general | solution.py:34
  76.3 0.0 slice-done.3
  76.3 0.0 slice-done.4
  76.3 0.0 slice-done.5
  76.3 8.9 %fusion = (f32[4,256]{1,0:T(4,128)S(1)}, bf16[4,256,768]{2,1,0:T(8,128)(2,1)}, bf16[4,256,768]{2,1,0:T(8,128)(2,1)S(1)}, bf16[4,256,768]{2,1,0:T(8,128)(2,1)S(1)}) fusion(f32[4,768]{1,0:T(4,128)S(1)} %bitcast.110, f32[256,4,768]{2,0,1:T(8,128)} %fusion.14, f32[256,4,768]{2,0,1:T(8,128)} %fusion.16, f32[4,256]{1,0:T(4,128)S(1)} %copy.48, ...), kind=kOutput, calls=%fused_computation.2 | convolution fusion | flops 3237739520 | bytes 24674304 | tf_op jit(solution)/shard_map/td,efd->etf/dot_general | solution.py:36
  85.2 0.1 constant_dynamic-slice_fusion
  85.3 0.1 copy.65
  85.4 0.0 copy-start.1
  85.4 9.5 %convolution_bitcast_fusion.3 = f32[64,2048]{1,0:T(8,128)} fusion(bf16[4,2048,768]{2,1,0:T(8,128)(2,1)} %param.12, bf16[4,256,768]{2,1,0:T(8,128)(2,1)} %get-tuple-element.31, s32[]{:T(128)S(6)} %select_n.23), kind=kOutput, calls=%fused_computation.22 | convolution fusion | flops 805306368 | bytes 13500420 | tf_op jit(solution)/shard_map/etf,edf->td/dot_general | solution.py:51
  95.0 0.0 copy-done.1
  95.0 1.2 fusion.40
  96.2 0.6 copy-done
  96.8 4.2 %convolution_bitcast_fusion.1 = f32[4,512,768]{1,2,0:T(8,128)} fusion(bf16[4,256,768]{2,1,0:T(8,128)(2,1)S(1)} %copy-done, bf16[256,2048]{1,0:T(8,128)(2,1)S(1)} %get-tuple-element.35, s32[]{:T(128)S(6)} %select_n.25), kind=kOutput, calls=%fused_computation.19 | convolution fusion | flops 805306368 | bytes 8126468 | tf_op jit(solution)/shard_map/td,etf->edf/dot_general | solution.py:71
  101.0 3.9 %convolution_bitcast_fusion = f32[4,512,768]{1,2,0:T(8,128)} fusion(bf16[4,256,768]{2,1,0:T(8,128)(2,1)S(1)} %get-tuple-element.33, bf16[256,2048]{1,0:T(8,128)(2,1)S(1)} %get-tuple-element.35, s32[]{:T(128)S(6)} %select_n.25), kind=kOutput, calls=%fused_computation.18 | convolution fusion | flops 805306368 | bytes 8126468 | tf_op jit(solution)/shard_map/td,etf->edf/dot_general | solution.py:72
  104.9 0.0 slice-done
  104.9 0.0 slice-done.1
  104.9 0.6 slice-done.2
  105.5 4.9 %fusion.10 = bf16[64,2048]{1,0:T(8,128)(2,1)S(1)} fusion(f32[64,2048]{1,0:T(8,128)} %convolution_bitcast_fusion.3, bf16[4,2048,768]{2,1,0:T(8,128)(2,1)S(1)} %bitcast.104, bf16[4,256,768]{2,1,0:T(8,128)(2,1)S(1)} %get-tuple-element.33, s32[]{:T(128)S(6)} %select_n.23), kind=kOutput, calls=%fused_computation.24 | convolution fusion | flops 805568512 | bytes 13762564 | tf_op jit(solution)/shard_map/etf,edf->td/dot_general | solution.py:53
  110.4 6.9 %fusion.11 = bf16[64,2048]{1,0:T(8,128)(2,1)S(1)} fusion(bf16[4,768,2048]{2,1,0:T(8,128)(2,1)} %param.14, bf16[4,256,768]{2,1,0:T(8,128)(2,1)S(1)} %get-tuple-element.32, s32[]{:T(128)S(6)} %select_n.23), kind=kOutput, calls=%fused_computation.25 | convolution fusion | flops 805437440 | bytes 13238276 | tf_op jit(solution)/shard_map/etf,efd->td/dot_general | solution.py:50
  117.3 0.9 concatenate.7
  118.3 3.7 %all-to-all-start = ((bf16[4,16,4224]{2,1,0:T(8,128)(2,1)}), bf16[4,16,4224]{2,1,0:T(8,128)(2,1)S(1)}, u32[]{:S(2)}, u32[]{:S(2)}) async-start(bf16[4,16,4224]{2,1,0:T(8,128)(2,1)} %bitcast.10), calls=%async_computation | async-start | bytes 1081344 | tf_op jit(solution)/shard_map/all_to_all | solution.py:60
  122.0 6.6 %copy.59 = f32[4,512,768]{2,1,0:T(8,128)} copy(f32[4,512,768]{1,2,0:T(8,128)} %convolution_bitcast_fusion.1) | data formatting | bytes 12582912
  128.5 6.6 %copy.60 = f32[4,512,768]{2,1,0:T(8,128)} copy(f32[4,512,768]{1,2,0:T(8,128)} %convolution_bitcast_fusion) | data formatting | bytes 12582912
  135.1 4.7 %fusion.22 = f32[4,768,512]{2,1,0:T(8,128)} fusion(bf16[4,256,768]{2,1,0:T(8,128)(2,1)S(1)} %get-tuple-element.32, bf16[256,2048]{1,0:T(8,128)(2,1)} %get-tuple-element.34, s32[]{:T(128)S(6)} %select_n.25), kind=kOutput, calls=%fused_computation.38 | convolution fusion | flops 805306368 | bytes 8126468 | tf_op jit(solution)/shard_map/etf,td->efd/dot_general | solution.py:73
  139.7 0.0 all-to-all-done
  139.8 0.1 convert_element_type.53
  139.8 0.1 slice_reduce_fusion
  139.9 0.1 fusion.30
  140.0 0.5 copy.64
  140.4 0.1 fusion.41
  140.5 0.8 copy.56
  141.3 0.8 copy.57
  142.2 0.1 copy.51
  142.2 0.1 copy.52
  142.3 0.2 select_reduce_fusion
  142.5 0.7 copy.58
  (12 shorter events, 0.0 us)
Async XLA Ops:
  7.2 47.9 %all-gather.2.cloned.1.call-start = ((), (), s32[]{:S(2)}) async-start(), calls=%async_computation.1 | async-start | bytes 2297856 | tf_op jit(solution)/shard_map/all_gather | solution.py:26
  56.1 20.3 %slice-start.3 = ((s8[12582912]{0:T(1024)(128)(4,1)}), s8[4194304]{0:T(1024)(128)(4,1)S(1)}, s32[]{:S(2)}) async-start(s8[12582912]{0:T(1024)(128)(4,1)} %bitcast.105), calls=%async_computation.5 | async-start | bytes 8388608
  56.1 20.3 %slice-start.4 = ((s8[12582912]{0:T(1024)(128)(4,1)}), s8[4194304]{0:T(1024)(128)(4,1)S(1)}, s32[]{:S(2)}) async-start(s8[12582912]{0:T(1024)(128)(4,1)} %bitcast.105), calls=%async_computation.6 | async-start | bytes 8388608
  66.2 10.1 %slice-start.5 = ((s8[12582912]{0:T(1024)(128)(4,1)}), s8[4194304]{0:T(1024)(128)(4,1)S(1)}, s32[]{:S(2)}) async-start(s8[12582912]{0:T(1024)(128)(4,1)} %bitcast.105), calls=%async_computation.7 | async-start | bytes 8388608
  85.4 9.5 %copy-start.1 = (bf16[256,4224]{1,0:T(8,128)(2,1)S(1)}, bf16[256,4224]{1,0:T(8,128)(2,1)}, u32[]{:S(2)}) copy-start(bf16[256,4224]{1,0:T(8,128)(2,1)} %all-gather.2.cloned.1.call-done) | copy-start | bytes 6488068
  95.0 1.8 %copy-start = (bf16[4,256,768]{2,1,0:T(8,128)(2,1)S(1)}, bf16[4,256,768]{2,1,0:T(8,128)(2,1)}, u32[]{:S(2)}) copy-start(bf16[4,256,768]{2,1,0:T(8,128)(2,1)} %get-tuple-element.31) | copy-start | bytes 4718596
  96.8 8.1 %slice-start = ((s8[12582912]{0:T(1024)(128)(4,1)}), s8[4194304]{0:T(1024)(128)(4,1)S(1)}, s32[]{:S(2)}) async-start(s8[12582912]{0:T(1024)(128)(4,1)} %bitcast.103), calls=%async_computation.2 | async-start | bytes 8388608
  96.8 8.1 %slice-start.1 = ((s8[12582912]{0:T(1024)(128)(4,1)}), s8[4194304]{0:T(1024)(128)(4,1)S(1)}, s32[]{:S(2)}) async-start(s8[12582912]{0:T(1024)(128)(4,1)} %bitcast.103), calls=%async_computation.3 | async-start | bytes 8388608
  101.0 4.5 %slice-start.2 = ((s8[12582912]{0:T(1024)(128)(4,1)}), s8[4194304]{0:T(1024)(128)(4,1)S(1)}, s32[]{:S(2)}) async-start(s8[12582912]{0:T(1024)(128)(4,1)} %bitcast.103), calls=%async_computation.4 | async-start | bytes 8388608
  118.3 21.5 %all-to-all-start = ((bf16[4,16,4224]{2,1,0:T(8,128)(2,1)}), bf16[4,16,4224]{2,1,0:T(8,128)(2,1)S(1)}, u32[]{:S(2)}, u32[]{:S(2)}) async-start(bf16[4,16,4224]{2,1,0:T(8,128)(2,1)} %bitcast.10), calls=%async_computation | async-start | bytes 1081344 | tf_op jit(solution)/shard_map/all_to_all | solution.py:60
Sparse Core Ops, SparseCore 0:
  10.8 44.1 all-gather.1

commit v2 on v1

v2 whole, which is shorter than its diff:
```python
import functools

import jax
import jax.numpy as jnp
from jax import lax
from jax.experimental import pallas as pl
from jax.experimental.pallas import tpu as pltpu
from jax.sharding import PartitionSpec as P

BLK = 128
LANES = 128
CHUNK = 256
WIDE = 512
MIB = 1 << 20

VMEM = pl.BlockSpec(memory_space=pltpu.VMEM)
SMEM = pl.BlockSpec(memory_space=pltpu.SMEM)
ANY = pl.BlockSpec(memory_space=pl.ANY)

NN = (((1,), (0,)), ((), ()))
NT = (((1,), (1,)), ((), ()))
TN = (((0,), (0,)), ((), ()))


def dot(a, b, dims):
    return lax.dot_general(a, b, dims, preferred_element_type=jnp.float32)


def lane_ids(rows, lanes):
    return lax.broadcasted_iota(jnp.int32, (rows, lanes), 1)


def pack_kernel(tokens, cotangent, expert_ids, route_weights, packet):
    rows, width = tokens.shape
    lanes = packet.shape[1] - 2 * width
    packet[:, :width] = tokens[...]
    packet[:, width : 2 * width] = cotangent[...]
    at = lane_ids(rows, lanes)
    values = route_weights[...].astype(jnp.float32)
    dense = jnp.zeros((rows, lanes), jnp.float32)
    for k in range(expert_ids.shape[1]):
        dense += jnp.where(expert_ids[:, k : k + 1] == at, values[:, k : k + 1], 0.0)
    packet[:, 2 * width :] = dense.astype(packet.dtype)


def load_kernel(*refs):
    count = len(refs) // 2
    sems = refs[-1]
    copies = [
        pltpu.make_async_copy(refs[i], refs[count + i], sems.at[i]) for i in range(count)
    ]
    for copy in copies:
        copy.start()
    for copy in copies:
        copy.wait()


def hidden_terms(x, cot, weights, masks, w_gate, w_up, w_down, expert, start):
    cols = pl.ds(start, CHUNK)
    gate_pre = dot(x, w_gate[expert, :, cols], NN)
    up_proj = dot(x, w_up[expert, :, cols], NN)
    back = dot(cot, w_down[expert, cols, :], NT)
    at = lane_ids(1, CHUNK)
    keep = jnp.zeros((1, CHUNK), jnp.float32)
    for j in range(CHUNK // BLK):
        kept = masks[expert, start // BLK + j].astype(jnp.float32)
        keep = jnp.where(at // BLK == j, kept, keep)
    sigma = 1.0 / (1.0 + jnp.exp(-gate_pre))
    silu = gate_pre * sigma
    hidden = silu * up_proj * keep
    d_hidden = back * (weights * keep)
    d_up = d_hidden * silu
    d_gate = d_hidden * up_proj * (sigma + silu * (1.0 - sigma))
    inner = jnp.sum(hidden * back, axis=1, keepdims=True)
    bf16 = jnp.bfloat16
    return (hidden * weights).astype(bf16), d_gate.astype(bf16), d_up.astype(bf16), inner


def weight_column(dense, index):
    at = lane_ids(*dense.shape)
    return jnp.sum(jnp.where(at == index, dense, 0.0), axis=1, keepdims=True)


def own_kernel(count, *refs):
    packets, refs = refs[:count], refs[count:]
    masks, w_gate, w_up, w_down, hidden_ref, d_gate_ref, d_up_ref, inner_ref, x, cot = refs
    rows = packets[0].shape[0]
    width = w_gate.shape[1]
    for i, packet in enumerate(packets):
        x[i * rows : (i + 1) * rows] = packet[:, :width]
        cot[i * rows : (i + 1) * rows] = packet[:, width : 2 * width]
    dense = jnp.concatenate([packet[:, 2 * width :].astype(jnp.float32) for packet in packets])
    local_experts, _, hidden_units = w_gate.shape
    base = lax.axis_index("expert") * local_experts
    at = lane_ids(*dense.shape)

    def body(expert, inner):
        weights = weight_column(dense, base + expert)
        total = jnp.zeros((dense.shape[0], 1), jnp.float32)
        for start in range(0, hidden_units, CHUNK):
            hidden, d_gate, d_up, part = hidden_terms(
                x[...], cot[...], weights, masks, w_gate, w_up, w_down, expert, start
            )
            hidden_ref[expert, :, start : start + CHUNK] = hidden
            d_gate_ref[expert, :, start : start + CHUNK] = d_gate
            d_up_ref[expert, :, start : start + CHUNK] = d_up
            total += part
        return inner + jnp.where(at == base + expert, total, 0.0)

    inner = lax.fori_loop(0, local_experts, body, jnp.zeros(dense.shape, jnp.float32))
    high = inner.astype(jnp.bfloat16)
    lanes = dense.shape[1]
    inner_ref[:, :lanes] = high
    inner_ref[:, lanes:] = (inner - high.astype(jnp.float32)).astype(jnp.bfloat16)


def back_kernel(hidden, d_gate, d_up, inner, w_gate, w_up, w_down, *outs):
    local_experts, width, _ = w_gate.shape
    rows = outs[0].shape[0]

    def body(step, carry):
        start = pl.multiple_of(step * WIDE, WIDE)
        cols = pl.ds(start, WIDE)
        mixed = jnp.zeros((hidden.shape[1], WIDE), jnp.float32)
        token_grad = jnp.zeros((hidden.shape[1], WIDE), jnp.float32)
        for e in range(local_experts):
            mixed += dot(hidden[e], w_down[e, :, cols], NN)
            token_grad += dot(d_gate[e], w_gate[e, cols, :], NT)
            token_grad += dot(d_up[e], w_up[e, cols, :], NT)
        for i, out in enumerate(outs):
            block = slice(i * rows, (i + 1) * rows)
            out[:, cols] = mixed[block].astype(out.dtype)
            out[:, pl.ds(start + width, WIDE)] = token_grad[block].astype(out.dtype)
        return carry

    lax.fori_loop(0, width // WIDE, body, 0)
    for i, out in enumerate(outs):
        out[:, 2 * width :] = inner[i * rows : (i + 1) * rows]


def grad_kernel(count, *refs):
    own, others, refs = refs[:count], refs[count : 2 * count], refs[2 * count :]
    hidden_own, d_gate_own, d_up_own, masks, w_gate, w_up, w_down = refs[:7]
    grad_gate, grad_up, grad_down = refs[7:10]
    x, cot, dense, x_part, cot_part, hidden, d_gate, d_up, out_gate, out_up, out_down, sems = refs[
        10:
    ]
    local_experts, width, hidden_units = w_gate.shape
    part = x_part.shape[0]
    rows, more = own[0].shape[0], others[0].shape[0]
    own_rows, other_rows = count * rows, count * more
    column = lax.axis_index("dp")
    base = lax.axis_index("expert") * local_experts
    mine = pl.ds(pl.multiple_of(column * part, part), part)
    theirs = pl.ds(pl.multiple_of(column * part + width, part), part)
    for i in range(count):
        cot_part[i * rows : (i + 1) * rows] = own[i][:, theirs]
        low = i * more
        x[low : low + more] = others[i][:, :width]
        cot[low : low + more] = others[i][:, width : 2 * width]
        dense[low : low + more] = others[i][:, 2 * width :].astype(jnp.float32)
        cot_part[own_rows + low : own_rows + low + more] = others[i][:, theirs]
    every = jnp.concatenate([ref[:, mine] for ref in own + others])
    x_part[...] = every.T
    chunks = hidden_units // CHUNK

    def copies(step, slot):
        expert, start = step // chunks, pl.multiple_of(step % chunks * CHUNK, CHUNK)
        cols = pl.ds(start, CHUNK)
        return [
            pltpu.make_async_copy(out_gate.at[slot], grad_gate.at[expert, :, cols], sems.at[slot, 0]),
            pltpu.make_async_copy(out_up.at[slot], grad_up.at[expert, :, cols], sems.at[slot, 1]),
            pltpu.make_async_copy(out_down.at[slot], grad_down.at[expert, cols, :], sems.at[slot, 2]),
        ]

    tile = other_rows if other_rows <= 256 else 128

    def body(step, carry):
        expert, start = step // chunks, pl.multiple_of(step % chunks * CHUNK, CHUNK)
        cols = pl.ds(start, CHUNK)
        slot = step % 2
        hidden[:own_rows] = hidden_own[expert, :, cols]
        d_gate[:own_rows] = d_gate_own[expert, :, cols]
        d_up[:own_rows] = d_up_own[expert, :, cols]
        for low in range(0, other_rows, tile):
            weights = weight_column(dense[low : low + tile], base + expert)
            terms = hidden_terms(
                x[low : low + tile],
                cot[low : low + tile],
                weights,
                masks,
                w_gate,
                w_up,
                w_down,
                expert,
                start,
            )
            put = slice(own_rows + low, own_rows + low + tile)
            hidden[put], d_gate[put], d_up[put] = terms[:3]

        @pl.when(step >= 2)
        def _():
            for copy in copies(step - 2, slot):
                copy.wait()

        out_gate[slot] = dot(x_part[...], d_gate[...], NN)
        out_up[slot] = dot(x_part[...], d_up[...], NN)
        out_down[slot] = dot(hidden[...], cot_part[...], TN)
        for copy in copies(step, slot):
            copy.start()
        return carry

    steps = local_experts * chunks
    lax.fori_loop(0, steps, body, 0)
    for step in range(max(steps - 2, 0), steps):
        for copy in copies(step, step % 2):
            copy.wait()


def sum_kernel(count, *refs):
    blocks, (expert_ids, mixed, token_grad, route_grad) = refs[:count], refs[count:]
    width = mixed.shape[1]
    lanes = (blocks[0].shape[1] - 2 * width) // 2
    for out, low in ((mixed, 0), (token_grad, width)):
        total = blocks[0][:, low : low + width].astype(jnp.float32)
        for block in blocks[1:]:
            total += block[:, low : low + width].astype(jnp.float32)
        out[...] = total.astype(out.dtype)
    inner = jnp.zeros((mixed.shape[0], lanes), jnp.float32)
    for block in blocks:
        tail = block[:, 2 * width :].astype(jnp.float32)
        inner += tail[:, :lanes] + tail[:, lanes:]
    at = lane_ids(*inner.shape)
    for k in range(expert_ids.shape[1]):
        hit = jnp.where(expert_ids[:, k : k + 1] == at, inner, 0.0)
        route_grad[:, k : k + 1] = jnp.sum(hit, axis=1, keepdims=True)


def shift(value, axis, by):
    size = lax.axis_size(axis)
    return lax.ppermute(value, axis, [(i, (i + by) % size) for i in range(size)])


def cost(flops, moved):
    return pl.CostEstimate(flops=flops, bytes_accessed=moved, transcendentals=0)


def per_device(
    tokens, expert_ids, slot_index, route_weights, w_gate, w_up, w_down, block_masks, cotangent
):
    rows, width = tokens.shape
    local_experts, _, hidden_units = w_gate.shape
    sources, columns = lax.axis_size("expert"), lax.axis_size("dp")
    lanes = -(-local_experts * sources // LANES) * LANES
    bf16, f32 = jnp.bfloat16, jnp.float32
    struct = jax.ShapeDtypeStruct
    one = 2 * local_experts * width * hidden_units

    packet = pl.pallas_call(
        pack_kernel,
        out_shape=struct((rows, 2 * width + lanes), bf16),
        in_specs=[VMEM] * 4,
        out_specs=VMEM,
        compiler_params=pltpu.CompilerParams(vmem_limit_bytes=4 * MIB),
        name="pack",
    )(tokens, cotangent, expert_ids, route_weights)

    same_column = [packet] + [shift(packet, "expert", i) for i in range(1, sources)]
    same_expert = [shift(packet, "dp", i) for i in range(1, columns)]

    weights = (w_gate, w_up, w_down)
    weights = pl.pallas_call(
        load_kernel,
        out_shape=[pltpu.VMEM(w.shape, w.dtype) for w in weights],
        in_specs=[ANY] * 3,
        out_specs=[VMEM] * 3,
        scratch_shapes=[pltpu.SemaphoreType.DMA((3,))],
        cost_estimate=cost(0, 3 * one),
        compiler_params=pltpu.CompilerParams(vmem_limit_bytes=1 * MIB),
        name="load",
    )(*weights)
    weights = [pltpu.with_memory_space_constraint(w, pltpu.VMEM) for w in weights]

    own = sources * rows
    hidden, d_gate, d_up, inner = pl.pallas_call(
        functools.partial(own_kernel, sources),
        out_shape=[struct((local_experts, own, hidden_units), bf16)] * 3
        + [struct((own, 2 * lanes), bf16)],
        in_specs=[VMEM] * sources + [SMEM] + [VMEM] * 3,
        out_specs=[VMEM] * 4,
        scratch_shapes=[pltpu.VMEM((own, width), bf16)] * 2,
        cost_estimate=cost(3 * own * one, 3 * one),
        compiler_params=pltpu.CompilerParams(vmem_limit_bytes=16 * MIB),
        name="own_hidden",
    )(*same_column, block_masks, *weights)

    theirs = jnp.concatenate(same_expert)
    others = [theirs] + [shift(theirs, "expert", i) for i in range(1, sources)]

    partials = pl.pallas_call(
        back_kernel,
        out_shape=[struct((rows, 2 * width + 2 * lanes), bf16)] * sources,
        in_specs=[VMEM] * 7,
        out_specs=[VMEM] * sources,
        cost_estimate=cost(3 * own * one, 3 * one),
        compiler_params=pltpu.CompilerParams(vmem_limit_bytes=16 * MIB),
        name="own_back",
    )(hidden, d_gate, d_up, inner, *weights)
    arrived = [partials[0]] + [shift(partials[i], "expert", -i) for i in range(1, sources)]

    part = width // columns
    other_rows = own * (columns - 1)
    everyone = own * columns
    grad_gate, grad_up, grad_down = pl.pallas_call(
        functools.partial(grad_kernel, sources),
        out_shape=[
            struct((local_experts, part, hidden_units), f32),
            struct((local_experts, part, hidden_units), f32),
            struct((local_experts, hidden_units, part), f32),
        ],
        in_specs=[VMEM] * (2 * sources + 3) + [SMEM] + [VMEM] * 3,
        out_specs=[ANY] * 3,
        scratch_shapes=[
            pltpu.VMEM((other_rows, width), bf16),
            pltpu.VMEM((other_rows, width), bf16),
            pltpu.VMEM((other_rows, lanes), f32),
            pltpu.VMEM((part, everyone), bf16),
            pltpu.VMEM((everyone, part), bf16),
            pltpu.VMEM((everyone, CHUNK), bf16),
            pltpu.VMEM((everyone, CHUNK), bf16),
            pltpu.VMEM((everyone, CHUNK), bf16),
            pltpu.VMEM((2, part, CHUNK), f32),
            pltpu.VMEM((2, part, CHUNK), f32),
            pltpu.VMEM((2, CHUNK, part), f32),
            pltpu.SemaphoreType.DMA((2, 3)),
        ],
        cost_estimate=cost((3 * other_rows + 3 * own) * one, 3 * one),
        compiler_params=pltpu.CompilerParams(vmem_limit_bytes=24 * MIB),
        name="grads",
    )(*same_column, *others, hidden, d_gate, d_up, block_masks, *weights)

    mixed, token_grad, route_grad = pl.pallas_call(
        functools.partial(sum_kernel, sources),
        out_shape=[
            struct((rows, width), bf16),
            struct((rows, width), bf16),
            struct(expert_ids.shape, f32),
        ],
        in_specs=[VMEM] * (sources + 1),
        out_specs=[VMEM] * 3,
        compiler_params=pltpu.CompilerParams(vmem_limit_bytes=4 * MIB),
        name="sum",
    )(*arrived, expert_ids)
    return (mixed, token_grad, route_grad, grad_gate, grad_up, grad_down)


def solution(mesh):
    rows = P(("groups", "expert", "dp"), None)
    experts = P("expert", None, None)
    return jax.shard_map(
        per_device,
        mesh=mesh,
        in_specs=(rows, rows, rows, rows, experts, experts, experts, P("expert", None), rows),
        out_specs=(
            rows,
            rows,
            rows,
            P(("groups", "expert"), "dp", None),
            P(("groups", "expert"), "dp", None),
            P(("groups", "expert"), None, "dp"),
        ),
        check_vma=False,
    )
```

time: 151 us -> 135 us (0.89)
  matrix products: 63.3 us -> 0 us
  Pallas kernels: 0 us -> 53 us
  local copies, waits for them, and re-layouts: 21.3 us -> 56.3 us
  waiting for transfers between devices: 43.9 us -> 9.12 us
  between operations: 14.1 us -> 0.87 us
  starting transfers between devices: 3.73 us -> 15.4 us
  other arithmetic: 3.64 us -> 0 us
    dot_general x9 -> x0, matrix products: 63.3 us -> none  [the longest x1 10.1 us: per_device(): jnp.einsum('td,edf->etf', x, w_up, preferred_element_type=jnp.float32)]
    pallas_call x0 -> x6, Pallas kernels: none -> 53 us  [the longest x1 23.1 us: per_device(): pl.pallas_call(functools.partial(grad_kernel, sources), out_shape=[struct...]
    all_gather x1 -> x0, waiting for transfers between devices: 43.9 us -> none  [per_device(): everyone = lax.all_gather(packet, ('dp', 'expert'), axis=0, tiled=True)]
    unnamed x26 -> x57, local copies, waits for them, and re-layouts: 18.1 us -> 56.2 us
    ppermute x0 -> x12, starting transfers between devices: none -> 15.4 us  [shift(): lax.ppermute(value, axis, [(i, (i + by) % size) for i in range(size)])]
    ppermute x0 -> x12, waiting for transfers between devices: none -> 9.12 us  [shift(): lax.ppermute(value, axis, [(i, (i + by) % size) for i in range(size)])]
    all_to_all x1 -> x0, starting transfers between devices: 3.69 us -> none  [per_device(): lax.all_to_all(back_packet, 'expert', split_axis=0, concat_axis=0, tiled=...]
    concatenate x1 -> x0, other arithmetic: 1.54 us -> none  [per_device(): packet = jnp.concatenate([tokens, cotangent, dense], axis=1)]
  transfers between devices with their start and end apart: 2 -> 12, of which waited for: 1 -> 4; matrix products, arithmetic and copies ran while one was open for 12% -> 1% of each run, Pallas kernels for 0% -> 22%
where the time goes in v2:
time: 135 us
  local copies, waits for them, and re-layouts  56.3 us (42%)
  Pallas kernels  53 us (39%)
  starting transfers between devices  15.4 us (11%)
  waiting for transfers between devices  9.12 us (7%)
    unnamed x57, local copies, waits for them, and re-layouts  56.2 us
    pallas_call x1, Pallas kernels, per_device(): pl.pallas_call(functools.partial(grad_kernel, sources), out_shape=[struct...  23.1 us
    ppermute x12, starting transfers between devices, shift(): lax.ppermute(value, axis, [(i, (i + by) % size) for i in range(size)])  15.4 us
    pallas_call x1, Pallas kernels, per_device(): pl.pallas_call(back_kernel, out_shape=[struct((rows, 2 * width + 2 * lane...  10.3 us
    pallas_call x1, Pallas kernels, per_device(): pl.pallas_call(functools.partial(own_kernel, sources), out_shape=[struct(...  9.57 us
    ppermute x12, waiting for transfers between devices, shift(): lax.ppermute(value, axis, [(i, (i + by) % size) for i in range(size)])  9.12 us
    pallas_call x1, Pallas kernels, per_device(): pl.pallas_call(load_kernel, out_shape=[pltpu.VMEM(w.shape, w.dtype) for w...  9.01 us
  transfers between devices with their start and end apart: 12, of which 4 were waited for; matrix products, arithmetic and copies ran while one was open for 1% of the time, Pallas kernels for 22%

profile of v2, /device:TPU:0, one launch (start us, length us, event | category | flops | bytes accessed | tf_op | source)
XLA Modules:
  0.0 134.7 jit_solution(1643635050069954529)
XLA Ops:
  0.6 0.8 copy.14.expert_ids.refs_4_
  1.4 0.8 copy.15.route_weights
  2.1 0.8 copy-done.19
  3.0 0.8 copy-done.20
  3.8 0.1 pack.1.refs_0_
  3.9 3.1 %collective-permute-start.6 = (bf16[16,4224]{1,0:T(8,128)(2,1)S(1)}, bf16[16,4224]{1,0:T(8,128)(2,1)S(1)}, u32[]{:S(2)}, u32[]{:S(2)}) collective-permute-start(bf16[16,4224]{1,0:T(8,128)(2,1)S(1)} %pack.1.refs_0_), channel_id=1, source_target_pairs={{0,1},{1,2},{2,3},{3,0},{4,5},{5,6},{6,7},{7,4},{8,9},{9,10},{10,1... | collective-permute-start | bytes 405512 | tf_op jit(solution)/shard_map/ppermute | solution.py:241
  7.0 0.0 collective-permute-start
  7.0 1.5 %collective-permute-start.1 = (bf16[16,4224]{1,0:T(8,128)(2,1)S(1)}, bf16[16,4224]{1,0:T(8,128)(2,1)S(1)}, u32[]{:S(2)}, u32[]{:S(2)}) collective-permute-start(bf16[16,4224]{1,0:T(8,128)(2,1)S(1)} %pack.1.refs_0_), channel_id=1, source_target_pairs={{0,8},{4,12},{8,0},{12,4},{1,9},{5,13},{9,1},{13,5},{2,10},{6,14},... | collective-permute-start | bytes 405512 | tf_op jit(solution)/shard_map/ppermute | solution.py:241
  8.5 1.4 %collective-permute-start.2 = (bf16[16,4224]{1,0:T(8,128)(2,1)S(1)}, bf16[16,4224]{1,0:T(8,128)(2,1)S(1)}, u32[]{:S(2)}, u32[]{:S(2)}) collective-permute-start(bf16[16,4224]{1,0:T(8,128)(2,1)S(1)} %pack.1.refs_0_), channel_id=1, source_target_pairs={{0,12},{4,0},{8,4},{12,8},{1,13},{5,1},{9,5},{13,9},{2,14},{6,2},{... | collective-permute-start | bytes 405512 | tf_op jit(solution)/shard_map/ppermute | solution.py:241
  10.0 2.6 %collective-permute-start.7 = (bf16[16,4224]{1,0:T(8,128)(2,1)S(1)}, bf16[16,4224]{1,0:T(8,128)(2,1)S(1)}, u32[]{:S(2)}, u32[]{:S(2)}) collective-permute-start(bf16[16,4224]{1,0:T(8,128)(2,1)S(1)} %pack.1.refs_0_), channel_id=1, source_target_pairs={{0,2},{1,3},{2,0},{3,1},{4,6},{5,7},{6,4},{7,5},{8,10},{9,11},{10,... | collective-permute-start | bytes 405512 | tf_op jit(solution)/shard_map/ppermute | solution.py:241
  12.6 4.6 %copy-done.11 = bf16[4,2048,768]{2,1,0:T(8,128)(2,1)S(1)} copy-done((bf16[4,2048,768]{2,1,0:T(8,128)(2,1)S(1)}, bf16[4,2048,768]{2,1,0:T(8,128)(2,1)}, u32[]{:S(2)}) %copy-start.11) | copy-done | bytes 12582936
  17.1 9.0 %load.1 = (bf16[4,2048,768]{2,1,0:T(8,128)(2,1)S(1)}, bf16[4,2048,768]{2,1,0:T(8,128)(2,1)S(1)}, bf16[4,768,2048]{2,1,0:T(8,128)(2,1)S(1)}) custom-call(bf16[4,2048,768]{2,1,0:T(8,128)(2,1)S(1)} %copy-done.11, bf16[4,2048,768]{2,1,0:T(8,128)(2,1)} %refs_1_.1, bf16[4,768,2048]{2,1,0:T(8,128)(2,1)} %refs_2_.1), custom_call_target="tpu_custom_call" | custom-call | bytes 37748736 | tf_op jit(solution)/shard_map/load/pallas_call | solution.py:272
  26.2 4.5 %copy-done = bf16[4,2048,768]{2,1,0:T(8,128)(2,1)} copy-done((bf16[4,2048,768]{2,1,0:T(8,128)(2,1)}, bf16[4,2048,768]{2,1,0:T(8,128)(2,1)S(1)}, u32[]{:S(2)}) %copy-start) | copy-done | bytes 12582936
  30.7 4.5 %copy-done.4 = bf16[4,2048,768]{2,1,0:T(8,128)(2,1)} copy-done((bf16[4,2048,768]{2,1,0:T(8,128)(2,1)}, bf16[4,2048,768]{2,1,0:T(8,128)(2,1)S(1)}, u32[]{:S(2)}) %copy-start.4) | copy-done | bytes 12582936
  35.2 0.0 collective-permute-done.6
  35.2 1.3 %collective-permute-start.8 = (bf16[16,4224]{1,0:T(8,128)(2,1)S(1)}, bf16[16,4224]{1,0:T(8,128)(2,1)S(1)}, u32[]{:S(2)}, u32[]{:S(2)}) collective-permute-start(bf16[16,4224]{1,0:T(8,128)(2,1)S(1)} %pack.1.refs_0_), channel_id=1, source_target_pairs={{0,3},{1,0},{2,1},{3,2},{4,7},{5,4},{6,5},{7,6},{8,11},{9,8},{10,9... | collective-permute-start | bytes 405512 | tf_op jit(solution)/shard_map/ppermute | solution.py:241
  36.6 0.0 collective-permute-done.7
  36.6 3.6 %collective-permute-done.8 = bf16[16,4224]{1,0:T(8,128)(2,1)S(1)} collective-permute-done((bf16[16,4224]{1,0:T(8,128)(2,1)S(1)}, bf16[16,4224]{1,0:T(8,128)(2,1)S(1)}, u32[]{:S(2)}, u32[]{:S(2)}) %collective-permute-start.8) | collective-permute-done | bytes 135200 | tf_op jit(solution)/shard_map/ppermute | solution.py:241
  40.3 0.7 collective-permute-start.10
  40.9 0.0 collective-permute-start.11
  41.0 0.0 collective-permute-done.refs_1_
  41.0 0.5 collective-permute-start.9
  41.5 0.0 collective-permute-done.1.refs_2_
  41.5 0.0 collective-permute-done.2.refs_3_
  41.5 4.6 %copy-done.1 = bf16[4,2048,768]{2,1,0:T(8,128)(2,1)S(1)} copy-done((bf16[4,2048,768]{2,1,0:T(8,128)(2,1)S(1)}, bf16[4,2048,768]{2,1,0:T(8,128)(2,1)}, u32[]{:S(2)}) %copy-start.1) | copy-done | bytes 12582936
  46.2 4.6 %copy-done.5 = bf16[4,2048,768]{2,1,0:T(8,128)(2,1)S(1)} copy-done((bf16[4,2048,768]{2,1,0:T(8,128)(2,1)S(1)}, bf16[4,2048,768]{2,1,0:T(8,128)(2,1)}, u32[]{:S(2)}) %copy-start.5) | copy-done | bytes 12582936
  50.7 9.6 %own_hidden.1 = (bf16[4,64,768]{2,1,0:T(8,128)(2,1)S(1)}, bf16[4,64,768]{2,1,0:T(8,128)(2,1)S(1)}, bf16[4,64,768]{2,1,0:T(8,128)(2,1)S(1)}, bf16[64,256]{1,0:T(8,128)(2,1)S(1)}) custom-call(bf16[16,4224]{1,0:T(8,128)(2,1)S(1)} %pack.1.refs_0_, bf16[16,4224]{1,0:T(8,128)(2,1)S(1)} %collective-permute-done.refs_1_, ...), custom_call_target="tpu_custom_call" | custom-call | flops 2415919104 | bytes 37748736 | tf_op jit(solution)/shard_map/own_hidden/pallas_call | solution.py:285
  60.4 5.0 %copy-done.2 = bf16[4,2048,768]{2,1,0:T(8,128)(2,1)S(1)} copy-done((bf16[4,2048,768]{2,1,0:T(8,128)(2,1)S(1)}, bf16[4,2048,768]{2,1,0:T(8,128)(2,1)}, u32[]{:S(2)}) %copy-start.2) | copy-done | bytes 12582936
  65.4 4.6 %copy-done.6 = bf16[4,2048,768]{2,1,0:T(8,128)(2,1)S(1)} copy-done((bf16[4,2048,768]{2,1,0:T(8,128)(2,1)S(1)}, bf16[4,2048,768]{2,1,0:T(8,128)(2,1)}, u32[]{:S(2)}) %copy-start.6) | copy-done | bytes 12582936
  70.0 4.6 %copy-done.9 = bf16[4,768,2048]{2,1,0:T(8,128)(2,1)S(1)} copy-done((bf16[4,768,2048]{2,1,0:T(8,128)(2,1)S(1)}, bf16[4,768,2048]{2,1,0:T(8,128)(2,1)}, u32[]{:S(2)}) %copy-start.9) | copy-done | bytes 12582936
  74.5 10.3 %own_back.1 = (bf16[16,4352]{1,0:T(8,128)(2,1)S(1)}, bf16[16,4352]{1,0:T(8,128)(2,1)S(1)}, bf16[16,4352]{1,0:T(8,128)(2,1)S(1)}, bf16[16,4352]{1,0:T(8,128)(2,1)S(1)}) custom-call(bf16[4,64,768]{2,1,0:T(8,128)(2,1)S(1)} %get-tuple-element.26.hidden.refs_8_, bf16[4,64,768]{2,1,0:T(8,128)(2,1)S(1)} %get-tuple-element.27.d_gate.refs_9_, ...), custom_call_target="tpu_custom_call" | custom-call | flops 2415919104 | bytes 37748736 | tf_op jit(solution)/shard_map/own_back/pallas_call | solution.py:300
  84.8 1.3 collective-permute-start.3
  86.2 1.4 %collective-permute-start.4 = (bf16[16,4352]{1,0:T(8,128)(2,1)S(1)}, bf16[16,4352]{1,0:T(8,128)(2,1)S(1)}, u32[]{:S(2)}, u32[]{:S(2)}) collective-permute-start(bf16[16,4352]{1,0:T(8,128)(2,1)S(1)} %get-tuple-element.32), channel_id=1, source_target_pairs={{0,8},{4,12},{8,0},{12,4},{1,9},{5,13},{9,1},{13,5},{2,10},{6,14},... | collective-permute-start | bytes 417800 | tf_op jit(solution)/shard_map/ppermute | solution.py:241
  87.6 2.3 %collective-permute-done.3.refs_1_ = bf16[16,4352]{1,0:T(8,128)(2,1)S(1)} collective-permute-done((bf16[16,4352]{1,0:T(8,128)(2,1)S(1)}, bf16[16,4352]{1,0:T(8,128)(2,1)S(1)}, u32[]{:S(2)}, u32[]{:S(2)}) %collective-permute-start.3) | collective-permute-done | bytes 139296 | tf_op jit(solution)/shard_map/ppermute | solution.py:241
  89.9 1.5 %collective-permute-start.5 = (bf16[16,4352]{1,0:T(8,128)(2,1)S(1)}, bf16[16,4352]{1,0:T(8,128)(2,1)S(1)}, u32[]{:S(2)}, u32[]{:S(2)}) collective-permute-start(bf16[16,4352]{1,0:T(8,128)(2,1)S(1)} %get-tuple-element.33), channel_id=1, source_target_pairs={{0,4},{4,8},{8,12},{12,0},{1,5},{5,9},{9,13},{13,1},{2,6},{6,10},{... | collective-permute-start | bytes 417800 | tf_op jit(solution)/shard_map/ppermute | solution.py:241
  91.4 1.7 %collective-permute-done.4.refs_2_ = bf16[16,4352]{1,0:T(8,128)(2,1)S(1)} collective-permute-done((bf16[16,4352]{1,0:T(8,128)(2,1)S(1)}, bf16[16,4352]{1,0:T(8,128)(2,1)S(1)}, u32[]{:S(2)}, u32[]{:S(2)}) %collective-permute-start.4) | collective-permute-done | bytes 139296 | tf_op jit(solution)/shard_map/ppermute | solution.py:241
  93.1 1.5 %collective-permute-done.5.refs_3_ = bf16[16,4352]{1,0:T(8,128)(2,1)S(1)} collective-permute-done((bf16[16,4352]{1,0:T(8,128)(2,1)S(1)}, bf16[16,4352]{1,0:T(8,128)(2,1)S(1)}, u32[]{:S(2)}, u32[]{:S(2)}) %collective-permute-start.5) | collective-permute-done | bytes 139296 | tf_op jit(solution)/shard_map/ppermute | solution.py:241
  94.6 0.9 sum.1
  95.6 0.7 copy.17
  96.2 0.0 collective-permute-done.10.refs_6_
  96.2 0.0 collective-permute-done.11.refs_7_
  96.2 0.7 copy-done.23
  97.0 0.1 copy-done.24
  97.1 0.8 copy-done.25
  97.8 4.6 %copy-done.3 = bf16[4,2048,768]{2,1,0:T(8,128)(2,1)S(1)} copy-done((bf16[4,2048,768]{2,1,0:T(8,128)(2,1)S(1)}, bf16[4,2048,768]{2,1,0:T(8,128)(2,1)}, u32[]{:S(2)}) %copy-start.3) | copy-done | bytes 12582936
  102.4 4.6 %copy-done.7 = bf16[4,2048,768]{2,1,0:T(8,128)(2,1)S(1)} copy-done((bf16[4,2048,768]{2,1,0:T(8,128)(2,1)S(1)}, bf16[4,2048,768]{2,1,0:T(8,128)(2,1)}, u32[]{:S(2)}) %copy-start.7) | copy-done | bytes 12582936
  107.0 4.6 %copy-done.10 = bf16[4,768,2048]{2,1,0:T(8,128)(2,1)S(1)} copy-done((bf16[4,768,2048]{2,1,0:T(8,128)(2,1)S(1)}, bf16[4,768,2048]{2,1,0:T(8,128)(2,1)}, u32[]{:S(2)}) %copy-start.10) | copy-done | bytes 12582936
  111.6 23.1 %grads.1 = (f32[4,512,768]{2,1,0:T(8,128)}, f32[4,512,768]{2,1,0:T(8,128)}, f32[4,768,512]{2,1,0:T(8,128)}) custom-call(bf16[16,4224]{1,0:T(8,128)(2,1)} %copy-done.15, bf16[16,4224]{1,0:T(8,128)(2,1)} %copy-done.16, bf16[16,4224]{1,0:T(8,128)(2,1)} %copy-done.17, bf16[16,4224]{1,0:T(8,128)(2,1)} %copy-done.18, bf16[48,4224]{1,0:T(8,128)(2,1)} %copy-done.22, ...), custom_call_target="tpu_custom_call" | custom-call | flops 9663676416 | bytes 37748736 | tf_op jit(solution)/shard_map/grads/pallas_call | solution.py:314
  (40 shorter events, 0.1 us)
Async XLA Ops:
  2.1 0.8 copy-start.19
  3.0 0.8 copy-start.20
  3.8 37.7 %copy-start.21 = (s32[4,6]{1,0:T(4,128)S(1)}, s32[4,6]{1,0:T(4,128)}, u32[]{:S(2)}) copy-start(s32[4,6]{1,0:T(4,128)} %refs_11_.1) | copy-start | bytes 292
  3.9 37.6 %copy-start.15 = (bf16[16,4224]{1,0:T(8,128)(2,1)}, bf16[16,4224]{1,0:T(8,128)(2,1)S(1)}, u32[]{:S(2)}) copy-start(bf16[16,4224]{1,0:T(8,128)(2,1)S(1)} %pack.1.refs_0_) | copy-start | bytes 405508
  3.9 31.3 %collective-permute-start.6 = (bf16[16,4224]{1,0:T(8,128)(2,1)S(1)}, bf16[16,4224]{1,0:T(8,128)(2,1)S(1)}, u32[]{:S(2)}, u32[]{:S(2)}) collective-permute-start(bf16[16,4224]{1,0:T(8,128)(2,1)S(1)} %pack.1.refs_0_), channel_id=1, source_target_pairs={{0,1},{1,2},{2,3},{3,0},{4,5},{5,6},{6,7},{7,4},{8,9},{9,10},{10,1... | collective-permute-start | bytes 405512 | tf_op jit(solution)/shard_map/ppermute | solution.py:241
  7.0 33.9 %collective-permute-start = (bf16[16,4224]{1,0:T(8,128)(2,1)S(1)}, bf16[16,4224]{1,0:T(8,128)(2,1)S(1)}, u32[]{:S(2)}, u32[]{:S(2)}) collective-permute-start(bf16[16,4224]{1,0:T(8,128)(2,1)S(1)} %pack.1.refs_0_), channel_id=1, source_target_pairs={{0,4},{4,8},{8,12},{12,0},{1,5},{5,9},{9,13},{13,1},{2,6},{6,10},{... | collective-permute-start | bytes 405512 | tf_op jit(solution)/shard_map/ppermute | solution.py:241
  7.0 34.4 %collective-permute-start.1 = (bf16[16,4224]{1,0:T(8,128)(2,1)S(1)}, bf16[16,4224]{1,0:T(8,128)(2,1)S(1)}, u32[]{:S(2)}, u32[]{:S(2)}) collective-permute-start(bf16[16,4224]{1,0:T(8,128)(2,1)S(1)} %pack.1.refs_0_), channel_id=1, source_target_pairs={{0,8},{4,12},{8,0},{12,4},{1,9},{5,13},{9,1},{13,5},{2,10},{6,14},... | collective-permute-start | bytes 405512 | tf_op jit(solution)/shard_map/ppermute | solution.py:241
  8.5 32.9 %collective-permute-start.2 = (bf16[16,4224]{1,0:T(8,128)(2,1)S(1)}, bf16[16,4224]{1,0:T(8,128)(2,1)S(1)}, u32[]{:S(2)}, u32[]{:S(2)}) collective-permute-start(bf16[16,4224]{1,0:T(8,128)(2,1)S(1)} %pack.1.refs_0_), channel_id=1, source_target_pairs={{0,12},{4,0},{8,4},{12,8},{1,13},{5,1},{9,5},{13,9},{2,14},{6,2},{... | collective-permute-start | bytes 405512 | tf_op jit(solution)/shard_map/ppermute | solution.py:241
  10.0 26.6 %collective-permute-start.7 = (bf16[16,4224]{1,0:T(8,128)(2,1)S(1)}, bf16[16,4224]{1,0:T(8,128)(2,1)S(1)}, u32[]{:S(2)}, u32[]{:S(2)}) collective-permute-start(bf16[16,4224]{1,0:T(8,128)(2,1)S(1)} %pack.1.refs_0_), channel_id=1, source_target_pairs={{0,2},{1,3},{2,0},{3,1},{4,6},{5,7},{6,4},{7,5},{8,10},{9,11},{10,... | collective-permute-start | bytes 405512 | tf_op jit(solution)/shard_map/ppermute | solution.py:241
  12.6 4.6 %copy-start.11 = (bf16[4,2048,768]{2,1,0:T(8,128)(2,1)S(1)}, bf16[4,2048,768]{2,1,0:T(8,128)(2,1)}, u32[]{:S(2)}) copy-start(bf16[4,2048,768]{2,1,0:T(8,128)(2,1)} %refs_0_.1) | copy-start | bytes 37748740
  26.2 4.5 %copy-start = (bf16[4,2048,768]{2,1,0:T(8,128)(2,1)}, bf16[4,2048,768]{2,1,0:T(8,128)(2,1)S(1)}, u32[]{:S(2)}) copy-start(bf16[4,2048,768]{2,1,0:T(8,128)(2,1)S(1)} %get-tuple-element.23.refs_5_.w_gate.refs_12_) | copy-start | bytes 37748740
  30.7 4.5 %copy-start.4 = (bf16[4,2048,768]{2,1,0:T(8,128)(2,1)}, bf16[4,2048,768]{2,1,0:T(8,128)(2,1)S(1)}, u32[]{:S(2)}) copy-start(bf16[4,2048,768]{2,1,0:T(8,128)(2,1)S(1)} %get-tuple-element.24.refs_6_.w_up.refs_13_) | copy-start | bytes 37748740
  35.2 25.1 %copy-start.8 = (bf16[4,768,2048]{2,1,0:T(8,128)(2,1)}, bf16[4,768,2048]{2,1,0:T(8,128)(2,1)S(1)}, u32[]{:S(2)}) copy-start(bf16[4,768,2048]{2,1,0:T(8,128)(2,1)S(1)} %get-tuple-element.25.refs_7_.w_down.refs_14_) | copy-start | bytes 37748740
  35.2 5.0 %collective-permute-start.8 = (bf16[16,4224]{1,0:T(8,128)(2,1)S(1)}, bf16[16,4224]{1,0:T(8,128)(2,1)S(1)}, u32[]{:S(2)}, u32[]{:S(2)}) collective-permute-start(bf16[16,4224]{1,0:T(8,128)(2,1)S(1)} %pack.1.refs_0_), channel_id=1, source_target_pairs={{0,3},{1,0},{2,1},{3,2},{4,7},{5,4},{6,5},{7,6},{8,11},{9,8},{10,9... | collective-permute-start | bytes 405512 | tf_op jit(solution)/shard_map/ppermute | solution.py:241
  40.3 20.1 %copy-start.22 = (bf16[48,4224]{1,0:T(8,128)(2,1)}, bf16[48,4224]{1,0:T(8,128)(2,1)S(1)}, u32[]{:S(2)}) copy-start(bf16[48,4224]{1,0:T(8,128)(2,1)S(1)} %constant_dynamic-update-slice_fusion.refs_4_) | copy-start | bytes 1216516
  40.3 55.9 %collective-permute-start.10 = (bf16[48,4224]{1,0:T(8,128)(2,1)S(1)}, bf16[48,4224]{1,0:T(8,128)(2,1)S(1)}, u32[]{:S(2)}, u32[]{:S(2)}) collective-permute-start(bf16[48,4224]{1,0:T(8,128)(2,1)S(1)} %constant_dynamic-update-slice_fusion.refs_4_), channel_id=1, source_target_pairs={{0,8},{4,12},{8,0},{12,4},{1,9},{5,13},{9,1},{13,5},{2,10},{6,14},... | collective-permute-start | bytes 1216520 | tf_op jit(solution)/shard_map/ppermute | solution.py:241
  40.9 55.3 %collective-permute-start.11 = (bf16[48,4224]{1,0:T(8,128)(2,1)S(1)}, bf16[48,4224]{1,0:T(8,128)(2,1)S(1)}, u32[]{:S(2)}, u32[]{:S(2)}) collective-permute-start(bf16[48,4224]{1,0:T(8,128)(2,1)S(1)} %constant_dynamic-update-slice_fusion.refs_4_), channel_id=1, source_target_pairs={{0,12},{4,0},{8,4},{12,8},{1,13},{5,1},{9,5},{13,9},{2,14},{6,2},{... | collective-permute-start | bytes 1216520 | tf_op jit(solution)/shard_map/ppermute | solution.py:241
  41.0 19.4 %copy-start.16 = (bf16[16,4224]{1,0:T(8,128)(2,1)}, bf16[16,4224]{1,0:T(8,128)(2,1)S(1)}, u32[]{:S(2)}) copy-start(bf16[16,4224]{1,0:T(8,128)(2,1)S(1)} %collective-permute-done.refs_1_) | copy-start | bytes 405508
  41.0 55.3 %collective-permute-start.9 = (bf16[48,4224]{1,0:T(8,128)(2,1)S(1)}, bf16[48,4224]{1,0:T(8,128)(2,1)S(1)}, u32[]{:S(2)}, u32[]{:S(2)}) collective-permute-start(bf16[48,4224]{1,0:T(8,128)(2,1)S(1)} %constant_dynamic-update-slice_fusion.refs_4_), channel_id=1, source_target_pairs={{0,4},{4,8},{8,12},{12,0},{1,5},{5,9},{9,13},{13,1},{2,6},{6,10},{... | collective-permute-start | bytes 1216520 | tf_op jit(solution)/shard_map/ppermute | solution.py:241
  41.5 18.9 %copy-start.17 = (bf16[16,4224]{1,0:T(8,128)(2,1)}, bf16[16,4224]{1,0:T(8,128)(2,1)S(1)}, u32[]{:S(2)}) copy-start(bf16[16,4224]{1,0:T(8,128)(2,1)S(1)} %collective-permute-done.1.refs_2_) | copy-start | bytes 405508
  41.5 18.9 %copy-start.18 = (bf16[16,4224]{1,0:T(8,128)(2,1)}, bf16[16,4224]{1,0:T(8,128)(2,1)S(1)}, u32[]{:S(2)}) copy-start(bf16[16,4224]{1,0:T(8,128)(2,1)S(1)} %collective-permute-done.2.refs_3_) | copy-start | bytes 405508
  41.5 4.7 %copy-start.1 = (bf16[4,2048,768]{2,1,0:T(8,128)(2,1)S(1)}, bf16[4,2048,768]{2,1,0:T(8,128)(2,1)}, u32[]{:S(2)}) copy-start(bf16[4,2048,768]{2,1,0:T(8,128)(2,1)} %copy-done) | copy-start | bytes 37748740
  46.2 4.6 %copy-start.5 = (bf16[4,2048,768]{2,1,0:T(8,128)(2,1)S(1)}, bf16[4,2048,768]{2,1,0:T(8,128)(2,1)}, u32[]{:S(2)}) copy-start(bf16[4,2048,768]{2,1,0:T(8,128)(2,1)} %copy-done.4) | copy-start | bytes 37748740
  60.4 24.4 %copy-start.12 = (bf16[4,64,768]{2,1,0:T(8,128)(2,1)}, bf16[4,64,768]{2,1,0:T(8,128)(2,1)S(1)}, u32[]{:S(2)}) copy-start(bf16[4,64,768]{2,1,0:T(8,128)(2,1)S(1)} %get-tuple-element.26.hidden.refs_8_) | copy-start | bytes 1179652
  60.4 24.4 %copy-start.13 = (bf16[4,64,768]{2,1,0:T(8,128)(2,1)}, bf16[4,64,768]{2,1,0:T(8,128)(2,1)S(1)}, u32[]{:S(2)}) copy-start(bf16[4,64,768]{2,1,0:T(8,128)(2,1)S(1)} %get-tuple-element.27.d_gate.refs_9_) | copy-start | bytes 1179652
  60.4 24.4 %copy-start.14 = (bf16[4,64,768]{2,1,0:T(8,128)(2,1)}, bf16[4,64,768]{2,1,0:T(8,128)(2,1)S(1)}, u32[]{:S(2)}) copy-start(bf16[4,64,768]{2,1,0:T(8,128)(2,1)S(1)} %get-tuple-element.28.d_up.refs_10_) | copy-start | bytes 1179652
  60.4 5.0 %copy-start.2 = (bf16[4,2048,768]{2,1,0:T(8,128)(2,1)S(1)}, bf16[4,2048,768]{2,1,0:T(8,128)(2,1)}, u32[]{:S(2)}) copy-start(bf16[4,2048,768]{2,1,0:T(8,128)(2,1)} %copy-done) | copy-start | bytes 37748740
  65.4 4.6 %copy-start.6 = (bf16[4,2048,768]{2,1,0:T(8,128)(2,1)S(1)}, bf16[4,2048,768]{2,1,0:T(8,128)(2,1)}, u32[]{:S(2)}) copy-start(bf16[4,2048,768]{2,1,0:T(8,128)(2,1)} %copy-done.4) | copy-start | bytes 37748740
  70.0 4.6 %copy-start.9 = (bf16[4,768,2048]{2,1,0:T(8,128)(2,1)S(1)}, bf16[4,768,2048]{2,1,0:T(8,128)(2,1)}, u32[]{:S(2)}) copy-start(bf16[4,768,2048]{2,1,0:T(8,128)(2,1)} %copy-done.8) | copy-start | bytes 37748740
  84.8 5.1 %collective-permute-start.3 = (bf16[16,4352]{1,0:T(8,128)(2,1)S(1)}, bf16[16,4352]{1,0:T(8,128)(2,1)S(1)}, u32[]{:S(2)}, u32[]{:S(2)}) collective-permute-start(bf16[16,4352]{1,0:T(8,128)(2,1)S(1)} %get-tuple-element.31), channel_id=1, source_target_pairs={{0,12},{4,0},{8,4},{12,8},{1,13},{5,1},{9,5},{13,9},{2,14},{6,2},{... | collective-permute-start | bytes 417800 | tf_op jit(solution)/shard_map/ppermute | solution.py:241
  86.2 6.9 %collective-permute-start.4 = (bf16[16,4352]{1,0:T(8,128)(2,1)S(1)}, bf16[16,4352]{1,0:T(8,128)(2,1)S(1)}, u32[]{:S(2)}, u32[]{:S(2)}) collective-permute-start(bf16[16,4352]{1,0:T(8,128)(2,1)S(1)} %get-tuple-element.32), channel_id=1, source_target_pairs={{0,8},{4,12},{8,0},{12,4},{1,9},{5,13},{9,1},{13,5},{2,10},{6,14},... | collective-permute-start | bytes 417800 | tf_op jit(solution)/shard_map/ppermute | solution.py:241
  89.9 4.7 %collective-permute-start.5 = (bf16[16,4352]{1,0:T(8,128)(2,1)S(1)}, bf16[16,4352]{1,0:T(8,128)(2,1)S(1)}, u32[]{:S(2)}, u32[]{:S(2)}) collective-permute-start(bf16[16,4352]{1,0:T(8,128)(2,1)S(1)} %get-tuple-element.33), channel_id=1, source_target_pairs={{0,4},{4,8},{8,12},{12,0},{1,5},{5,9},{9,13},{13,1},{2,6},{6,10},{... | collective-permute-start | bytes 417800 | tf_op jit(solution)/shard_map/ppermute | solution.py:241
  96.2 0.7 copy-start.23
  96.2 0.9 copy-start.24
  97.1 0.8 copy-start.25
  97.8 4.6 %copy-start.3 = (bf16[4,2048,768]{2,1,0:T(8,128)(2,1)S(1)}, bf16[4,2048,768]{2,1,0:T(8,128)(2,1)}, u32[]{:S(2)}) copy-start(bf16[4,2048,768]{2,1,0:T(8,128)(2,1)} %copy-done) | copy-start | bytes 37748740
  102.4 4.6 %copy-start.7 = (bf16[4,2048,768]{2,1,0:T(8,128)(2,1)S(1)}, bf16[4,2048,768]{2,1,0:T(8,128)(2,1)}, u32[]{:S(2)}) copy-start(bf16[4,2048,768]{2,1,0:T(8,128)(2,1)} %copy-done.4) | copy-start | bytes 37748740
  107.0 4.6 %copy-start.10 = (bf16[4,768,2048]{2,1,0:T(8,128)(2,1)S(1)}, bf16[4,768,2048]{2,1,0:T(8,128)(2,1)}, u32[]{:S(2)}) copy-start(bf16[4,768,2048]{2,1,0:T(8,128)(2,1)} %copy-done.8) | copy-start | bytes 37748740

commit v3 on v2

v3 whole, which is shorter than its diff:
```python
import functools

import jax
import jax.numpy as jnp
from jax import lax
from jax.experimental import pallas as pl
from jax.experimental.pallas import tpu as pltpu
from jax.sharding import PartitionSpec as P

BLK = 128
LANES = 128
CHUNK = 256
WIDE = 512
TILE = 256
MIB = 1 << 20

VMEM = pl.BlockSpec(memory_space=pltpu.VMEM)
SMEM = pl.BlockSpec(memory_space=pltpu.SMEM)
ANY = pl.BlockSpec(memory_space=pl.ANY)

NN = (((1,), (0,)), ((), ()))
NT = (((1,), (1,)), ((), ()))
TN = (((0,), (0,)), ((), ()))


def dot(a, b, dims):
    return lax.dot_general(a, b, dims, preferred_element_type=jnp.float32)


def lane_ids(rows, lanes):
    return lax.broadcasted_iota(jnp.int32, (rows, lanes), 1)


def route_kernel(cotangent, expert_ids, route_weights, packet):
    rows, width = cotangent.shape
    lanes = packet.shape[1] - width
    packet[:, :width] = cotangent[...]
    at = lane_ids(rows, lanes)
    values = route_weights[...].astype(jnp.float32)
    dense = jnp.zeros((rows, lanes), jnp.float32)
    for k in range(expert_ids.shape[1]):
        dense += jnp.where(expert_ids[:, k : k + 1] == at, values[:, k : k + 1], 0.0)
    packet[:, width:] = dense.astype(packet.dtype)


def load_kernel(*refs):
    count = len(refs) // 2
    sems = refs[-1]
    copies = [
        pltpu.make_async_copy(refs[i], refs[count + i], sems.at[i]) for i in range(count)
    ]
    for copy in copies:
        copy.start()
    for copy in copies:
        copy.wait()


def over_tiles(local_experts, tokens, body):
    tiles = tokens // TILE

    def step(index, carry):
        body(index // tiles, pl.ds(pl.multiple_of(index % tiles * TILE, TILE), TILE))
        return carry

    lax.fori_loop(0, local_experts * tiles, step, 0)


def gate_up_kernel(x, masks, w_gate, w_up, hidden, slope_up, slope_gate):
    local_experts, _, hidden_units = w_gate.shape

    def body(expert, rows):
        for start in range(0, hidden_units, CHUNK):
            cols = slice(start, start + CHUNK)
            gate_pre = dot(x[rows, :], w_gate[expert, :, cols], NN)
            up_proj = dot(x[rows, :], w_up[expert, :, cols], NN)
            at = lane_ids(1, CHUNK)
            keep = jnp.zeros((1, CHUNK), jnp.float32)
            for j in range(CHUNK // BLK):
                kept = masks[expert, start // BLK + j].astype(jnp.float32)
                keep = jnp.where(at // BLK == j, kept, keep)
            sigma = 1.0 / (1.0 + jnp.exp(-gate_pre))
            silu = gate_pre * sigma
            up_kept = up_proj * keep
            hidden[expert, rows, cols] = silu * up_kept
            slope_up[expert, rows, cols] = silu * keep
            slope_gate[expert, rows, cols] = up_kept * (sigma + silu * (1.0 - sigma))

    over_tiles(local_experts, x.shape[0], body)


def hidden_kernel(packet, hidden, slope_up, slope_gate, w_down, out, d_gate, d_up, inner):
    local_experts, hidden_units, width = w_down.shape
    tokens = packet.shape[0]
    lanes = packet.shape[1] - width
    base = lax.axis_index("expert") * local_experts
    inner[...] = jnp.zeros(inner.shape, inner.dtype)

    def body(expert, rows):
        at = lane_ids(TILE, lanes)
        dense = packet[rows, width:].astype(jnp.float32)
        hit = at == base + expert
        weights = jnp.sum(jnp.where(hit, dense, 0.0), axis=1, keepdims=True)
        total = jnp.zeros((TILE, 1), jnp.float32)
        for start in range(0, hidden_units, CHUNK):
            cols = slice(start, start + CHUNK)
            back = dot(packet[rows, :width], w_down[expert, cols, :], NT)
            units = hidden[expert, rows, cols]
            total += jnp.sum(units * back, axis=1, keepdims=True)
            back = back * weights
            out[expert, rows, cols] = (units * weights).astype(out.dtype)
            d_gate[expert, rows, cols] = (back * slope_gate[expert, rows, cols]).astype(out.dtype)
            d_up[expert, rows, cols] = (back * slope_up[expert, rows, cols]).astype(out.dtype)
        inner[rows, :] += jnp.where(hit, total, 0.0)

    over_tiles(local_experts, tokens, body)


def back_kernel(hidden, d_gate, d_up, inner, w_gate, w_up, w_down, *outs):
    local_experts, width, _ = w_gate.shape
    rows = outs[0].shape[0]
    own = rows * len(outs)
    mine = pl.ds(pl.multiple_of(lax.axis_index("dp") * own, own), own)

    def body(step, carry):
        start = pl.multiple_of(step * WIDE, WIDE)
        cols = pl.ds(start, WIDE)
        mixed = jnp.zeros((own, WIDE), jnp.float32)
        token_grad = jnp.zeros((own, WIDE), jnp.float32)
        for e in range(local_experts):
            mixed += dot(hidden[e, mine, :], w_down[e, :, cols], NN)
            token_grad += dot(d_gate[e, mine, :], w_gate[e, cols, :], NT)
            token_grad += dot(d_up[e, mine, :], w_up[e, cols, :], NT)
        for i, out in enumerate(outs):
            block = slice(i * rows, (i + 1) * rows)
            out[:, cols] = mixed[block].astype(out.dtype)
            out[:, pl.ds(start + width, WIDE)] = token_grad[block].astype(out.dtype)
        return carry

    lax.fori_loop(0, width // WIDE, body, 0)
    lanes = inner.shape[1]
    part = inner[mine, :]
    high = part.astype(jnp.bfloat16)
    low = (part - high.astype(jnp.float32)).astype(jnp.bfloat16)
    for i, out in enumerate(outs):
        block = slice(i * rows, (i + 1) * rows)
        out[:, 2 * width : 2 * width + lanes] = high[block]
        out[:, 2 * width + lanes :] = low[block]


def grad_kernel(x, packet, hidden, d_gate, d_up, *refs):
    grad_gate, grad_up, grad_down, done, x_part, cot_part, out_gate, out_up, out_down, sems = refs
    local_experts, _, hidden_units = hidden.shape
    part = x_part.shape[0]
    mine = pl.ds(pl.multiple_of(lax.axis_index("dp") * part, part), part)
    x_part[...] = x[:, mine].T
    cot_part[...] = packet[:, mine]
    done[...] = jnp.zeros(done.shape, done.dtype)
    chunks = hidden_units // CHUNK

    def copies(step, slot):
        expert, start = step // chunks, pl.multiple_of(step % chunks * CHUNK, CHUNK)
        cols = pl.ds(start, CHUNK)
        return [
            pltpu.make_async_copy(out_gate.at[slot], grad_gate.at[expert, :, cols], sems.at[slot, 0]),
            pltpu.make_async_copy(out_up.at[slot], grad_up.at[expert, :, cols], sems.at[slot, 1]),
            pltpu.make_async_copy(out_down.at[slot], grad_down.at[expert, cols, :], sems.at[slot, 2]),
        ]

    def body(step, carry):
        expert, start = step // chunks, pl.multiple_of(step % chunks * CHUNK, CHUNK)
        cols = pl.ds(start, CHUNK)
        slot = step % 2

        @pl.when(step >= 2)
        def _():
            for copy in copies(step - 2, slot):
                copy.wait()

        out_gate[slot] = dot(x_part[...], d_gate[expert, :, cols], NN)
        out_up[slot] = dot(x_part[...], d_up[expert, :, cols], NN)
        out_down[slot] = dot(hidden[expert, :, cols], cot_part[...], TN)
        for copy in copies(step, slot):
            copy.start()
        return carry

    steps = local_experts * chunks
    lax.fori_loop(0, steps, body, 0)
    for step in range(max(steps - 2, 0), steps):
        for copy in copies(step, step % 2):
            copy.wait()


def sum_kernel(count, *refs):
    blocks, (expert_ids, _, mixed, token_grad, route_grad) = refs[:count], refs[count:]
    width = mixed.shape[1]
    lanes = (blocks[0].shape[1] - 2 * width) // 2
    for out, low in ((mixed, 0), (token_grad, width)):
        total = blocks[0][:, low : low + width].astype(jnp.float32)
        for block in blocks[1:]:
            total += block[:, low : low + width].astype(jnp.float32)
        out[...] = total.astype(out.dtype)
    inner = jnp.zeros((mixed.shape[0], lanes), jnp.float32)
    for block in blocks:
        tail = block[:, 2 * width :].astype(jnp.float32)
        inner += tail[:, :lanes] + tail[:, lanes:]
    at = lane_ids(*inner.shape)
    for k in range(expert_ids.shape[1]):
        hit = jnp.where(expert_ids[:, k : k + 1] == at, inner, 0.0)
        route_grad[:, k : k + 1] = jnp.sum(hit, axis=1, keepdims=True)


def shift(value, axis, by):
    size = lax.axis_size(axis)
    return lax.ppermute(value, axis, [(i, (i + by) % size) for i in range(size)])


def cost(flops, moved):
    return pl.CostEstimate(flops=flops, bytes_accessed=moved, transcendentals=0)


def per_device(
    tokens, expert_ids, slot_index, route_weights, w_gate, w_up, w_down, block_masks, cotangent
):
    rows, width = tokens.shape
    local_experts, _, hidden_units = w_gate.shape
    sources, columns = lax.axis_size("expert"), lax.axis_size("dp")
    lanes = -(-local_experts * sources // LANES) * LANES
    own = sources * rows
    everyone = own * columns
    bf16, f32 = jnp.bfloat16, jnp.float32
    struct = jax.ShapeDtypeStruct
    one = 2 * local_experts * width * hidden_units

    packet = pl.pallas_call(
        route_kernel,
        out_shape=struct((rows, width + lanes), bf16),
        in_specs=[VMEM] * 3,
        out_specs=VMEM,
        compiler_params=pltpu.CompilerParams(vmem_limit_bytes=4 * MIB),
        name="route",
    )(cotangent, expert_ids, route_weights)
    x = lax.all_gather(tokens, ("dp", "expert"), axis=0, tiled=True)
    packets = lax.all_gather(packet, ("dp", "expert"), axis=0, tiled=True)

    weights = (w_gate, w_up, w_down)
    weights = pl.pallas_call(
        load_kernel,
        out_shape=[pltpu.VMEM(w.shape, w.dtype) for w in weights],
        in_specs=[ANY] * 3,
        out_specs=[VMEM] * 3,
        scratch_shapes=[pltpu.SemaphoreType.DMA((3,))],
        cost_estimate=cost(0, 3 * one),
        compiler_params=pltpu.CompilerParams(vmem_limit_bytes=1 * MIB),
        name="load",
    )(*weights)
    gate, up, down = [pltpu.with_memory_space_constraint(w, pltpu.VMEM) for w in weights]

    units = struct((local_experts, everyone, hidden_units), f32)
    factors = pl.pallas_call(
        gate_up_kernel,
        out_shape=[units] * 3,
        in_specs=[VMEM, SMEM, VMEM, VMEM],
        out_specs=[VMEM] * 3,
        cost_estimate=cost(2 * everyone * one, 2 * one),
        compiler_params=pltpu.CompilerParams(vmem_limit_bytes=12 * MIB),
        name="gate_up",
    )(x, block_masks, gate, up)

    units = struct((local_experts, everyone, hidden_units), bf16)
    hidden, d_gate, d_up, inner = pl.pallas_call(
        hidden_kernel,
        out_shape=[units] * 3 + [struct((everyone, lanes), f32)],
        in_specs=[VMEM] * 5,
        out_specs=[VMEM] * 4,
        cost_estimate=cost(everyone * one, one),
        compiler_params=pltpu.CompilerParams(vmem_limit_bytes=12 * MIB),
        name="hidden",
    )(packets, *factors, down)

    partials = pl.pallas_call(
        back_kernel,
        out_shape=[struct((rows, 2 * width + 2 * lanes), bf16)] * sources,
        in_specs=[VMEM] * 7,
        out_specs=[VMEM] * sources,
        cost_estimate=cost(3 * own * one, 3 * one),
        compiler_params=pltpu.CompilerParams(vmem_limit_bytes=12 * MIB),
        name="back",
    )(hidden, d_gate, d_up, inner, gate, up, down)
    stacked = jnp.stack(partials)
    arrived = lax.all_to_all(stacked, "expert", split_axis=0, concat_axis=0, tiled=True)
    arrived = [arrived[i] for i in range(sources)]

    part = width // columns
    grad_gate, grad_up, grad_down, done = pl.pallas_call(
        grad_kernel,
        out_shape=[
            struct((local_experts, part, hidden_units), f32),
            struct((local_experts, part, hidden_units), f32),
            struct((local_experts, hidden_units, part), f32),
            struct((8, LANES), f32),
        ],
        in_specs=[VMEM] * 5,
        out_specs=[ANY] * 3 + [VMEM],
        scratch_shapes=[
            pltpu.VMEM((part, everyone), bf16),
            pltpu.VMEM((everyone, part), bf16),
            pltpu.VMEM((2, part, CHUNK), f32),
            pltpu.VMEM((2, part, CHUNK), f32),
            pltpu.VMEM((2, CHUNK, part), f32),
            pltpu.SemaphoreType.DMA((2, 3)),
        ],
        cost_estimate=cost(3 * everyone * one // columns, 6 * one // columns),
        compiler_params=pltpu.CompilerParams(vmem_limit_bytes=16 * MIB),
        name="grads",
    )(x, packets, hidden, d_gate, d_up)

    mixed, token_grad, route_grad = pl.pallas_call(
        functools.partial(sum_kernel, sources),
        out_shape=[
            struct((rows, width), bf16),
            struct((rows, width), bf16),
            struct(expert_ids.shape, f32),
        ],
        in_specs=[VMEM] * (sources + 2),
        out_specs=[VMEM] * 3,
        compiler_params=pltpu.CompilerParams(vmem_limit_bytes=4 * MIB),
        name="sum",
    )(*arrived, expert_ids, done)
    return (mixed, token_grad, route_grad, grad_gate, grad_up, grad_down)


def solution(mesh):
    rows = P(("groups", "expert", "dp"), None)
    experts = P("expert", None, None)
    return jax.shard_map(
        per_device,
        mesh=mesh,
        in_specs=(rows, rows, rows, rows, experts, experts, experts, P("expert", None), rows),
        out_specs=(
            rows,
            rows,
            rows,
            P(("groups", "expert"), "dp", None),
            P(("groups", "expert"), "dp", None),
            P(("groups", "expert"), None, "dp"),
        ),
        check_vma=False,
    )
```

time: 135 us -> 158 us (1.17)
  waiting for transfers between devices: 9.12 us -> 30.8 us
  between operations: 0.87 us -> 14.2 us
  starting transfers between devices: 15.4 us -> 3.55 us
  Pallas kernels: 53 us -> 43.4 us
  local copies, waits for them, and re-layouts: 56.3 us -> 64.2 us
    all_gather x0 -> x2, waiting for transfers between devices: none -> 30.1 us  [the longest x1 17.7 us: per_device(): packets = lax.all_gather(packet, ('dp', 'expert'), axis=0, tiled=True)]
    ppermute x12 -> x0, starting transfers between devices: 15.4 us -> none  [shift(): lax.ppermute(value, axis, [(i, (i + by) % size) for i in range(size)])]
    pallas_call x3 -> x4, Pallas kernels: 32.8 us -> 23.1 us  [the longest x1 9.2 us: per_device(): pl.pallas_call(grad_kernel, out_shape=[struct((local_experts, part, hidde...]
    ppermute x12 -> x0, waiting for transfers between devices: 9.12 us -> none  [shift(): lax.ppermute(value, axis, [(i, (i + by) % size) for i in range(size)])]
    unnamed x57 -> x55, local copies, waits for them, and re-layouts: 56.2 us -> 64.2 us
    all_to_all x0 -> x1, starting transfers between devices: none -> 3.47 us  [per_device(): lax.all_to_all(stacked, 'expert', split_axis=0, concat_axis=0, tiled=True)]
  transfers between devices with their start and end apart: 12 -> 3, of which waited for: 4 -> 2; matrix products, arithmetic and copies ran while one was open for 1% -> 1% of each run, Pallas kernels for 22% -> 18%
where the time goes in v3:
time: 158 us; the launch traced here: 157 us
  local copies, waits for them, and re-layouts  64.2 us (41%)
  Pallas kernels  43.4 us (27%)
  waiting for transfers between devices  30.8 us (19%)
  between operations  14.2 us (9%)
  starting transfers between devices  3.55 us (2%)
    unnamed x55, local copies, waits for them, and re-layouts  64.2 us
    all_gather x1, waiting for transfers between devices, per_device(): packets = lax.all_gather(packet, ('dp', 'expert'), axis=0, tiled=True)  17.7 us
    all_gather x1, waiting for transfers between devices, per_device(): x = lax.all_gather(tokens, ('dp', 'expert'), axis=0, tiled=True)  12.4 us
    pallas_call x1, Pallas kernels, per_device(): pl.pallas_call(back_kernel, out_shape=[struct((rows, 2 * width + 2 * lane...  10.3 us
    pallas_call x1, Pallas kernels, per_device(): pl.pallas_call(grad_kernel, out_shape=[struct((local_experts, part, hidde...  9.2 us
    pallas_call x1, Pallas kernels, per_device(): pl.pallas_call(load_kernel, out_shape=[pltpu.VMEM(w.shape, w.dtype) for w...  9.1 us
    pallas_call x1, Pallas kernels, per_device(): pl.pallas_call(gate_up_kernel, out_shape=[units] * 3, in_specs=[VMEM, SME...  8.49 us
    pallas_call x1, Pallas kernels, per_device(): pl.pallas_call(hidden_kernel, out_shape=[units] * 3 + [struct((everyone,...  4.67 us
  transfers between devices with their start and end apart: 3, of which 2 were waited for; matrix products, arithmetic and copies ran while one was open for 1% of the time, Pallas kernels for 18%

profile of v3, /device:TPU:0, one launch (start us, length us, event | category | flops | bytes accessed | tf_op | source)
XLA Modules:
  0.0 157.1 jit_solution(4486761443981527253)
XLA Ops:
  7.2 0.0 all-gather.5.cloned.1.call-start
  7.2 0.7 all-gather.5.cloned.1.call-update
  7.9 0.0 all-gather.3.cloned.1.call-start
  7.9 0.8 copy.15.route_weights
  8.7 0.8 copy.14.expert_ids.refs_4_
  9.5 0.8 copy-done.24
  10.3 0.7 route.1
  11.0 0.0 all-gather.3.cloned.1.call-update
  11.1 0.0 copy-start.9
  11.1 4.6 %copy-done.9 = bf16[4,2048,768]{2,1,0:T(8,128)(2,1)S(1)} copy-done((bf16[4,2048,768]{2,1,0:T(8,128)(2,1)S(1)}, bf16[4,2048,768]{2,1,0:T(8,128)(2,1)}, u32[]{:S(2)}) %copy-start.9) | copy-done | bytes 12582936
  15.7 9.1 %load.1 = (bf16[4,2048,768]{2,1,0:T(8,128)(2,1)S(1)}, bf16[4,2048,768]{2,1,0:T(8,128)(2,1)S(1)}, bf16[4,768,2048]{2,1,0:T(8,128)(2,1)S(1)}) custom-call(bf16[4,2048,768]{2,1,0:T(8,128)(2,1)S(1)} %copy-done.9, bf16[4,2048,768]{2,1,0:T(8,128)(2,1)} %refs_1_.1, bf16[4,768,2048]{2,1,0:T(8,128)(2,1)} %refs_2_.1), custom_call_target="tpu_custom_call" | custom-call | bytes 37748736 | tf_op jit(solution)/shard_map/load/pallas_call | solution.py:246
  24.8 0.0 copy-start
  24.8 4.5 %copy-done = bf16[4,2048,768]{2,1,0:T(8,128)(2,1)} copy-done((bf16[4,2048,768]{2,1,0:T(8,128)(2,1)}, bf16[4,2048,768]{2,1,0:T(8,128)(2,1)S(1)}, u32[]{:S(2)}) %copy-start) | copy-done | bytes 12582936
  29.3 4.5 %copy-done.3 = bf16[4,2048,768]{2,1,0:T(8,128)(2,1)} copy-done((bf16[4,2048,768]{2,1,0:T(8,128)(2,1)}, bf16[4,2048,768]{2,1,0:T(8,128)(2,1)S(1)}, u32[]{:S(2)}) %copy-start.3) | copy-done | bytes 12582936
  33.8 4.6 %copy-done.6 = bf16[4,768,2048]{2,1,0:T(8,128)(2,1)} copy-done((bf16[4,768,2048]{2,1,0:T(8,128)(2,1)}, bf16[4,768,2048]{2,1,0:T(8,128)(2,1)S(1)}, u32[]{:S(2)}) %copy-start.6) | copy-done | bytes 12582936
  38.4 12.4 %all-gather.5.cloned.1.call-done.x = bf16[256,2048]{1,0:T(8,128)(2,1)} async-done(((bf16[16,2048]{1,0:T(8,128)(2,1)}), bf16[256,2048]{1,0:T(8,128)(2,1)}) %all-gather.5.cloned.1.call-update) | async-done | bytes 1048592 | tf_op jit(solution)/shard_map/all_gather | solution.py:242
  50.8 0.0 copy-done.25
  50.8 4.6 %copy-done.1 = bf16[4,2048,768]{2,1,0:T(8,128)(2,1)S(1)} copy-done((bf16[4,2048,768]{2,1,0:T(8,128)(2,1)S(1)}, bf16[4,2048,768]{2,1,0:T(8,128)(2,1)}, u32[]{:S(2)}) %copy-start.1) | copy-done | bytes 12582936
  55.4 4.6 %copy-done.4 = bf16[4,2048,768]{2,1,0:T(8,128)(2,1)S(1)} copy-done((bf16[4,2048,768]{2,1,0:T(8,128)(2,1)S(1)}, bf16[4,2048,768]{2,1,0:T(8,128)(2,1)}, u32[]{:S(2)}) %copy-start.4) | copy-done | bytes 12582936
  60.0 1.2 copy-done.22
  61.2 8.5 %gate_up.1 = (f32[4,256,768]{2,1,0:T(8,128)S(1)}, f32[4,256,768]{2,1,0:T(8,128)S(1)}, f32[4,256,768]{2,1,0:T(8,128)S(1)}) custom-call(bf16[256,2048]{1,0:T(8,128)(2,1)S(1)} %copy-done.22, s32[4,6]{1,0:T(4,128)S(1)} %copy-done.25, bf16[4,2048,768]{2,1,0:T(8,128)(2,1)S(1)} %copy-done.1, bf16[4,2048,768]{2,1,0:T(8,128)(2,1)S(1)} %copy-done.4), custom_call_target="tpu_custom_call" | custom-call | flops 6442450944 | bytes 25165824 | tf_op jit(solution)/shard_map/gate_up/pallas_call | solution.py:259
  69.7 0.0 copy-start.10
  69.7 1.7 %copy-done.10 = f32[4,256,768]{2,1,0:T(8,128)} copy-done((f32[4,256,768]{2,1,0:T(8,128)}, f32[4,256,768]{2,1,0:T(8,128)S(1)}, u32[]{:S(2)}) %copy-start.10) | copy-done | bytes 3145752
  71.4 1.7 %copy-done.12 = f32[4,256,768]{2,1,0:T(8,128)} copy-done((f32[4,256,768]{2,1,0:T(8,128)}, f32[4,256,768]{2,1,0:T(8,128)S(1)}, u32[]{:S(2)}) %copy-start.12) | copy-done | bytes 3145752
  73.1 17.7 %all-gather.3.cloned.1.call-done.packet = bf16[256,2176]{1,0:T(8,128)(2,1)} async-done(((bf16[16,2176]{1,0:T(8,128)(2,1)}), bf16[256,2176]{1,0:T(8,128)(2,1)}) %all-gather.3.cloned.1.call-update) | async-done | bytes 1114128 | tf_op jit(solution)/shard_map/all_gather | solution.py:243
  90.8 4.6 %copy-done.7 = bf16[4,768,2048]{2,1,0:T(8,128)(2,1)S(1)} copy-done((bf16[4,768,2048]{2,1,0:T(8,128)(2,1)S(1)}, bf16[4,768,2048]{2,1,0:T(8,128)(2,1)}, u32[]{:S(2)}) %copy-start.7) | copy-done | bytes 12582936
  95.4 1.9 %copy-done.11 = f32[4,256,768]{2,1,0:T(8,128)S(1)} copy-done((f32[4,256,768]{2,1,0:T(8,128)S(1)}, f32[4,256,768]{2,1,0:T(8,128)}, u32[]{:S(2)}) %copy-start.11) | copy-done | bytes 3145752
  97.2 1.9 %copy-done.13 = f32[4,256,768]{2,1,0:T(8,128)S(1)} copy-done((f32[4,256,768]{2,1,0:T(8,128)S(1)}, f32[4,256,768]{2,1,0:T(8,128)}, u32[]{:S(2)}) %copy-start.13) | copy-done | bytes 3145752
  99.1 1.2 copy-done.20
  100.4 4.7 %hidden.1 = (bf16[4,256,768]{2,1,0:T(8,128)(2,1)S(1)}, bf16[4,256,768]{2,1,0:T(8,128)(2,1)S(1)}, bf16[4,256,768]{2,1,0:T(8,128)(2,1)S(1)}, f32[256,128]{1,0:T(8,128)S(1)}) custom-call(bf16[256,2176]{1,0:T(8,128)(2,1)S(1)} %copy-done.20, f32[4,256,768]{2,1,0:T(8,128)S(1)} %get-tuple-element.29.hidden, f32[4,256,768]{2,1,0:T(8,128)S(1)} %copy-done.11, ...), custom_call_target="tpu_custom_call" | custom-call | flops 3221225472 | bytes 12582912 | tf_op jit(solution)/shard_map/hidden/pallas_call | solution.py:270
  105.1 0.0 copy-start.14
  105.1 0.0 copy-start.16
  105.1 0.0 copy-start.18
  105.1 0.0 copy-start.2
  105.1 6.3 %copy-done.2 = bf16[4,2048,768]{2,1,0:T(8,128)(2,1)S(1)} copy-done((bf16[4,2048,768]{2,1,0:T(8,128)(2,1)S(1)}, bf16[4,2048,768]{2,1,0:T(8,128)(2,1)}, u32[]{:S(2)}) %copy-start.2) | copy-done | bytes 12582936
  111.4 4.6 %copy-done.5 = bf16[4,2048,768]{2,1,0:T(8,128)(2,1)S(1)} copy-done((bf16[4,2048,768]{2,1,0:T(8,128)(2,1)S(1)}, bf16[4,2048,768]{2,1,0:T(8,128)(2,1)}, u32[]{:S(2)}) %copy-start.5) | copy-done | bytes 12582936
  115.9 4.6 %copy-done.8 = bf16[4,768,2048]{2,1,0:T(8,128)(2,1)S(1)} copy-done((bf16[4,768,2048]{2,1,0:T(8,128)(2,1)S(1)}, bf16[4,768,2048]{2,1,0:T(8,128)(2,1)}, u32[]{:S(2)}) %copy-start.8) | copy-done | bytes 12582936
  120.5 10.3 %back.1 = (bf16[16,4352]{1,0:T(8,128)(2,1)S(1)}, bf16[16,4352]{1,0:T(8,128)(2,1)S(1)}, bf16[16,4352]{1,0:T(8,128)(2,1)S(1)}, bf16[16,4352]{1,0:T(8,128)(2,1)S(1)}) custom-call(bf16[4,256,768]{2,1,0:T(8,128)(2,1)S(1)} %get-tuple-element.33.hidden, bf16[4,256,768]{2,1,0:T(8,128)(2,1)S(1)} %get-tuple-element.34.d_gate, ...), custom_call_target="tpu_custom_call" | custom-call | flops 2415919104 | bytes 37748736 | tf_op jit(solution)/shard_map/back/pallas_call | solution.py:280
  130.8 0.9 pad_maximum_fusion
  131.7 3.5 %all-to-all-start = ((bf16[4,16,4352]{2,1,0:T(8,128)(2,1)}), bf16[4,16,4352]{2,1,0:T(8,128)(2,1)S(1)}, u32[]{:S(2)}, u32[]{:S(2)}) async-start(bf16[4,16,4352]{2,1,0:T(8,128)(2,1)} %pad_maximum_fusion), calls=%async_computation | async-start | bytes 1114112 | tf_op jit(solution)/shard_map/all_to_all | solution.py:290
  135.2 0.0 copy-start.15
  135.2 1.4 copy-done.15
  136.6 1.4 copy-done.17
  138.0 1.4 copy-done.19
  139.4 9.2 %grads.1 = (f32[4,512,768]{2,1,0:T(8,128)}, f32[4,512,768]{2,1,0:T(8,128)}, f32[4,768,512]{2,1,0:T(8,128)}, f32[8,128]{1,0:T(8,128)S(1)}) custom-call(bf16[256,2048]{1,0:T(8,128)(2,1)S(1)} %copy-done.23, bf16[256,2176]{1,0:T(8,128)(2,1)S(1)} %copy-done.21, bf16[4,256,768]{2,1,0:T(8,128)(2,1)S(1)} %copy-done.15, bf16[4,256,768]{2,1,0:T(8,128)(2,1)S(1)} %copy-done.17, ...), custom_call_target="tpu_custom_call" | custom-call | flops 2415919104 | bytes 18874368 | tf_op jit(solution)/shard_map/grads/pallas_call | solution.py:294
  148.6 0.0 all-to-all-done
  148.7 0.9 sum.1
  149.6 0.7 copy.17
  (24 shorter events, 0.1 us)
Async XLA Ops:
  7.2 43.7 %all-gather.5.cloned.1.call-start = ((), (), s32[]{:S(2)}) async-start(), calls=%async_computation.2 | async-start | bytes 1114112 | tf_op jit(solution)/shard_map/all_gather | solution.py:242
  7.9 82.9 %all-gather.3.cloned.1.call-start = ((), (), s32[]{:S(2)}) async-start(), calls=%async_computation.1 | async-start | bytes 1183744 | tf_op jit(solution)/shard_map/all_gather | solution.py:243
  9.5 0.8 copy-start.24
  11.1 4.6 %copy-start.9 = (bf16[4,2048,768]{2,1,0:T(8,128)(2,1)S(1)}, bf16[4,2048,768]{2,1,0:T(8,128)(2,1)}, u32[]{:S(2)}) copy-start(bf16[4,2048,768]{2,1,0:T(8,128)(2,1)} %refs_0_.1) | copy-start | bytes 37748740
  15.6 35.2 %copy-start.25 = (s32[4,6]{1,0:T(4,128)S(1)}, s32[4,6]{1,0:T(4,128)}, u32[]{:S(2)}) copy-start(s32[4,6]{1,0:T(4,128)} %masks.1) | copy-start | bytes 292
  24.8 4.5 %copy-start = (bf16[4,2048,768]{2,1,0:T(8,128)(2,1)}, bf16[4,2048,768]{2,1,0:T(8,128)(2,1)S(1)}, u32[]{:S(2)}) copy-start(bf16[4,2048,768]{2,1,0:T(8,128)(2,1)S(1)} %get-tuple-element.27.w_gate) | copy-start | bytes 37748740
  29.3 4.5 %copy-start.3 = (bf16[4,2048,768]{2,1,0:T(8,128)(2,1)}, bf16[4,2048,768]{2,1,0:T(8,128)(2,1)S(1)}, u32[]{:S(2)}) copy-start(bf16[4,2048,768]{2,1,0:T(8,128)(2,1)S(1)} %get-tuple-element.28.w_up) | copy-start | bytes 37748740
  33.8 4.6 %copy-start.6 = (bf16[4,768,2048]{2,1,0:T(8,128)(2,1)}, bf16[4,768,2048]{2,1,0:T(8,128)(2,1)S(1)}, u32[]{:S(2)}) copy-start(bf16[4,768,2048]{2,1,0:T(8,128)(2,1)S(1)} %get-tuple-element.32.w_down) | copy-start | bytes 37748740
  50.8 4.6 %copy-start.1 = (bf16[4,2048,768]{2,1,0:T(8,128)(2,1)S(1)}, bf16[4,2048,768]{2,1,0:T(8,128)(2,1)}, u32[]{:S(2)}) copy-start(bf16[4,2048,768]{2,1,0:T(8,128)(2,1)} %copy-done) | copy-start | bytes 37748740
  55.4 4.6 %copy-start.4 = (bf16[4,2048,768]{2,1,0:T(8,128)(2,1)S(1)}, bf16[4,2048,768]{2,1,0:T(8,128)(2,1)}, u32[]{:S(2)}) copy-start(bf16[4,2048,768]{2,1,0:T(8,128)(2,1)} %copy-done.3) | copy-start | bytes 37748740
  60.0 1.2 copy-start.22
  69.7 1.7 %copy-start.10 = (f32[4,256,768]{2,1,0:T(8,128)}, f32[4,256,768]{2,1,0:T(8,128)S(1)}, u32[]{:S(2)}) copy-start(f32[4,256,768]{2,1,0:T(8,128)S(1)} %get-tuple-element.30.slope_up) | copy-start | bytes 9437188
  71.4 1.7 %copy-start.12 = (f32[4,256,768]{2,1,0:T(8,128)}, f32[4,256,768]{2,1,0:T(8,128)S(1)}, u32[]{:S(2)}) copy-start(f32[4,256,768]{2,1,0:T(8,128)S(1)} %get-tuple-element.31.slope_gate) | copy-start | bytes 9437188
  90.8 4.6 %copy-start.7 = (bf16[4,768,2048]{2,1,0:T(8,128)(2,1)S(1)}, bf16[4,768,2048]{2,1,0:T(8,128)(2,1)}, u32[]{:S(2)}) copy-start(bf16[4,768,2048]{2,1,0:T(8,128)(2,1)} %copy-done.6) | copy-start | bytes 37748740
  95.4 1.9 %copy-start.11 = (f32[4,256,768]{2,1,0:T(8,128)S(1)}, f32[4,256,768]{2,1,0:T(8,128)}, u32[]{:S(2)}) copy-start(f32[4,256,768]{2,1,0:T(8,128)} %copy-done.10) | copy-start | bytes 9437188
  97.2 1.9 %copy-start.13 = (f32[4,256,768]{2,1,0:T(8,128)S(1)}, f32[4,256,768]{2,1,0:T(8,128)}, u32[]{:S(2)}) copy-start(f32[4,256,768]{2,1,0:T(8,128)} %copy-done.12) | copy-start | bytes 9437188
  99.1 1.2 copy-start.20
  105.1 25.7 %copy-start.14 = (bf16[4,256,768]{2,1,0:T(8,128)(2,1)}, bf16[4,256,768]{2,1,0:T(8,128)(2,1)S(1)}, u32[]{:S(2)}) copy-start(bf16[4,256,768]{2,1,0:T(8,128)(2,1)S(1)} %get-tuple-element.33.hidden) | copy-start | bytes 4718596
  105.1 25.7 %copy-start.16 = (bf16[4,256,768]{2,1,0:T(8,128)(2,1)}, bf16[4,256,768]{2,1,0:T(8,128)(2,1)S(1)}, u32[]{:S(2)}) copy-start(bf16[4,256,768]{2,1,0:T(8,128)(2,1)S(1)} %get-tuple-element.34.d_gate) | copy-start | bytes 4718596
  105.1 25.7 %copy-start.18 = (bf16[4,256,768]{2,1,0:T(8,128)(2,1)}, bf16[4,256,768]{2,1,0:T(8,128)(2,1)S(1)}, u32[]{:S(2)}) copy-start(bf16[4,256,768]{2,1,0:T(8,128)(2,1)S(1)} %get-tuple-element.35.d_up) | copy-start | bytes 4718596
  105.1 6.3 %copy-start.2 = (bf16[4,2048,768]{2,1,0:T(8,128)(2,1)S(1)}, bf16[4,2048,768]{2,1,0:T(8,128)(2,1)}, u32[]{:S(2)}) copy-start(bf16[4,2048,768]{2,1,0:T(8,128)(2,1)} %copy-done) | copy-start | bytes 37748740
  111.4 4.6 %copy-start.5 = (bf16[4,2048,768]{2,1,0:T(8,128)(2,1)S(1)}, bf16[4,2048,768]{2,1,0:T(8,128)(2,1)}, u32[]{:S(2)}) copy-start(bf16[4,2048,768]{2,1,0:T(8,128)(2,1)} %copy-done.3) | copy-start | bytes 37748740
  115.9 4.6 %copy-start.8 = (bf16[4,768,2048]{2,1,0:T(8,128)(2,1)S(1)}, bf16[4,768,2048]{2,1,0:T(8,128)(2,1)}, u32[]{:S(2)}) copy-start(bf16[4,768,2048]{2,1,0:T(8,128)(2,1)} %copy-done.6) | copy-start | bytes 37748740
  120.5 14.6 %copy-start.21 = (bf16[256,2176]{1,0:T(8,128)(2,1)S(1)}, bf16[256,2176]{1,0:T(8,128)(2,1)}, u32[]{:S(2)}) copy-start(bf16[256,2176]{1,0:T(8,128)(2,1)} %all-gather.3.cloned.1.call-done.packet) | copy-start | bytes 3342340
  120.5 14.7 %copy-start.23 = (bf16[256,2048]{1,0:T(8,128)(2,1)S(1)}, bf16[256,2048]{1,0:T(8,128)(2,1)}, u32[]{:S(2)}) copy-start(bf16[256,2048]{1,0:T(8,128)(2,1)} %all-gather.5.cloned.1.call-done.x) | copy-start | bytes 3145732
  131.7 16.9 %all-to-all-start = ((bf16[4,16,4352]{2,1,0:T(8,128)(2,1)}), bf16[4,16,4352]{2,1,0:T(8,128)(2,1)S(1)}, u32[]{:S(2)}, u32[]{:S(2)}) async-start(bf16[4,16,4352]{2,1,0:T(8,128)(2,1)} %pad_maximum_fusion), calls=%async_computation | async-start | bytes 1114112 | tf_op jit(solution)/shard_map/all_to_all | solution.py:290
  135.2 1.4 copy-start.15
  136.6 1.4 copy-start.17
  138.0 1.4 copy-start.19
Sparse Core Ops, SparseCore 0:
  10.2 40.6 all-gather.4
  53.7 37.0 all-gather.2

commit v4 on v1

v4 whole, which is shorter than its diff:
```python
import functools

import jax
import jax.numpy as jnp
from jax import lax
from jax.experimental import pallas as pl
from jax.experimental.pallas import tpu as pltpu
from jax.sharding import PartitionSpec as P

BLK = 128
LANES = 128
CHUNK = 256
TILE = 256
BUFFERS = 3
MIB = 1 << 20

VMEM = pl.BlockSpec(memory_space=pltpu.VMEM)
SMEM = pl.BlockSpec(memory_space=pltpu.SMEM)
HBM = pl.BlockSpec(memory_space=pltpu.HBM)

NN = (((1,), (0,)), ((), ()))
NT = (((1,), (1,)), ((), ()))
TN = (((0,), (0,)), ((), ()))


def dot(a, b, dims):
    return lax.dot_general(a, b, dims, preferred_element_type=jnp.float32)


def ids_along(shape, axis):
    return lax.broadcasted_iota(jnp.int32, shape, axis)


def aligned(index, size):
    return pl.ds(pl.multiple_of(index * size, size), size)


def route_kernel(cotangent, expert_ids, route_weights, packet):
    rows, width = cotangent.shape
    lanes = packet.shape[1] - width
    packet[:, :width] = cotangent[...]
    at = ids_along((lanes, rows), 0)
    values = route_weights[...].astype(jnp.float32)
    dense = jnp.zeros((lanes, rows), jnp.float32)
    for k in range(expert_ids.shape[0]):
        dense += jnp.where(expert_ids[k : k + 1, :] == at, values[k : k + 1, :], 0.0)
    packet[:, width:] = dense.T.astype(packet.dtype)


def stream(steps, copies, body):
    ahead = BUFFERS - 1
    for step in range(min(ahead, steps)):
        for copy in copies(step, step % BUFFERS):
            copy.start()

    def turn(step, carry):
        later = step + ahead

        @pl.when(later < steps)
        def _():
            for copy in copies(later, lax.rem(later, BUFFERS)):
                copy.start()

        slot = lax.rem(step, BUFFERS)
        for copy in copies(step, slot):
            copy.wait()
        body(step, slot)
        return carry

    lax.fori_loop(0, steps, turn, 0)


def over_tiles(tokens, body):
    if tokens == TILE:
        body(slice(0, TILE))
    else:

        def turn(tile, carry):
            body(aligned(tile, TILE))
            return carry

        lax.fori_loop(0, tokens // TILE, turn, 0)


def gate_up_kernel(x, masks, w_gate, w_up, hidden, slope_up, slope_gate, gate_buf, up_buf, sems):
    local_experts, _, hidden_units = w_gate.shape
    chunks = hidden_units // CHUNK

    def place(step):
        return step // chunks, lax.rem(step, chunks)

    def copies(step, slot):
        expert, chunk = place(step)
        cols = aligned(chunk, CHUNK)
        return [
            pltpu.make_async_copy(w_gate.at[expert, :, cols], gate_buf.at[slot], sems.at[slot, 0]),
            pltpu.make_async_copy(w_up.at[expert, :, cols], up_buf.at[slot], sems.at[slot, 1]),
        ]

    def body(step, slot):
        expert, chunk = place(step)
        cols = aligned(chunk, CHUNK)
        at = ids_along((1, CHUNK), 1)
        keep = jnp.zeros((1, CHUNK), jnp.float32)
        for j in range(CHUNK // BLK):
            kept = masks[expert, chunk * (CHUNK // BLK) + j].astype(jnp.float32)
            keep = jnp.where(at // BLK == j, kept, keep)

        def tile(rows):
            gate_pre = dot(x[rows, :], gate_buf[slot], NN)
            up_proj = dot(x[rows, :], up_buf[slot], NN)
            sigma = 1.0 / (1.0 + jnp.exp(-gate_pre))
            silu = gate_pre * sigma
            up_kept = up_proj * keep
            hidden[expert, rows, cols] = silu * up_kept
            slope_up[expert, rows, cols] = silu * keep
            slope_gate[expert, rows, cols] = up_kept * (sigma + silu * (1.0 - sigma))

        over_tiles(x.shape[0], tile)

    stream(local_experts * chunks, copies, body)


def hidden_kernel(order, *refs):
    packet, units, slope_up, slope_gate, w_gate, w_up, w_down, hidden, d_gate, d_up = refs[:10]
    outs, refs = refs[10 : 10 + len(order)], refs[10 + len(order) :]
    inner, mixed, token_grad, gate_buf, up_buf, down_buf, sems = refs
    local_experts, hidden_units, width = w_down.shape
    tokens, part = mixed.shape
    lanes = packet.shape[1] - width
    chunks = hidden_units // CHUNK
    base = lax.axis_index("expert") * local_experts
    mine = aligned(lax.axis_index("dp"), part)
    inner[...] = jnp.zeros(inner.shape, inner.dtype)
    mixed[...] = jnp.zeros(mixed.shape, mixed.dtype)
    token_grad[...] = jnp.zeros(token_grad.shape, token_grad.dtype)

    def place(step):
        return step // chunks, lax.rem(step, chunks)

    def copies(step, slot):
        expert, chunk = place(step)
        cols = aligned(chunk, CHUNK)
        return [
            pltpu.make_async_copy(w_down.at[expert, cols, :], down_buf.at[slot], sems.at[slot, 0]),
            pltpu.make_async_copy(w_gate.at[expert, mine, cols], gate_buf.at[slot], sems.at[slot, 1]),
            pltpu.make_async_copy(w_up.at[expert, mine, cols], up_buf.at[slot], sems.at[slot, 2]),
        ]

    def body(step, slot):
        expert, chunk = place(step)
        cols = aligned(chunk, CHUNK)

        def tile(rows):
            back = dot(packet[rows, :width], down_buf[slot], NT)
            dense = packet[rows, width:].astype(jnp.float32)
            hit = ids_along((TILE, lanes), 1) == base + expert
            weights = jnp.sum(jnp.where(hit, dense, 0.0), axis=1, keepdims=True)
            part_units = units[expert, rows, cols]
            total = jnp.sum(part_units * back, axis=1, keepdims=True)
            inner[rows, :] += jnp.where(hit, total, 0.0)
            back = back * weights
            new_hidden = (part_units * weights).astype(jnp.bfloat16)
            new_gate = (back * slope_gate[expert, rows, cols]).astype(jnp.bfloat16)
            new_up = (back * slope_up[expert, rows, cols]).astype(jnp.bfloat16)
            hidden[expert, rows, cols] = new_hidden
            d_gate[expert, rows, cols] = new_gate
            d_up[expert, rows, cols] = new_up
            mixed[rows, :] += dot(new_hidden, down_buf[slot, :, mine], NN)
            token_grad[rows, :] += dot(new_gate, gate_buf[slot], NT) + dot(new_up, up_buf[slot], NT)

        over_tiles(tokens, tile)

    stream(local_experts * chunks, copies, body)
    rows = outs[0].shape[0]
    for i, out in enumerate(outs):
        block = slice(i * rows, (i + 1) * rows)
        out[:, :part] = mixed[block].astype(out.dtype)
        out[:, part : 2 * part] = token_grad[block].astype(out.dtype)
        high = inner[block].astype(jnp.bfloat16)
        out[:, 2 * part : 2 * part + lanes] = high
        out[:, 2 * part + lanes :] = (inner[block] - high.astype(jnp.float32)).astype(jnp.bfloat16)


def write_out(steps, place, outs, bufs, sems, body):
    def copies(step, slot):
        return [
            pltpu.make_async_copy(buf.at[slot], out.at[place(step)], sems.at[slot, i])
            for i, (out, buf) in enumerate(zip(outs, bufs))
        ]

    def turn(step, carry):
        slot = lax.rem(step, 2)

        @pl.when(step >= 2)
        def _():
            for copy in copies(step - 2, slot):
                copy.wait()

        body(step, slot)
        for copy in copies(step, slot):
            copy.start()
        return carry

    lax.fori_loop(0, steps, turn, 0)
    for step in range(max(steps - 2, 0), steps):
        for copy in copies(step, step % 2):
            copy.wait()


def grad_in_kernel(x, d_gate, d_up, grad_gate, grad_up, done, x_part, out_gate, out_up, sems):
    local_experts, _, hidden_units = d_gate.shape
    part = x_part.shape[0]
    x_part[...] = x[:, aligned(lax.axis_index("dp"), part)].T
    done[...] = jnp.zeros(done.shape, done.dtype)
    chunks = hidden_units // CHUNK

    def place(step):
        return step // chunks, slice(None), aligned(lax.rem(step, chunks), CHUNK)

    def body(step, slot):
        out_gate[slot] = dot(x_part[...], d_gate[place(step)], NN)
        out_up[slot] = dot(x_part[...], d_up[place(step)], NN)

    write_out(
        local_experts * chunks, place, (grad_gate, grad_up), (out_gate, out_up), sems, body
    )


def grad_out_kernel(packet, hidden, after, grad_down, done, cot_part, out_down, sems):
    local_experts, _, hidden_units = hidden.shape
    part = cot_part.shape[1]
    cot_part[...] = packet[:, aligned(lax.axis_index("dp"), part)]
    done[...] = jnp.zeros(done.shape, done.dtype)
    chunks = hidden_units // CHUNK

    def place(step):
        return step // chunks, aligned(lax.rem(step, chunks), CHUNK), slice(None)

    def body(step, slot):
        units = hidden[step // chunks, :, aligned(lax.rem(step, chunks), CHUNK)]
        out_down[slot] = dot(units, cot_part[...], TN)

    write_out(local_experts * chunks, place, (grad_down,), (out_down,), sems, body)


def reduce_kernel(count, *refs):
    blocks, refs = refs[:count], refs[count:]
    expert_ids, after, route_grad = refs[:3]
    outs, done = refs[3:-1], refs[-1]
    done[...] = jnp.zeros(done.shape, done.dtype)
    rows, both = outs[0].shape
    lanes = (blocks[0].shape[1] - both) // 2
    for j, out in enumerate(outs):
        total = jnp.zeros((rows, both), jnp.float32)
        for block in blocks:
            total += block[j * rows : (j + 1) * rows, :both].astype(jnp.float32)
        out[...] = total.astype(out.dtype)
    inner = jnp.zeros((rows, lanes), jnp.float32)
    for block in blocks:
        tail = block[:rows, both:].astype(jnp.float32)
        inner += tail[:, :lanes] + tail[:, lanes:]
    inner = inner.T
    at = ids_along(inner.shape, 0)
    for k in range(expert_ids.shape[0]):
        hit = jnp.where(expert_ids[k : k + 1, :] == at, inner, 0.0)
        route_grad[k : k + 1, :] = jnp.sum(hit, axis=0, keepdims=True)


def join_kernel(order, *refs):
    blocks, (after, mixed, token_grad) = refs[: len(order)], refs[len(order) :]
    part = blocks[0].shape[1] // 2
    column = lax.axis_index("dp")
    for other, block in zip(order, blocks):
        cols = aligned(column ^ other, part)
        mixed[:, cols] = block[:, :part]
        token_grad[:, cols] = block[:, part:]


def swap(value, axis, mask):
    size = lax.axis_size(axis)
    return lax.ppermute(value, axis, [(i, i ^ mask) for i in range(size)])


def gather(value, axis, masks):
    for mask in masks:
        value = jnp.concatenate([value, swap(value, axis, mask)])
    return value


def masks_of(size):
    masks = [1 << bit for bit in reversed(range(size.bit_length() - 1))]
    order = [0]
    for mask in masks:
        order = order + [other ^ mask for other in order]
    return masks, order


def cost(flops, moved):
    return pl.CostEstimate(flops=flops, bytes_accessed=moved, transcendentals=0)


def params(mib):
    return pltpu.CompilerParams(vmem_limit_bytes=mib * MIB)


def per_device(
    tokens, expert_ids, slot_index, route_weights, w_gate, w_up, w_down, block_masks, cotangent
):
    rows, width = tokens.shape
    local_experts, _, hidden_units = w_gate.shape
    sources, columns = lax.axis_size("expert"), lax.axis_size("dp")
    expert_masks, expert_order = masks_of(sources)
    column_masks, column_order = masks_of(columns)
    lanes = -(-local_experts * sources // LANES) * LANES
    part = width // columns
    everyone = sources * columns * rows
    bf16, f32 = jnp.bfloat16, jnp.float32
    struct = jax.ShapeDtypeStruct
    one = 2 * local_experts * width * hidden_units
    dummy = struct((8, LANES), f32)
    ids_t = expert_ids.T
    w_gate, w_up, w_down = [
        pltpu.with_memory_space_constraint(w, pltpu.HBM) for w in (w_gate, w_up, w_down)
    ]

    packet = pl.pallas_call(
        route_kernel,
        out_shape=struct((rows, width + lanes), bf16),
        in_specs=[VMEM] * 3,
        out_specs=VMEM,
        compiler_params=params(4),
        name="route",
    )(cotangent, ids_t, route_weights.T)
    x = gather(gather(tokens, "dp", column_masks), "expert", expert_masks)
    packets = gather(gather(packet, "dp", column_masks), "expert", expert_masks)

    units = struct((local_experts, everyone, hidden_units), f32)
    factors = pl.pallas_call(
        gate_up_kernel,
        out_shape=[units] * 3,
        in_specs=[VMEM, SMEM, HBM, HBM],
        out_specs=[VMEM] * 3,
        scratch_shapes=[pltpu.VMEM((BUFFERS, width, CHUNK), bf16)] * 2
        + [pltpu.SemaphoreType.DMA((BUFFERS, 2))],
        cost_estimate=cost(2 * everyone * one, 2 * one),
        compiler_params=params(16),
        name="gate_up",
    )(x, block_masks, w_gate, w_up)

    units = struct((local_experts, everyone, hidden_units), bf16)
    hidden, d_gate, d_up, *partials = pl.pallas_call(
        functools.partial(hidden_kernel, expert_order),
        out_shape=[units] * 3
        + [struct((columns * rows, 2 * part + 2 * lanes), bf16)] * sources,
        in_specs=[VMEM] * 4 + [HBM] * 3,
        out_specs=[VMEM] * (3 + sources),
        scratch_shapes=[
            pltpu.VMEM((everyone, lanes), f32),
            pltpu.VMEM((everyone, part), f32),
            pltpu.VMEM((everyone, part), f32),
            pltpu.VMEM((BUFFERS, part, CHUNK), bf16),
            pltpu.VMEM((BUFFERS, part, CHUNK), bf16),
            pltpu.VMEM((BUFFERS, CHUNK, width), bf16),
            pltpu.SemaphoreType.DMA((BUFFERS, 3)),
        ],
        cost_estimate=cost(2 * everyone * one, 2 * one),
        compiler_params=params(24),
        name="hidden",
    )(packets, *factors, w_gate, w_up, w_down)
    arrived = [
        swap(partial, "expert", other) if other else partial
        for other, partial in zip(expert_order, partials)
    ]

    grad_gate, grad_up, done_in = pl.pallas_call(
        grad_in_kernel,
        out_shape=[struct((local_experts, part, hidden_units), f32)] * 2 + [dummy],
        in_specs=[VMEM] * 3,
        out_specs=[HBM] * 2 + [VMEM],
        scratch_shapes=[
            pltpu.VMEM((part, everyone), bf16),
            pltpu.VMEM((2, part, CHUNK), f32),
            pltpu.VMEM((2, part, CHUNK), f32),
            pltpu.SemaphoreType.DMA((2, 2)),
        ],
        cost_estimate=cost(2 * everyone * one // columns, 4 * one // columns),
        compiler_params=params(16),
        name="grad_in",
    )(x, d_gate, d_up)

    route_grad, *blocks, done_sum = pl.pallas_call(
        functools.partial(reduce_kernel, sources),
        out_shape=[struct(ids_t.shape, f32)] + [struct((rows, 2 * part), bf16)] * columns + [dummy],
        in_specs=[VMEM] * (sources + 2),
        out_specs=[VMEM] * (columns + 2),
        compiler_params=params(4),
        name="reduce",
    )(*arrived, ids_t, done_in)
    blocks = [
        swap(block, "dp", other) if other else block for other, block in zip(column_order, blocks)
    ]

    grad_down, done_out = pl.pallas_call(
        grad_out_kernel,
        out_shape=[struct((local_experts, hidden_units, part), f32), dummy],
        in_specs=[VMEM] * 3,
        out_specs=[HBM, VMEM],
        scratch_shapes=[
            pltpu.VMEM((everyone, part), bf16),
            pltpu.VMEM((2, CHUNK, part), f32),
            pltpu.SemaphoreType.DMA((2, 1)),
        ],
        cost_estimate=cost(everyone * one // columns, 2 * one // columns),
        compiler_params=params(16),
        name="grad_out",
    )(packets, hidden, done_sum)

    mixed, token_grad = pl.pallas_call(
        functools.partial(join_kernel, column_order),
        out_shape=[struct((rows, width), bf16)] * 2,
        in_specs=[VMEM] * (columns + 1),
        out_specs=[VMEM] * 2,
        compiler_params=params(4),
        name="join",
    )(*blocks, done_out)
    return (mixed, token_grad, route_grad.T, grad_gate, grad_up, grad_down)


def solution(mesh):
    rows = P(("groups", "expert", "dp"), None)
    experts = P("expert", None, None)
    return jax.shard_map(
        per_device,
        mesh=mesh,
        in_specs=(rows, rows, rows, rows, experts, experts, experts, P("expert", None), rows),
        out_specs=(
            rows,
            rows,
            rows,
            P(("groups", "expert"), "dp", None),
            P(("groups", "expert"), "dp", None),
            P(("groups", "expert"), None, "dp"),
        ),
        check_vma=False,
    )
```

time: 151 us -> 77.1 us (0.51)
  matrix products: 63.3 us -> 0 us
  Pallas kernels: 0 us -> 42 us
  waiting for transfers between devices: 43.9 us -> 12 us
  local copies, waits for them, and re-layouts: 21.3 us -> 3.26 us
  starting transfers between devices: 3.73 us -> 17.5 us
  between operations: 14.1 us -> 0.84 us
  other arithmetic: 3.64 us -> 0.99 us
    dot_general x9 -> x0, matrix products: 63.3 us -> none  [the longest x1 10.1 us: per_device(): jnp.einsum('td,edf->etf', x, w_up, preferred_element_type=jnp.float32)]
    all_gather x1 -> x0, waiting for transfers between devices: 43.9 us -> none  [per_device(): everyone = lax.all_gather(packet, ('dp', 'expert'), axis=0, tiled=True)]
    pallas_call x0 -> x7, Pallas kernels: none -> 42 us  [the longest x1 13.8 us: per_device(): pl.pallas_call(functools.partial(hidden_kernel, expert_order), out_shape=...]
    ppermute x0 -> x14, starting transfers between devices: none -> 17.5 us  [swap(): return lax.ppermute(value, axis, [(i, i ^ mask) for i in range(size)])]
    unnamed x26 -> x20, local copies, waits for them, and re-layouts: 18.1 us -> 3.16 us
    ppermute x0 -> x14, waiting for transfers between devices: none -> 12 us  [swap(): return lax.ppermute(value, axis, [(i, i ^ mask) for i in range(size)])]
    all_to_all x1 -> x0, starting transfers between devices: 3.69 us -> none  [per_device(): lax.all_to_all(back_packet, 'expert', split_axis=0, concat_axis=0, tiled=...]
  transfers between devices with their start and end apart: 2 -> 14, of which waited for: 1 -> 6; matrix products, arithmetic and copies ran while one was open for 12% -> 3% of each run, Pallas kernels for 0% -> 35%
where the time goes in v4:
time: 77.1 us; the launch traced here: 76.7 us
  Pallas kernels  42 us (54%)
  starting transfers between devices  17.5 us (23%)
  waiting for transfers between devices  12 us (16%)
  local copies, waits for them, and re-layouts  3.26 us (4%)
  other arithmetic  0.99 us (1%)
  between operations  0.84 us (1%)
    ppermute x14, starting transfers between devices, swap(): return lax.ppermute(value, axis, [(i, i ^ mask) for i in range(size)])  17.5 us
    pallas_call x1, Pallas kernels, per_device(): pl.pallas_call(functools.partial(hidden_kernel, expert_order), out_shape=...  13.8 us
    pallas_call x1, Pallas kernels, per_device(): pl.pallas_call(gate_up_kernel, out_shape=[units] * 3, in_specs=[VMEM, SME...  12.1 us
    ppermute x14, waiting for transfers between devices, swap(): return lax.ppermute(value, axis, [(i, i ^ mask) for i in range(size)])  12 us
    pallas_call x1, Pallas kernels, per_device(): pl.pallas_call(grad_in_kernel, out_shape=[struct((local_experts, part, hi...  8.02 us
    pallas_call x1, Pallas kernels, per_device(): pl.pallas_call(grad_out_kernel, out_shape=[struct((local_experts, hidden_...  6.61 us
    unnamed x20, local copies, waits for them, and re-layouts  3.16 us
  transfers between devices with their start and end apart: 14, of which 6 were waited for; matrix products, arithmetic and copies ran while one was open for 3% of the time, Pallas kernels for 35%

profile of v4, /device:TPU:0, one launch (start us, length us, event | category | flops | bytes accessed | tf_op | source)
XLA Modules:
  0.0 76.7 jit_solution(8945599163193040989)
XLA Ops:
  0.6 4.1 %collective-permute-start.4 = (bf16[16,2048]{1,0:T(8,128)(2,1)}, bf16[16,2048]{1,0:T(8,128)(2,1)S(1)}, u32[]{:S(2)}, u32[]{:S(2)}) collective-permute-start(bf16[16,2048]{1,0:T(8,128)(2,1)} %param.9), channel_id=1, source_target_pairs={{0,2},{1,3},{2,0},{3,1},{4,6},{5,7},{6,4},{7,5},{8,10},{9,11},{10,... | collective-permute-start | bytes 196616 | tf_op jit(solution)/shard_map/ppermute | solution.py:282
  4.7 0.0 copy-start
  4.7 0.8 %copy-done = bf16[16,2048]{1,0:T(8,128)(2,1)S(1)} copy-done((bf16[16,2048]{1,0:T(8,128)(2,1)S(1)}, bf16[16,2048]{1,0:T(8,128)(2,1)}, u32[]{:S(2)}) %copy-start) | copy-done | bytes 65560
  5.6 0.0 copy-start.1
  5.6 0.7 copy-done.1
  6.3 0.0 copy-start.3
  6.3 0.7 copy-done.3
  6.9 0.1 route.1
  7.0 0.0 collective-permute-start
  7.1 0.8 %constant_dynamic-update-slice_fusion.9 = bf16[256,2048]{1,0:T(8,128)(2,1)S(1)} fusion(bf16[16,2048]{1,0:T(8,128)(2,1)} %param.9), kind=kLoop, calls=%fused_computation.15 | loop fusion | bytes 131072
  8.0 0.6 collective-permute-done.4
  8.6 0.8 %pad_maximum_fusion.5 = bf16[32,2048]{1,0:T(8,128)(2,1)S(1)} fusion(bf16[16,2048]{1,0:T(8,128)(2,1)S(1)} %collective-permute-done.4, bf16[16,2048]{1,0:T(8,128)(2,1)} %param.9), kind=kLoop, calls=%fused_computation.5 | loop fusion | flops 262144 | bytes 262144 | tf_op jit(solution)/shard_map/concatenate | solution.py:287
  9.4 2.5 %collective-permute-start.5 = (bf16[32,2048]{1,0:T(8,128)(2,1)S(1)}, bf16[32,2048]{1,0:T(8,128)(2,1)S(1)}, u32[]{:S(2)}, u32[]{:S(2)}) collective-permute-start(bf16[32,2048]{1,0:T(8,128)(2,1)S(1)} %pad_maximum_fusion.5), channel_id=1, source_target_pairs={{0,1},{1,0},{2,3},{3,2},{4,5},{5,4},{6,7},{7,6},{8,9},{9,8},{10,11... | collective-permute-start | bytes 393224 | tf_op jit(solution)/shard_map/ppermute | solution.py:282
  12.0 0.8 collective-permute-done
  12.8 1.3 %collective-permute-start.1 = (bf16[32,2176]{1,0:T(8,128)(2,1)S(1)}, bf16[32,2176]{1,0:T(8,128)(2,1)S(1)}, u32[]{:S(2)}, u32[]{:S(2)}) collective-permute-start(bf16[32,2176]{1,0:T(8,128)(2,1)S(1)} %pad_maximum_fusion.4), channel_id=1, source_target_pairs={{0,1},{1,0},{2,3},{3,2},{4,5},{5,4},{6,7},{7,6},{8,9},{9,8},{10,11... | collective-permute-start | bytes 417800 | tf_op jit(solution)/shard_map/ppermute | solution.py:282
  14.0 2.2 %collective-permute-done.5 = bf16[32,2048]{1,0:T(8,128)(2,1)S(1)} collective-permute-done((bf16[32,2048]{1,0:T(8,128)(2,1)S(1)}, bf16[32,2048]{1,0:T(8,128)(2,1)S(1)}, u32[]{:S(2)}, u32[]{:S(2)}) %collective-permute-start.5) | collective-permute-done | bytes 131104 | tf_op jit(solution)/shard_map/ppermute | solution.py:282
  16.3 0.0 copy-done.5
  16.3 1.3 %collective-permute-start.6 = (bf16[64,2048]{1,0:T(8,128)(2,1)S(1)}, bf16[64,2048]{1,0:T(8,128)(2,1)S(1)}, u32[]{:S(2)}, u32[]{:S(2)}) collective-permute-start(bf16[64,2048]{1,0:T(8,128)(2,1)S(1)} %pad_maximum_fusion.3), channel_id=1, source_target_pairs={{0,8},{4,12},{8,0},{12,4},{1,9},{5,13},{9,1},{13,5},{2,10},{6,14},... | collective-permute-start | bytes 786440 | tf_op jit(solution)/shard_map/ppermute | solution.py:282
  17.6 0.3 collective-permute-done.1
  17.9 1.6 %collective-permute-start.2 = (bf16[64,2176]{1,0:T(8,128)(2,1)S(1)}, bf16[64,2176]{1,0:T(8,128)(2,1)S(1)}, u32[]{:S(2)}, u32[]{:S(2)}) collective-permute-start(bf16[64,2176]{1,0:T(8,128)(2,1)S(1)} %pad_maximum_fusion.2), channel_id=1, source_target_pairs={{0,8},{4,12},{8,0},{12,4},{1,9},{5,13},{9,1},{13,5},{2,10},{6,14},... | collective-permute-start | bytes 835592 | tf_op jit(solution)/shard_map/ppermute | solution.py:282
  19.5 5.3 %collective-permute-done.6 = bf16[64,2048]{1,0:T(8,128)(2,1)S(1)} collective-permute-done((bf16[64,2048]{1,0:T(8,128)(2,1)S(1)}, bf16[64,2048]{1,0:T(8,128)(2,1)S(1)}, u32[]{:S(2)}, u32[]{:S(2)}) %collective-permute-start.6) | collective-permute-done | bytes 262176 | tf_op jit(solution)/shard_map/ppermute | solution.py:282
  24.8 0.1 collective-permute-start.7
  24.9 0.0 copy-start.4
  24.9 2.8 %collective-permute-done.2 = bf16[64,2176]{1,0:T(8,128)(2,1)S(1)} collective-permute-done((bf16[64,2176]{1,0:T(8,128)(2,1)S(1)}, bf16[64,2176]{1,0:T(8,128)(2,1)S(1)}, u32[]{:S(2)}, u32[]{:S(2)}) %collective-permute-start.2) | collective-permute-done | bytes 278560 | tf_op jit(solution)/shard_map/ppermute | solution.py:282
  27.8 0.1 collective-permute-start.3
  27.9 0.0 collective-permute-done.7
  28.0 0.0 copy-done.4
  28.0 12.1 %gate_up.1 = (f32[4,256,768]{2,1,0:T(8,128)S(1)}, f32[4,256,768]{2,1,0:T(8,128)S(1)}, f32[4,256,768]{2,1,0:T(8,128)S(1)}) custom-call(bf16[256,2048]{1,0:T(8,128)(2,1)S(1)} %constant_dynamic-update-slice_fusion.5.x, s32[4,6]{1,0:T(4,128)S(1)} %copy-done.4, bf16[4,2048,768]{2,1,0:T(8,128)(2,1)} %refs_4_.1, bf16[4,2048,768]{2,1,0:T(8,128)(2,1)} %refs_5_.1), custom_call_target="tpu_custom_call" | custom-call | flops 6442450944 | bytes 25165824 | tf_op jit(solution)/shard_map/gate_up/pallas_call | solution.py:339
  40.1 0.0 collective-permute-done.3
  40.1 0.1 constant_dynamic-update-slice_fusion.refs_0_.packet
  40.2 13.8 %hidden.1 = (bf16[4,256,768]{2,1,0:T(8,128)(2,1)S(1)}, bf16[4,256,768]{2,1,0:T(8,128)(2,1)S(1)}, bf16[4,256,768]{2,1,0:T(8,128)(2,1)S(1)}, bf16[64,1280]{1,0:T(8...) custom-call(bf16[256,2176]{1,0:T(8,128)(2,1)S(1)} %constant_dynamic-update-, ...), custom_call_target="tpu_custom_call" | custom-call | flops 6442450944 | bytes 25165824 | tf_op jit(solution)/shard_map/hidden/pallas_call | solution.py:352
  54.0 1.4 %collective-permute-start.8 = (bf16[64,1280]{1,0:T(8,128)(2,1)S(1)}, bf16[64,1280]{1,0:T(8,128)(2,1)S(1)}, u32[]{:S(2)}, u32[]{:S(2)}) collective-permute-start(bf16[64,1280]{1,0:T(8,128)(2,1)S(1)} %get-tuple-element.33), channel_id=1, source_target_pairs={{0,8},{4,12},{8,0},{12,4},{1,9},{5,13},{9,1},{13,5},{2,10},{6,14},... | collective-permute-start | bytes 491528 | tf_op jit(solution)/shard_map/ppermute | solution.py:282
  55.3 0.2 collective-permute-start.9
  55.6 0.6 collective-permute-start.10
  56.2 8.0 %grad_in.1 = (f32[4,512,768]{2,1,0:T(8,128)}, f32[4,512,768]{2,1,0:T(8,128)}, f32[8,128]{1,0:T(8,128)S(1)}) custom-call(bf16[256,2048]{1,0:T(8,128)(2,1)S(1)} %constant_dynamic-update-slice_fusion.5.x, bf16[4,256,768]{2,1,0:T(8,128)(2,1)S(1)} %get-tuple-element.36.d_gate, bf16[4,256,768]{2,1,0:T(8,128)(2,1)S(1)} %get-tuple-element.37.d_up), custom_call_target="tpu_custom_call" | custom-call | flops 1610612736 | bytes 12582912 | tf_op jit(solution)/shard_map/grad_in/pallas_call | solution.py:376
  64.2 0.0 collective-permute-done.8.refs_1_
  64.2 0.0 collective-permute-done.9.refs_2_
  64.2 0.0 collective-permute-done.10.refs_3_
  64.2 0.0 copy-done.2
  64.2 0.8 %reduce.1 = (f32[8,16]{1,0:T(8,128)}, bf16[16,1024]{1,0:T(8,128)(2,1)S(1)}, bf16[16,1024]{1,0:T(8,128)(2,1)S(1)}, bf16[16,1024]{1,0:T(8,128)(2,1)S(1)}, bf16[16,...) custom-call(bf16[64,1280]{1,0:T(8,128)(2,1)S(1)} %get-tuple-element.32.refs_0_, ...), custom_call_target="tpu_custom_call" | custom-call | tf_op jit(solution)/shard_map/reduce/pallas_call | solution.py:392
  65.0 2.5 %collective-permute-start.11 = (bf16[16,1024]{1,0:T(8,128)(2,1)S(1)}, bf16[16,1024]{1,0:T(8,128)(2,1)S(1)}, u32[]{:S(2)}, u32[]{:S(2)}) collective-permute-start(bf16[16,1024]{1,0:T(8,128)(2,1)S(1)} %get-tuple-element.40), channel_id=1, source_target_pairs={{0,2},{1,3},{2,0},{3,1},{4,6},{5,7},{6,4},{7,5},{8,10},{9,11},{10,... | collective-permute-start | bytes 98312 | tf_op jit(solution)/shard_map/ppermute | solution.py:282
  67.5 1.7 %collective-permute-start.12 = (bf16[16,1024]{1,0:T(8,128)(2,1)S(1)}, bf16[16,1024]{1,0:T(8,128)(2,1)S(1)}, u32[]{:S(2)}, u32[]{:S(2)}) collective-permute-start(bf16[16,1024]{1,0:T(8,128)(2,1)S(1)} %get-tuple-element.41), channel_id=1, source_target_pairs={{0,1},{1,0},{2,3},{3,2},{4,5},{5,4},{6,7},{7,6},{8,9},{9,8},{10,11... | collective-permute-start | bytes 98312 | tf_op jit(solution)/shard_map/ppermute | solution.py:282
  69.2 0.2 collective-permute-start.13
  69.4 6.6 %grad_out.1 = (f32[4,768,512]{2,1,0:T(8,128)}, f32[8,128]{1,0:T(8,128)S(1)}) custom-call(bf16[256,2176]{1,0:T(8,128)(2,1)S(1)} %constant_dynamic-update-slice_fusion.refs_0_.packet, bf16[4,256,768]{2,1,0:T(8,128)(2,1)S(1)} %get-tuple-element.43.hidden, f32[8,128]{1,0:T(8,128)S(1)} %get-tuple-element.44.after), custom_call_target="tpu_custom_call" | custom-call | flops 805306368 | bytes 6291456 | tf_op jit(solution)/shard_map/grad_out/pallas_call | solution.py:404
  76.0 0.0 collective-permute-done.11.refs_1_
  76.0 0.0 collective-permute-done.12.refs_2_
  76.0 0.0 collective-permute-done.13.refs_3_
  76.1 0.7 join.1
  (15 shorter events, 0.3 us)
Async XLA Ops:
  0.6 8.0 %collective-permute-start.4 = (bf16[16,2048]{1,0:T(8,128)(2,1)}, bf16[16,2048]{1,0:T(8,128)(2,1)S(1)}, u32[]{:S(2)}, u32[]{:S(2)}) collective-permute-start(bf16[16,2048]{1,0:T(8,128)(2,1)} %param.9), channel_id=1, source_target_pairs={{0,2},{1,3},{2,0},{3,1},{4,6},{5,7},{6,4},{7,5},{8,10},{9,11},{10,... | collective-permute-start | bytes 196616 | tf_op jit(solution)/shard_map/ppermute | solution.py:282
  4.7 0.8 %copy-start = (bf16[16,2048]{1,0:T(8,128)(2,1)S(1)}, bf16[16,2048]{1,0:T(8,128)(2,1)}, u32[]{:S(2)}) copy-start(bf16[16,2048]{1,0:T(8,128)(2,1)} %cotangent.1) | copy-start | bytes 196612
  5.6 0.7 copy-start.1
  6.3 0.7 copy-start.3
  6.9 9.3 %copy-start.5 = (bf16[16,2048]{1,0:T(8,128)(2,1)S(1)}, bf16[16,2048]{1,0:T(8,128)(2,1)}, u32[]{:S(2)}) copy-start(bf16[16,2048]{1,0:T(8,128)(2,1)} %param.9) | copy-start | bytes 196612
  7.0 5.7 %collective-permute-start = (bf16[16,2176]{1,0:T(8,128)(2,1)S(1)}, bf16[16,2176]{1,0:T(8,128)(2,1)S(1)}, u32[]{:S(2)}, u32[]{:S(2)}) collective-permute-start(bf16[16,2176]{1,0:T(8,128)(2,1)S(1)} %route.1), channel_id=1, source_target_pairs={{0,2},{1,3},{2,0},{3,1},{4,6},{5,7},{6,4},{7,5},{8,10},{9,11},{10,... | collective-permute-start | bytes 208904 | tf_op jit(solution)/shard_map/ppermute | solution.py:282
  9.4 6.8 %collective-permute-start.5 = (bf16[32,2048]{1,0:T(8,128)(2,1)S(1)}, bf16[32,2048]{1,0:T(8,128)(2,1)S(1)}, u32[]{:S(2)}, u32[]{:S(2)}) collective-permute-start(bf16[32,2048]{1,0:T(8,128)(2,1)S(1)} %pad_maximum_fusion.5), channel_id=1, source_target_pairs={{0,1},{1,0},{2,3},{3,2},{4,5},{5,4},{6,7},{7,6},{8,9},{9,8},{10,11... | collective-permute-start | bytes 393224 | tf_op jit(solution)/shard_map/ppermute | solution.py:282
  12.8 5.1 %collective-permute-start.1 = (bf16[32,2176]{1,0:T(8,128)(2,1)S(1)}, bf16[32,2176]{1,0:T(8,128)(2,1)S(1)}, u32[]{:S(2)}, u32[]{:S(2)}) collective-permute-start(bf16[32,2176]{1,0:T(8,128)(2,1)S(1)} %pad_maximum_fusion.4), channel_id=1, source_target_pairs={{0,1},{1,0},{2,3},{3,2},{4,5},{5,4},{6,7},{7,6},{8,9},{9,8},{10,11... | collective-permute-start | bytes 417800 | tf_op jit(solution)/shard_map/ppermute | solution.py:282
  16.3 8.5 %collective-permute-start.6 = (bf16[64,2048]{1,0:T(8,128)(2,1)S(1)}, bf16[64,2048]{1,0:T(8,128)(2,1)S(1)}, u32[]{:S(2)}, u32[]{:S(2)}) collective-permute-start(bf16[64,2048]{1,0:T(8,128)(2,1)S(1)} %pad_maximum_fusion.3), channel_id=1, source_target_pairs={{0,8},{4,12},{8,0},{12,4},{1,9},{5,13},{9,1},{13,5},{2,10},{6,14},... | collective-permute-start | bytes 786440 | tf_op jit(solution)/shard_map/ppermute | solution.py:282
  17.9 9.9 %collective-permute-start.2 = (bf16[64,2176]{1,0:T(8,128)(2,1)S(1)}, bf16[64,2176]{1,0:T(8,128)(2,1)S(1)}, u32[]{:S(2)}, u32[]{:S(2)}) collective-permute-start(bf16[64,2176]{1,0:T(8,128)(2,1)S(1)} %pad_maximum_fusion.2), channel_id=1, source_target_pairs={{0,8},{4,12},{8,0},{12,4},{1,9},{5,13},{9,1},{13,5},{2,10},{6,14},... | collective-permute-start | bytes 835592 | tf_op jit(solution)/shard_map/ppermute | solution.py:282
  24.8 3.1 %collective-permute-start.7 = (bf16[128,2048]{1,0:T(8,128)(2,1)S(1)}, bf16[128,2048]{1,0:T(8,128)(2,1)S(1)}, u32[]{:S(2)}, u32[]{:S(2)}) collective-permute-start(bf16[128,2048]{1,0:T(8,128)(2,1)S(1)} %pad_maximum_fusion.1), channel_id=1, source_target_pairs={{0,4},{4,0},{8,12},{12,8},{1,5},{5,1},{9,13},{13,9},{2,6},{6,2},{1... | collective-permute-start | bytes 1572872 | tf_op jit(solution)/shard_map/ppermute | solution.py:282
  24.9 3.1 %copy-start.4 = (s32[4,6]{1,0:T(4,128)S(1)}, s32[4,6]{1,0:T(4,128)}, u32[]{:S(2)}) copy-start(s32[4,6]{1,0:T(4,128)} %masks.1) | copy-start | bytes 292
  27.8 12.3 %collective-permute-start.3 = (bf16[128,2176]{1,0:T(8,128)(2,1)S(1)}, bf16[128,2176]{1,0:T(8,128)(2,1)S(1)}, u32[]{:S(2)}, u32[]{:S(2)}) collective-permute-start(bf16[128,2176]{1,0:T(8,128)(2,1)S(1)} %pad_maximum_fusion), channel_id=1, source_target_pairs={{0,4},{4,0},{8,12},{12,8},{1,5},{5,1},{9,13},{13,9},{2,6},{6,2},{1... | collective-permute-start | bytes 1671176 | tf_op jit(solution)/shard_map/ppermute | solution.py:282
  54.0 10.2 %collective-permute-start.8 = (bf16[64,1280]{1,0:T(8,128)(2,1)S(1)}, bf16[64,1280]{1,0:T(8,128)(2,1)S(1)}, u32[]{:S(2)}, u32[]{:S(2)}) collective-permute-start(bf16[64,1280]{1,0:T(8,128)(2,1)S(1)} %get-tuple-element.33), channel_id=1, source_target_pairs={{0,8},{4,12},{8,0},{12,4},{1,9},{5,13},{9,1},{13,5},{2,10},{6,14},... | collective-permute-start | bytes 491528 | tf_op jit(solution)/shard_map/ppermute | solution.py:282
  55.3 8.9 %collective-permute-start.9 = (bf16[64,1280]{1,0:T(8,128)(2,1)S(1)}, bf16[64,1280]{1,0:T(8,128)(2,1)S(1)}, u32[]{:S(2)}, u32[]{:S(2)}) collective-permute-start(bf16[64,1280]{1,0:T(8,128)(2,1)S(1)} %get-tuple-element.34), channel_id=1, source_target_pairs={{0,4},{4,0},{8,12},{12,8},{1,5},{5,1},{9,13},{13,9},{2,6},{6,2},{1... | collective-permute-start | bytes 491528 | tf_op jit(solution)/shard_map/ppermute | solution.py:282
  55.6 8.7 %collective-permute-start.10 = (bf16[64,1280]{1,0:T(8,128)(2,1)S(1)}, bf16[64,1280]{1,0:T(8,128)(2,1)S(1)}, u32[]{:S(2)}, u32[]{:S(2)}) collective-permute-start(bf16[64,1280]{1,0:T(8,128)(2,1)S(1)} %get-tuple-element.35), channel_id=1, source_target_pairs={{0,12},{4,8},{8,4},{12,0},{1,13},{5,9},{9,5},{13,1},{2,14},{6,10},... | collective-permute-start | bytes 491528 | tf_op jit(solution)/shard_map/ppermute | solution.py:282
  56.2 8.1 %copy-start.2 = (s32[16,8]{0,1:T(8,128)S(1)}, s32[16,8]{0,1:T(8,128)}, u32[]{:S(2)}) copy-start(s32[16,8]{0,1:T(8,128)} %param.10) | copy-start | bytes 1540
  65.0 11.0 %collective-permute-start.11 = (bf16[16,1024]{1,0:T(8,128)(2,1)S(1)}, bf16[16,1024]{1,0:T(8,128)(2,1)S(1)}, u32[]{:S(2)}, u32[]{:S(2)}) collective-permute-start(bf16[16,1024]{1,0:T(8,128)(2,1)S(1)} %get-tuple-element.40), channel_id=1, source_target_pairs={{0,2},{1,3},{2,0},{3,1},{4,6},{5,7},{6,4},{7,5},{8,10},{9,11},{10,... | collective-permute-start | bytes 98312 | tf_op jit(solution)/shard_map/ppermute | solution.py:282
  67.5 8.5 %collective-permute-start.12 = (bf16[16,1024]{1,0:T(8,128)(2,1)S(1)}, bf16[16,1024]{1,0:T(8,128)(2,1)S(1)}, u32[]{:S(2)}, u32[]{:S(2)}) collective-permute-start(bf16[16,1024]{1,0:T(8,128)(2,1)S(1)} %get-tuple-element.41), channel_id=1, source_target_pairs={{0,1},{1,0},{2,3},{3,2},{4,5},{5,4},{6,7},{7,6},{8,9},{9,8},{10,11... | collective-permute-start | bytes 98312 | tf_op jit(solution)/shard_map/ppermute | solution.py:282
  69.2 6.8 %collective-permute-start.13 = (bf16[16,1024]{1,0:T(8,128)(2,1)S(1)}, bf16[16,1024]{1,0:T(8,128)(2,1)S(1)}, u32[]{:S(2)}, u32[]{:S(2)}) collective-permute-start(bf16[16,1024]{1,0:T(8,128)(2,1)S(1)} %get-tuple-element.42), channel_id=1, source_target_pairs={{0,3},{1,2},{2,1},{3,0},{4,7},{5,6},{6,5},{7,4},{8,11},{9,10},{10,... | collective-permute-start | bytes 98312 | tf_op jit(solution)/shard_map/ppermute | solution.py:282

commit v5 on v4

v5 whole, which is shorter than its diff:
```python
import functools

import jax
import jax.numpy as jnp
from jax import lax
from jax.experimental import pallas as pl
from jax.experimental.pallas import tpu as pltpu
from jax.sharding import PartitionSpec as P

BLK = 128
LANES = 128
CHUNK = 256
TILE = 256
MIB = 1 << 20

VMEM = pl.BlockSpec(memory_space=pltpu.VMEM)
SMEM = pl.BlockSpec(memory_space=pltpu.SMEM)
HBM = pl.BlockSpec(memory_space=pltpu.HBM)

NN = (((1,), (0,)), ((), ()))
NT = (((1,), (1,)), ((), ()))


def dot(a, b, dims):
    return lax.dot_general(a, b, dims, preferred_element_type=jnp.float32)


def ids_along(shape, axis):
    return lax.broadcasted_iota(jnp.int32, shape, axis)


def aligned(index, size):
    return pl.ds(pl.multiple_of(index * size, size), size)


def route_kernel(
    tokens, cotangent, expert_ids, route_weights, own_tokens, packet, ids, values, sems
):
    rows, width = tokens.shape
    lanes = packet.shape[1] - width
    copies = [
        pltpu.make_async_copy(expert_ids, ids, sems.at[0]),
        pltpu.make_async_copy(route_weights, values, sems.at[1]),
        pltpu.make_async_copy(tokens, own_tokens, sems.at[2]),
        pltpu.make_async_copy(cotangent, packet.at[:, :width], sems.at[3]),
    ]
    for copy in copies:
        copy.start()
    for copy in copies:
        copy.wait()
    at = ids_along((lanes, rows), 0)
    weights = values[...].astype(jnp.float32)
    dense = jnp.zeros((lanes, rows), jnp.float32)
    for k in range(ids.shape[0]):
        dense += jnp.where(ids[k : k + 1, :] == at, weights[k : k + 1, :], 0.0)
    packet[:, width:] = dense.T.astype(packet.dtype)


def load_kernel(source, value, target, same, sem):
    copy = pltpu.make_async_copy(source, target, sem)
    copy.start()
    same[...] = value[...]
    copy.wait()


def over_tiles(tokens, body):
    if tokens == TILE:
        body(slice(0, TILE))
    else:

        def turn(tile, carry):
            body(aligned(tile, TILE))
            return carry

        lax.fori_loop(0, tokens // TILE, turn, 0)


def gate_up_kernel(x, masks, gate, up, hidden, slope_up, slope_gate):
    local_experts, _, hidden_units = gate.shape
    bf16 = jnp.bfloat16

    def one_expert(expert, carry):
        def tile(rows):
            for start in range(0, hidden_units, CHUNK):
                cols = slice(start, start + CHUNK)
                gate_pre = dot(x[rows, :], gate[expert, :, cols], NN)
                up_proj = dot(x[rows, :], up[expert, :, cols], NN)
                at = ids_along((1, CHUNK), 1)
                keep = jnp.zeros((1, CHUNK), jnp.float32)
                for j in range(CHUNK // BLK):
                    kept = masks[expert, start // BLK + j].astype(jnp.float32)
                    keep = jnp.where(at // BLK == j, kept, keep)
                sigma = 1.0 / (1.0 + jnp.exp(-gate_pre))
                silu = gate_pre * sigma
                up_kept = up_proj * keep
                hidden[expert, rows, cols] = (silu * up_kept).astype(bf16)
                slope_up[expert, rows, cols] = (silu * keep).astype(bf16)
                slope = up_kept * (sigma + silu * (1.0 - sigma))
                slope_gate[expert, rows, cols] = slope.astype(bf16)

        over_tiles(x.shape[0], tile)
        return carry

    lax.fori_loop(0, local_experts, one_expert, 0)


def stack(pieces, target, cols=slice(None)):
    rows = pieces[0].shape[0]
    for i, piece in enumerate(pieces):
        target[i * rows : (i + 1) * rows] = piece[:, cols]


def hidden_kernel(count, *refs):
    pieces, refs = refs[:count], refs[count:]
    units, slope_up, slope_gate, gate, up, w_down, hidden, d_gate, d_up = refs[:9]
    outs, refs = refs[9 : 9 + count], refs[9 + count :]
    packet, inner, mixed, token_grad, down_buf, sems = refs
    local_experts, hidden_units, width = w_down.shape
    tokens, part = mixed.shape
    lanes = packet.shape[1] - width
    base = lax.axis_index("expert") * local_experts
    mine = aligned(lax.axis_index("dp"), part)
    inner[...] = jnp.zeros(inner.shape, inner.dtype)
    mixed[...] = jnp.zeros(mixed.shape, mixed.dtype)
    token_grad[...] = jnp.zeros(token_grad.shape, token_grad.dtype)

    def copies(expert):
        slot = lax.rem(expert, 2)
        return [
            pltpu.make_async_copy(
                w_down.at[expert, slice(start, start + CHUNK), :],
                down_buf.at[slot, slice(start, start + CHUNK), :],
                sems.at[slot, start // CHUNK],
            )
            for start in range(0, hidden_units, CHUNK)
        ]

    for copy in copies(0):
        copy.start()
    stack(pieces, packet)

    def one_expert(expert, carry):
        @pl.when(expert + 1 < local_experts)
        def _():
            for copy in copies(expert + 1):
                copy.start()

        down = down_buf.at[lax.rem(expert, 2)]
        for copy in copies(expert):
            copy.wait()

        def tile(rows):
            dense = packet[rows, width:].astype(jnp.float32)
            hit = ids_along((TILE, lanes), 1) == base + expert
            weights = jnp.sum(jnp.where(hit, dense, 0.0), axis=1, keepdims=True)
            total = jnp.zeros((TILE, 1), jnp.float32)
            for start in range(0, hidden_units, CHUNK):
                cols = slice(start, start + CHUNK)
                back = dot(packet[rows, :width], down[cols, :], NT)
                part_units = units[expert, rows, cols].astype(jnp.float32)
                total += jnp.sum(part_units * back, axis=1, keepdims=True)
                back = back * weights
                bf16, f32 = jnp.bfloat16, jnp.float32
                hidden[expert, rows, cols] = (part_units * weights).astype(bf16)
                d_gate[expert, rows, cols] = (back * slope_gate[expert, rows, cols].astype(f32)).astype(bf16)
                d_up[expert, rows, cols] = (back * slope_up[expert, rows, cols].astype(f32)).astype(bf16)
            inner[rows, :] += jnp.where(hit, total, 0.0)
            mixed[rows, :] += dot(hidden[expert, rows, :], down[:, mine], NN)
            token_grad[rows, :] += dot(d_gate[expert, rows, :], gate[expert, mine, :], NT) + dot(
                d_up[expert, rows, :], up[expert, mine, :], NT
            )

        over_tiles(tokens, tile)
        return carry

    lax.fori_loop(0, local_experts, one_expert, 0)
    rows = outs[0].shape[0]
    for i, out in enumerate(outs):
        block = slice(i * rows, (i + 1) * rows)
        out[:, :part] = mixed[block].astype(out.dtype)
        out[:, part : 2 * part] = token_grad[block].astype(out.dtype)
        high = inner[block].astype(jnp.bfloat16)
        out[:, 2 * part : 2 * part + lanes] = high
        out[:, 2 * part + lanes :] = (inner[block] - high.astype(jnp.float32)).astype(jnp.bfloat16)


def write_out(steps, place, outs, bufs, sems, body):
    def copies(step, slot):
        return [
            pltpu.make_async_copy(buf.at[slot], out.at[place(step)], sems.at[slot, i])
            for i, (out, buf) in enumerate(zip(outs, bufs))
        ]

    def turn(step, carry):
        slot = lax.rem(step, 2)

        @pl.when(step >= 2)
        def _():
            for copy in copies(step - 2, slot):
                copy.wait()

        body(step, slot)
        for copy in copies(step, slot):
            copy.start()
        return carry

    lax.fori_loop(0, steps, turn, 0)
    for step in range(max(steps - 2, 0), steps):
        for copy in copies(step, step % 2):
            copy.wait()


def grad_in_kernel(x, d_gate, d_up, grad_gate, grad_up, done, x_part, out_gate, out_up, sems):
    local_experts, _, hidden_units = d_gate.shape
    part, rows = x_part.shape[0], out_gate.shape[1]
    x_part[...] = x[:, aligned(lax.axis_index("dp"), part)].T
    done[...] = jnp.zeros(done.shape, done.dtype)
    blocks = part // rows

    def place(step):
        return step // blocks, aligned(lax.rem(step, blocks), rows), slice(None)

    def body(step, slot):
        expert, block, _ = place(step)
        out_gate[slot] = dot(x_part[block, :], d_gate[expert], NN)
        out_up[slot] = dot(x_part[block, :], d_up[expert], NN)

    write_out(
        local_experts * blocks, place, (grad_gate, grad_up), (out_gate, out_up), sems, body
    )


def grad_out_kernel(count, *refs):
    pieces, refs = refs[:count], refs[count:]
    hidden, after, grad_down, done, cot_part, out_down, sems = refs
    local_experts, _, hidden_units = hidden.shape
    part = cot_part.shape[1]
    stack(pieces, cot_part, aligned(lax.axis_index("dp"), part))
    done[...] = jnp.zeros(done.shape, done.dtype)
    chunks = hidden_units // CHUNK

    def place(step):
        return step // chunks, aligned(lax.rem(step, chunks), CHUNK), slice(None)

    def body(step, slot):
        units = hidden[step // chunks, :, aligned(lax.rem(step, chunks), CHUNK)]
        out_down[slot] = dot(units.T, cot_part[...], NN)

    write_out(local_experts * chunks, place, (grad_down,), (out_down,), sems, body)


def reduce_kernel(count, *refs):
    blocks, refs = refs[:count], refs[count:]
    expert_ids, after, route_grad = refs[:3]
    outs, done = refs[3:-1], refs[-1]
    done[...] = jnp.zeros(done.shape, done.dtype)
    rows, both = outs[0].shape
    lanes = (blocks[0].shape[1] - both) // 2
    for j, out in enumerate(outs):
        total = jnp.zeros((rows, both), jnp.float32)
        for block in blocks:
            total += block[j * rows : (j + 1) * rows, :both].astype(jnp.float32)
        out[...] = total.astype(out.dtype)
    inner = jnp.zeros((rows, lanes), jnp.float32)
    for block in blocks:
        tail = block[:rows, both:].astype(jnp.float32)
        inner += tail[:, :lanes] + tail[:, lanes:]
    inner = inner.T
    at = ids_along(inner.shape, 0)
    for k in range(expert_ids.shape[0]):
        hit = jnp.where(expert_ids[k : k + 1, :] == at, inner, 0.0)
        route_grad[k : k + 1, :] = jnp.sum(hit, axis=0, keepdims=True)


def join_kernel(order, *refs):
    blocks, (after, mixed, token_grad) = refs[: len(order)], refs[len(order) :]
    part = blocks[0].shape[1] // 2
    column = lax.axis_index("dp")
    for other, block in zip(order, blocks):
        cols = aligned(column ^ other, part)
        mixed[:, cols] = block[:, :part]
        token_grad[:, cols] = block[:, part:]


def swap(value, axis, mask):
    size = lax.axis_size(axis)
    return lax.ppermute(value, axis, [(i, i ^ mask) for i in range(size)])


def exchange(value, axis, masks):
    return [swap(value, axis, mask) for mask in masks]


def in_hbm(array):
    return pltpu.with_memory_space_constraint(array, pltpu.HBM)


def in_vmem(array):
    return pltpu.with_memory_space_constraint(array, pltpu.VMEM)


def cost(flops, moved):
    return pl.CostEstimate(flops=flops, bytes_accessed=moved, transcendentals=0)


def params(mib):
    return pltpu.CompilerParams(vmem_limit_bytes=mib * MIB)


def per_device(
    tokens, expert_ids, slot_index, route_weights, w_gate, w_up, w_down, block_masks, cotangent
):
    rows, width = tokens.shape
    local_experts, _, hidden_units = w_gate.shape
    sources, columns = lax.axis_size("expert"), lax.axis_size("dp")
    column_order = list(range(columns))
    chips = list(range(2, sources, 2))
    expert_order = [0] + chips + [chip ^ 1 for chip in [0] + chips]
    lanes = -(-local_experts * sources // LANES) * LANES
    part = width // columns
    everyone = sources * columns * rows
    bf16, f32 = jnp.bfloat16, jnp.float32
    struct = jax.ShapeDtypeStruct
    one = 2 * local_experts * width * hidden_units
    dummy = struct((8, LANES), f32)
    ids_t = expert_ids.T
    w_gate, w_up, w_down = [in_hbm(w) for w in (w_gate, w_up, w_down)]

    own_tokens, packet = pl.pallas_call(
        route_kernel,
        out_shape=[struct(tokens.shape, bf16), struct((rows, width + lanes), bf16)],
        in_specs=[HBM] * 4,
        out_specs=[VMEM] * 2,
        scratch_shapes=[
            pltpu.VMEM(ids_t.shape, jnp.int32),
            pltpu.VMEM(ids_t.shape, bf16),
            pltpu.SemaphoreType.DMA((4,)),
        ],
        compiler_params=params(2),
        name="route",
    )(*[in_hbm(a) for a in (tokens, cotangent, ids_t, route_weights.T)])

    def load(weight, value, name):
        return pl.pallas_call(
            load_kernel,
            out_shape=[
                pltpu.VMEM(weight.shape, weight.dtype),
                struct(value.shape, value.dtype),
            ],
            in_specs=[HBM, VMEM],
            out_specs=[VMEM] * 2,
            scratch_shapes=[pltpu.SemaphoreType.DMA],
            cost_estimate=cost(0, one),
            compiler_params=params(1),
            name=name,
        )(weight, value)

    arrived = exchange(own_tokens, "dp", column_order[1:])
    gate, own_tokens = load(w_gate, own_tokens, "load_gate")
    x_column = jnp.concatenate([own_tokens] + arrived)
    across = exchange(x_column, "expert", chips)
    packet_column = jnp.concatenate([packet] + exchange(packet, "dp", column_order[1:]))
    packet_column, across = lax.optimization_barrier((packet_column, across))
    up, x_column = load(w_up, x_column, "load_up")
    gate, up = in_vmem(gate), in_vmem(up)
    x = jnp.concatenate([x_column] + across)
    x = jnp.concatenate([x, swap(x, "expert", 1)])
    pieces = exchange(packet_column, "expert", expert_order[1:])

    units = struct((local_experts, everyone, hidden_units), bf16)
    factors = pl.pallas_call(
        gate_up_kernel,
        out_shape=[units] * 3,
        in_specs=[VMEM, SMEM, VMEM, VMEM],
        out_specs=[VMEM] * 3,
        cost_estimate=cost(2 * everyone * one, 2 * one),
        compiler_params=params(6),
        name="gate_up",
    )(x, block_masks, gate, up)
    pieces = [packet_column] + pieces

    hidden, d_gate, d_up, *partials = pl.pallas_call(
        functools.partial(hidden_kernel, sources),
        out_shape=[units] * 3
        + [struct((columns * rows, 2 * part + 2 * lanes), bf16)] * sources,
        in_specs=[VMEM] * (5 + sources) + [HBM],
        out_specs=[VMEM] * (3 + sources),
        scratch_shapes=[
            pltpu.VMEM((everyone, width + lanes), bf16),
            pltpu.VMEM((everyone, lanes), f32),
            pltpu.VMEM((everyone, part), f32),
            pltpu.VMEM((everyone, part), f32),
            pltpu.VMEM((min(2, local_experts), hidden_units, width), bf16),
            pltpu.SemaphoreType.DMA((2, hidden_units // CHUNK)),
        ],
        cost_estimate=cost(2 * everyone * one, 2 * one),
        compiler_params=params(12 + (everyone - TILE) * (2 * part + lanes) * 14 // MIB),
        name="hidden",
    )(*pieces, *factors, gate, up, w_down)
    arrived = [
        swap(partial, "expert", other) if other else partial
        for other, partial in zip(expert_order, partials)
    ]

    grad_gate, grad_up, done_in = pl.pallas_call(
        grad_in_kernel,
        out_shape=[struct((local_experts, part, hidden_units), f32)] * 2 + [dummy],
        in_specs=[VMEM] * 3,
        out_specs=[HBM] * 2 + [VMEM],
        scratch_shapes=[
            pltpu.VMEM((part, everyone), bf16),
            pltpu.VMEM((2, min(part, CHUNK), hidden_units), f32),
            pltpu.VMEM((2, min(part, CHUNK), hidden_units), f32),
            pltpu.SemaphoreType.DMA((2, 2)),
        ],
        cost_estimate=cost(2 * everyone * one // columns, 4 * one // columns),
        compiler_params=params(16),
        name="grad_in",
    )(x, d_gate, d_up)

    route_grad, *blocks, done_sum = pl.pallas_call(
        functools.partial(reduce_kernel, sources),
        out_shape=[struct(ids_t.shape, f32)] + [struct((rows, 2 * part), bf16)] * columns + [dummy],
        in_specs=[VMEM] * (sources + 2),
        out_specs=[VMEM] * (columns + 2),
        compiler_params=params(4),
        name="reduce",
    )(*arrived, ids_t, done_in)
    blocks = [
        swap(block, "dp", other) if other else block for other, block in zip(column_order, blocks)
    ]

    grad_down, done_out = pl.pallas_call(
        functools.partial(grad_out_kernel, sources),
        out_shape=[struct((local_experts, hidden_units, part), f32), dummy],
        in_specs=[VMEM] * (2 + sources),
        out_specs=[HBM, VMEM],
        scratch_shapes=[
            pltpu.VMEM((everyone, part), bf16),
            pltpu.VMEM((2, CHUNK, part), f32),
            pltpu.SemaphoreType.DMA((2, 1)),
        ],
        cost_estimate=cost(everyone * one // columns, 2 * one // columns),
        compiler_params=params(16),
        name="grad_out",
    )(*pieces, hidden, done_sum)

    mixed, token_grad = pl.pallas_call(
        functools.partial(join_kernel, column_order),
        out_shape=[struct((rows, width), bf16)] * 2,
        in_specs=[VMEM] * (columns + 1),
        out_specs=[VMEM] * 2,
        compiler_params=params(4),
        name="join",
    )(*blocks, done_out)
    return (mixed, token_grad, route_grad.T, grad_gate, grad_up, grad_down)


def solution(mesh):
    rows = P(("groups", "expert", "dp"), None)
    experts = P("expert", None, None)
    return jax.shard_map(
        per_device,
        mesh=mesh,
        in_specs=(rows, rows, rows, rows, experts, experts, experts, P("expert", None), rows),
        out_specs=(
            rows,
            rows,
            rows,
            P(("groups", "expert"), "dp", None),
            P(("groups", "expert"), "dp", None),
            P(("groups", "expert"), None, "dp"),
        ),
        check_vma=False,
    )
```

time: 77.1 us -> 68.9 us (0.89)
  waiting for transfers between devices: 12 us -> 4.61 us
  starting transfers between devices: 17.5 us -> 20.8 us
  local copies, waits for them, and re-layouts: 3.26 us -> 0.11 us
  other arithmetic: 0.99 us -> 0.06 us
    ppermute x14 -> x17, waiting for transfers between devices: 12 us -> 4.61 us  [swap(): return lax.ppermute(value, axis, [(i, i ^ mask) for i in range(size)])]
    pallas_call x3 -> x5, Pallas kernels: 20.5 us -> 25.9 us  [the longest x2 9.17 us: load(): pl.pallas_call(load_kernel, out_shape=[pltpu.VMEM(weight.shape, weight.dt...]
    pallas_call x1, Pallas kernels: 12.1 us -> 8.45 us  [per_device(): pl.pallas_call(gate_up_kernel, out_shape=[units] * 3, in_specs=[VMEM, SME...]
    ppermute x14 -> x17, starting transfers between devices: 17.5 us -> 20.8 us  [swap(): return lax.ppermute(value, axis, [(i, i ^ mask) for i in range(size)])]
    unnamed x20 -> x9, local copies, waits for them, and re-layouts: 3.16 us -> 0.07 us
    pallas_call x1, Pallas kernels: 8.02 us -> 6.37 us  [per_device(): pl.pallas_call(grad_in_kernel, out_shape=[struct((local_experts, part, hi...]
    concatenate x6 -> x2, other arithmetic: 0.99 us -> 0.06 us  [the longest x1 0.04 us: per_device(): x = jnp.concatenate([x_column] + across)]
  transfers between devices with their start and end apart: 14 -> 17, of which waited for: 6 -> 2; matrix products, arithmetic and copies ran while one was open for 3% -> 0% of each run, Pallas kernels for 35% -> 45%
where the time goes in v5:
time: 68.9 us; the launch traced here: 68.6 us
  Pallas kernels  42.2 us (61%)
  starting transfers between devices  20.8 us (30%)
  waiting for transfers between devices  4.61 us (7%)
  between operations  0.9 us (1%)
    ppermute x17, starting transfers between devices, swap(): return lax.ppermute(value, axis, [(i, i ^ mask) for i in range(size)])  20.8 us
    pallas_call x2, Pallas kernels, load(): pl.pallas_call(load_kernel, out_shape=[pltpu.VMEM(weight.shape, weight.dt...  9.17 us
    pallas_call x1, Pallas kernels, per_device(): pl.pallas_call(functools.partial(hidden_kernel, sources), out_shape=[unit...  9.09 us
    pallas_call x1, Pallas kernels, per_device(): pl.pallas_call(gate_up_kernel, out_shape=[units] * 3, in_specs=[VMEM, SME...  8.45 us
    pallas_call x1, Pallas kernels, per_device(): pl.pallas_call(functools.partial(grad_out_kernel, sources), out_shape=[st...  6.62 us
    pallas_call x1, Pallas kernels, per_device(): pl.pallas_call(grad_in_kernel, out_shape=[struct((local_experts, part, hi...  6.37 us
    ppermute x17, waiting for transfers between devices, swap(): return lax.ppermute(value, axis, [(i, i ^ mask) for i in range(size)])  4.61 us
  transfers between devices with their start and end apart: 17, of which 2 were waited for; matrix products, arithmetic and copies ran while one was open for 0% of the time, Pallas kernels for 45%

profile of v5, /device:TPU:0, one launch (start us, length us, event | category | flops | bytes accessed | tf_op | source)
XLA Modules:
  0.0 68.6 jit_solution(14483332763467754286)
XLA Ops:
  0.6 1.0 %route.1 = (bf16[16,2048]{1,0:T(8,128)(2,1)S(1)}, bf16[16,2176]{1,0:T(8,128)(2,1)S(1)}) custom-call(bf16[16,2048]{1,0:T(8,128)(2,1)} %tokens.1, bf16[16,2048]{1,0:T(8,128)(2,1)} %cotangent.1, s32[8,16]{1,0:T(8,128)} %bitcast.3, bf16[8,16]{1,0:T(8,128)(2,1)} %bitcast.5), custom_call_target="tpu_custom_call" | custom-call | tf_op jit(solution)/shard_map/route/pallas_call | solution.py:329
  1.7 5.1 %collective-permute-start.5 = (bf16[16,2048]{1,0:T(8,128)(2,1)S(1)}, bf16[16,2048]{1,0:T(8,128)(2,1)S(1)}, u32[]{:S(2)}, u32[]{:S(2)}) collective-permute-start(bf16[16,2048]{1,0:T(8,128)(2,1)S(1)} %get-tuple-element.38.value), channel_id=1, source_target_pairs={{0,3},{1,2},{2,1},{3,0},{4,7},{5,6},{6,5},{7,4},{8,11},{9,10},{10,... | collective-permute-start | bytes 196616 | tf_op jit(solution)/shard_map/ppermute | solution.py:287
  6.8 0.0 collective-permute-start.4
  6.8 0.6 collective-permute-start.3
  7.4 3.7 %collective-permute-start.2 = (bf16[16,2176]{1,0:T(8,128)(2,1)S(1)}, bf16[16,2176]{1,0:T(8,128)(2,1)S(1)}, u32[]{:S(2)}, u32[]{:S(2)}) collective-permute-start(bf16[16,2176]{1,0:T(8,128)(2,1)S(1)} %get-tuple-element.37), channel_id=1, source_target_pairs={{0,3},{1,2},{2,1},{3,0},{4,7},{5,6},{6,5},{7,4},{8,11},{9,10},{10,... | collective-permute-start | bytes 208904 | tf_op jit(solution)/shard_map/ppermute | solution.py:287
  11.2 0.0 collective-permute-start.1
  11.2 4.6 %load_gate.1 = (bf16[4,2048,768]{2,1,0:T(8,128)(2,1)S(1)}, bf16[16,2048]{1,0:T(8,128)(2,1)S(1)}) custom-call(bf16[4,2048,768]{2,1,0:T(8,128)(2,1)} %source.2, bf16[16,2048]{1,0:T(8,128)(2,1)S(1)} %get-tuple-element.38.value), custom_call_target="tpu_custom_call" | custom-call | bytes 12582912 | tf_op jit(solution)/shard_map/load_gate/pallas_call | solution.py:344
  15.8 0.0 collective-permute-done.3
  15.8 0.7 %collective-permute-start = (bf16[16,2176]{1,0:T(8,128)(2,1)S(1)}, bf16[16,2176]{1,0:T(8,128)(2,1)S(1)}, u32[]{:S(2)}, u32[]{:S(2)}) collective-permute-start(bf16[16,2176]{1,0:T(8,128)(2,1)S(1)} %get-tuple-element.37), channel_id=1, source_target_pairs={{0,1},{1,0},{2,3},{3,2},{4,5},{5,4},{6,7},{7,6},{8,9},{9,8},{10,11... | collective-permute-start | bytes 208904 | tf_op jit(solution)/shard_map/ppermute | solution.py:287
  16.5 0.0 collective-permute-done.4
  16.5 0.0 collective-permute-done.5
  16.6 0.0 copy-start.1
  16.6 1.7 %collective-permute-start.6 = (bf16[64,2048]{1,0:T(8,128)(2,1)S(1)}, bf16[64,2048]{1,0:T(8,128)(2,1)S(1)}, u32[]{:S(2)}, u32[]{:S(2)}) collective-permute-start(bf16[64,2048]{1,0:T(8,128)(2,1)S(1)} %constant_dynamic-update-slice_fusion.value), channel_id=1, source_target_pairs={{0,8},{4,12},{8,0},{12,4},{1,9},{5,13},{9,1},{13,5},{2,10},{6,14},... | collective-permute-start | bytes 786440 | tf_op jit(solution)/shard_map/ppermute | solution.py:287
  18.3 4.6 %load_up.1 = (bf16[4,2048,768]{2,1,0:T(8,128)(2,1)S(1)}, bf16[64,2048]{1,0:T(8,128)(2,1)S(1)}) custom-call(bf16[4,2048,768]{2,1,0:T(8,128)(2,1)} %source.3, bf16[64,2048]{1,0:T(8,128)(2,1)S(1)} %constant_dynamic-update-slice_fusion.value), custom_call_target="tpu_custom_call" | custom-call | bytes 12582912 | tf_op jit(solution)/shard_map/load_up/pallas_call | solution.py:344
  22.9 0.0 collective-permute-done.2
  22.9 0.0 collective-permute-done.1
  22.9 0.0 collective-permute-done
  22.9 0.4 collective-permute-done.6
  23.3 0.1 collective-permute-start.10
  23.4 1.7 %collective-permute-start.9 = (bf16[64,2176]{1,0:T(8,128)(2,1)S(1)}, bf16[64,2176]{1,0:T(8,128)(2,1)S(1)}, u32[]{:S(2)}, u32[]{:S(2)}) collective-permute-start(bf16[64,2176]{1,0:T(8,128)(2,1)S(1)} %pad_maximum_fusion.1.refs_0_), channel_id=1, source_target_pairs={{0,12},{4,8},{8,4},{12,0},{1,13},{5,9},{9,5},{13,1},{2,14},{6,10},... | collective-permute-start | bytes 835592 | tf_op jit(solution)/shard_map/ppermute | solution.py:287
  25.1 0.0 collective-permute-start.8
  25.1 0.5 collective-permute-start.7
  25.7 0.0 collective-permute-done.10
  25.7 0.0 copy-done.1
  25.7 8.5 %gate_up.1 = (bf16[4,256,768]{2,1,0:T(8,128)(2,1)S(1)}, bf16[4,256,768]{2,1,0:T(8,128)(2,1)S(1)}, bf16[4,256,768]{2,1,0:T(8,128)(2,1)S(1)}) custom-call(bf16[256,2048]{1,0:T(8,128)(2,1)S(1)} %constant_dynamic-update-slice_fusion.4.x, s32[4,6]{1,0:T(4,128)S(1)} %copy-done.1, bf16[4,2048,768]{2,1,0:T(8,128)(2,1)S(1)} %get-tuple-element.43.gate.refs_7_, ...), custom_call_target="tpu_custom_call" | custom-call | flops 6442450944 | bytes 25165824 | tf_op jit(solution)/shard_map/gate_up/pallas_call | solution.py:371
  34.2 0.0 collective-permute-done.9.refs_3_
  34.2 0.0 collective-permute-done.8.refs_2_
  34.2 4.2 %collective-permute-done.7.refs_1_ = bf16[64,2176]{1,0:T(8,128)(2,1)S(1)} collective-permute-done((bf16[64,2176]{1,0:T(8,128)(2,1)S(1)}, bf16[64,2176]{1,0:T(8,128)(2,1)S(1)}, u32[]{:S(2)}, u32[]{:S(2)}) %collective-permute-start.7) | collective-permute-done | bytes 278560 | tf_op jit(solution)/shard_map/ppermute | solution.py:287
  38.4 0.0 copy-start
  38.4 9.1 %hidden.1 = (bf16[4,256,768]{2,1,0:T(8,128)(2,1)S(1)}, bf16[4,256,768]{2,1,0:T(8,128)(2,1)S(1)}, bf16[4,256,768]{2,1,0:T(8,128)(2,1)S(1)}, bf16[64,1280]{1,0:T(8...) custom-call(bf16[64,2176]{1,0:T(8,128)(2,1)S(1)} %pad_maximum_fusion.1.refs, ...), custom_call_target="tpu_custom_call" | custom-call | flops 6442450944 | bytes 25165824 | tf_op jit(solution)/shard_map/hidden/pallas_call | solution.py:382
  47.5 1.6 %collective-permute-start.11 = (bf16[64,1280]{1,0:T(8,128)(2,1)S(1)}, bf16[64,1280]{1,0:T(8,128)(2,1)S(1)}, u32[]{:S(2)}, u32[]{:S(2)}) collective-permute-start(bf16[64,1280]{1,0:T(8,128)(2,1)S(1)} %get-tuple-element.49), channel_id=1, source_target_pairs={{0,8},{4,12},{8,0},{12,4},{1,9},{5,13},{9,1},{13,5},{2,10},{6,14},... | collective-permute-start | bytes 491528 | tf_op jit(solution)/shard_map/ppermute | solution.py:287
  49.1 0.0 collective-permute-start.12
  49.1 0.7 collective-permute-start.13
  49.7 6.4 %grad_in.1 = (f32[4,512,768]{2,1,0:T(8,128)}, f32[4,512,768]{2,1,0:T(8,128)}, f32[8,128]{1,0:T(8,128)S(1)}) custom-call(bf16[256,2048]{1,0:T(8,128)(2,1)S(1)} %constant_dynamic-update-slice_fusion.4.x, bf16[4,256,768]{2,1,0:T(8,128)(2,1)S(1)} %get-tuple-element.52.d_gate, bf16[4,256,768]{2,1,0:T(8,128)(2,1)S(1)} %get-tuple-element.53.d_up), custom_call_target="tpu_custom_call" | custom-call | flops 1610612736 | bytes 12582912 | tf_op jit(solution)/shard_map/grad_in/pallas_call | solution.py:405
  56.1 0.0 collective-permute-done.11.refs_1_
  56.1 0.0 collective-permute-done.12.refs_2_
  56.1 0.0 collective-permute-done.13.refs_3_
  56.1 0.0 copy-done
  56.2 0.8 %reduce.1 = (f32[8,16]{1,0:T(8,128)}, bf16[16,1024]{1,0:T(8,128)(2,1)S(1)}, bf16[16,1024]{1,0:T(8,128)(2,1)S(1)}, bf16[16,1024]{1,0:T(8,128)(2,1)S(1)}, bf16[16,...) custom-call(bf16[64,1280]{1,0:T(8,128)(2,1)S(1)} %get-tuple-element.48.refs_0_, ...), custom_call_target="tpu_custom_call" | custom-call | tf_op jit(solution)/shard_map/reduce/pallas_call | solution.py:421
  56.9 1.5 %collective-permute-start.14 = (bf16[16,1024]{1,0:T(8,128)(2,1)S(1)}, bf16[16,1024]{1,0:T(8,128)(2,1)S(1)}, u32[]{:S(2)}, u32[]{:S(2)}) collective-permute-start(bf16[16,1024]{1,0:T(8,128)(2,1)S(1)} %get-tuple-element.56), channel_id=1, source_target_pairs={{0,1},{1,0},{2,3},{3,2},{4,5},{5,4},{6,7},{7,6},{8,9},{9,8},{10,11... | collective-permute-start | bytes 98312 | tf_op jit(solution)/shard_map/ppermute | solution.py:287
  58.4 2.7 %collective-permute-start.15 = (bf16[16,1024]{1,0:T(8,128)(2,1)S(1)}, bf16[16,1024]{1,0:T(8,128)(2,1)S(1)}, u32[]{:S(2)}, u32[]{:S(2)}) collective-permute-start(bf16[16,1024]{1,0:T(8,128)(2,1)S(1)} %get-tuple-element.57), channel_id=1, source_target_pairs={{0,2},{1,3},{2,0},{3,1},{4,6},{5,7},{6,4},{7,5},{8,10},{9,11},{10,... | collective-permute-start | bytes 98312 | tf_op jit(solution)/shard_map/ppermute | solution.py:287
  61.0 0.3 collective-permute-start.16
  61.3 6.6 %grad_out.1 = (f32[4,768,512]{2,1,0:T(8,128)}, f32[8,128]{1,0:T(8,128)S(1)}) custom-call(bf16[64,2176]{1,0:T(8,128)(2,1)S(1)} %pad_maximum_fusion.1.refs_0_, bf16[64,2176]{1,0:T(8,128)(2,1)S(1)} %collective-permute-done.7.refs_1_, bf16[64,2176]{1,0:T(8,128)(2,1)S(1)} %collective-permute-done.8.refs_2_, bf16[64,2176]{1,0:T(8,128)(2,1)S(1)} %collective-permute-done.9.refs_3_, ...), custom_call_target="tpu_custom_call" | custom-call | flops 805306368 | bytes 6291456 | tf_op jit(solution)/shard_map/grad_out/pallas_call | solution.py:433
  67.9 0.0 collective-permute-done.14.refs_1_
  68.0 0.0 collective-permute-done.15.refs_2_
  68.0 0.0 collective-permute-done.16.refs_3_
  68.0 0.7 join.1
  (9 shorter events, 0.2 us)
Async XLA Ops:
  1.7 14.9 %collective-permute-start.5 = (bf16[16,2048]{1,0:T(8,128)(2,1)S(1)}, bf16[16,2048]{1,0:T(8,128)(2,1)S(1)}, u32[]{:S(2)}, u32[]{:S(2)}) collective-permute-start(bf16[16,2048]{1,0:T(8,128)(2,1)S(1)} %get-tuple-element.38.value), channel_id=1, source_target_pairs={{0,3},{1,2},{2,1},{3,0},{4,7},{5,6},{6,5},{7,4},{8,11},{9,10},{10,... | collective-permute-start | bytes 196616 | tf_op jit(solution)/shard_map/ppermute | solution.py:287
  6.8 9.7 %collective-permute-start.4 = (bf16[16,2048]{1,0:T(8,128)(2,1)S(1)}, bf16[16,2048]{1,0:T(8,128)(2,1)S(1)}, u32[]{:S(2)}, u32[]{:S(2)}) collective-permute-start(bf16[16,2048]{1,0:T(8,128)(2,1)S(1)} %get-tuple-element.38.value), channel_id=1, source_target_pairs={{0,2},{1,3},{2,0},{3,1},{4,6},{5,7},{6,4},{7,5},{8,10},{9,11},{10,... | collective-permute-start | bytes 196616 | tf_op jit(solution)/shard_map/ppermute | solution.py:287
  6.8 9.0 %collective-permute-start.3 = (bf16[16,2048]{1,0:T(8,128)(2,1)S(1)}, bf16[16,2048]{1,0:T(8,128)(2,1)S(1)}, u32[]{:S(2)}, u32[]{:S(2)}) collective-permute-start(bf16[16,2048]{1,0:T(8,128)(2,1)S(1)} %get-tuple-element.38.value), channel_id=1, source_target_pairs={{0,1},{1,0},{2,3},{3,2},{4,5},{5,4},{6,7},{7,6},{8,9},{9,8},{10,11... | collective-permute-start | bytes 196616 | tf_op jit(solution)/shard_map/ppermute | solution.py:287
  7.4 15.4 %collective-permute-start.2 = (bf16[16,2176]{1,0:T(8,128)(2,1)S(1)}, bf16[16,2176]{1,0:T(8,128)(2,1)S(1)}, u32[]{:S(2)}, u32[]{:S(2)}) collective-permute-start(bf16[16,2176]{1,0:T(8,128)(2,1)S(1)} %get-tuple-element.37), channel_id=1, source_target_pairs={{0,3},{1,2},{2,1},{3,0},{4,7},{5,6},{6,5},{7,4},{8,11},{9,10},{10,... | collective-permute-start | bytes 208904 | tf_op jit(solution)/shard_map/ppermute | solution.py:287
  11.2 11.7 %collective-permute-start.1 = (bf16[16,2176]{1,0:T(8,128)(2,1)S(1)}, bf16[16,2176]{1,0:T(8,128)(2,1)S(1)}, u32[]{:S(2)}, u32[]{:S(2)}) collective-permute-start(bf16[16,2176]{1,0:T(8,128)(2,1)S(1)} %get-tuple-element.37), channel_id=1, source_target_pairs={{0,2},{1,3},{2,0},{3,1},{4,6},{5,7},{6,4},{7,5},{8,10},{9,11},{10,... | collective-permute-start | bytes 208904 | tf_op jit(solution)/shard_map/ppermute | solution.py:287
  15.8 7.1 %collective-permute-start = (bf16[16,2176]{1,0:T(8,128)(2,1)S(1)}, bf16[16,2176]{1,0:T(8,128)(2,1)S(1)}, u32[]{:S(2)}, u32[]{:S(2)}) collective-permute-start(bf16[16,2176]{1,0:T(8,128)(2,1)S(1)} %get-tuple-element.37), channel_id=1, source_target_pairs={{0,1},{1,0},{2,3},{3,2},{4,5},{5,4},{6,7},{7,6},{8,9},{9,8},{10,11... | collective-permute-start | bytes 208904 | tf_op jit(solution)/shard_map/ppermute | solution.py:287
  16.6 9.2 %copy-start.1 = (s32[4,6]{1,0:T(4,128)S(1)}, s32[4,6]{1,0:T(4,128)}, u32[]{:S(2)}) copy-start(s32[4,6]{1,0:T(4,128)} %masks.1) | copy-start | bytes 292
  16.6 6.7 %collective-permute-start.6 = (bf16[64,2048]{1,0:T(8,128)(2,1)S(1)}, bf16[64,2048]{1,0:T(8,128)(2,1)S(1)}, u32[]{:S(2)}, u32[]{:S(2)}) collective-permute-start(bf16[64,2048]{1,0:T(8,128)(2,1)S(1)} %constant_dynamic-update-slice_fusion.value), channel_id=1, source_target_pairs={{0,8},{4,12},{8,0},{12,4},{1,9},{5,13},{9,1},{13,5},{2,10},{6,14},... | collective-permute-start | bytes 786440 | tf_op jit(solution)/shard_map/ppermute | solution.py:287
  23.3 2.3 %collective-permute-start.10 = (bf16[128,2048]{1,0:T(8,128)(2,1)S(1)}, bf16[128,2048]{1,0:T(8,128)(2,1)S(1)}, u32[]{:S(2)}, u32[]{:S(2)}) collective-permute-start(bf16[128,2048]{1,0:T(8,128)(2,1)S(1)} %pad_maximum_fusion), channel_id=1, source_target_pairs={{0,4},{4,0},{8,12},{12,8},{1,5},{5,1},{9,13},{13,9},{2,6},{6,2},{1... | collective-permute-start | bytes 1572872 | tf_op jit(solution)/shard_map/ppermute | solution.py:287
  23.4 10.8 %collective-permute-start.9 = (bf16[64,2176]{1,0:T(8,128)(2,1)S(1)}, bf16[64,2176]{1,0:T(8,128)(2,1)S(1)}, u32[]{:S(2)}, u32[]{:S(2)}) collective-permute-start(bf16[64,2176]{1,0:T(8,128)(2,1)S(1)} %pad_maximum_fusion.1.refs_0_), channel_id=1, source_target_pairs={{0,12},{4,8},{8,4},{12,0},{1,13},{5,9},{9,5},{13,1},{2,14},{6,10},... | collective-permute-start | bytes 835592 | tf_op jit(solution)/shard_map/ppermute | solution.py:287
  25.1 9.1 %collective-permute-start.8 = (bf16[64,2176]{1,0:T(8,128)(2,1)S(1)}, bf16[64,2176]{1,0:T(8,128)(2,1)S(1)}, u32[]{:S(2)}, u32[]{:S(2)}) collective-permute-start(bf16[64,2176]{1,0:T(8,128)(2,1)S(1)} %pad_maximum_fusion.1.refs_0_), channel_id=1, source_target_pairs={{0,4},{4,0},{8,12},{12,8},{1,5},{5,1},{9,13},{13,9},{2,6},{6,2},{1... | collective-permute-start | bytes 835592 | tf_op jit(solution)/shard_map/ppermute | solution.py:287
  25.1 13.3 %collective-permute-start.7 = (bf16[64,2176]{1,0:T(8,128)(2,1)S(1)}, bf16[64,2176]{1,0:T(8,128)(2,1)S(1)}, u32[]{:S(2)}, u32[]{:S(2)}) collective-permute-start(bf16[64,2176]{1,0:T(8,128)(2,1)S(1)} %pad_maximum_fusion.1.refs_0_), channel_id=1, source_target_pairs={{0,8},{4,12},{8,0},{12,4},{1,9},{5,13},{9,1},{13,5},{2,10},{6,14},... | collective-permute-start | bytes 835592 | tf_op jit(solution)/shard_map/ppermute | solution.py:287
  38.4 17.7 %copy-start = (s32[16,8]{0,1:T(8,128)S(1)}, s32[16,8]{0,1:T(8,128)}, u32[]{:S(2)}) copy-start(s32[16,8]{0,1:T(8,128)} %param.10) | copy-start | bytes 1540
  47.5 8.6 %collective-permute-start.11 = (bf16[64,1280]{1,0:T(8,128)(2,1)S(1)}, bf16[64,1280]{1,0:T(8,128)(2,1)S(1)}, u32[]{:S(2)}, u32[]{:S(2)}) collective-permute-start(bf16[64,1280]{1,0:T(8,128)(2,1)S(1)} %get-tuple-element.49), channel_id=1, source_target_pairs={{0,8},{4,12},{8,0},{12,4},{1,9},{5,13},{9,1},{13,5},{2,10},{6,14},... | collective-permute-start | bytes 491528 | tf_op jit(solution)/shard_map/ppermute | solution.py:287
  49.1 7.0 %collective-permute-start.12 = (bf16[64,1280]{1,0:T(8,128)(2,1)S(1)}, bf16[64,1280]{1,0:T(8,128)(2,1)S(1)}, u32[]{:S(2)}, u32[]{:S(2)}) collective-permute-start(bf16[64,1280]{1,0:T(8,128)(2,1)S(1)} %get-tuple-element.50), channel_id=1, source_target_pairs={{0,4},{4,0},{8,12},{12,8},{1,5},{5,1},{9,13},{13,9},{2,6},{6,2},{1... | collective-permute-start | bytes 491528 | tf_op jit(solution)/shard_map/ppermute | solution.py:287
  49.1 7.1 %collective-permute-start.13 = (bf16[64,1280]{1,0:T(8,128)(2,1)S(1)}, bf16[64,1280]{1,0:T(8,128)(2,1)S(1)}, u32[]{:S(2)}, u32[]{:S(2)}) collective-permute-start(bf16[64,1280]{1,0:T(8,128)(2,1)S(1)} %get-tuple-element.51), channel_id=1, source_target_pairs={{0,12},{4,8},{8,4},{12,0},{1,13},{5,9},{9,5},{13,1},{2,14},{6,10},... | collective-permute-start | bytes 491528 | tf_op jit(solution)/shard_map/ppermute | solution.py:287
  56.9 11.0 %collective-permute-start.14 = (bf16[16,1024]{1,0:T(8,128)(2,1)S(1)}, bf16[16,1024]{1,0:T(8,128)(2,1)S(1)}, u32[]{:S(2)}, u32[]{:S(2)}) collective-permute-start(bf16[16,1024]{1,0:T(8,128)(2,1)S(1)} %get-tuple-element.56), channel_id=1, source_target_pairs={{0,1},{1,0},{2,3},{3,2},{4,5},{5,4},{6,7},{7,6},{8,9},{9,8},{10,11... | collective-permute-start | bytes 98312 | tf_op jit(solution)/shard_map/ppermute | solution.py:287
  58.4 9.6 %collective-permute-start.15 = (bf16[16,1024]{1,0:T(8,128)(2,1)S(1)}, bf16[16,1024]{1,0:T(8,128)(2,1)S(1)}, u32[]{:S(2)}, u32[]{:S(2)}) collective-permute-start(bf16[16,1024]{1,0:T(8,128)(2,1)S(1)} %get-tuple-element.57), channel_id=1, source_target_pairs={{0,2},{1,3},{2,0},{3,1},{4,6},{5,7},{6,4},{7,5},{8,10},{9,11},{10,... | collective-permute-start | bytes 98312 | tf_op jit(solution)/shard_map/ppermute | solution.py:287
  61.0 6.9 %collective-permute-start.16 = (bf16[16,1024]{1,0:T(8,128)(2,1)S(1)}, bf16[16,1024]{1,0:T(8,128)(2,1)S(1)}, u32[]{:S(2)}, u32[]{:S(2)}) collective-permute-start(bf16[16,1024]{1,0:T(8,128)(2,1)S(1)} %get-tuple-element.58), channel_id=1, source_target_pairs={{0,3},{1,2},{2,1},{3,0},{4,7},{5,6},{6,5},{7,4},{8,11},{9,10},{10,... | collective-permute-start | bytes 98312 | tf_op jit(solution)/shard_map/ppermute | solution.py:287

commit v6 on v5

--- a/solution.py
+++ b/solution.py
@@ -33,16 +33,14 @@
     return pl.ds(pl.multiple_of(index * size, size), size)
 
 
-def route_kernel(
-    tokens, cotangent, expert_ids, route_weights, own_tokens, packet, ids, values, sems
-):
+def route_kernel(tokens, cotangent, expert_ids, route_weights, packet, ids, values, sems):
     rows, width = tokens.shape
-    lanes = packet.shape[1] - width
+    lanes = packet.shape[1] - 2 * width
     copies = [
         pltpu.make_async_copy(expert_ids, ids, sems.at[0]),
         pltpu.make_async_copy(route_weights, values, sems.at[1]),
-        pltpu.make_async_copy(tokens, own_tokens, sems.at[2]),
-        pltpu.make_async_copy(cotangent, packet.at[:, :width], sems.at[3]),
+        pltpu.make_async_copy(tokens, packet.at[:, :width], sems.at[2]),
+        pltpu.make_async_copy(cotangent, packet.at[:, width : 2 * width], sems.at[3]),
     ]
     for copy in copies:
         copy.start()
@@ -53,7 +51,7 @@
     dense = jnp.zeros((lanes, rows), jnp.float32)
     for k in range(ids.shape[0]):
         dense += jnp.where(ids[k : k + 1, :] == at, weights[k : k + 1, :], 0.0)
-    packet[:, width:] = dense.T.astype(packet.dtype)
+    packet[:, 2 * width :] = dense.T.astype(packet.dtype)
 
 
 def load_kernel(source, value, target, same, sem):
@@ -75,12 +73,13 @@
         lax.fori_loop(0, tokens // TILE, turn, 0)
 
 
-def gate_up_kernel(x, masks, gate, up, hidden, slope_up, slope_gate):
+def gate_up_kernel(x, masks, gate, up, value, hidden, slope_up, slope_gate, same):
     local_experts, _, hidden_units = gate.shape
     bf16 = jnp.bfloat16
-
-    def one_expert(expert, carry):
-        def tile(rows):
+    same[...] = value[...]
+
+    def tile(rows):
+        for expert in range(local_experts):
             for start in range(0, hidden_units, CHUNK):
                 cols = slice(start, start + CHUNK)
                 gate_pre = dot(x[rows, :], gate[expert, :, cols], NN)
@@ -90,7 +89,7 @@
                 for j in range(CHUNK // BLK):
                     kept = masks[expert, start // BLK + j].astype(jnp.float32)
                     keep = jnp.where(at // BLK == j, kept, keep)
-                sigma = 1.0 / (1.0 + jnp.exp(-gate_pre))
+                sigma = 0.5 + 0.5 * jnp.tanh(0.5 * gate_pre)
                 silu = gate_pre * sigma
                 up_kept = up_proj * keep
                 hidden[expert, rows, cols] = (silu * up_kept).astype(bf16)
@@ -98,10 +97,7 @@
                 slope = up_kept * (sigma + silu * (1.0 - sigma))
                 slope_gate[expert, rows, cols] = slope.astype(bf16)
 
-        over_tiles(x.shape[0], tile)
-        return carry
-
-    lax.fori_loop(0, local_experts, one_expert, 0)
+    over_tiles(x.shape[0], tile)
 
 
 def stack(pieces, target, cols=slice(None)):
@@ -110,27 +106,25 @@
         target[i * rows : (i + 1) * rows] = piece[:, cols]
 
 
-def hidden_kernel(count, *refs):
+def hidden_kernel(count, blocks, *refs):
     pieces, refs = refs[:count], refs[count:]
     units, slope_up, slope_gate, gate, up, w_down, hidden, d_gate, d_up = refs[:9]
-    outs, refs = refs[9 : 9 + count], refs[9 + count :]
+    outs, refs = refs[9 : 9 + blocks], refs[9 + blocks :]
     packet, inner, mixed, token_grad, down_buf, sems = refs
     local_experts, hidden_units, width = w_down.shape
     tokens, part = mixed.shape
     lanes = packet.shape[1] - width
+    half = lanes // 2
     base = lax.axis_index("expert") * local_experts
     mine = aligned(lax.axis_index("dp"), part)
-    inner[...] = jnp.zeros(inner.shape, inner.dtype)
-    mixed[...] = jnp.zeros(mixed.shape, mixed.dtype)
-    token_grad[...] = jnp.zeros(token_grad.shape, token_grad.dtype)
+    bf16, f32 = jnp.bfloat16, jnp.float32
 
     def copies(expert):
-        slot = lax.rem(expert, 2)
         return [
             pltpu.make_async_copy(
                 w_down.at[expert, slice(start, start + CHUNK), :],
-                down_buf.at[slot, slice(start, start + CHUNK), :],
-                sems.at[slot, start // CHUNK],
+                down_buf.at[expert % 2, slice(start, start + CHUNK), :],
+                sems.at[expert % 2, start // CHUNK],
             )
             for start in range(0, hidden_units, CHUNK)
         ]
@@ -138,50 +132,52 @@
     for copy in copies(0):
         copy.start()
     stack(pieces, packet)
-
-    def one_expert(expert, carry):
-        @pl.when(expert + 1 < local_experts)
-        def _():
+    for expert in range(local_experts):
+        if expert + 1 < local_experts:
             for copy in copies(expert + 1):
                 copy.start()
-
-        down = down_buf.at[lax.rem(expert, 2)]
+        down = down_buf.at[expert % 2]
         for copy in copies(expert):
             copy.wait()
 
-        def tile(rows):
-            dense = packet[rows, width:].astype(jnp.float32)
-            hit = ids_along((TILE, lanes), 1) == base + expert
+        def tile(rows, expert=expert, down=down):
+            dense = packet[rows, width:].astype(f32)
+            at = ids_along((TILE, lanes), 1)
+            hit = at == base + expert
             weights = jnp.sum(jnp.where(hit, dense, 0.0), axis=1, keepdims=True)
-            total = jnp.zeros((TILE, 1), jnp.float32)
+            total = jnp.zeros((TILE, 1), f32)
             for start in range(0, hidden_units, CHUNK):
                 cols = slice(start, start + CHUNK)
                 back = dot(packet[rows, :width], down[cols, :], NT)
-                part_units = units[expert, rows, cols].astype(jnp.float32)
+                part_units = units[expert, rows, cols].astype(f32)
                 total += jnp.sum(part_units * back, axis=1, keepdims=True)
                 back = back * weights
-                bf16, f32 = jnp.bfloat16, jnp.float32
                 hidden[expert, rows, cols] = (part_units * weights).astype(bf16)
                 d_gate[expert, rows, cols] = (back * slope_gate[expert, rows, cols].astype(f32)).astype(bf16)
                 d_up[expert, rows, cols] = (back * slope_up[expert, rows, cols].astype(f32)).astype(bf16)
-            inner[rows, :] += jnp.where(hit, total, 0.0)
-            mixed[rows, :] += dot(hidden[expert, rows, :], down[:, mine], NN)
-            token_grad[rows, :] += dot(d_gate[expert, rows, :], gate[expert, mine, :], NT) + dot(
+            high = total.astype(bf16).astype(f32)
+            both = jnp.where(hit, high, jnp.where(at == base + expert + half, total - high, 0.0))
+            new_mixed = dot(hidden[expert, rows, :], down[:, mine], NN)
+            new_grad = dot(d_gate[expert, rows, :], gate[expert, mine, :], NT) + dot(
                 d_up[expert, rows, :], up[expert, mine, :], NT
             )
+            if expert == 0:
+                inner[rows, :] = both
+                mixed[rows, :] = new_mixed
+                token_grad[rows, :] = new_grad
+            else:
+                inner[rows, :] += both
+                mixed[rows, :] += new_mixed
+                token_grad[rows, :] += new_grad
 
         over_tiles(tokens, tile)
-        return carry
-
-    lax.fori_loop(0, local_experts, one_expert, 0)
+
     rows = outs[0].shape[0]
     for i, out in enumerate(outs):
         block = slice(i * rows, (i + 1) * rows)
-        out[:, :part] = mixed[block].astype(out.dtype)
-        out[:, part : 2 * part] = token_grad[block].astype(out.dtype)
-        high = inner[block].astype(jnp.bfloat16)
-        out[:, 2 * part : 2 * part + lanes] = high
-        out[:, 2 * part + lanes :] = (inner[block] - high.astype(jnp.float32)).astype(jnp.bfloat16)
+        out[:, :part] = mixed[block].astype(bf16)
+        out[:, part : 2 * part] = token_grad[block].astype(bf16)
+        out[:, 2 * part :] = inner[block].astype(bf16)
 
 
 def write_out(steps, place, outs, bufs, sems, body):
@@ -233,20 +229,18 @@
 def grad_out_kernel(count, *refs):
     pieces, refs = refs[:count], refs[count:]
     hidden, after, grad_down, done, cot_part, out_down, sems = refs
-    local_experts, _, hidden_units = hidden.shape
+    local_experts = hidden.shape[0]
     part = cot_part.shape[1]
     stack(pieces, cot_part, aligned(lax.axis_index("dp"), part))
     done[...] = jnp.zeros(done.shape, done.dtype)
-    chunks = hidden_units // CHUNK
 
     def place(step):
-        return step // chunks, aligned(lax.rem(step, chunks), CHUNK), slice(None)
+        return (step,)
 
     def body(step, slot):
-        units = hidden[step // chunks, :, aligned(lax.rem(step, chunks), CHUNK)]
-        out_down[slot] = dot(units.T, cot_part[...], NN)
-
-    write_out(local_experts * chunks, place, (grad_down,), (out_down,), sems, body)
+        out_down[slot] = dot(hidden[step].T, cot_part[...], NN)
+
+    write_out(local_experts, place, (grad_down,), (out_down,), sems, body)
 
 
 def reduce_kernel(count, *refs):
@@ -255,28 +249,28 @@
     outs, done = refs[3:-1], refs[-1]
     done[...] = jnp.zeros(done.shape, done.dtype)
     rows, both = outs[0].shape
-    lanes = (blocks[0].shape[1] - both) // 2
+    half = (blocks[0].shape[1] - both) // 2
     for j, out in enumerate(outs):
         total = jnp.zeros((rows, both), jnp.float32)
         for block in blocks:
             total += block[j * rows : (j + 1) * rows, :both].astype(jnp.float32)
         out[...] = total.astype(out.dtype)
-    inner = jnp.zeros((rows, lanes), jnp.float32)
+    inner = jnp.zeros((rows, 2 * half), jnp.float32)
     for block in blocks:
-        tail = block[:rows, both:].astype(jnp.float32)
-        inner += tail[:, :lanes] + tail[:, lanes:]
+        inner += block[:rows, both:].astype(jnp.float32)
     inner = inner.T
+    inner = inner[:half] + inner[half:]
     at = ids_along(inner.shape, 0)
     for k in range(expert_ids.shape[0]):
         hit = jnp.where(expert_ids[k : k + 1, :] == at, inner, 0.0)
         route_grad[k : k + 1, :] = jnp.sum(hit, axis=0, keepdims=True)
 
 
-def join_kernel(order, *refs):
-    blocks, (after, mixed, token_grad) = refs[: len(order)], refs[len(order) :]
+def join_kernel(count, *refs):
+    blocks, (after, mixed, token_grad) = refs[:count], refs[count:]
     part = blocks[0].shape[1] // 2
     column = lax.axis_index("dp")
-    for other, block in zip(order, blocks):
+    for other, block in enumerate(blocks):
         cols = aligned(column ^ other, part)
         mixed[:, cols] = block[:, :part]
         token_grad[:, cols] = block[:, part:]
@@ -313,10 +307,9 @@
     rows, width = tokens.shape
     local_experts, _, hidden_units = w_gate.shape
     sources, columns = lax.axis_size("expert"), lax.axis_size("dp")
-    column_order = list(range(columns))
     chips = list(range(2, sources, 2))
     expert_order = [0] + chips + [chip ^ 1 for chip in [0] + chips]
-    lanes = -(-local_experts * sources // LANES) * LANES
+    lanes = -(-2 * local_experts * sources // LANES) * LANES
     part = width // columns
     everyone = sources * columns * rows
     bf16, f32 = jnp.bfloat16, jnp.float32
@@ -326,11 +319,11 @@
     ids_t = expert_ids.T
     w_gate, w_up, w_down = [in_hbm(w) for w in (w_gate, w_up, w_down)]
 
-    own_tokens, packet = pl.pallas_call(
+    packet = pl.pallas_call(
         route_kernel,
-        out_shape=[struct(tokens.shape, bf16), struct((rows, width + lanes), bf16)],
+        out_shape=struct((rows, 2 * width + lanes), bf16),
         in_specs=[HBM] * 4,
-        out_specs=[VMEM] * 2,
+        out_specs=VMEM,
         scratch_shapes=[
             pltpu.VMEM(ids_t.shape, jnp.int32),
             pltpu.VMEM(ids_t.shape, bf16),
@@ -355,35 +348,35 @@
             name=name,
         )(weight, value)
 
-    arrived = exchange(own_tokens, "dp", column_order[1:])
-    gate, own_tokens = load(w_gate, own_tokens, "load_gate")
-    x_column = jnp.concatenate([own_tokens] + arrived)
-    across = exchange(x_column, "expert", chips)
-    packet_column = jnp.concatenate([packet] + exchange(packet, "dp", column_order[1:]))
-    packet_column, across = lax.optimization_barrier((packet_column, across))
+    arrived = exchange(packet, "dp", range(1, columns))
+    gate, packet = load(w_gate, packet, "load_gate")
+    x_column = jnp.concatenate([p[:, :width] for p in [packet] + arrived])
+    c_column = jnp.concatenate([p[:, width:] for p in [packet] + arrived])
+    x_across = exchange(x_column, "expert", chips)
+    c_across = exchange(c_column, "expert", chips)
     up, x_column = load(w_up, x_column, "load_up")
     gate, up = in_vmem(gate), in_vmem(up)
-    x = jnp.concatenate([x_column] + across)
+    x = jnp.concatenate([x_column] + x_across)
     x = jnp.concatenate([x, swap(x, "expert", 1)])
-    pieces = exchange(packet_column, "expert", expert_order[1:])
 
     units = struct((local_experts, everyone, hidden_units), bf16)
-    factors = pl.pallas_call(
+    *factors, c_column = pl.pallas_call(
         gate_up_kernel,
-        out_shape=[units] * 3,
-        in_specs=[VMEM, SMEM, VMEM, VMEM],
-        out_specs=[VMEM] * 3,
+        out_shape=[units] * 3 + [struct(c_column.shape, bf16)],
+        in_specs=[VMEM, SMEM] + [VMEM] * 3,
+        out_specs=[VMEM] * 4,
         cost_estimate=cost(2 * everyone * one, 2 * one),
         compiler_params=params(6),
         name="gate_up",
-    )(x, block_masks, gate, up)
-    pieces = [packet_column] + pieces
+    )(x, block_masks, gate, up, c_column)
+    c_half = jnp.concatenate([c_column] + c_across)
+    pieces = [c_half, swap(c_half, "expert", 1)]
 
     hidden, d_gate, d_up, *partials = pl.pallas_call(
-        functools.partial(hidden_kernel, sources),
+        functools.partial(hidden_kernel, 2, sources),
         out_shape=[units] * 3
-        + [struct((columns * rows, 2 * part + 2 * lanes), bf16)] * sources,
-        in_specs=[VMEM] * (5 + sources) + [HBM],
+        + [struct((columns * rows, 2 * part + lanes), bf16)] * sources,
+        in_specs=[VMEM] * 7 + [HBM],
         out_specs=[VMEM] * (3 + sources),
         scratch_shapes=[
             pltpu.VMEM((everyone, width + lanes), bf16),
@@ -427,17 +420,17 @@
         name="reduce",
     )(*arrived, ids_t, done_in)
     blocks = [
-        swap(block, "dp", other) if other else block for other, block in zip(column_order, blocks)
+        swap(block, "dp", other) if other else block for other, block in enumerate(blocks)
     ]
 
     grad_down, done_out = pl.pallas_call(
-        functools.partial(grad_out_kernel, sources),
+        functools.partial(grad_out_kernel, 2),
         out_shape=[struct((local_experts, hidden_units, part), f32), dummy],
-        in_specs=[VMEM] * (2 + sources),
+        in_specs=[VMEM] * 4,
         out_specs=[HBM, VMEM],
         scratch_shapes=[
             pltpu.VMEM((everyone, part), bf16),
-            pltpu.VMEM((2, CHUNK, part), f32),
+            pltpu.VMEM((2, hidden_units, part), f32),
             pltpu.SemaphoreType.DMA((2, 1)),
         ],
         cost_estimate=cost(everyone * one // columns, 2 * one // columns),
@@ -446,7 +439,7 @@
     )(*pieces, hidden, done_sum)
 
     mixed, token_grad = pl.pallas_call(
-        functools.partial(join_kernel, column_order),
+        functools.partial(join_kernel, columns),
         out_shape=[struct((rows, width), bf16)] * 2,
         in_specs=[VMEM] * (columns + 1),
         out_specs=[VMEM] * 2,

time: 68.9 us -> 66.5 us (0.965)
  waiting for transfers between devices: 4.61 us -> 10.1 us
  starting transfers between devices: 20.8 us -> 15.8 us
  Pallas kernels: 42.2 us -> 39.3 us
    ppermute x17 -> x13, waiting for transfers between devices: 4.61 us -> 10.1 us  [swap(): return lax.ppermute(value, axis, [(i, i ^ mask) for i in range(size)])]
    ppermute x17 -> x13, starting transfers between devices: 20.8 us -> 15.8 us  [swap(): return lax.ppermute(value, axis, [(i, i ^ mask) for i in range(size)])]
    pallas_call x5, Pallas kernels: 25.9 us -> 23 us  [the longest x1 9.54 us: per_device(): pl.pallas_call(functools.partial(hidden_kernel, 2, sources), out_shape=[u...]
  transfers between devices with their start and end apart: 17 -> 13, of which waited for: 2 -> 5; matrix products, arithmetic and copies ran while one was open for 0% -> 0% of each run, Pallas kernels for 45% -> 41%
where the time goes in v6:
time: 66.5 us; the launch traced here: 66.3 us
  Pallas kernels  39.3 us (59%)
  starting transfers between devices  15.8 us (24%)
  waiting for transfers between devices  10.1 us (15%)
  between operations  0.88 us (1%)
    ppermute x13, starting transfers between devices, swap(): return lax.ppermute(value, axis, [(i, i ^ mask) for i in range(size)])  15.8 us
    ppermute x13, waiting for transfers between devices, swap(): return lax.ppermute(value, axis, [(i, i ^ mask) for i in range(size)])  10.1 us
    pallas_call x1, Pallas kernels, per_device(): pl.pallas_call(functools.partial(hidden_kernel, 2, sources), out_shape=[u...  9.54 us
    pallas_call x2, Pallas kernels, load(): pl.pallas_call(load_kernel, out_shape=[pltpu.VMEM(weight.shape, weight.dt...  9.18 us
    pallas_call x1, Pallas kernels, per_device(): pl.pallas_call(gate_up_kernel, out_shape=[units] * 3 + [struct(c_column.s...  8.13 us
    pallas_call x1, Pallas kernels, per_device(): pl.pallas_call(grad_in_kernel, out_shape=[struct((local_experts, part, hi...  6.37 us
    pallas_call x1, Pallas kernels, per_device(): pl.pallas_call(functools.partial(grad_out_kernel, 2), out_shape=[struct((...  3.63 us
  transfers between devices with their start and end apart: 13, of which 5 were waited for; matrix products, arithmetic and copies ran while one was open for 0% of the time, Pallas kernels for 41%

profile of v6, /device:TPU:0, one launch (start us, length us, event | category | flops | bytes accessed | tf_op | source)
XLA Modules:
  0.0 66.3 jit_solution(5082264932614711778)
XLA Ops:
  0.6 1.0 %route.1.value = bf16[16,4224]{1,0:T(8,128)(2,1)S(1)} custom-call(bf16[16,2048]{1,0:T(8,128)(2,1)} %tokens.1, bf16[16,2048]{1,0:T(8,128)(2,1)} %cotangent.1, s32[8,16]{1,0:T(8,128)} %bitcast.3, bf16[8,16]{1,0:T(8,128)(2,1)} %bitcast.5), custom_call_target="tpu_custom_call" | custom-call | tf_op jit(solution)/shard_map/route/pallas_call | solution.py:322
  1.7 5.1 %collective-permute-start.2 = (bf16[16,4224]{1,0:T(8,128)(2,1)S(1)}, bf16[16,4224]{1,0:T(8,128)(2,1)S(1)}, u32[]{:S(2)}, u32[]{:S(2)}) collective-permute-start(bf16[16,4224]{1,0:T(8,128)(2,1)S(1)} %route.1.value), channel_id=1, source_target_pairs={{0,3},{1,2},{2,1},{3,0},{4,7},{5,6},{6,5},{7,4},{8,11},{9,10},{10,... | collective-permute-start | bytes 405512 | tf_op jit(solution)/shard_map/ppermute | solution.py:281
  6.8 0.0 collective-permute-start.1
  6.8 0.6 collective-permute-start
  7.4 4.6 %load_gate.1 = (bf16[4,2048,768]{2,1,0:T(8,128)(2,1)S(1)}, bf16[16,4224]{1,0:T(8,128)(2,1)S(1)}) custom-call(bf16[4,2048,768]{2,1,0:T(8,128)(2,1)} %source.2, bf16[16,4224]{1,0:T(8,128)(2,1)S(1)} %route.1.value), custom_call_target="tpu_custom_call" | custom-call | bytes 12582912 | tf_op jit(solution)/shard_map/load_gate/pallas_call | solution.py:337
  12.0 0.0 collective-permute-done.2
  12.1 6.2 %collective-permute-done.1 = bf16[16,4224]{1,0:T(8,128)(2,1)S(1)} collective-permute-done((bf16[16,4224]{1,0:T(8,128)(2,1)S(1)}, bf16[16,4224]{1,0:T(8,128)(2,1)S(1)}, u32[]{:S(2)}, u32[]{:S(2)}) %collective-permute-start.1) | collective-permute-done | bytes 135200 | tf_op jit(solution)/shard_map/ppermute | solution.py:281
  18.2 0.0 collective-permute-done
  18.3 1.6 %collective-permute-start.3 = (bf16[64,2048]{1,0:T(8,128)(2,1)S(1)}, bf16[64,2048]{1,0:T(8,128)(2,1)S(1)}, u32[]{:S(2)}, u32[]{:S(2)}) collective-permute-start(bf16[64,2048]{1,0:T(8,128)(2,1)S(1)} %pad_maximum_fusion.2.value), channel_id=1, source_target_pairs={{0,8},{4,12},{8,0},{12,4},{1,9},{5,13},{9,1},{13,5},{2,10},{6,14},... | collective-permute-start | bytes 786440 | tf_op jit(solution)/shard_map/ppermute | solution.py:281
  19.8 0.0 copy-start.1
  19.8 4.6 %load_up.1 = (bf16[4,2048,768]{2,1,0:T(8,128)(2,1)S(1)}, bf16[64,2048]{1,0:T(8,128)(2,1)S(1)}) custom-call(bf16[4,2048,768]{2,1,0:T(8,128)(2,1)} %source.3, bf16[64,2048]{1,0:T(8,128)(2,1)S(1)} %pad_maximum_fusion.2.value), custom_call_target="tpu_custom_call" | custom-call | bytes 12582912 | tf_op jit(solution)/shard_map/load_up/pallas_call | solution.py:337
  24.5 1.2 %collective-permute-done.3 = bf16[64,2048]{1,0:T(8,128)(2,1)S(1)} collective-permute-done((bf16[64,2048]{1,0:T(8,128)(2,1)S(1)}, bf16[64,2048]{1,0:T(8,128)(2,1)S(1)}, u32[]{:S(2)}, u32[]{:S(2)}) %collective-permute-start.3) | collective-permute-done | bytes 262176 | tf_op jit(solution)/shard_map/ppermute | solution.py:281
  25.7 0.1 collective-permute-start.4
  25.9 1.6 %collective-permute-start.5 = (bf16[64,2176]{1,0:T(8,128)(2,1)S(1)}, bf16[64,2176]{1,0:T(8,128)(2,1)S(1)}, u32[]{:S(2)}, u32[]{:S(2)}) collective-permute-start(bf16[64,2176]{1,0:T(8,128)(2,1)S(1)} %pad_maximum_fusion.1.value), channel_id=1, source_target_pairs={{0,8},{4,12},{8,0},{12,4},{1,9},{5,13},{9,1},{13,5},{2,10},{6,14},... | collective-permute-start | bytes 835592 | tf_op jit(solution)/shard_map/ppermute | solution.py:281
  27.5 0.3 collective-permute-done.4
  27.8 0.0 copy-done.1
  27.8 8.1 %gate_up.1 = (bf16[4,256,768]{2,1,0:T(8,128)(2,1)S(1)}, bf16[4,256,768]{2,1,0:T(8,128)(2,1)S(1)}, bf16[4,256,768]{2,1,0:T(8,128)(2,1)S(1)}, bf16[64,2176]{1,0:T(8,128)(2,1)S(1)}) custom-call(bf16[256,2048]{1,0:T(8,128)(2,1)S(1)} %constant_dynamic-update-slice_fusion.x, s32[4,6]{1,0:T(4,128)S(1)} %copy-done.1, ...), custom_call_target="tpu_custom_call" | custom-call | flops 6442450944 | bytes 25165824 | tf_op jit(solution)/shard_map/gate_up/pallas_call | solution.py:363
  35.9 0.0 collective-permute-done.5
  36.0 0.2 collective-permute-start.6
  36.2 1.8 %collective-permute-done.6.refs_1_ = bf16[128,2176]{1,0:T(8,128)(2,1)S(1)} collective-permute-done((bf16[128,2176]{1,0:T(8,128)(2,1)S(1)}, bf16[128,2176]{1,0:T(8,128)(2,1)S(1)}, u32[]{:S(2)}, u32[]{:S(2)}) %collective-permute-start.6) | collective-permute-done | bytes 557088 | tf_op jit(solution)/shard_map/ppermute | solution.py:281
  38.0 0.0 copy-start
  38.0 9.5 %hidden.1 = (bf16[4,256,768]{2,1,0:T(8,128)(2,1)S(1)}, bf16[4,256,768]{2,1,0:T(8,128)(2,1)S(1)}, bf16[4,256,768]{2,1,0:T(8,128)(2,1)S(1)}, bf16[64,1152]{1,0:T(8...) custom-call(bf16[128,2176]{1,0:T(8,128)(2,1)S(1)} %constant_dynamic-update-, ...), custom_call_target="tpu_custom_call" | custom-call | flops 6442450944 | bytes 25165824 | tf_op jit(solution)/shard_map/hidden/pallas_call | solution.py:375
  47.6 1.6 %collective-permute-start.7 = (bf16[64,1152]{1,0:T(8,128)(2,1)S(1)}, bf16[64,1152]{1,0:T(8,128)(2,1)S(1)}, u32[]{:S(2)}, u32[]{:S(2)}) collective-permute-start(bf16[64,1152]{1,0:T(8,128)(2,1)S(1)} %get-tuple-element.43), channel_id=1, source_target_pairs={{0,8},{4,12},{8,0},{12,4},{1,9},{5,13},{9,1},{13,5},{2,10},{6,14},... | collective-permute-start | bytes 442376 | tf_op jit(solution)/shard_map/ppermute | solution.py:281
  49.1 0.0 collective-permute-start.8
  49.1 0.6 collective-permute-start.9
  49.8 6.4 %grad_in.1 = (f32[4,512,768]{2,1,0:T(8,128)}, f32[4,512,768]{2,1,0:T(8,128)}, f32[8,128]{1,0:T(8,128)S(1)}) custom-call(bf16[256,2048]{1,0:T(8,128)(2,1)S(1)} %constant_dynamic-update-slice_fusion.x, bf16[4,256,768]{2,1,0:T(8,128)(2,1)S(1)} %get-tuple-element.46.d_gate, bf16[4,256,768]{2,1,0:T(8,128)(2,1)S(1)} %get-tuple-element.47.d_up), custom_call_target="tpu_custom_call" | custom-call | flops 1610612736 | bytes 12582912 | tf_op jit(solution)/shard_map/grad_in/pallas_call | solution.py:398
  56.1 0.0 collective-permute-done.7.refs_1_
  56.2 0.0 collective-permute-done.8.refs_2_
  56.2 0.0 collective-permute-done.9.refs_3_
  56.2 0.0 copy-done
  56.2 0.8 %reduce.1 = (f32[8,16]{1,0:T(8,128)}, bf16[16,1024]{1,0:T(8,128)(2,1)S(1)}, bf16[16,1024]{1,0:T(8,128)(2,1)S(1)}, bf16[16,1024]{1,0:T(8,128)(2,1)S(1)}, bf16[16,...) custom-call(bf16[64,1152]{1,0:T(8,128)(2,1)S(1)} %get-tuple-element.42.refs_0_, ...), custom_call_target="tpu_custom_call" | custom-call | tf_op jit(solution)/shard_map/reduce/pallas_call | solution.py:414
  56.9 0.0 collective-permute-start.10
  57.0 3.0 %collective-permute-start.11 = (bf16[16,1024]{1,0:T(8,128)(2,1)S(1)}, bf16[16,1024]{1,0:T(8,128)(2,1)S(1)}, u32[]{:S(2)}, u32[]{:S(2)}) collective-permute-start(bf16[16,1024]{1,0:T(8,128)(2,1)S(1)} %get-tuple-element.51), channel_id=1, source_target_pairs={{0,2},{1,3},{2,0},{3,1},{4,6},{5,7},{6,4},{7,5},{8,10},{9,11},{10,... | collective-permute-start | bytes 98312 | tf_op jit(solution)/shard_map/ppermute | solution.py:281
  59.9 1.4 %collective-permute-start.12 = (bf16[16,1024]{1,0:T(8,128)(2,1)S(1)}, bf16[16,1024]{1,0:T(8,128)(2,1)S(1)}, u32[]{:S(2)}, u32[]{:S(2)}) collective-permute-start(bf16[16,1024]{1,0:T(8,128)(2,1)S(1)} %get-tuple-element.52), channel_id=1, source_target_pairs={{0,3},{1,2},{2,1},{3,0},{4,7},{5,6},{6,5},{7,4},{8,11},{9,10},{10,... | collective-permute-start | bytes 98312 | tf_op jit(solution)/shard_map/ppermute | solution.py:281
  61.3 3.6 %grad_out.1 = (f32[4,768,512]{2,1,0:T(8,128)}, f32[8,128]{1,0:T(8,128)S(1)}) custom-call(bf16[128,2176]{1,0:T(8,128)(2,1)S(1)} %constant_dynamic-update-slice_fusion.3.refs_0_, bf16[128,2176]{1,0:T(8,128)(2,1)S(1)} %collective-permute-done.6.refs_1_, bf16[4,256,768]{2,1,0:T(8,128)(2,1)S(1)} %get-tuple-element.53.refs_2_, f32[8,128]{1,0:T(8,128)S(1)} %get-tuple-element.54.refs_3_), custom_call_target="tpu_custom_call" | custom-call | flops 805306368 | bytes 6291456 | tf_op jit(solution)/shard_map/grad_out/pallas_call | solution.py:426
  65.0 0.0 collective-permute-done.10.refs_1_
  65.0 0.0 collective-permute-done.11.refs_2_
  65.0 0.6 collective-permute-done.12.refs_3_
  65.6 0.7 %join.1 = (bf16[16,2048]{1,0:T(8,128)(2,1)}, bf16[16,2048]{1,0:T(8,128)(2,1)}) custom-call(bf16[16,1024]{1,0:T(8,128)(2,1)S(1)} %get-tuple-element.49.refs_0_, bf16[16,1024]{1,0:T(8,128)(2,1)S(1)} %collective-permute-done.10.refs_1_, bf16[16,1024]{1,0:T(8,128)(2,1)S(1)} %collective-permute-done.11.refs_2_, ...), custom_call_target="tpu_custom_call" | custom-call | tf_op jit(solution)/shard_map/join/pallas_call | solution.py:441
  (16 shorter events, 0.3 us)
Async XLA Ops:
  1.7 10.4 %collective-permute-start.2 = (bf16[16,4224]{1,0:T(8,128)(2,1)S(1)}, bf16[16,4224]{1,0:T(8,128)(2,1)S(1)}, u32[]{:S(2)}, u32[]{:S(2)}) collective-permute-start(bf16[16,4224]{1,0:T(8,128)(2,1)S(1)} %route.1.value), channel_id=1, source_target_pairs={{0,3},{1,2},{2,1},{3,0},{4,7},{5,6},{6,5},{7,4},{8,11},{9,10},{10,... | collective-permute-start | bytes 405512 | tf_op jit(solution)/shard_map/ppermute | solution.py:281
  6.8 11.4 %collective-permute-start.1 = (bf16[16,4224]{1,0:T(8,128)(2,1)S(1)}, bf16[16,4224]{1,0:T(8,128)(2,1)S(1)}, u32[]{:S(2)}, u32[]{:S(2)}) collective-permute-start(bf16[16,4224]{1,0:T(8,128)(2,1)S(1)} %route.1.value), channel_id=1, source_target_pairs={{0,2},{1,3},{2,0},{3,1},{4,6},{5,7},{6,4},{7,5},{8,10},{9,11},{10,... | collective-permute-start | bytes 405512 | tf_op jit(solution)/shard_map/ppermute | solution.py:281
  6.8 11.4 %collective-permute-start = (bf16[16,4224]{1,0:T(8,128)(2,1)S(1)}, bf16[16,4224]{1,0:T(8,128)(2,1)S(1)}, u32[]{:S(2)}, u32[]{:S(2)}) collective-permute-start(bf16[16,4224]{1,0:T(8,128)(2,1)S(1)} %route.1.value), channel_id=1, source_target_pairs={{0,1},{1,0},{2,3},{3,2},{4,5},{5,4},{6,7},{7,6},{8,9},{9,8},{10,11... | collective-permute-start | bytes 405512 | tf_op jit(solution)/shard_map/ppermute | solution.py:281
  18.3 7.4 %collective-permute-start.3 = (bf16[64,2048]{1,0:T(8,128)(2,1)S(1)}, bf16[64,2048]{1,0:T(8,128)(2,1)S(1)}, u32[]{:S(2)}, u32[]{:S(2)}) collective-permute-start(bf16[64,2048]{1,0:T(8,128)(2,1)S(1)} %pad_maximum_fusion.2.value), channel_id=1, source_target_pairs={{0,8},{4,12},{8,0},{12,4},{1,9},{5,13},{9,1},{13,5},{2,10},{6,14},... | collective-permute-start | bytes 786440 | tf_op jit(solution)/shard_map/ppermute | solution.py:281
  19.8 7.9 %copy-start.1 = (s32[4,6]{1,0:T(4,128)S(1)}, s32[4,6]{1,0:T(4,128)}, u32[]{:S(2)}) copy-start(s32[4,6]{1,0:T(4,128)} %masks.1) | copy-start | bytes 292
  25.7 2.0 %collective-permute-start.4 = (bf16[128,2048]{1,0:T(8,128)(2,1)S(1)}, bf16[128,2048]{1,0:T(8,128)(2,1)S(1)}, u32[]{:S(2)}, u32[]{:S(2)}) collective-permute-start(bf16[128,2048]{1,0:T(8,128)(2,1)S(1)} %pad_maximum_fusion), channel_id=1, source_target_pairs={{0,4},{4,0},{8,12},{12,8},{1,5},{5,1},{9,13},{13,9},{2,6},{6,2},{1... | collective-permute-start | bytes 1572872 | tf_op jit(solution)/shard_map/ppermute | solution.py:281
  25.9 10.1 %collective-permute-start.5 = (bf16[64,2176]{1,0:T(8,128)(2,1)S(1)}, bf16[64,2176]{1,0:T(8,128)(2,1)S(1)}, u32[]{:S(2)}, u32[]{:S(2)}) collective-permute-start(bf16[64,2176]{1,0:T(8,128)(2,1)S(1)} %pad_maximum_fusion.1.value), channel_id=1, source_target_pairs={{0,8},{4,12},{8,0},{12,4},{1,9},{5,13},{9,1},{13,5},{2,10},{6,14},... | collective-permute-start | bytes 835592 | tf_op jit(solution)/shard_map/ppermute | solution.py:281
  36.0 2.0 %collective-permute-start.6 = (bf16[128,2176]{1,0:T(8,128)(2,1)S(1)}, bf16[128,2176]{1,0:T(8,128)(2,1)S(1)}, u32[]{:S(2)}, u32[]{:S(2)}) collective-permute-start(bf16[128,2176]{1,0:T(8,128)(2,1)S(1)} %constant_dynamic-update-slice_fusion.3.refs_0_), channel_id=1, source_target_pairs={{0,4},{4,0},{8,12},{12,8},{1,5},{5,1},{9,13},{13,9},{2,6},{6,2},{1... | collective-permute-start | bytes 1671176 | tf_op jit(solution)/shard_map/ppermute | solution.py:281
  38.0 18.2 %copy-start = (s32[16,8]{0,1:T(8,128)S(1)}, s32[16,8]{0,1:T(8,128)}, u32[]{:S(2)}) copy-start(s32[16,8]{0,1:T(8,128)} %param.10) | copy-start | bytes 1540
  47.6 8.6 %collective-permute-start.7 = (bf16[64,1152]{1,0:T(8,128)(2,1)S(1)}, bf16[64,1152]{1,0:T(8,128)(2,1)S(1)}, u32[]{:S(2)}, u32[]{:S(2)}) collective-permute-start(bf16[64,1152]{1,0:T(8,128)(2,1)S(1)} %get-tuple-element.43), channel_id=1, source_target_pairs={{0,8},{4,12},{8,0},{12,4},{1,9},{5,13},{9,1},{13,5},{2,10},{6,14},... | collective-permute-start | bytes 442376 | tf_op jit(solution)/shard_map/ppermute | solution.py:281
  49.1 7.0 %collective-permute-start.8 = (bf16[64,1152]{1,0:T(8,128)(2,1)S(1)}, bf16[64,1152]{1,0:T(8,128)(2,1)S(1)}, u32[]{:S(2)}, u32[]{:S(2)}) collective-permute-start(bf16[64,1152]{1,0:T(8,128)(2,1)S(1)} %get-tuple-element.44), channel_id=1, source_target_pairs={{0,4},{4,0},{8,12},{12,8},{1,5},{5,1},{9,13},{13,9},{2,6},{6,2},{1... | collective-permute-start | bytes 442376 | tf_op jit(solution)/shard_map/ppermute | solution.py:281
  49.1 7.0 %collective-permute-start.9 = (bf16[64,1152]{1,0:T(8,128)(2,1)S(1)}, bf16[64,1152]{1,0:T(8,128)(2,1)S(1)}, u32[]{:S(2)}, u32[]{:S(2)}) collective-permute-start(bf16[64,1152]{1,0:T(8,128)(2,1)S(1)} %get-tuple-element.45), channel_id=1, source_target_pairs={{0,12},{4,8},{8,4},{12,0},{1,13},{5,9},{9,5},{13,1},{2,14},{6,10},... | collective-permute-start | bytes 442376 | tf_op jit(solution)/shard_map/ppermute | solution.py:281
  56.9 8.0 %collective-permute-start.10 = (bf16[16,1024]{1,0:T(8,128)(2,1)S(1)}, bf16[16,1024]{1,0:T(8,128)(2,1)S(1)}, u32[]{:S(2)}, u32[]{:S(2)}) collective-permute-start(bf16[16,1024]{1,0:T(8,128)(2,1)S(1)} %get-tuple-element.50), channel_id=1, source_target_pairs={{0,1},{1,0},{2,3},{3,2},{4,5},{5,4},{6,7},{7,6},{8,9},{9,8},{10,11... | collective-permute-start | bytes 98312 | tf_op jit(solution)/shard_map/ppermute | solution.py:281
  57.0 8.0 %collective-permute-start.11 = (bf16[16,1024]{1,0:T(8,128)(2,1)S(1)}, bf16[16,1024]{1,0:T(8,128)(2,1)S(1)}, u32[]{:S(2)}, u32[]{:S(2)}) collective-permute-start(bf16[16,1024]{1,0:T(8,128)(2,1)S(1)} %get-tuple-element.51), channel_id=1, source_target_pairs={{0,2},{1,3},{2,0},{3,1},{4,6},{5,7},{6,4},{7,5},{8,10},{9,11},{10,... | collective-permute-start | bytes 98312 | tf_op jit(solution)/shard_map/ppermute | solution.py:281
  59.9 5.7 %collective-permute-start.12 = (bf16[16,1024]{1,0:T(8,128)(2,1)S(1)}, bf16[16,1024]{1,0:T(8,128)(2,1)S(1)}, u32[]{:S(2)}, u32[]{:S(2)}) collective-permute-start(bf16[16,1024]{1,0:T(8,128)(2,1)S(1)} %get-tuple-element.52), channel_id=1, source_target_pairs={{0,3},{1,2},{2,1},{3,0},{4,7},{5,6},{6,5},{7,4},{8,11},{9,10},{10,... | collective-permute-start | bytes 98312 | tf_op jit(solution)/shard_map/ppermute | solution.py:281

commit v7 on v6

--- a/solution.py
+++ b/solution.py
@@ -33,14 +33,16 @@
     return pl.ds(pl.multiple_of(index * size, size), size)
 
 
-def route_kernel(tokens, cotangent, expert_ids, route_weights, packet, ids, values, sems):
+def route_kernel(
+    tokens, cotangent, expert_ids, route_weights, own_tokens, packet, ids, values, sems
+):
     rows, width = tokens.shape
-    lanes = packet.shape[1] - 2 * width
+    lanes = packet.shape[1] - width
     copies = [
         pltpu.make_async_copy(expert_ids, ids, sems.at[0]),
         pltpu.make_async_copy(route_weights, values, sems.at[1]),
-        pltpu.make_async_copy(tokens, packet.at[:, :width], sems.at[2]),
-        pltpu.make_async_copy(cotangent, packet.at[:, width : 2 * width], sems.at[3]),
+        pltpu.make_async_copy(tokens, own_tokens, sems.at[2]),
+        pltpu.make_async_copy(cotangent, packet.at[:, :width], sems.at[3]),
     ]
     for copy in copies:
         copy.start()
@@ -51,7 +53,7 @@
     dense = jnp.zeros((lanes, rows), jnp.float32)
     for k in range(ids.shape[0]):
         dense += jnp.where(ids[k : k + 1, :] == at, weights[k : k + 1, :], 0.0)
-    packet[:, 2 * width :] = dense.T.astype(packet.dtype)
+    packet[:, width:] = dense.T.astype(packet.dtype)
 
 
 def load_kernel(source, value, target, same, sem):
@@ -73,31 +75,42 @@
         lax.fori_loop(0, tokens // TILE, turn, 0)
 
 
-def gate_up_kernel(x, masks, gate, up, value, hidden, slope_up, slope_gate, same):
+def gate_up_kernel(
+    x, masks, gate, w_up, value, hidden, slope_up, slope_gate, x_part, same, up, sems
+):
     local_experts, _, hidden_units = gate.shape
     bf16 = jnp.bfloat16
+    loads = [
+        pltpu.make_async_copy(w_up.at[e], up.at[e], sems.at[e]) for e in range(local_experts)
+    ]
+    for load in loads:
+        load.start()
     same[...] = value[...]
-
-    def tile(rows):
-        for expert in range(local_experts):
-            for start in range(0, hidden_units, CHUNK):
-                cols = slice(start, start + CHUNK)
-                gate_pre = dot(x[rows, :], gate[expert, :, cols], NN)
-                up_proj = dot(x[rows, :], up[expert, :, cols], NN)
-                at = ids_along((1, CHUNK), 1)
-                keep = jnp.zeros((1, CHUNK), jnp.float32)
-                for j in range(CHUNK // BLK):
-                    kept = masks[expert, start // BLK + j].astype(jnp.float32)
-                    keep = jnp.where(at // BLK == j, kept, keep)
-                sigma = 0.5 + 0.5 * jnp.tanh(0.5 * gate_pre)
-                silu = gate_pre * sigma
-                up_kept = up_proj * keep
-                hidden[expert, rows, cols] = (silu * up_kept).astype(bf16)
-                slope_up[expert, rows, cols] = (silu * keep).astype(bf16)
-                slope = up_kept * (sigma + silu * (1.0 - sigma))
-                slope_gate[expert, rows, cols] = slope.astype(bf16)
-
-    over_tiles(x.shape[0], tile)
+    x_part[...] = x[:, aligned(lax.axis_index("dp"), x_part.shape[0])].T
+
+    for expert in range(local_experts):
+        at = ids_along((1, hidden_units), 1)
+        keep = jnp.zeros((1, hidden_units), jnp.float32)
+        for j in range(hidden_units // BLK):
+            keep = jnp.where(at // BLK == j, masks[expert, j].astype(jnp.float32), keep)
+
+        def tile(rows, expert=expert, keep=keep, wait=True):
+            gate_pre = dot(x[rows, :], gate[expert], NN)
+            if wait:
+                loads[expert].wait()
+            up_kept = dot(x[rows, :], up[expert], NN) * keep
+            sigma = 0.5 + 0.5 * jnp.tanh(0.5 * gate_pre)
+            silu = gate_pre * sigma
+            hidden[expert, rows, :] = (silu * up_kept).astype(bf16)
+            slope_up[expert, rows, :] = (silu * keep).astype(bf16)
+            slope = up_kept * (sigma + silu * (1.0 - sigma))
+            slope_gate[expert, rows, :] = slope.astype(bf16)
+
+        if x.shape[0] == TILE:
+            tile(slice(0, TILE))
+        else:
+            loads[expert].wait()
+            over_tiles(x.shape[0], functools.partial(tile, wait=False))
 
 
 def stack(pieces, target, cols=slice(None)):
@@ -145,21 +158,21 @@
             at = ids_along((TILE, lanes), 1)
             hit = at == base + expert
             weights = jnp.sum(jnp.where(hit, dense, 0.0), axis=1, keepdims=True)
-            total = jnp.zeros((TILE, 1), f32)
-            for start in range(0, hidden_units, CHUNK):
-                cols = slice(start, start + CHUNK)
-                back = dot(packet[rows, :width], down[cols, :], NT)
-                part_units = units[expert, rows, cols].astype(f32)
-                total += jnp.sum(part_units * back, axis=1, keepdims=True)
-                back = back * weights
-                hidden[expert, rows, cols] = (part_units * weights).astype(bf16)
-                d_gate[expert, rows, cols] = (back * slope_gate[expert, rows, cols].astype(f32)).astype(bf16)
-                d_up[expert, rows, cols] = (back * slope_up[expert, rows, cols].astype(f32)).astype(bf16)
+            back = dot(packet[rows, :width], down[...], NT)
+            part_units = units[expert, rows, :].astype(f32)
+            total = jnp.sum(part_units * back, axis=1, keepdims=True)
+            back = back * weights
+            new_hidden = (part_units * weights).astype(bf16)
+            new_gate = (back * slope_gate[expert, rows, :].astype(f32)).astype(bf16)
+            new_up = (back * slope_up[expert, rows, :].astype(f32)).astype(bf16)
+            hidden[expert, rows, :] = new_hidden
+            d_gate[expert, rows, :] = new_gate
+            d_up[expert, rows, :] = new_up
             high = total.astype(bf16).astype(f32)
             both = jnp.where(hit, high, jnp.where(at == base + expert + half, total - high, 0.0))
-            new_mixed = dot(hidden[expert, rows, :], down[:, mine], NN)
-            new_grad = dot(d_gate[expert, rows, :], gate[expert, mine, :], NT) + dot(
-                d_up[expert, rows, :], up[expert, mine, :], NT
+            new_mixed = dot(new_hidden, down[:, mine], NN)
+            new_grad = dot(new_gate, gate[expert, mine, :], NT) + dot(
+                new_up, up[expert, mine, :], NT
             )
             if expert == 0:
                 inner[rows, :] = both
@@ -206,10 +219,9 @@
             copy.wait()
 
 
-def grad_in_kernel(x, d_gate, d_up, grad_gate, grad_up, done, x_part, out_gate, out_up, sems):
-    local_experts, _, hidden_units = d_gate.shape
+def grad_in_kernel(x_part, d_gate, d_up, grad_gate, grad_up, done, out_gate, out_up, sems):
+    local_experts = d_gate.shape[0]
     part, rows = x_part.shape[0], out_gate.shape[1]
-    x_part[...] = x[:, aligned(lax.axis_index("dp"), part)].T
     done[...] = jnp.zeros(done.shape, done.dtype)
     blocks = part // rows
 
@@ -319,11 +331,11 @@
     ids_t = expert_ids.T
     w_gate, w_up, w_down = [in_hbm(w) for w in (w_gate, w_up, w_down)]
 
-    packet = pl.pallas_call(
+    own_tokens, packet = pl.pallas_call(
         route_kernel,
-        out_shape=struct((rows, 2 * width + lanes), bf16),
+        out_shape=[struct(tokens.shape, bf16), struct((rows, width + lanes), bf16)],
         in_specs=[HBM] * 4,
-        out_specs=VMEM,
+        out_specs=[VMEM] * 2,
         scratch_shapes=[
             pltpu.VMEM(ids_t.shape, jnp.int32),
             pltpu.VMEM(ids_t.shape, bf16),
@@ -348,27 +360,29 @@
             name=name,
         )(weight, value)
 
-    arrived = exchange(packet, "dp", range(1, columns))
-    gate, packet = load(w_gate, packet, "load_gate")
-    x_column = jnp.concatenate([p[:, :width] for p in [packet] + arrived])
-    c_column = jnp.concatenate([p[:, width:] for p in [packet] + arrived])
+    x_column = jnp.concatenate([own_tokens] + exchange(own_tokens, "dp", range(1, columns)))
+    c_column = jnp.concatenate([packet] + exchange(packet, "dp", range(1, columns)))
     x_across = exchange(x_column, "expert", chips)
     c_across = exchange(c_column, "expert", chips)
-    up, x_column = load(w_up, x_column, "load_up")
-    gate, up = in_vmem(gate), in_vmem(up)
+    gate, x_column = load(w_gate, x_column, "load_gate")
+    gate = in_vmem(gate)
     x = jnp.concatenate([x_column] + x_across)
     x = jnp.concatenate([x, swap(x, "expert", 1)])
 
     units = struct((local_experts, everyone, hidden_units), bf16)
-    *factors, c_column = pl.pallas_call(
+    *factors, x_part, c_column, up = pl.pallas_call(
         gate_up_kernel,
-        out_shape=[units] * 3 + [struct(c_column.shape, bf16)],
-        in_specs=[VMEM, SMEM] + [VMEM] * 3,
-        out_specs=[VMEM] * 4,
+        out_shape=[units] * 3
+        + [struct((part, everyone), bf16), struct(c_column.shape, bf16)]
+        + [pltpu.VMEM(w_up.shape, bf16)],
+        in_specs=[VMEM, SMEM, VMEM, HBM, VMEM],
+        out_specs=[VMEM] * 6,
+        scratch_shapes=[pltpu.SemaphoreType.DMA((local_experts,))],
         cost_estimate=cost(2 * everyone * one, 2 * one),
         compiler_params=params(6),
         name="gate_up",
-    )(x, block_masks, gate, up, c_column)
+    )(x, block_masks, gate, w_up, c_column)
+    up = in_vmem(up)
     c_half = jnp.concatenate([c_column] + c_across)
     pieces = [c_half, swap(c_half, "expert", 1)]
 
@@ -401,7 +415,6 @@
         in_specs=[VMEM] * 3,
         out_specs=[HBM] * 2 + [VMEM],
         scratch_shapes=[
-            pltpu.VMEM((part, everyone), bf16),
             pltpu.VMEM((2, min(part, CHUNK), hidden_units), f32),
             pltpu.VMEM((2, min(part, CHUNK), hidden_units), f32),
             pltpu.SemaphoreType.DMA((2, 2)),
@@ -409,7 +422,7 @@
         cost_estimate=cost(2 * everyone * one // columns, 4 * one // columns),
         compiler_params=params(16),
         name="grad_in",
-    )(x, d_gate, d_up)
+    )(x_part, d_gate, d_up)
 
     route_grad, *blocks, done_sum = pl.pallas_call(
         functools.partial(reduce_kernel, sources),

time: 66.5 us -> 64.6 us (0.971)
  starting transfers between devices: 15.8 us -> 21.6 us
  waiting for transfers between devices: 10.1 us -> 5.49 us
  Pallas kernels: 39.3 us -> 36.3 us
    ppermute x13 -> x16, starting transfers between devices: 15.8 us -> 21.6 us  [swap(): return lax.ppermute(value, axis, [(i, i ^ mask) for i in range(size)])]
    ppermute x13 -> x16, waiting for transfers between devices: 10.1 us -> 5.49 us  [swap(): return lax.ppermute(value, axis, [(i, i ^ mask) for i in range(size)])]
    pallas_call x2 -> x1, Pallas kernels: 9.18 us -> 4.58 us  [load(): pl.pallas_call(load_kernel, out_shape=[pltpu.VMEM(weight.shape, weight.dt...]
    pallas_call x2, Pallas kernels: 9.16 us -> 10.6 us  [the longest x1 9.58 us: per_device(): pl.pallas_call(gate_up_kernel, out_shape=[units] * 3 + [struct((part, eve...]
  transfers between devices with their start and end apart: 13 -> 16, of which waited for: 5 -> 6; matrix products, arithmetic and copies ran while one was open for 0% -> 0% of each run, Pallas kernels for 41% -> 37%
where the time goes in v7:
time: 64.6 us; the launch traced here: 64.4 us
  Pallas kernels  36.3 us (56%)
  starting transfers between devices  21.6 us (33%)
  waiting for transfers between devices  5.49 us (8%)
  between operations  0.85 us (1%)
    ppermute x16, starting transfers between devices, swap(): return lax.ppermute(value, axis, [(i, i ^ mask) for i in range(size)])  21.6 us
    pallas_call x1, Pallas kernels, per_device(): pl.pallas_call(functools.partial(hidden_kernel, 2, sources), out_shape=[u...  9.75 us
    pallas_call x1, Pallas kernels, per_device(): pl.pallas_call(gate_up_kernel, out_shape=[units] * 3 + [struct((part, eve...  9.58 us
    pallas_call x1, Pallas kernels, per_device(): pl.pallas_call(grad_in_kernel, out_shape=[struct((local_experts, part, hi...  6.25 us
    ppermute x16, waiting for transfers between devices, swap(): return lax.ppermute(value, axis, [(i, i ^ mask) for i in range(size)])  5.49 us
    pallas_call x1, Pallas kernels, load(): pl.pallas_call(load_kernel, out_shape=[pltpu.VMEM(weight.shape, weight.dt...  4.58 us
    pallas_call x1, Pallas kernels, per_device(): pl.pallas_call(functools.partial(grad_out_kernel, 2), out_shape=[struct((...  3.63 us
  transfers between devices with their start and end apart: 16, of which 6 were waited for; matrix products, arithmetic and copies ran while one was open for 0% of the time, Pallas kernels for 37%

profile of v7, /device:TPU:0, one launch (start us, length us, event | category | flops | bytes accessed | tf_op | source)
XLA Modules:
  0.0 64.4 jit_solution(1159030878641637631)
XLA Ops:
  0.6 1.0 %route.1 = (bf16[16,2048]{1,0:T(8,128)(2,1)S(1)}, bf16[16,2176]{1,0:T(8,128)(2,1)S(1)}) custom-call(bf16[16,2048]{1,0:T(8,128)(2,1)} %tokens.1, bf16[16,2048]{1,0:T(8,128)(2,1)} %cotangent.1, s32[8,16]{1,0:T(8,128)} %bitcast.3, bf16[8,16]{1,0:T(8,128)(2,1)} %bitcast.5), custom_call_target="tpu_custom_call" | custom-call | tf_op jit(solution)/shard_map/route/pallas_call | solution.py:334
  1.7 5.1 %collective-permute-start.2 = (bf16[16,2048]{1,0:T(8,128)(2,1)S(1)}, bf16[16,2048]{1,0:T(8,128)(2,1)S(1)}, u32[]{:S(2)}, u32[]{:S(2)}) collective-permute-start(bf16[16,2048]{1,0:T(8,128)(2,1)S(1)} %get-tuple-element.36), channel_id=1, source_target_pairs={{0,3},{1,2},{2,1},{3,0},{4,7},{5,6},{6,5},{7,4},{8,11},{9,10},{10,... | collective-permute-start | bytes 196616 | tf_op jit(solution)/shard_map/ppermute | solution.py:293
  6.8 0.0 collective-permute-start.1
  6.8 0.6 collective-permute-start
  7.4 3.7 %collective-permute-start.7 = (bf16[16,2176]{1,0:T(8,128)(2,1)S(1)}, bf16[16,2176]{1,0:T(8,128)(2,1)S(1)}, u32[]{:S(2)}, u32[]{:S(2)}) collective-permute-start(bf16[16,2176]{1,0:T(8,128)(2,1)S(1)} %get-tuple-element.39), channel_id=1, source_target_pairs={{0,3},{1,2},{2,1},{3,0},{4,7},{5,6},{6,5},{7,4},{8,11},{9,10},{10,... | collective-permute-start | bytes 208904 | tf_op jit(solution)/shard_map/ppermute | solution.py:293
  11.2 0.0 collective-permute-start.6
  11.2 0.4 collective-permute-done
  11.6 2.5 %collective-permute-start.5 = (bf16[16,2176]{1,0:T(8,128)(2,1)S(1)}, bf16[16,2176]{1,0:T(8,128)(2,1)S(1)}, u32[]{:S(2)}, u32[]{:S(2)}) collective-permute-start(bf16[16,2176]{1,0:T(8,128)(2,1)S(1)} %get-tuple-element.39), channel_id=1, source_target_pairs={{0,1},{1,0},{2,3},{3,2},{4,5},{5,4},{6,7},{7,6},{8,9},{9,8},{10,11... | collective-permute-start | bytes 208904 | tf_op jit(solution)/shard_map/ppermute | solution.py:293
  14.1 1.3 %collective-permute-done.1 = bf16[16,2048]{1,0:T(8,128)(2,1)S(1)} collective-permute-done((bf16[16,2048]{1,0:T(8,128)(2,1)S(1)}, bf16[16,2048]{1,0:T(8,128)(2,1)S(1)}, u32[]{:S(2)}, u32[]{:S(2)}) %collective-permute-start.1) | collective-permute-done | bytes 65568 | tf_op jit(solution)/shard_map/ppermute | solution.py:293
  15.5 0.0 collective-permute-done.2
  15.5 1.2 %collective-permute-start.3 = (bf16[64,2048]{1,0:T(8,128)(2,1)S(1)}, bf16[64,2048]{1,0:T(8,128)(2,1)S(1)}, u32[]{:S(2)}, u32[]{:S(2)}) collective-permute-start(bf16[64,2048]{1,0:T(8,128)(2,1)S(1)} %constant_dynamic-update-slice_fusion.value), channel_id=1, source_target_pairs={{0,8},{4,12},{8,0},{12,4},{1,9},{5,13},{9,1},{13,5},{2,10},{6,14},... | collective-permute-start | bytes 786440 | tf_op jit(solution)/shard_map/ppermute | solution.py:293
  16.7 4.6 %load_gate.1 = (bf16[4,2048,768]{2,1,0:T(8,128)(2,1)S(1)}, bf16[64,2048]{1,0:T(8,128)(2,1)S(1)}) custom-call(bf16[4,2048,768]{2,1,0:T(8,128)(2,1)} %source.1, bf16[64,2048]{1,0:T(8,128)(2,1)S(1)} %constant_dynamic-update-slice_fusion.value), custom_call_target="tpu_custom_call" | custom-call | bytes 12582912 | tf_op jit(solution)/shard_map/load_gate/pallas_call | solution.py:349
  21.3 0.0 copy-start.1
  21.3 0.0 collective-permute-done.5
  21.3 0.6 collective-permute-done.3
  22.0 0.1 collective-permute-start.4
  22.0 0.0 collective-permute-done.6
  22.1 0.0 collective-permute-done.7
  22.1 1.6 %collective-permute-start.8 = (bf16[64,2176]{1,0:T(8,128)(2,1)S(1)}, bf16[64,2176]{1,0:T(8,128)(2,1)S(1)}, u32[]{:S(2)}, u32[]{:S(2)}) collective-permute-start(bf16[64,2176]{1,0:T(8,128)(2,1)S(1)} %constant_dynamic-update-slice_fusion.4.value), channel_id=1, source_target_pairs={{0,8},{4,12},{8,0},{12,4},{1,9},{5,13},{9,1},{13,5},{2,10},{6,14},... | collective-permute-start | bytes 835592 | tf_op jit(solution)/shard_map/ppermute | solution.py:293
  23.7 0.3 collective-permute-done.4
  23.9 0.1 pad_maximum_fusion.x
  24.0 0.0 copy-done.1
  24.0 9.6 %gate_up.1 = (bf16[4,256,768]{2,1,0:T(8,128)(2,1)S(1)}, bf16[4,256,768]{2,1,0:T(8,128)(2,1)S(1)}, bf16[4,256,768]{2,1,0:T(8,128)(2,1)S(1)}, bf16[512,256]{1,0:T(...) custom-call(bf16[256,2048]{1,0:T(8,128)(2,1)S(1)} %pad_maximum_fusion.x, ...), custom_call_target="tpu_custom_call" | custom-call | flops 6442450944 | bytes 25165824 | tf_op jit(solution)/shard_map/gate_up/pallas_call | solution.py:373
  33.6 0.0 collective-permute-done.8
  33.7 0.2 collective-permute-start.9
  33.9 1.8 %collective-permute-done.9.refs_1_ = bf16[128,2176]{1,0:T(8,128)(2,1)S(1)} collective-permute-done((bf16[128,2176]{1,0:T(8,128)(2,1)S(1)}, bf16[128,2176]{1,0:T(8,128)(2,1)S(1)}, u32[]{:S(2)}, u32[]{:S(2)}) %collective-permute-start.9) | collective-permute-done | bytes 557088 | tf_op jit(solution)/shard_map/ppermute | solution.py:293
  35.7 9.8 %hidden.1 = (bf16[4,256,768]{2,1,0:T(8,128)(2,1)S(1)}, bf16[4,256,768]{2,1,0:T(8,128)(2,1)S(1)}, bf16[4,256,768]{2,1,0:T(8,128)(2,1)S(1)}, bf16[64,1152]{1,0:T(8...) custom-call(bf16[128,2176]{1,0:T(8,128)(2,1)S(1)} %constant_dynamic-update-, ...), custom_call_target="tpu_custom_call" | custom-call | flops 6442450944 | bytes 25165824 | tf_op jit(solution)/shard_map/hidden/pallas_call | solution.py:389
  45.5 1.6 %collective-permute-start.10 = (bf16[64,1152]{1,0:T(8,128)(2,1)S(1)}, bf16[64,1152]{1,0:T(8,128)(2,1)S(1)}, u32[]{:S(2)}, u32[]{:S(2)}) collective-permute-start(bf16[64,1152]{1,0:T(8,128)(2,1)S(1)} %get-tuple-element.46), channel_id=1, source_target_pairs={{0,8},{4,12},{8,0},{12,4},{1,9},{5,13},{9,1},{13,5},{2,10},{6,14},... | collective-permute-start | bytes 442376 | tf_op jit(solution)/shard_map/ppermute | solution.py:293
  47.0 0.0 collective-permute-start.11
  47.0 0.6 collective-permute-start.12
  47.7 0.0 copy-start
  47.7 6.2 %grad_in.1 = (f32[4,512,768]{2,1,0:T(8,128)}, f32[4,512,768]{2,1,0:T(8,128)}, f32[8,128]{1,0:T(8,128)S(1)}) custom-call(bf16[512,256]{1,0:T(8,128)(2,1)S(1)} %get-tuple-element.49.x_part, bf16[4,256,768]{2,1,0:T(8,128)(2,1)S(1)} %get-tuple-element.50.d_gate, bf16[4,256,768]{2,1,0:T(8,128)(2,1)S(1)} %get-tuple-element.51.d_up), custom_call_target="tpu_custom_call" | custom-call | flops 1610612736 | bytes 12582912 | tf_op jit(solution)/shard_map/grad_in/pallas_call | solution.py:412
  53.9 0.0 collective-permute-done.10.refs_1_
  53.9 0.0 collective-permute-done.11.refs_2_
  54.0 0.0 collective-permute-done.12.refs_3_
  54.0 0.0 copy-done
  54.0 0.8 %reduce.1 = (f32[8,16]{1,0:T(8,128)}, bf16[16,1024]{1,0:T(8,128)(2,1)S(1)}, bf16[16,1024]{1,0:T(8,128)(2,1)S(1)}, bf16[16,1024]{1,0:T(8,128)(2,1)S(1)}, bf16[16,...) custom-call(bf16[64,1152]{1,0:T(8,128)(2,1)S(1)} %get-tuple-element.45.refs_0_, ...), custom_call_target="tpu_custom_call" | custom-call | tf_op jit(solution)/shard_map/reduce/pallas_call | solution.py:427
  54.7 0.0 collective-permute-start.13
  54.7 3.3 %collective-permute-start.14 = (bf16[16,1024]{1,0:T(8,128)(2,1)S(1)}, bf16[16,1024]{1,0:T(8,128)(2,1)S(1)}, u32[]{:S(2)}, u32[]{:S(2)}) collective-permute-start(bf16[16,1024]{1,0:T(8,128)(2,1)S(1)} %get-tuple-element.55), channel_id=1, source_target_pairs={{0,2},{1,3},{2,0},{3,1},{4,6},{5,7},{6,4},{7,5},{8,10},{9,11},{10,... | collective-permute-start | bytes 98312 | tf_op jit(solution)/shard_map/ppermute | solution.py:293
  58.0 1.1 %collective-permute-start.15 = (bf16[16,1024]{1,0:T(8,128)(2,1)S(1)}, bf16[16,1024]{1,0:T(8,128)(2,1)S(1)}, u32[]{:S(2)}, u32[]{:S(2)}) collective-permute-start(bf16[16,1024]{1,0:T(8,128)(2,1)S(1)} %get-tuple-element.56), channel_id=1, source_target_pairs={{0,3},{1,2},{2,1},{3,0},{4,7},{5,6},{6,5},{7,4},{8,11},{9,10},{10,... | collective-permute-start | bytes 98312 | tf_op jit(solution)/shard_map/ppermute | solution.py:293
  59.1 3.6 %grad_out.1 = (f32[4,768,512]{2,1,0:T(8,128)}, f32[8,128]{1,0:T(8,128)S(1)}) custom-call(bf16[128,2176]{1,0:T(8,128)(2,1)S(1)} %constant_dynamic-update-slice_fusion.8.refs_0_, bf16[128,2176]{1,0:T(8,128)(2,1)S(1)} %collective-permute-done.9.refs_1_, bf16[4,256,768]{2,1,0:T(8,128)(2,1)S(1)} %get-tuple-element.57.refs_2_, f32[8,128]{1,0:T(8,128)S(1)} %get-tuple-element.58.refs_3_), custom_call_target="tpu_custom_call" | custom-call | flops 805306368 | bytes 6291456 | tf_op jit(solution)/shard_map/grad_out/pallas_call | solution.py:439
  62.8 0.0 collective-permute-done.13.refs_1_
  62.8 0.0 collective-permute-done.14.refs_2_
  62.8 1.0 %collective-permute-done.15.refs_3_ = bf16[16,1024]{1,0:T(8,128)(2,1)S(1)} collective-permute-done((bf16[16,1024]{1,0:T(8,128)(2,1)S(1)}, bf16[16,1024]{1,0:T(8,128)(2,1)S(1)}, u32[]{:S(2)}, u32[]{:S(2)}) %collective-permute-start.15) | collective-permute-done | bytes 32800 | tf_op jit(solution)/shard_map/ppermute | solution.py:293
  63.8 0.7 %join.1 = (bf16[16,2048]{1,0:T(8,128)(2,1)}, bf16[16,2048]{1,0:T(8,128)(2,1)}) custom-call(bf16[16,1024]{1,0:T(8,128)(2,1)S(1)} %get-tuple-element.53.refs_0_, bf16[16,1024]{1,0:T(8,128)(2,1)S(1)} %collective-permute-done.13.refs_1_, bf16[16,1024]{1,0:T(8,128)(2,1)S(1)} %collective-permute-done.14.refs_2_, ...), custom_call_target="tpu_custom_call" | custom-call | tf_op jit(solution)/shard_map/join/pallas_call | solution.py:454
  (11 shorter events, 0.2 us)
Async XLA Ops:
  1.7 13.8 %collective-permute-start.2 = (bf16[16,2048]{1,0:T(8,128)(2,1)S(1)}, bf16[16,2048]{1,0:T(8,128)(2,1)S(1)}, u32[]{:S(2)}, u32[]{:S(2)}) collective-permute-start(bf16[16,2048]{1,0:T(8,128)(2,1)S(1)} %get-tuple-element.36), channel_id=1, source_target_pairs={{0,3},{1,2},{2,1},{3,0},{4,7},{5,6},{6,5},{7,4},{8,11},{9,10},{10,... | collective-permute-start | bytes 196616 | tf_op jit(solution)/shard_map/ppermute | solution.py:293
  6.8 8.7 %collective-permute-start.1 = (bf16[16,2048]{1,0:T(8,128)(2,1)S(1)}, bf16[16,2048]{1,0:T(8,128)(2,1)S(1)}, u32[]{:S(2)}, u32[]{:S(2)}) collective-permute-start(bf16[16,2048]{1,0:T(8,128)(2,1)S(1)} %get-tuple-element.36), channel_id=1, source_target_pairs={{0,2},{1,3},{2,0},{3,1},{4,6},{5,7},{6,4},{7,5},{8,10},{9,11},{10,... | collective-permute-start | bytes 196616 | tf_op jit(solution)/shard_map/ppermute | solution.py:293
  6.8 4.8 %collective-permute-start = (bf16[16,2048]{1,0:T(8,128)(2,1)S(1)}, bf16[16,2048]{1,0:T(8,128)(2,1)S(1)}, u32[]{:S(2)}, u32[]{:S(2)}) collective-permute-start(bf16[16,2048]{1,0:T(8,128)(2,1)S(1)} %get-tuple-element.36), channel_id=1, source_target_pairs={{0,1},{1,0},{2,3},{3,2},{4,5},{5,4},{6,7},{7,6},{8,9},{9,8},{10,11... | collective-permute-start | bytes 196616 | tf_op jit(solution)/shard_map/ppermute | solution.py:293
  7.4 14.6 %collective-permute-start.7 = (bf16[16,2176]{1,0:T(8,128)(2,1)S(1)}, bf16[16,2176]{1,0:T(8,128)(2,1)S(1)}, u32[]{:S(2)}, u32[]{:S(2)}) collective-permute-start(bf16[16,2176]{1,0:T(8,128)(2,1)S(1)} %get-tuple-element.39), channel_id=1, source_target_pairs={{0,3},{1,2},{2,1},{3,0},{4,7},{5,6},{6,5},{7,4},{8,11},{9,10},{10,... | collective-permute-start | bytes 208904 | tf_op jit(solution)/shard_map/ppermute | solution.py:293
  11.2 10.9 %collective-permute-start.6 = (bf16[16,2176]{1,0:T(8,128)(2,1)S(1)}, bf16[16,2176]{1,0:T(8,128)(2,1)S(1)}, u32[]{:S(2)}, u32[]{:S(2)}) collective-permute-start(bf16[16,2176]{1,0:T(8,128)(2,1)S(1)} %get-tuple-element.39), channel_id=1, source_target_pairs={{0,2},{1,3},{2,0},{3,1},{4,6},{5,7},{6,4},{7,5},{8,10},{9,11},{10,... | collective-permute-start | bytes 208904 | tf_op jit(solution)/shard_map/ppermute | solution.py:293
  11.6 9.7 %collective-permute-start.5 = (bf16[16,2176]{1,0:T(8,128)(2,1)S(1)}, bf16[16,2176]{1,0:T(8,128)(2,1)S(1)}, u32[]{:S(2)}, u32[]{:S(2)}) collective-permute-start(bf16[16,2176]{1,0:T(8,128)(2,1)S(1)} %get-tuple-element.39), channel_id=1, source_target_pairs={{0,1},{1,0},{2,3},{3,2},{4,5},{5,4},{6,7},{7,6},{8,9},{9,8},{10,11... | collective-permute-start | bytes 208904 | tf_op jit(solution)/shard_map/ppermute | solution.py:293
  15.5 6.4 %collective-permute-start.3 = (bf16[64,2048]{1,0:T(8,128)(2,1)S(1)}, bf16[64,2048]{1,0:T(8,128)(2,1)S(1)}, u32[]{:S(2)}, u32[]{:S(2)}) collective-permute-start(bf16[64,2048]{1,0:T(8,128)(2,1)S(1)} %constant_dynamic-update-slice_fusion.value), channel_id=1, source_target_pairs={{0,8},{4,12},{8,0},{12,4},{1,9},{5,13},{9,1},{13,5},{2,10},{6,14},... | collective-permute-start | bytes 786440 | tf_op jit(solution)/shard_map/ppermute | solution.py:293
  21.3 2.7 %copy-start.1 = (s32[4,6]{1,0:T(4,128)S(1)}, s32[4,6]{1,0:T(4,128)}, u32[]{:S(2)}) copy-start(s32[4,6]{1,0:T(4,128)} %masks.1) | copy-start | bytes 292
  22.0 2.0 %collective-permute-start.4 = (bf16[128,2048]{1,0:T(8,128)(2,1)S(1)}, bf16[128,2048]{1,0:T(8,128)(2,1)S(1)}, u32[]{:S(2)}, u32[]{:S(2)}) collective-permute-start(bf16[128,2048]{1,0:T(8,128)(2,1)S(1)} %pad_maximum_fusion.1), channel_id=1, source_target_pairs={{0,4},{4,0},{8,12},{12,8},{1,5},{5,1},{9,13},{13,9},{2,6},{6,2},{1... | collective-permute-start | bytes 1572872 | tf_op jit(solution)/shard_map/ppermute | solution.py:293
  22.1 11.5 %collective-permute-start.8 = (bf16[64,2176]{1,0:T(8,128)(2,1)S(1)}, bf16[64,2176]{1,0:T(8,128)(2,1)S(1)}, u32[]{:S(2)}, u32[]{:S(2)}) collective-permute-start(bf16[64,2176]{1,0:T(8,128)(2,1)S(1)} %constant_dynamic-update-slice_fusion.4.value), channel_id=1, source_target_pairs={{0,8},{4,12},{8,0},{12,4},{1,9},{5,13},{9,1},{13,5},{2,10},{6,14},... | collective-permute-start | bytes 835592 | tf_op jit(solution)/shard_map/ppermute | solution.py:293
  33.7 2.0 %collective-permute-start.9 = (bf16[128,2176]{1,0:T(8,128)(2,1)S(1)}, bf16[128,2176]{1,0:T(8,128)(2,1)S(1)}, u32[]{:S(2)}, u32[]{:S(2)}) collective-permute-start(bf16[128,2176]{1,0:T(8,128)(2,1)S(1)} %constant_dynamic-update-slice_fusion.8.refs_0_), channel_id=1, source_target_pairs={{0,4},{4,0},{8,12},{12,8},{1,5},{5,1},{9,13},{13,9},{2,6},{6,2},{1... | collective-permute-start | bytes 1671176 | tf_op jit(solution)/shard_map/ppermute | solution.py:293
  45.5 8.5 %collective-permute-start.10 = (bf16[64,1152]{1,0:T(8,128)(2,1)S(1)}, bf16[64,1152]{1,0:T(8,128)(2,1)S(1)}, u32[]{:S(2)}, u32[]{:S(2)}) collective-permute-start(bf16[64,1152]{1,0:T(8,128)(2,1)S(1)} %get-tuple-element.46), channel_id=1, source_target_pairs={{0,8},{4,12},{8,0},{12,4},{1,9},{5,13},{9,1},{13,5},{2,10},{6,14},... | collective-permute-start | bytes 442376 | tf_op jit(solution)/shard_map/ppermute | solution.py:293
  47.0 6.9 %collective-permute-start.11 = (bf16[64,1152]{1,0:T(8,128)(2,1)S(1)}, bf16[64,1152]{1,0:T(8,128)(2,1)S(1)}, u32[]{:S(2)}, u32[]{:S(2)}) collective-permute-start(bf16[64,1152]{1,0:T(8,128)(2,1)S(1)} %get-tuple-element.47), channel_id=1, source_target_pairs={{0,4},{4,0},{8,12},{12,8},{1,5},{5,1},{9,13},{13,9},{2,6},{6,2},{1... | collective-permute-start | bytes 442376 | tf_op jit(solution)/shard_map/ppermute | solution.py:293
  47.0 6.9 %collective-permute-start.12 = (bf16[64,1152]{1,0:T(8,128)(2,1)S(1)}, bf16[64,1152]{1,0:T(8,128)(2,1)S(1)}, u32[]{:S(2)}, u32[]{:S(2)}) collective-permute-start(bf16[64,1152]{1,0:T(8,128)(2,1)S(1)} %get-tuple-element.48), channel_id=1, source_target_pairs={{0,12},{4,8},{8,4},{12,0},{1,13},{5,9},{9,5},{13,1},{2,14},{6,10},... | collective-permute-start | bytes 442376 | tf_op jit(solution)/shard_map/ppermute | solution.py:293
  47.7 6.3 %copy-start = (s32[16,8]{0,1:T(8,128)S(1)}, s32[16,8]{0,1:T(8,128)}, u32[]{:S(2)}) copy-start(s32[16,8]{0,1:T(8,128)} %param.10) | copy-start | bytes 1540
  54.7 8.0 %collective-permute-start.13 = (bf16[16,1024]{1,0:T(8,128)(2,1)S(1)}, bf16[16,1024]{1,0:T(8,128)(2,1)S(1)}, u32[]{:S(2)}, u32[]{:S(2)}) collective-permute-start(bf16[16,1024]{1,0:T(8,128)(2,1)S(1)} %get-tuple-element.54), channel_id=1, source_target_pairs={{0,1},{1,0},{2,3},{3,2},{4,5},{5,4},{6,7},{7,6},{8,9},{9,8},{10,11... | collective-permute-start | bytes 98312 | tf_op jit(solution)/shard_map/ppermute | solution.py:293
  54.7 8.0 %collective-permute-start.14 = (bf16[16,1024]{1,0:T(8,128)(2,1)S(1)}, bf16[16,1024]{1,0:T(8,128)(2,1)S(1)}, u32[]{:S(2)}, u32[]{:S(2)}) collective-permute-start(bf16[16,1024]{1,0:T(8,128)(2,1)S(1)} %get-tuple-element.55), channel_id=1, source_target_pairs={{0,2},{1,3},{2,0},{3,1},{4,6},{5,7},{6,4},{7,5},{8,10},{9,11},{10,... | collective-permute-start | bytes 98312 | tf_op jit(solution)/shard_map/ppermute | solution.py:293
  58.0 5.7 %collective-permute-start.15 = (bf16[16,1024]{1,0:T(8,128)(2,1)S(1)}, bf16[16,1024]{1,0:T(8,128)(2,1)S(1)}, u32[]{:S(2)}, u32[]{:S(2)}) collective-permute-start(bf16[16,1024]{1,0:T(8,128)(2,1)S(1)} %get-tuple-element.56), channel_id=1, source_target_pairs={{0,3},{1,2},{2,1},{3,0},{4,7},{5,6},{6,5},{7,4},{8,11},{9,10},{10,... | collective-permute-start | bytes 98312 | tf_op jit(solution)/shard_map/ppermute | solution.py:293

commit v8 on v6

--- a/solution.py
+++ b/solution.py
@@ -33,17 +33,17 @@
     return pl.ds(pl.multiple_of(index * size, size), size)
 
 
-def route_kernel(tokens, cotangent, expert_ids, route_weights, packet, ids, values, sems):
-    rows, width = tokens.shape
-    lanes = packet.shape[1] - 2 * width
+def route_kernel(cotangent, expert_ids, route_weights, value, packet, same, ids, values, sems):
+    rows, width = cotangent.shape
+    lanes = packet.shape[1] - width
     copies = [
         pltpu.make_async_copy(expert_ids, ids, sems.at[0]),
         pltpu.make_async_copy(route_weights, values, sems.at[1]),
-        pltpu.make_async_copy(tokens, packet.at[:, :width], sems.at[2]),
-        pltpu.make_async_copy(cotangent, packet.at[:, width : 2 * width], sems.at[3]),
+        pltpu.make_async_copy(cotangent, packet.at[:, :width], sems.at[2]),
     ]
     for copy in copies:
         copy.start()
+    same[...] = value[...]
     for copy in copies:
         copy.wait()
     at = ids_along((lanes, rows), 0)
@@ -51,14 +51,22 @@
     dense = jnp.zeros((lanes, rows), jnp.float32)
     for k in range(ids.shape[0]):
         dense += jnp.where(ids[k : k + 1, :] == at, weights[k : k + 1, :], 0.0)
-    packet[:, 2 * width :] = dense.T.astype(packet.dtype)
-
-
-def load_kernel(source, value, target, same, sem):
-    copy = pltpu.make_async_copy(source, target, sem)
-    copy.start()
-    same[...] = value[...]
-    copy.wait()
+    packet[:, width:] = dense.T.astype(packet.dtype)
+
+
+def load_kernel(weight, tokens, target, own_tokens, sems):
+    copies = [
+        pltpu.make_async_copy(tokens, own_tokens, sems.at[0]),
+        pltpu.make_async_copy(weight, target, sems.at[1]),
+    ]
+    for copy in copies:
+        copy.start()
+    for copy in copies:
+        copy.wait()
+
+
+def turn_kernel(x, after, x_part):
+    x_part[...] = x[:, aligned(lax.axis_index("dp"), x_part.shape[0])].T
 
 
 def over_tiles(tokens, body):
@@ -73,17 +81,28 @@
         lax.fori_loop(0, tokens // TILE, turn, 0)
 
 
-def gate_up_kernel(x, masks, gate, up, value, hidden, slope_up, slope_gate, same):
-    local_experts, _, hidden_units = gate.shape
+def gate_up_kernel(first, last, *refs):
+    x, masks, gate, w_up, value = refs[:5]
+    hidden, slope_up, slope_gate, same, up_buf, sems = refs[-6:]
+    hidden_units = gate.shape[2]
     bf16 = jnp.bfloat16
+    loads = [
+        pltpu.make_async_copy(w_up.at[e], up_buf.at[(e - first) % 2], sems.at[(e - first) % 2])
+        for e in range(first, last)
+    ]
+    for load in loads[:2]:
+        load.start()
     same[...] = value[...]
 
-    def tile(rows):
-        for expert in range(local_experts):
+    for expert in range(first, last):
+        up = up_buf.at[(expert - first) % 2]
+        loads[expert - first].wait()
+
+        def tile(rows, expert=expert, up=up):
             for start in range(0, hidden_units, CHUNK):
                 cols = slice(start, start + CHUNK)
                 gate_pre = dot(x[rows, :], gate[expert, :, cols], NN)
-                up_proj = dot(x[rows, :], up[expert, :, cols], NN)
+                up_proj = dot(x[rows, :], up[:, cols], NN)
                 at = ids_along((1, CHUNK), 1)
                 keep = jnp.zeros((1, CHUNK), jnp.float32)
                 for j in range(CHUNK // BLK):
@@ -97,20 +116,15 @@
                 slope = up_kept * (sigma + silu * (1.0 - sigma))
                 slope_gate[expert, rows, cols] = slope.astype(bf16)
 
-    over_tiles(x.shape[0], tile)
-
-
-def stack(pieces, target, cols=slice(None)):
-    rows = pieces[0].shape[0]
-    for i, piece in enumerate(pieces):
-        target[i * rows : (i + 1) * rows] = piece[:, cols]
-
-
-def hidden_kernel(count, blocks, *refs):
-    pieces, refs = refs[:count], refs[count:]
-    units, slope_up, slope_gate, gate, up, w_down, hidden, d_gate, d_up = refs[:9]
-    outs, refs = refs[9 : 9 + blocks], refs[9 + blocks :]
-    packet, inner, mixed, token_grad, down_buf, sems = refs
+        over_tiles(x.shape[0], tile)
+        if expert + 2 < last:
+            loads[expert + 2 - first].start()
+
+
+def hidden_kernel(count, *refs):
+    packet, units, slope_up, slope_gate, w_gate, w_up, w_down, hidden, d_gate, d_up = refs[:10]
+    outs, refs = refs[10 : 10 + count], refs[10 + count :]
+    inner, mixed, token_grad, down_buf, gate_buf, up_buf, sems = refs
     local_experts, hidden_units, width = w_down.shape
     tokens, part = mixed.shape
     lanes = packet.shape[1] - width
@@ -120,27 +134,39 @@
     bf16, f32 = jnp.bfloat16, jnp.float32
 
     def copies(expert):
+        slot = lax.rem(expert, 2)
         return [
             pltpu.make_async_copy(
-                w_down.at[expert, slice(start, start + CHUNK), :],
-                down_buf.at[expert % 2, slice(start, start + CHUNK), :],
-                sems.at[expert % 2, start // CHUNK],
+                w_down.at[expert, slice(i * CHUNK, (i + 1) * CHUNK), :],
+                down_buf.at[slot, slice(i * CHUNK, (i + 1) * CHUNK), :],
+                sems.at[slot, 2 + i],
             )
-            for start in range(0, hidden_units, CHUNK)
+            for i in range(hidden_units // CHUNK)
+        ] + [
+            pltpu.make_async_copy(w_gate.at[expert, mine, :], gate_buf.at[slot], sems.at[slot, 0]),
+            pltpu.make_async_copy(w_up.at[expert, mine, :], up_buf.at[slot], sems.at[slot, 1]),
         ]
 
     for copy in copies(0):
         copy.start()
-    stack(pieces, packet)
-    for expert in range(local_experts):
-        if expert + 1 < local_experts:
+    inner[...] = jnp.zeros(inner.shape, inner.dtype)
+    mixed[...] = jnp.zeros(mixed.shape, mixed.dtype)
+    token_grad[...] = jnp.zeros(token_grad.shape, token_grad.dtype)
+
+    def one_expert(expert, carry):
+        @pl.when(expert + 1 < local_experts)
+        def _():
             for copy in copies(expert + 1):
                 copy.start()
-        down = down_buf.at[expert % 2]
-        for copy in copies(expert):
-            copy.wait()
-
-        def tile(rows, expert=expert, down=down):
+
+        slot = lax.rem(expert, 2)
+        down, gate, up = down_buf.at[slot], gate_buf.at[slot], up_buf.at[slot]
+        arriving = copies(expert)
+        if tokens != TILE:
+            for copy in arriving:
+                copy.wait()
+
+        def tile(rows):
             dense = packet[rows, width:].astype(f32)
             at = ids_along((TILE, lanes), 1)
             hit = at == base + expert
@@ -148,30 +174,33 @@
             total = jnp.zeros((TILE, 1), f32)
             for start in range(0, hidden_units, CHUNK):
                 cols = slice(start, start + CHUNK)
+                if tokens == TILE:
+                    arriving[start // CHUNK].wait()
                 back = dot(packet[rows, :width], down[cols, :], NT)
                 part_units = units[expert, rows, cols].astype(f32)
                 total += jnp.sum(part_units * back, axis=1, keepdims=True)
                 back = back * weights
+                new_gate = back * slope_gate[expert, rows, cols].astype(f32)
+                new_up = back * slope_up[expert, rows, cols].astype(f32)
                 hidden[expert, rows, cols] = (part_units * weights).astype(bf16)
-                d_gate[expert, rows, cols] = (back * slope_gate[expert, rows, cols].astype(f32)).astype(bf16)
-                d_up[expert, rows, cols] = (back * slope_up[expert, rows, cols].astype(f32)).astype(bf16)
+                d_gate[expert, rows, cols] = new_gate.astype(bf16)
+                d_up[expert, rows, cols] = new_up.astype(bf16)
             high = total.astype(bf16).astype(f32)
-            both = jnp.where(hit, high, jnp.where(at == base + expert + half, total - high, 0.0))
-            new_mixed = dot(hidden[expert, rows, :], down[:, mine], NN)
-            new_grad = dot(d_gate[expert, rows, :], gate[expert, mine, :], NT) + dot(
-                d_up[expert, rows, :], up[expert, mine, :], NT
+            inner[rows, :] += jnp.where(
+                hit, high, jnp.where(at == base + expert + half, total - high, 0.0)
             )
-            if expert == 0:
-                inner[rows, :] = both
-                mixed[rows, :] = new_mixed
-                token_grad[rows, :] = new_grad
-            else:
-                inner[rows, :] += both
-                mixed[rows, :] += new_mixed
-                token_grad[rows, :] += new_grad
+            if tokens == TILE:
+                for copy in arriving[-2:]:
+                    copy.wait()
+            mixed[rows, :] += dot(hidden[expert, rows, :], down[:, mine], NN)
+            token_grad[rows, :] += dot(d_gate[expert, rows, :], gate[...], NT) + dot(
+                d_up[expert, rows, :], up[...], NT
+            )
 
         over_tiles(tokens, tile)
-
+        return carry
+
+    lax.fori_loop(0, local_experts, one_expert, 0)
     rows = outs[0].shape[0]
     for i, out in enumerate(outs):
         block = slice(i * rows, (i + 1) * rows)
@@ -206,10 +235,9 @@
             copy.wait()
 
 
-def grad_in_kernel(x, d_gate, d_up, grad_gate, grad_up, done, x_part, out_gate, out_up, sems):
-    local_experts, _, hidden_units = d_gate.shape
+def grad_in_kernel(x_part, d_gate, d_up, grad_gate, grad_up, done, out_gate, out_up, sems):
+    local_experts = d_gate.shape[0]
     part, rows = x_part.shape[0], out_gate.shape[1]
-    x_part[...] = x[:, aligned(lax.axis_index("dp"), part)].T
     done[...] = jnp.zeros(done.shape, done.dtype)
     blocks = part // rows
 
@@ -226,12 +254,10 @@
     )
 
 
-def grad_out_kernel(count, *refs):
-    pieces, refs = refs[:count], refs[count:]
-    hidden, after, grad_down, done, cot_part, out_down, sems = refs
+def grad_out_kernel(packet, hidden, after, grad_down, done, cot_part, out_down, sems):
     local_experts = hidden.shape[0]
     part = cot_part.shape[1]
-    stack(pieces, cot_part, aligned(lax.axis_index("dp"), part))
+    cot_part[...] = packet[:, aligned(lax.axis_index("dp"), part)]
     done[...] = jnp.zeros(done.shape, done.dtype)
 
     def place(step):
@@ -315,81 +341,98 @@
     bf16, f32 = jnp.bfloat16, jnp.float32
     struct = jax.ShapeDtypeStruct
     one = 2 * local_experts * width * hidden_units
+    room = 16 + (everyone - TILE) * (2 * part + lanes) * 14 // MIB
     dummy = struct((8, LANES), f32)
     ids_t = expert_ids.T
     w_gate, w_up, w_down = [in_hbm(w) for w in (w_gate, w_up, w_down)]
 
-    packet = pl.pallas_call(
+    tokens_near = exchange(tokens, "dp", range(1, columns))
+    gate, own_tokens = pl.pallas_call(
+        load_kernel,
+        out_shape=[pltpu.VMEM(w_gate.shape, bf16), struct(tokens.shape, bf16)],
+        in_specs=[HBM] * 2,
+        out_specs=[VMEM] * 2,
+        scratch_shapes=[pltpu.SemaphoreType.DMA((2,))],
+        cost_estimate=cost(0, one),
+        compiler_params=params(room),
+        name="load_gate",
+    )(w_gate, in_hbm(tokens))
+    gate = in_vmem(gate)
+    x_column = jnp.concatenate([own_tokens] + tokens_near)
+    x_across = exchange(x_column, "expert", chips)
+
+    packet, x_column = pl.pallas_call(
         route_kernel,
-        out_shape=struct((rows, 2 * width + lanes), bf16),
-        in_specs=[HBM] * 4,
-        out_specs=VMEM,
+        out_shape=[struct((rows, width + lanes), bf16), struct(x_column.shape, bf16)],
+        in_specs=[HBM] * 3 + [VMEM],
+        out_specs=[VMEM] * 2,
         scratch_shapes=[
             pltpu.VMEM(ids_t.shape, jnp.int32),
             pltpu.VMEM(ids_t.shape, bf16),
-            pltpu.SemaphoreType.DMA((4,)),
+            pltpu.SemaphoreType.DMA((3,)),
         ],
-        compiler_params=params(2),
+        compiler_params=params(room),
         name="route",
-    )(*[in_hbm(a) for a in (tokens, cotangent, ids_t, route_weights.T)])
-
-    def load(weight, value, name):
-        return pl.pallas_call(
-            load_kernel,
-            out_shape=[
-                pltpu.VMEM(weight.shape, weight.dtype),
-                struct(value.shape, value.dtype),
-            ],
-            in_specs=[HBM, VMEM],
-            out_specs=[VMEM] * 2,
-            scratch_shapes=[pltpu.SemaphoreType.DMA],
-            cost_estimate=cost(0, one),
-            compiler_params=params(1),
-            name=name,
-        )(weight, value)
-
-    arrived = exchange(packet, "dp", range(1, columns))
-    gate, packet = load(w_gate, packet, "load_gate")
-    x_column = jnp.concatenate([p[:, :width] for p in [packet] + arrived])
-    c_column = jnp.concatenate([p[:, width:] for p in [packet] + arrived])
-    x_across = exchange(x_column, "expert", chips)
-    c_across = exchange(c_column, "expert", chips)
-    up, x_column = load(w_up, x_column, "load_up")
-    gate, up = in_vmem(gate), in_vmem(up)
+    )(*[in_hbm(a) for a in (cotangent, ids_t, route_weights.T)], x_column)
+    c_column = jnp.concatenate([packet] + exchange(packet, "dp", range(1, columns)))
     x = jnp.concatenate([x_column] + x_across)
     x = jnp.concatenate([x, swap(x, "expert", 1)])
 
     units = struct((local_experts, everyone, hidden_units), bf16)
-    *factors, c_column = pl.pallas_call(
-        gate_up_kernel,
-        out_shape=[units] * 3 + [struct(c_column.shape, bf16)],
-        in_specs=[VMEM, SMEM] + [VMEM] * 3,
-        out_specs=[VMEM] * 4,
-        cost_estimate=cost(2 * everyone * one, 2 * one),
-        compiler_params=params(6),
-        name="gate_up",
-    )(x, block_masks, gate, up, c_column)
+    def gate_up(first, last, value, known):
+        return pl.pallas_call(
+            functools.partial(gate_up_kernel, first, last),
+            out_shape=[units] * 3
+            + [struct(value.shape, value.dtype)],
+            in_specs=[VMEM, SMEM, VMEM, HBM] + [VMEM] * (1 + len(known)),
+            out_specs=[VMEM] * 4,
+            scratch_shapes=[
+                pltpu.VMEM((min(2, last - first), width, hidden_units), bf16),
+                pltpu.SemaphoreType.DMA((2,)),
+            ],
+            input_output_aliases={5 + i: i for i in range(len(known))},
+            cost_estimate=cost(
+                2 * everyone * one * (last - first) // local_experts,
+                2 * one * (last - first) // local_experts,
+            ),
+            compiler_params=params(room),
+            name="gate_up",
+        )(x, block_masks, gate, w_up, value, *known)
+
+    *factors, c_column = gate_up(0, 1, c_column, [])
+    c_across = exchange(c_column, "expert", chips)
+    if local_experts > 1:
+        *factors, c_column = gate_up(1, local_experts, c_column, factors)
     c_half = jnp.concatenate([c_column] + c_across)
-    pieces = [c_half, swap(c_half, "expert", 1)]
+    packets = jnp.concatenate([c_half, swap(c_half, "expert", 1)])
+    x_part = pl.pallas_call(
+        turn_kernel,
+        out_shape=struct((part, everyone), bf16),
+        in_specs=[VMEM] * 2,
+        out_specs=VMEM,
+        compiler_params=params(room),
+        name="turn",
+    )(x, c_half)
 
     hidden, d_gate, d_up, *partials = pl.pallas_call(
-        functools.partial(hidden_kernel, 2, sources),
+        functools.partial(hidden_kernel, sources),
         out_shape=[units] * 3
         + [struct((columns * rows, 2 * part + lanes), bf16)] * sources,
-        in_specs=[VMEM] * 7 + [HBM],
+        in_specs=[VMEM] * 4 + [HBM] * 3,
         out_specs=[VMEM] * (3 + sources),
         scratch_shapes=[
-            pltpu.VMEM((everyone, width + lanes), bf16),
             pltpu.VMEM((everyone, lanes), f32),
             pltpu.VMEM((everyone, part), f32),
             pltpu.VMEM((everyone, part), f32),
             pltpu.VMEM((min(2, local_experts), hidden_units, width), bf16),
-            pltpu.SemaphoreType.DMA((2, hidden_units // CHUNK)),
+            pltpu.VMEM((min(2, local_experts), part, hidden_units), bf16),
+            pltpu.VMEM((min(2, local_experts), part, hidden_units), bf16),
+            pltpu.SemaphoreType.DMA((2, 2 + hidden_units // CHUNK)),
         ],
         cost_estimate=cost(2 * everyone * one, 2 * one),
-        compiler_params=params(12 + (everyone - TILE) * (2 * part + lanes) * 14 // MIB),
+        compiler_params=params(room),
         name="hidden",
-    )(*pieces, *factors, gate, up, w_down)
+    )(packets, *factors, w_gate, w_up, w_down)
     arrived = [
         swap(partial, "expert", other) if other else partial
         for other, partial in zip(expert_order, partials)
@@ -401,22 +444,21 @@
         in_specs=[VMEM] * 3,
         out_specs=[HBM] * 2 + [VMEM],
         scratch_shapes=[
-            pltpu.VMEM((part, everyone), bf16),
             pltpu.VMEM((2, min(part, CHUNK), hidden_units), f32),
             pltpu.VMEM((2, min(part, CHUNK), hidden_units), f32),
             pltpu.SemaphoreType.DMA((2, 2)),
         ],
         cost_estimate=cost(2 * everyone * one // columns, 4 * one // columns),
-        compiler_params=params(16),
+        compiler_params=params(room),
         name="grad_in",
-    )(x, d_gate, d_up)
+    )(x_part, d_gate, d_up)
 
     route_grad, *blocks, done_sum = pl.pallas_call(
         functools.partial(reduce_kernel, sources),
         out_shape=[struct(ids_t.shape, f32)] + [struct((rows, 2 * part), bf16)] * columns + [dummy],
         in_specs=[VMEM] * (sources + 2),
         out_specs=[VMEM] * (columns + 2),
-        compiler_params=params(4),
+        compiler_params=params(room),
         name="reduce",
     )(*arrived, ids_t, done_in)
     blocks = [
@@ -424,9 +466,9 @@
     ]
 
     grad_down, done_out = pl.pallas_call(
-        functools.partial(grad_out_kernel, 2),
+        grad_out_kernel,
         out_shape=[struct((local_experts, hidden_units, part), f32), dummy],
-        in_specs=[VMEM] * 4,
+        in_specs=[VMEM] * 3,
         out_specs=[HBM, VMEM],
         scratch_shapes=[
             pltpu.VMEM((everyone, part), bf16),
@@ -434,16 +476,16 @@
             pltpu.SemaphoreType.DMA((2, 1)),
         ],
         cost_estimate=cost(everyone * one // columns, 2 * one // columns),
-        compiler_params=params(16),
+        compiler_params=params(room),
         name="grad_out",
-    )(*pieces, hidden, done_sum)
+    )(packets, hidden, done_sum)
 
     mixed, token_grad = pl.pallas_call(
         functools.partial(join_kernel, columns),
         out_shape=[struct((rows, width), bf16)] * 2,
         in_specs=[VMEM] * (columns + 1),
         out_specs=[VMEM] * 2,
-        compiler_params=params(4),
+        compiler_params=params(room),
         name="join",
     )(*blocks, done_out)
     return (mixed, token_grad, route_grad.T, grad_gate, grad_up, grad_down)

time: 66.5 us -> 73.9 us (1.11)
  Pallas kernels: 39.3 us -> 45.4 us
  starting transfers between devices: 15.8 us -> 19 us
  waiting for transfers between devices: 10.1 us -> 8.13 us
    pallas_call x6 -> x7, Pallas kernels: 31.5 us -> 37.7 us  [the longest x1 15.1 us: per_device(): pl.pallas_call(functools.partial(hidden_kernel, sources), out_shape=[unit...]
    ppermute x13 -> x16, starting transfers between devices: 15.8 us -> 19 us  [swap(): return lax.ppermute(value, axis, [(i, i ^ mask) for i in range(size)])]
    ppermute x13 -> x16, waiting for transfers between devices: 10.1 us -> 8.13 us  [swap(): return lax.ppermute(value, axis, [(i, i ^ mask) for i in range(size)])]
  transfers between devices with their start and end apart: 13 -> 16, of which waited for: 5 -> 6; matrix products, arithmetic and copies ran while one was open for 0% -> 0% of each run, Pallas kernels for 41% -> 33%
where the time goes in v8:
time: 73.9 us; the launch traced here: 73.7 us
  Pallas kernels  45.4 us (61%)
  starting transfers between devices  19 us (26%)
  waiting for transfers between devices  8.13 us (11%)
  between operations  0.88 us (1%)
    ppermute x16, starting transfers between devices, swap(): return lax.ppermute(value, axis, [(i, i ^ mask) for i in range(size)])  19 us
    pallas_call x1, Pallas kernels, per_device(): pl.pallas_call(functools.partial(hidden_kernel, sources), out_shape=[unit...  15.1 us
    pallas_call x2, Pallas kernels, gate_up(): pl.pallas_call(functools.partial(gate_up_kernel, first, last), out_shape=...  13.2 us
    ppermute x16, waiting for transfers between devices, swap(): return lax.ppermute(value, axis, [(i, i ^ mask) for i in range(size)])  8.13 us
    pallas_call x1, Pallas kernels, per_device(): pl.pallas_call(grad_in_kernel, out_shape=[struct((local_experts, part, hi...  6.25 us
    pallas_call x1, Pallas kernels, per_device(): pl.pallas_call(load_kernel, out_shape=[pltpu.VMEM(w_gate.shape, bf16), st...  4.63 us
    pallas_call x1, Pallas kernels, per_device(): pl.pallas_call(grad_out_kernel, out_shape=[struct((local_experts, hidden_...  3.62 us
  transfers between devices with their start and end apart: 16, of which 6 were waited for; matrix products, arithmetic and copies ran while one was open for 0% of the time, Pallas kernels for 33%

profile of v8, /device:TPU:0, one launch (start us, length us, event | category | flops | bytes accessed | tf_op | source)
XLA Modules:
  0.0 73.7 jit_solution(6854695685946663442)
XLA Ops:
  0.6 3.1 %collective-permute-start = (bf16[16,2048]{1,0:T(8,128)(2,1)}, bf16[16,2048]{1,0:T(8,128)(2,1)S(1)}, u32[]{:S(2)}, u32[]{:S(2)}) collective-permute-start(bf16[16,2048]{1,0:T(8,128)(2,1)} %tokens.1), channel_id=1, source_target_pairs={{0,1},{1,0},{2,3},{3,2},{4,5},{5,4},{6,7},{7,6},{8,9},{9,8},{10,11... | collective-permute-start | bytes 196616 | tf_op jit(solution)/shard_map/ppermute | solution.py:307
  3.7 2.5 %collective-permute-start.2 = (bf16[16,2048]{1,0:T(8,128)(2,1)}, bf16[16,2048]{1,0:T(8,128)(2,1)S(1)}, u32[]{:S(2)}, u32[]{:S(2)}) collective-permute-start(bf16[16,2048]{1,0:T(8,128)(2,1)} %tokens.1), channel_id=1, source_target_pairs={{0,3},{1,2},{2,1},{3,0},{4,7},{5,6},{6,5},{7,4},{8,11},{9,10},{10,... | collective-permute-start | bytes 196616 | tf_op jit(solution)/shard_map/ppermute | solution.py:307
  6.2 0.1 collective-permute-start.1
  6.3 4.6 %load_gate.1 = (bf16[4,2048,768]{2,1,0:T(8,128)(2,1)S(1)}, bf16[16,2048]{1,0:T(8,128)(2,1)S(1)}) custom-call(bf16[4,2048,768]{2,1,0:T(8,128)(2,1)} %refs_4_.1, bf16[16,2048]{1,0:T(8,128)(2,1)} %tokens.1), custom_call_target="tpu_custom_call" | custom-call | bytes 12582912 | tf_op jit(solution)/shard_map/load_gate/pallas_call | solution.py:350
  11.0 0.0 collective-permute-done
  11.0 1.9 %collective-permute-done.1 = bf16[16,2048]{1,0:T(8,128)(2,1)S(1)} collective-permute-done((bf16[16,2048]{1,0:T(8,128)(2,1)}, bf16[16,2048]{1,0:T(8,128)(2,1)S(1)}, u32[]{:S(2)}, u32[]{:S(2)}) %collective-permute-start.1) | collective-permute-done | bytes 65568 | tf_op jit(solution)/shard_map/ppermute | solution.py:307
  12.9 0.0 collective-permute-done.2
  12.9 1.6 %collective-permute-start.3 = (bf16[64,2048]{1,0:T(8,128)(2,1)S(1)}, bf16[64,2048]{1,0:T(8,128)(2,1)S(1)}, u32[]{:S(2)}, u32[]{:S(2)}) collective-permute-start(bf16[64,2048]{1,0:T(8,128)(2,1)S(1)} %constant_dynamic-update-slice_fusion.value), channel_id=1, source_target_pairs={{0,8},{4,12},{8,0},{12,4},{1,9},{5,13},{9,1},{13,5},{2,10},{6,14},... | collective-permute-start | bytes 786440 | tf_op jit(solution)/shard_map/ppermute | solution.py:307
  14.5 1.0 %route.1 = (bf16[16,2176]{1,0:T(8,128)(2,1)S(1)}, bf16[64,2048]{1,0:T(8,128)(2,1)S(1)}) custom-call(bf16[16,2048]{1,0:T(8,128)(2,1)} %cotangent.1, s32[8,16]{1,0:T(8,128)} %bitcast.3, bf16[8,16]{1,0:T(8,128)(2,1)} %bitcast.5, bf16[64,2048]{1,0:T(8,128)(2,1)S(1)} %constant_dynamic-update-slice_fusion.value), custom_call_target="tpu_custom_call" | custom-call | tf_op jit(solution)/shard_map/route/pallas_call | solution.py:364
  15.5 2.5 %collective-permute-start.7 = (bf16[16,2176]{1,0:T(8,128)(2,1)S(1)}, bf16[16,2176]{1,0:T(8,128)(2,1)S(1)}, u32[]{:S(2)}, u32[]{:S(2)}) collective-permute-start(bf16[16,2176]{1,0:T(8,128)(2,1)S(1)} %get-tuple-element.41), channel_id=1, source_target_pairs={{0,3},{1,2},{2,1},{3,0},{4,7},{5,6},{6,5},{7,4},{8,11},{9,10},{10,... | collective-permute-start | bytes 208904 | tf_op jit(solution)/shard_map/ppermute | solution.py:307
  17.9 0.0 collective-permute-start.6
  17.9 2.0 %collective-permute-start.5 = (bf16[16,2176]{1,0:T(8,128)(2,1)S(1)}, bf16[16,2176]{1,0:T(8,128)(2,1)S(1)}, u32[]{:S(2)}, u32[]{:S(2)}) collective-permute-start(bf16[16,2176]{1,0:T(8,128)(2,1)S(1)} %get-tuple-element.41), channel_id=1, source_target_pairs={{0,1},{1,0},{2,3},{3,2},{4,5},{5,4},{6,7},{7,6},{8,9},{9,8},{10,11... | collective-permute-start | bytes 208904 | tf_op jit(solution)/shard_map/ppermute | solution.py:307
  19.9 0.0 copy-start.1
  19.9 1.2 %collective-permute-done.3 = bf16[64,2048]{1,0:T(8,128)(2,1)S(1)} collective-permute-done((bf16[64,2048]{1,0:T(8,128)(2,1)S(1)}, bf16[64,2048]{1,0:T(8,128)(2,1)S(1)}, u32[]{:S(2)}, u32[]{:S(2)}) %collective-permute-start.3) | collective-permute-done | bytes 262176 | tf_op jit(solution)/shard_map/ppermute | solution.py:307
  21.2 0.1 collective-permute-start.4
  21.3 1.2 %collective-permute-done.7 = bf16[16,2176]{1,0:T(8,128)(2,1)S(1)} collective-permute-done((bf16[16,2176]{1,0:T(8,128)(2,1)S(1)}, bf16[16,2176]{1,0:T(8,128)(2,1)S(1)}, u32[]{:S(2)}, u32[]{:S(2)}) %collective-permute-start.7) | collective-permute-done | bytes 69664 | tf_op jit(solution)/shard_map/ppermute | solution.py:307
  22.5 1.6 %collective-permute-done.6 = bf16[16,2176]{1,0:T(8,128)(2,1)S(1)} collective-permute-done((bf16[16,2176]{1,0:T(8,128)(2,1)S(1)}, bf16[16,2176]{1,0:T(8,128)(2,1)S(1)}, u32[]{:S(2)}, u32[]{:S(2)}) %collective-permute-start.6) | collective-permute-done | bytes 69664 | tf_op jit(solution)/shard_map/ppermute | solution.py:307
  24.1 0.0 collective-permute-done.5
  24.1 0.0 collective-permute-done.4
  24.2 0.0 copy-done.1
  24.2 4.5 %gate_up.2 = (bf16[4,256,768]{2,1,0:T(8,128)(2,1)S(1)}, bf16[4,256,768]{2,1,0:T(8,128)(2,1)S(1)}, bf16[4,256,768]{2,1,0:T(8,128)(2,1)S(1)}, bf16[64,2176]{1,0:T(8,128)(2,1)S(1)}) custom-call(bf16[256,2048]{1,0:T(8,128)(2,1)S(1)} %constant_dynamic-update-slice_fusion.4.refs_0_.x, s32[4,6]{1,0:T(4,128)S(1)} %copy-done.1, ...), custom_call_target="tpu_custom_call" | custom-call | flops 1610612736 | bytes 6291456 | tf_op jit(solution)/shard_map/gate_up/pallas_call | solution.py:383
  28.7 0.6 collective-permute-start.8
  29.3 8.7 %gate_up.3 = (bf16[4,256,768]{2,1,0:T(8,128)(2,1)S(1)}, bf16[4,256,768]{2,1,0:T(8,128)(2,1)S(1)}, bf16[4,256,768]{2,1,0:T(8,128)(2,1)S(1)}, bf16[64,2176]{1,0:T(8,128)(2,1)S(1)}) custom-call(bf16[256,2048]{1,0:T(8,128)(2,1)S(1)} %constant_dynamic-update-slice_fusion.4.refs_0_.x, ...), custom_call_target="tpu_custom_call", output_to_operand_aliasing={{0}: (5, {}), {1}: (6, {}), {2}: (7, {})} | custom-call | flops 4831838208 | bytes 18874368 | tf_op jit(solution)/shard_map/gate_up/pallas_call | solution.py:383
  38.1 0.0 collective-permute-done.8
  38.1 0.1 constant_dynamic-update-slice_fusion.7
  38.1 0.1 collective-permute-start.9
  38.2 0.1 turn.1.x_part
  38.4 1.8 %collective-permute-done.9 = bf16[128,2176]{1,0:T(8,128)(2,1)S(1)} collective-permute-done((bf16[128,2176]{1,0:T(8,128)(2,1)S(1)}, bf16[128,2176]{1,0:T(8,128)(2,1)S(1)}, u32[]{:S(2)}, u32[]{:S(2)}) %collective-permute-start.9) | collective-permute-done | bytes 557088 | tf_op jit(solution)/shard_map/ppermute | solution.py:307
  40.2 0.1 constant_dynamic-update-slice_fusion.9.refs_0_.packet
  40.2 15.1 %hidden.1 = (bf16[4,256,768]{2,1,0:T(8,128)(2,1)S(1)}, bf16[4,256,768]{2,1,0:T(8,128)(2,1)S(1)}, bf16[4,256,768]{2,1,0:T(8,128)(2,1)S(1)}, bf16[64,1152]{1,0:T(8...) custom-call(bf16[256,2176]{1,0:T(8,128)(2,1)S(1)} %constant_dynamic-update-, ...), custom_call_target="tpu_custom_call" | custom-call | flops 6442450944 | bytes 25165824 | tf_op jit(solution)/shard_map/hidden/pallas_call | solution.py:417
  55.3 1.6 %collective-permute-start.10 = (bf16[64,1152]{1,0:T(8,128)(2,1)S(1)}, bf16[64,1152]{1,0:T(8,128)(2,1)S(1)}, u32[]{:S(2)}, u32[]{:S(2)}) collective-permute-start(bf16[64,1152]{1,0:T(8,128)(2,1)S(1)} %get-tuple-element.51), channel_id=1, source_target_pairs={{0,8},{4,12},{8,0},{12,4},{1,9},{5,13},{9,1},{13,5},{2,10},{6,14},... | collective-permute-start | bytes 442376 | tf_op jit(solution)/shard_map/ppermute | solution.py:307
  56.9 0.0 collective-permute-start.11
  56.9 0.6 collective-permute-start.12
  57.5 0.0 copy-start
  57.5 6.2 %grad_in.1 = (f32[4,512,768]{2,1,0:T(8,128)}, f32[4,512,768]{2,1,0:T(8,128)}, f32[8,128]{1,0:T(8,128)S(1)}) custom-call(bf16[512,256]{1,0:T(8,128)(2,1)S(1)} %turn.1.x_part, bf16[4,256,768]{2,1,0:T(8,128)(2,1)S(1)} %get-tuple-element.54.d_gate, bf16[4,256,768]{2,1,0:T(8,128)(2,1)S(1)} %get-tuple-element.55.d_up), custom_call_target="tpu_custom_call" | custom-call | flops 1610612736 | bytes 12582912 | tf_op jit(solution)/shard_map/grad_in/pallas_call | solution.py:441
  63.8 0.0 collective-permute-done.10.refs_1_
  63.8 0.0 collective-permute-done.11.refs_2_
  63.8 0.0 collective-permute-done.12.refs_3_
  63.8 0.0 copy-done
  63.8 0.8 %reduce.1 = (f32[8,16]{1,0:T(8,128)}, bf16[16,1024]{1,0:T(8,128)(2,1)S(1)}, bf16[16,1024]{1,0:T(8,128)(2,1)S(1)}, bf16[16,1024]{1,0:T(8,128)(2,1)S(1)}, bf16[16,...) custom-call(bf16[64,1152]{1,0:T(8,128)(2,1)S(1)} %get-tuple-element.50.refs_0_, ...), custom_call_target="tpu_custom_call" | custom-call | tf_op jit(solution)/shard_map/reduce/pallas_call | solution.py:456
  64.6 0.5 collective-permute-start.13
  65.1 2.3 %collective-permute-start.14 = (bf16[16,1024]{1,0:T(8,128)(2,1)S(1)}, bf16[16,1024]{1,0:T(8,128)(2,1)S(1)}, u32[]{:S(2)}, u32[]{:S(2)}) collective-permute-start(bf16[16,1024]{1,0:T(8,128)(2,1)S(1)} %get-tuple-element.59), channel_id=1, source_target_pairs={{0,2},{1,3},{2,0},{3,1},{4,6},{5,7},{6,4},{7,5},{8,10},{9,11},{10,... | collective-permute-start | bytes 98312 | tf_op jit(solution)/shard_map/ppermute | solution.py:307
  67.3 1.7 %collective-permute-start.15 = (bf16[16,1024]{1,0:T(8,128)(2,1)S(1)}, bf16[16,1024]{1,0:T(8,128)(2,1)S(1)}, u32[]{:S(2)}, u32[]{:S(2)}) collective-permute-start(bf16[16,1024]{1,0:T(8,128)(2,1)S(1)} %get-tuple-element.60), channel_id=1, source_target_pairs={{0,3},{1,2},{2,1},{3,0},{4,7},{5,6},{6,5},{7,4},{8,11},{9,10},{10,... | collective-permute-start | bytes 98312 | tf_op jit(solution)/shard_map/ppermute | solution.py:307
  69.0 3.6 %grad_out.1 = (f32[4,768,512]{2,1,0:T(8,128)}, f32[8,128]{1,0:T(8,128)S(1)}) custom-call(bf16[256,2176]{1,0:T(8,128)(2,1)S(1)} %constant_dynamic-update-slice_fusion.9.refs_0_.packet, bf16[4,256,768]{2,1,0:T(8,128)(2,1)S(1)} %get-tuple-element.61.hidden, f32[8,128]{1,0:T(8,128)S(1)} %get-tuple-element.62.after), custom_call_target="tpu_custom_call" | custom-call | flops 805306368 | bytes 6291456 | tf_op jit(solution)/shard_map/grad_out/pallas_call | solution.py:468
  72.6 0.0 collective-permute-done.13.refs_1_
  72.6 0.0 collective-permute-done.14.refs_2_
  72.6 0.4 collective-permute-done.15.refs_3_
  73.1 0.7 join.1
  (10 shorter events, 0.2 us)
Async XLA Ops:
  0.6 10.3 %collective-permute-start = (bf16[16,2048]{1,0:T(8,128)(2,1)}, bf16[16,2048]{1,0:T(8,128)(2,1)S(1)}, u32[]{:S(2)}, u32[]{:S(2)}) collective-permute-start(bf16[16,2048]{1,0:T(8,128)(2,1)} %tokens.1), channel_id=1, source_target_pairs={{0,1},{1,0},{2,3},{3,2},{4,5},{5,4},{6,7},{7,6},{8,9},{9,8},{10,11... | collective-permute-start | bytes 196616 | tf_op jit(solution)/shard_map/ppermute | solution.py:307
  3.7 9.2 %collective-permute-start.2 = (bf16[16,2048]{1,0:T(8,128)(2,1)}, bf16[16,2048]{1,0:T(8,128)(2,1)S(1)}, u32[]{:S(2)}, u32[]{:S(2)}) collective-permute-start(bf16[16,2048]{1,0:T(8,128)(2,1)} %tokens.1), channel_id=1, source_target_pairs={{0,3},{1,2},{2,1},{3,0},{4,7},{5,6},{6,5},{7,4},{8,11},{9,10},{10,... | collective-permute-start | bytes 196616 | tf_op jit(solution)/shard_map/ppermute | solution.py:307
  6.2 6.7 %collective-permute-start.1 = (bf16[16,2048]{1,0:T(8,128)(2,1)}, bf16[16,2048]{1,0:T(8,128)(2,1)S(1)}, u32[]{:S(2)}, u32[]{:S(2)}) collective-permute-start(bf16[16,2048]{1,0:T(8,128)(2,1)} %tokens.1), channel_id=1, source_target_pairs={{0,2},{1,3},{2,0},{3,1},{4,6},{5,7},{6,4},{7,5},{8,10},{9,11},{10,... | collective-permute-start | bytes 196616 | tf_op jit(solution)/shard_map/ppermute | solution.py:307
  12.9 8.2 %collective-permute-start.3 = (bf16[64,2048]{1,0:T(8,128)(2,1)S(1)}, bf16[64,2048]{1,0:T(8,128)(2,1)S(1)}, u32[]{:S(2)}, u32[]{:S(2)}) collective-permute-start(bf16[64,2048]{1,0:T(8,128)(2,1)S(1)} %constant_dynamic-update-slice_fusion.value), channel_id=1, source_target_pairs={{0,8},{4,12},{8,0},{12,4},{1,9},{5,13},{9,1},{13,5},{2,10},{6,14},... | collective-permute-start | bytes 786440 | tf_op jit(solution)/shard_map/ppermute | solution.py:307
  15.5 7.0 %collective-permute-start.7 = (bf16[16,2176]{1,0:T(8,128)(2,1)S(1)}, bf16[16,2176]{1,0:T(8,128)(2,1)S(1)}, u32[]{:S(2)}, u32[]{:S(2)}) collective-permute-start(bf16[16,2176]{1,0:T(8,128)(2,1)S(1)} %get-tuple-element.41), channel_id=1, source_target_pairs={{0,3},{1,2},{2,1},{3,0},{4,7},{5,6},{6,5},{7,4},{8,11},{9,10},{10,... | collective-permute-start | bytes 208904 | tf_op jit(solution)/shard_map/ppermute | solution.py:307
  17.9 6.2 %collective-permute-start.6 = (bf16[16,2176]{1,0:T(8,128)(2,1)S(1)}, bf16[16,2176]{1,0:T(8,128)(2,1)S(1)}, u32[]{:S(2)}, u32[]{:S(2)}) collective-permute-start(bf16[16,2176]{1,0:T(8,128)(2,1)S(1)} %get-tuple-element.41), channel_id=1, source_target_pairs={{0,2},{1,3},{2,0},{3,1},{4,6},{5,7},{6,4},{7,5},{8,10},{9,11},{10,... | collective-permute-start | bytes 208904 | tf_op jit(solution)/shard_map/ppermute | solution.py:307
  17.9 6.2 %collective-permute-start.5 = (bf16[16,2176]{1,0:T(8,128)(2,1)S(1)}, bf16[16,2176]{1,0:T(8,128)(2,1)S(1)}, u32[]{:S(2)}, u32[]{:S(2)}) collective-permute-start(bf16[16,2176]{1,0:T(8,128)(2,1)S(1)} %get-tuple-element.41), channel_id=1, source_target_pairs={{0,1},{1,0},{2,3},{3,2},{4,5},{5,4},{6,7},{7,6},{8,9},{9,8},{10,11... | collective-permute-start | bytes 208904 | tf_op jit(solution)/shard_map/ppermute | solution.py:307
  19.9 4.3 %copy-start.1 = (s32[4,6]{1,0:T(4,128)S(1)}, s32[4,6]{1,0:T(4,128)}, u32[]{:S(2)}) copy-start(s32[4,6]{1,0:T(4,128)} %refs_1_.3) | copy-start | bytes 292
  21.2 2.9 %collective-permute-start.4 = (bf16[128,2048]{1,0:T(8,128)(2,1)S(1)}, bf16[128,2048]{1,0:T(8,128)(2,1)S(1)}, u32[]{:S(2)}, u32[]{:S(2)}) collective-permute-start(bf16[128,2048]{1,0:T(8,128)(2,1)S(1)} %pad_maximum_fusion), channel_id=1, source_target_pairs={{0,4},{4,0},{8,12},{12,8},{1,5},{5,1},{9,13},{13,9},{2,6},{6,2},{1... | collective-permute-start | bytes 1572872 | tf_op jit(solution)/shard_map/ppermute | solution.py:307
  28.7 9.3 %collective-permute-start.8 = (bf16[64,2176]{1,0:T(8,128)(2,1)S(1)}, bf16[64,2176]{1,0:T(8,128)(2,1)S(1)}, u32[]{:S(2)}, u32[]{:S(2)}) collective-permute-start(bf16[64,2176]{1,0:T(8,128)(2,1)S(1)} %get-tuple-element.42.refs_4_), channel_id=1, source_target_pairs={{0,8},{4,12},{8,0},{12,4},{1,9},{5,13},{9,1},{13,5},{2,10},{6,14},... | collective-permute-start | bytes 835592 | tf_op jit(solution)/shard_map/ppermute | solution.py:307
  38.1 2.0 %collective-permute-start.9 = (bf16[128,2176]{1,0:T(8,128)(2,1)S(1)}, bf16[128,2176]{1,0:T(8,128)(2,1)S(1)}, u32[]{:S(2)}, u32[]{:S(2)}) collective-permute-start(bf16[128,2176]{1,0:T(8,128)(2,1)S(1)} %get-tuple-element.70.after), channel_id=1, source_target_pairs={{0,4},{4,0},{8,12},{12,8},{1,5},{5,1},{9,13},{13,9},{2,6},{6,2},{1... | collective-permute-start | bytes 1671176 | tf_op jit(solution)/shard_map/ppermute | solution.py:307
  55.3 8.5 %collective-permute-start.10 = (bf16[64,1152]{1,0:T(8,128)(2,1)S(1)}, bf16[64,1152]{1,0:T(8,128)(2,1)S(1)}, u32[]{:S(2)}, u32[]{:S(2)}) collective-permute-start(bf16[64,1152]{1,0:T(8,128)(2,1)S(1)} %get-tuple-element.51), channel_id=1, source_target_pairs={{0,8},{4,12},{8,0},{12,4},{1,9},{5,13},{9,1},{13,5},{2,10},{6,14},... | collective-permute-start | bytes 442376 | tf_op jit(solution)/shard_map/ppermute | solution.py:307
  56.9 6.9 %collective-permute-start.11 = (bf16[64,1152]{1,0:T(8,128)(2,1)S(1)}, bf16[64,1152]{1,0:T(8,128)(2,1)S(1)}, u32[]{:S(2)}, u32[]{:S(2)}) collective-permute-start(bf16[64,1152]{1,0:T(8,128)(2,1)S(1)} %get-tuple-element.52), channel_id=1, source_target_pairs={{0,4},{4,0},{8,12},{12,8},{1,5},{5,1},{9,13},{13,9},{2,6},{6,2},{1... | collective-permute-start | bytes 442376 | tf_op jit(solution)/shard_map/ppermute | solution.py:307
  56.9 6.9 %collective-permute-start.12 = (bf16[64,1152]{1,0:T(8,128)(2,1)S(1)}, bf16[64,1152]{1,0:T(8,128)(2,1)S(1)}, u32[]{:S(2)}, u32[]{:S(2)}) collective-permute-start(bf16[64,1152]{1,0:T(8,128)(2,1)S(1)} %get-tuple-element.53), channel_id=1, source_target_pairs={{0,12},{4,8},{8,4},{12,0},{1,13},{5,9},{9,5},{13,1},{2,14},{6,10},... | collective-permute-start | bytes 442376 | tf_op jit(solution)/shard_map/ppermute | solution.py:307
  57.5 6.3 %copy-start = (s32[16,8]{0,1:T(8,128)S(1)}, s32[16,8]{0,1:T(8,128)}, u32[]{:S(2)}) copy-start(s32[16,8]{0,1:T(8,128)} %param.10) | copy-start | bytes 1540
  64.6 8.0 %collective-permute-start.13 = (bf16[16,1024]{1,0:T(8,128)(2,1)S(1)}, bf16[16,1024]{1,0:T(8,128)(2,1)S(1)}, u32[]{:S(2)}, u32[]{:S(2)}) collective-permute-start(bf16[16,1024]{1,0:T(8,128)(2,1)S(1)} %get-tuple-element.58), channel_id=1, source_target_pairs={{0,1},{1,0},{2,3},{3,2},{4,5},{5,4},{6,7},{7,6},{8,9},{9,8},{10,11... | collective-permute-start | bytes 98312 | tf_op jit(solution)/shard_map/ppermute | solution.py:307
  65.1 7.6 %collective-permute-start.14 = (bf16[16,1024]{1,0:T(8,128)(2,1)S(1)}, bf16[16,1024]{1,0:T(8,128)(2,1)S(1)}, u32[]{:S(2)}, u32[]{:S(2)}) collective-permute-start(bf16[16,1024]{1,0:T(8,128)(2,1)S(1)} %get-tuple-element.59), channel_id=1, source_target_pairs={{0,2},{1,3},{2,0},{3,1},{4,6},{5,7},{6,4},{7,5},{8,10},{9,11},{10,... | collective-permute-start | bytes 98312 | tf_op jit(solution)/shard_map/ppermute | solution.py:307
  67.3 5.7 %collective-permute-start.15 = (bf16[16,1024]{1,0:T(8,128)(2,1)S(1)}, bf16[16,1024]{1,0:T(8,128)(2,1)S(1)}, u32[]{:S(2)}, u32[]{:S(2)}) collective-permute-start(bf16[16,1024]{1,0:T(8,128)(2,1)S(1)} %get-tuple-element.60), channel_id=1, source_target_pairs={{0,3},{1,2},{2,1},{3,0},{4,7},{5,6},{6,5},{7,4},{8,11},{9,10},{10,... | collective-permute-start | bytes 98312 | tf_op jit(solution)/shard_map/ppermute | solution.py:307

commit v9 on v8

--- a/solution.py
+++ b/solution.py
@@ -33,17 +33,19 @@
     return pl.ds(pl.multiple_of(index * size, size), size)
 
 
-def route_kernel(cotangent, expert_ids, route_weights, value, packet, same, ids, values, sems):
-    rows, width = cotangent.shape
+def route_kernel(
+    tokens, cotangent, expert_ids, route_weights, own_tokens, packet, ids, values, sems
+):
+    rows, width = tokens.shape
     lanes = packet.shape[1] - width
     copies = [
         pltpu.make_async_copy(expert_ids, ids, sems.at[0]),
         pltpu.make_async_copy(route_weights, values, sems.at[1]),
-        pltpu.make_async_copy(cotangent, packet.at[:, :width], sems.at[2]),
+        pltpu.make_async_copy(tokens, own_tokens, sems.at[2]),
+        pltpu.make_async_copy(cotangent, packet.at[:, :width], sems.at[3]),
     ]
     for copy in copies:
         copy.start()
-    same[...] = value[...]
     for copy in copies:
         copy.wait()
     at = ids_along((lanes, rows), 0)
@@ -54,15 +56,11 @@
     packet[:, width:] = dense.T.astype(packet.dtype)
 
 
-def load_kernel(weight, tokens, target, own_tokens, sems):
-    copies = [
-        pltpu.make_async_copy(tokens, own_tokens, sems.at[0]),
-        pltpu.make_async_copy(weight, target, sems.at[1]),
-    ]
-    for copy in copies:
-        copy.start()
-    for copy in copies:
-        copy.wait()
+def load_kernel(source, value, target, same, sem):
+    copy = pltpu.make_async_copy(source, target, sem)
+    copy.start()
+    same[...] = value[...]
+    copy.wait()
 
 
 def turn_kernel(x, after, x_part):
@@ -81,91 +79,84 @@
         lax.fori_loop(0, tokens // TILE, turn, 0)
 
 
-def gate_up_kernel(first, last, *refs):
-    x, masks, gate, w_up, value = refs[:5]
-    hidden, slope_up, slope_gate, same, up_buf, sems = refs[-6:]
-    hidden_units = gate.shape[2]
+def gate_kernel(x, gate, w_up, gate_pre, gate_part, up, sems):
+    local_experts, _, hidden_units = gate.shape
+    mine = aligned(lax.axis_index("dp"), gate_part.shape[1])
+    loads = [
+        pltpu.make_async_copy(w_up, up, sems.at[0]),
+        pltpu.make_async_copy(gate.at[:, mine, :], gate_part, sems.at[1]),
+    ]
+    for load in loads:
+        load.start()
+
+    def tile(rows):
+        for expert in range(local_experts):
+            for start in range(0, hidden_units, CHUNK):
+                cols = slice(start, start + CHUNK)
+                gate_pre[expert, rows, cols] = dot(x[rows, :], gate[expert, :, cols], NN)
+
+    over_tiles(x.shape[0], tile)
+    for load in loads:
+        load.wait()
+
+
+def up_kernel(first, last, *refs):
+    x, masks, gate_pre, up, w_down, value = refs[:6]
+    hidden, slope_up, slope_gate, down, up_part, same, sems = refs[-7:]
+    hidden_units = up.shape[2]
     bf16 = jnp.bfloat16
+    mine = aligned(lax.axis_index("dp"), up_part.shape[1])
     loads = [
-        pltpu.make_async_copy(w_up.at[e], up_buf.at[(e - first) % 2], sems.at[(e - first) % 2])
-        for e in range(first, last)
+        pltpu.make_async_copy(w_down.at[first:last], down, sems.at[0]),
+        pltpu.make_async_copy(up.at[first:last, mine, :], up_part, sems.at[1]),
     ]
-    for load in loads[:2]:
+    for load in loads:
         load.start()
     same[...] = value[...]
 
-    for expert in range(first, last):
-        up = up_buf.at[(expert - first) % 2]
-        loads[expert - first].wait()
-
-        def tile(rows, expert=expert, up=up):
+    def tile(rows):
+        for expert in range(first, last):
             for start in range(0, hidden_units, CHUNK):
                 cols = slice(start, start + CHUNK)
-                gate_pre = dot(x[rows, :], gate[expert, :, cols], NN)
-                up_proj = dot(x[rows, :], up[:, cols], NN)
+                up_proj = dot(x[rows, :], up[expert, :, cols], NN)
                 at = ids_along((1, CHUNK), 1)
                 keep = jnp.zeros((1, CHUNK), jnp.float32)
                 for j in range(CHUNK // BLK):
                     kept = masks[expert, start // BLK + j].astype(jnp.float32)
                     keep = jnp.where(at // BLK == j, kept, keep)
-                sigma = 0.5 + 0.5 * jnp.tanh(0.5 * gate_pre)
-                silu = gate_pre * sigma
+                gated = gate_pre[expert, rows, cols]
+                sigma = 0.5 + 0.5 * jnp.tanh(0.5 * gated)
+                silu = gated * sigma
                 up_kept = up_proj * keep
                 hidden[expert, rows, cols] = (silu * up_kept).astype(bf16)
                 slope_up[expert, rows, cols] = (silu * keep).astype(bf16)
                 slope = up_kept * (sigma + silu * (1.0 - sigma))
                 slope_gate[expert, rows, cols] = slope.astype(bf16)
 
-        over_tiles(x.shape[0], tile)
-        if expert + 2 < last:
-            loads[expert + 2 - first].start()
-
-
-def hidden_kernel(count, *refs):
-    packet, units, slope_up, slope_gate, w_gate, w_up, w_down, hidden, d_gate, d_up = refs[:10]
-    outs, refs = refs[10 : 10 + count], refs[10 + count :]
-    inner, mixed, token_grad, down_buf, gate_buf, up_buf, sems = refs
-    local_experts, hidden_units, width = w_down.shape
+    over_tiles(x.shape[0], tile)
+    for load in loads:
+        load.wait()
+
+
+def hidden_kernel(halves, count, *refs):
+    packet, units, slope_up, slope_gate, gate = refs[:5]
+    ups, refs = refs[5 : 5 + len(halves)], refs[5 + len(halves) :]
+    downs, refs = refs[: len(halves)], refs[len(halves) :]
+    hidden, d_gate, d_up = refs[:3]
+    outs, (inner, mixed, token_grad) = refs[3 : 3 + count], refs[3 + count :]
+    hidden_units, width = downs[0].shape[1:]
     tokens, part = mixed.shape
+    local_experts = gate.shape[0]
     lanes = packet.shape[1] - width
     half = lanes // 2
     base = lax.axis_index("expert") * local_experts
     mine = aligned(lax.axis_index("dp"), part)
     bf16, f32 = jnp.bfloat16, jnp.float32
-
-    def copies(expert):
-        slot = lax.rem(expert, 2)
-        return [
-            pltpu.make_async_copy(
-                w_down.at[expert, slice(i * CHUNK, (i + 1) * CHUNK), :],
-                down_buf.at[slot, slice(i * CHUNK, (i + 1) * CHUNK), :],
-                sems.at[slot, 2 + i],
-            )
-            for i in range(hidden_units // CHUNK)
-        ] + [
-            pltpu.make_async_copy(w_gate.at[expert, mine, :], gate_buf.at[slot], sems.at[slot, 0]),
-            pltpu.make_async_copy(w_up.at[expert, mine, :], up_buf.at[slot], sems.at[slot, 1]),
-        ]
-
-    for copy in copies(0):
-        copy.start()
     inner[...] = jnp.zeros(inner.shape, inner.dtype)
     mixed[...] = jnp.zeros(mixed.shape, mixed.dtype)
     token_grad[...] = jnp.zeros(token_grad.shape, token_grad.dtype)
 
-    def one_expert(expert, carry):
-        @pl.when(expert + 1 < local_experts)
-        def _():
-            for copy in copies(expert + 1):
-                copy.start()
-
-        slot = lax.rem(expert, 2)
-        down, gate, up = down_buf.at[slot], gate_buf.at[slot], up_buf.at[slot]
-        arriving = copies(expert)
-        if tokens != TILE:
-            for copy in arriving:
-                copy.wait()
-
+    def one_expert(up, down, first, expert, carry):
         def tile(rows):
             dense = packet[rows, width:].astype(f32)
             at = ids_along((TILE, lanes), 1)
@@ -174,9 +165,7 @@
             total = jnp.zeros((TILE, 1), f32)
             for start in range(0, hidden_units, CHUNK):
                 cols = slice(start, start + CHUNK)
-                if tokens == TILE:
-                    arriving[start // CHUNK].wait()
-                back = dot(packet[rows, :width], down[cols, :], NT)
+                back = dot(packet[rows, :width], down[expert - first, cols, :], NT)
                 part_units = units[expert, rows, cols].astype(f32)
                 total += jnp.sum(part_units * back, axis=1, keepdims=True)
                 back = back * weights
@@ -189,18 +178,16 @@
             inner[rows, :] += jnp.where(
                 hit, high, jnp.where(at == base + expert + half, total - high, 0.0)
             )
-            if tokens == TILE:
-                for copy in arriving[-2:]:
-                    copy.wait()
-            mixed[rows, :] += dot(hidden[expert, rows, :], down[:, mine], NN)
-            token_grad[rows, :] += dot(d_gate[expert, rows, :], gate[...], NT) + dot(
-                d_up[expert, rows, :], up[...], NT
+            mixed[rows, :] += dot(hidden[expert, rows, :], down[expert - first, :, mine], NN)
+            token_grad[rows, :] += dot(d_gate[expert, rows, :], gate[expert], NT) + dot(
+                d_up[expert, rows, :], up[expert - first], NT
             )
 
         over_tiles(tokens, tile)
         return carry
 
-    lax.fori_loop(0, local_experts, one_expert, 0)
+    for (first, last), up, down in zip(halves, ups, downs):
+        lax.fori_loop(first, last, functools.partial(one_expert, up, down, first), 0)
     rows = outs[0].shape[0]
     for i, out in enumerate(outs):
         block = slice(i * rows, (i + 1) * rows)
@@ -341,68 +328,95 @@
     bf16, f32 = jnp.bfloat16, jnp.float32
     struct = jax.ShapeDtypeStruct
     one = 2 * local_experts * width * hidden_units
-    room = 16 + (everyone - TILE) * (2 * part + lanes) * 14 // MIB
+    room = 8 + (everyone - TILE) * (2 * part + lanes) * 10 // MIB
     dummy = struct((8, LANES), f32)
     ids_t = expert_ids.T
     w_gate, w_up, w_down = [in_hbm(w) for w in (w_gate, w_up, w_down)]
 
-    tokens_near = exchange(tokens, "dp", range(1, columns))
-    gate, own_tokens = pl.pallas_call(
-        load_kernel,
-        out_shape=[pltpu.VMEM(w_gate.shape, bf16), struct(tokens.shape, bf16)],
-        in_specs=[HBM] * 2,
-        out_specs=[VMEM] * 2,
-        scratch_shapes=[pltpu.SemaphoreType.DMA((2,))],
-        cost_estimate=cost(0, one),
-        compiler_params=params(room),
-        name="load_gate",
-    )(w_gate, in_hbm(tokens))
-    gate = in_vmem(gate)
-    x_column = jnp.concatenate([own_tokens] + tokens_near)
-    x_across = exchange(x_column, "expert", chips)
-
-    packet, x_column = pl.pallas_call(
+    own_tokens, packet = pl.pallas_call(
         route_kernel,
-        out_shape=[struct((rows, width + lanes), bf16), struct(x_column.shape, bf16)],
-        in_specs=[HBM] * 3 + [VMEM],
+        out_shape=[struct(tokens.shape, bf16), struct((rows, width + lanes), bf16)],
+        in_specs=[HBM] * 4,
         out_specs=[VMEM] * 2,
         scratch_shapes=[
             pltpu.VMEM(ids_t.shape, jnp.int32),
             pltpu.VMEM(ids_t.shape, bf16),
-            pltpu.SemaphoreType.DMA((3,)),
+            pltpu.SemaphoreType.DMA((4,)),
         ],
         compiler_params=params(room),
         name="route",
-    )(*[in_hbm(a) for a in (cotangent, ids_t, route_weights.T)], x_column)
+    )(*[in_hbm(a) for a in (tokens, cotangent, ids_t, route_weights.T)])
+
+    def load(weight, value, name):
+        return pl.pallas_call(
+            load_kernel,
+            out_shape=[
+                pltpu.VMEM(weight.shape, weight.dtype),
+                struct(value.shape, value.dtype),
+            ],
+            in_specs=[HBM, VMEM],
+            out_specs=[VMEM] * 2,
+            scratch_shapes=[pltpu.SemaphoreType.DMA],
+            cost_estimate=cost(0, one),
+            compiler_params=params(room),
+            name=name,
+        )(weight, value)
+
+    x_column = jnp.concatenate([own_tokens] + exchange(tokens, "dp", range(1, columns)))
     c_column = jnp.concatenate([packet] + exchange(packet, "dp", range(1, columns)))
+    x_across = exchange(x_column, "expert", chips)
+    c_across = exchange(c_column, "expert", chips)
+    gate, x_column = load(w_gate, x_column, "load_gate")
+    gate = in_vmem(gate)
     x = jnp.concatenate([x_column] + x_across)
     x = jnp.concatenate([x, swap(x, "expert", 1)])
 
+    gate_pre, gate_part, up = pl.pallas_call(
+        gate_kernel,
+        out_shape=[
+            struct((local_experts, everyone, hidden_units), f32),
+            pltpu.VMEM((local_experts, part, hidden_units), bf16),
+            pltpu.VMEM(w_up.shape, bf16),
+        ],
+        in_specs=[VMEM] * 2 + [HBM],
+        out_specs=[VMEM] * 3,
+        scratch_shapes=[pltpu.SemaphoreType.DMA((2,))],
+        cost_estimate=cost(everyone * one, one),
+        compiler_params=params(room),
+        name="gate",
+    )(x, gate, w_up)
+    up = in_vmem(up)
+
     units = struct((local_experts, everyone, hidden_units), bf16)
-    def gate_up(first, last, value, known):
+
+    def up_call(first, last, value, known):
         return pl.pallas_call(
-            functools.partial(gate_up_kernel, first, last),
+            functools.partial(up_kernel, first, last),
             out_shape=[units] * 3
+            + [pltpu.VMEM((last - first,) + w_down.shape[1:], bf16)]
+            + [pltpu.VMEM((last - first, part, hidden_units), bf16)]
             + [struct(value.shape, value.dtype)],
-            in_specs=[VMEM, SMEM, VMEM, HBM] + [VMEM] * (1 + len(known)),
-            out_specs=[VMEM] * 4,
-            scratch_shapes=[
-                pltpu.VMEM((min(2, last - first), width, hidden_units), bf16),
-                pltpu.SemaphoreType.DMA((2,)),
-            ],
-            input_output_aliases={5 + i: i for i in range(len(known))},
+            in_specs=[VMEM, SMEM, VMEM, VMEM, HBM] + [VMEM] * (1 + len(known)),
+            out_specs=[VMEM] * 6,
+            scratch_shapes=[pltpu.SemaphoreType.DMA((2,))],
+            input_output_aliases={6 + i: i for i in range(len(known))},
             cost_estimate=cost(
-                2 * everyone * one * (last - first) // local_experts,
-                2 * one * (last - first) // local_experts,
+                everyone * one * (last - first) // local_experts,
+                one * (last - first) // local_experts,
             ),
             compiler_params=params(room),
-            name="gate_up",
-        )(x, block_masks, gate, w_up, value, *known)
-
-    *factors, c_column = gate_up(0, 1, c_column, [])
-    c_across = exchange(c_column, "expert", chips)
-    if local_experts > 1:
-        *factors, c_column = gate_up(1, local_experts, c_column, factors)
+            name="up",
+        )(x, block_masks, gate_pre, up, w_down, value, *known)
+
+    middle = local_experts // 2
+    halves = [(0, middle), (middle, local_experts)] if middle else [(0, local_experts)]
+    factors, downs, ups = [], [], []
+    for first, last in halves:
+        *factors, down, up_part, same = up_call(first, last, c_column, factors)
+        downs.append(in_vmem(down))
+        ups.append(in_vmem(up_part))
+        if first == 0:
+            c_column = same
     c_half = jnp.concatenate([c_column] + c_across)
     packets = jnp.concatenate([c_half, swap(c_half, "expert", 1)])
     x_part = pl.pallas_call(
@@ -415,24 +429,20 @@
     )(x, c_half)
 
     hidden, d_gate, d_up, *partials = pl.pallas_call(
-        functools.partial(hidden_kernel, sources),
+        functools.partial(hidden_kernel, halves, sources),
         out_shape=[units] * 3
         + [struct((columns * rows, 2 * part + lanes), bf16)] * sources,
-        in_specs=[VMEM] * 4 + [HBM] * 3,
+        in_specs=[VMEM] * (5 + 2 * len(halves)),
         out_specs=[VMEM] * (3 + sources),
         scratch_shapes=[
             pltpu.VMEM((everyone, lanes), f32),
             pltpu.VMEM((everyone, part), f32),
             pltpu.VMEM((everyone, part), f32),
-            pltpu.VMEM((min(2, local_experts), hidden_units, width), bf16),
-            pltpu.VMEM((min(2, local_experts), part, hidden_units), bf16),
-            pltpu.VMEM((min(2, local_experts), part, hidden_units), bf16),
-            pltpu.SemaphoreType.DMA((2, 2 + hidden_units // CHUNK)),
         ],
         cost_estimate=cost(2 * everyone * one, 2 * one),
         compiler_params=params(room),
         name="hidden",
-    )(packets, *factors, w_gate, w_up, w_down)
+    )(packets, *factors, in_vmem(gate_part), *ups, *downs)
     arrived = [
         swap(partial, "expert", other) if other else partial
         for other, partial in zip(expert_order, partials)

time: 73.9 us -> 64.7 us (0.88)
  Pallas kernels: 45.4 us -> 36.4 us
  waiting for transfers between devices: 8.13 us -> 6.57 us
  starting transfers between devices: 19 us -> 20.2 us
    pallas_call x5 -> x6, Pallas kernels: 34 us -> 25 us  [the longest x2 7.45 us: up_call(): pl.pallas_call(functools.partial(up_kernel, first, last), out_shape=[unit...]
    ppermute x16, waiting for transfers between devices: 8.13 us -> 6.57 us  [swap(): return lax.ppermute(value, axis, [(i, i ^ mask) for i in range(size)])]
    ppermute x16, starting transfers between devices: 19 us -> 20.2 us  [swap(): return lax.ppermute(value, axis, [(i, i ^ mask) for i in range(size)])]
  transfers between devices with their start and end apart: 16 -> 16, of which waited for: 6 -> 4; matrix products, arithmetic and copies ran while one was open for 0% -> 0% of each run, Pallas kernels for 33% -> 43%
where the time goes in v9:
time: 64.7 us; the launch traced here: 64.4 us
  Pallas kernels  36.4 us (56%)
  starting transfers between devices  20.2 us (31%)
  waiting for transfers between devices  6.57 us (10%)
  between operations  0.89 us (1%)
    ppermute x16, starting transfers between devices, swap(): return lax.ppermute(value, axis, [(i, i ^ mask) for i in range(size)])  20.2 us
    pallas_call x2, Pallas kernels, up_call(): pl.pallas_call(functools.partial(up_kernel, first, last), out_shape=[unit...  7.45 us
    pallas_call x1, Pallas kernels, per_device(): pl.pallas_call(functools.partial(hidden_kernel, halves, sources), out_sha...  7.29 us
    ppermute x16, waiting for transfers between devices, swap(): return lax.ppermute(value, axis, [(i, i ^ mask) for i in range(size)])  6.57 us
    pallas_call x1, Pallas kernels, per_device(): pl.pallas_call(grad_in_kernel, out_shape=[struct((local_experts, part, hi...  6.25 us
    pallas_call x1, Pallas kernels, per_device(): pl.pallas_call(gate_kernel, out_shape=[struct((local_experts, everyone, h...  4.6 us
    pallas_call x1, Pallas kernels, load(): pl.pallas_call(load_kernel, out_shape=[pltpu.VMEM(weight.shape, weight.dt...  4.58 us
    pallas_call x1, Pallas kernels, per_device(): pl.pallas_call(grad_out_kernel, out_shape=[struct((local_experts, hidden_...  3.62 us
  transfers between devices with their start and end apart: 16, of which 4 were waited for; matrix products, arithmetic and copies ran while one was open for 0% of the time, Pallas kernels for 43%

profile of v9, /device:TPU:0, one launch (start us, length us, event | category | flops | bytes accessed | tf_op | source)
XLA Modules:
  0.0 64.4 jit_solution(6860075112740653840)
XLA Ops:
  0.6 3.1 %collective-permute-start = (bf16[16,2048]{1,0:T(8,128)(2,1)}, bf16[16,2048]{1,0:T(8,128)(2,1)S(1)}, u32[]{:S(2)}, u32[]{:S(2)}) collective-permute-start(bf16[16,2048]{1,0:T(8,128)(2,1)} %tokens.1), channel_id=1, source_target_pairs={{0,1},{1,0},{2,3},{3,2},{4,5},{5,4},{6,7},{7,6},{8,9},{9,8},{10,11... | collective-permute-start | bytes 196616 | tf_op jit(solution)/shard_map/ppermute | solution.py:294
  3.7 2.5 %collective-permute-start.2 = (bf16[16,2048]{1,0:T(8,128)(2,1)}, bf16[16,2048]{1,0:T(8,128)(2,1)S(1)}, u32[]{:S(2)}, u32[]{:S(2)}) collective-permute-start(bf16[16,2048]{1,0:T(8,128)(2,1)} %tokens.1), channel_id=1, source_target_pairs={{0,3},{1,2},{2,1},{3,0},{4,7},{5,6},{6,5},{7,4},{8,11},{9,10},{10,... | collective-permute-start | bytes 196616 | tf_op jit(solution)/shard_map/ppermute | solution.py:294
  6.2 0.1 collective-permute-start.1
  6.3 1.0 %route.1 = (bf16[16,2048]{1,0:T(8,128)(2,1)S(1)}, bf16[16,2176]{1,0:T(8,128)(2,1)S(1)}) custom-call(bf16[16,2048]{1,0:T(8,128)(2,1)} %tokens.1, bf16[16,2048]{1,0:T(8,128)(2,1)} %cotangent.1, s32[8,16]{1,0:T(8,128)} %bitcast.3, bf16[8,16]{1,0:T(8,128)(2,1)} %bitcast.5), custom_call_target="tpu_custom_call" | custom-call | tf_op jit(solution)/shard_map/route/pallas_call | solution.py:336
  7.4 3.0 %collective-permute-start.7 = (bf16[16,2176]{1,0:T(8,128)(2,1)S(1)}, bf16[16,2176]{1,0:T(8,128)(2,1)S(1)}, u32[]{:S(2)}, u32[]{:S(2)}) collective-permute-start(bf16[16,2176]{1,0:T(8,128)(2,1)S(1)} %get-tuple-element.49), channel_id=1, source_target_pairs={{0,3},{1,2},{2,1},{3,0},{4,7},{5,6},{6,5},{7,4},{8,11},{9,10},{10,... | collective-permute-start | bytes 208904 | tf_op jit(solution)/shard_map/ppermute | solution.py:294
  10.3 0.3 collective-permute-start.6
  10.7 0.0 collective-permute-done
  10.7 1.2 %collective-permute-start.5 = (bf16[16,2176]{1,0:T(8,128)(2,1)S(1)}, bf16[16,2176]{1,0:T(8,128)(2,1)S(1)}, u32[]{:S(2)}, u32[]{:S(2)}) collective-permute-start(bf16[16,2176]{1,0:T(8,128)(2,1)S(1)} %get-tuple-element.49), channel_id=1, source_target_pairs={{0,1},{1,0},{2,3},{3,2},{4,5},{5,4},{6,7},{7,6},{8,9},{9,8},{10,11... | collective-permute-start | bytes 208904 | tf_op jit(solution)/shard_map/ppermute | solution.py:294
  11.9 4.1 %collective-permute-done.1 = bf16[16,2048]{1,0:T(8,128)(2,1)S(1)} collective-permute-done((bf16[16,2048]{1,0:T(8,128)(2,1)}, bf16[16,2048]{1,0:T(8,128)(2,1)S(1)}, u32[]{:S(2)}, u32[]{:S(2)}) %collective-permute-start.1) | collective-permute-done | bytes 65568 | tf_op jit(solution)/shard_map/ppermute | solution.py:294
  16.0 0.0 collective-permute-done.2
  16.0 1.6 %collective-permute-start.3 = (bf16[64,2048]{1,0:T(8,128)(2,1)S(1)}, bf16[64,2048]{1,0:T(8,128)(2,1)S(1)}, u32[]{:S(2)}, u32[]{:S(2)}) collective-permute-start(bf16[64,2048]{1,0:T(8,128)(2,1)S(1)} %constant_dynamic-update-slice_fusion.value), channel_id=1, source_target_pairs={{0,8},{4,12},{8,0},{12,4},{1,9},{5,13},{9,1},{13,5},{2,10},{6,14},... | collective-permute-start | bytes 786440 | tf_op jit(solution)/shard_map/ppermute | solution.py:294
  17.6 4.6 %load_gate.1 = (bf16[4,2048,768]{2,1,0:T(8,128)(2,1)S(1)}, bf16[64,2048]{1,0:T(8,128)(2,1)S(1)}) custom-call(bf16[4,2048,768]{2,1,0:T(8,128)(2,1)} %source.1, bf16[64,2048]{1,0:T(8,128)(2,1)S(1)} %constant_dynamic-update-slice_fusion.value), custom_call_target="tpu_custom_call" | custom-call | bytes 12582912 | tf_op jit(solution)/shard_map/load_gate/pallas_call | solution.py:351
  22.2 0.0 collective-permute-done.5
  22.2 0.0 collective-permute-done.6
  22.3 1.9 %collective-permute-done.3 = bf16[64,2048]{1,0:T(8,128)(2,1)S(1)} collective-permute-done((bf16[64,2048]{1,0:T(8,128)(2,1)S(1)}, bf16[64,2048]{1,0:T(8,128)(2,1)S(1)}, u32[]{:S(2)}, u32[]{:S(2)}) %collective-permute-start.3) | collective-permute-done | bytes 262176 | tf_op jit(solution)/shard_map/ppermute | solution.py:294
  24.2 0.1 collective-permute-start.4
  24.3 0.0 collective-permute-done.7
  24.3 1.6 %collective-permute-start.8 = (bf16[64,2176]{1,0:T(8,128)(2,1)S(1)}, bf16[64,2176]{1,0:T(8,128)(2,1)S(1)}, u32[]{:S(2)}, u32[]{:S(2)}) collective-permute-start(bf16[64,2176]{1,0:T(8,128)(2,1)S(1)} %constant_dynamic-update-slice_fusion.7.refs_5_), channel_id=1, source_target_pairs={{0,8},{4,12},{8,0},{12,4},{1,9},{5,13},{9,1},{13,5},{2,10},{6,14},... | collective-permute-start | bytes 835592 | tf_op jit(solution)/shard_map/ppermute | solution.py:294
  25.9 0.3 collective-permute-done.4
  26.2 0.0 copy-start.1
  26.2 4.6 %gate.1 = (f32[4,256,768]{2,1,0:T(8,128)S(1)}, bf16[4,512,768]{2,1,0:T(8,128)(2,1)S(1)}, bf16[4,2048,768]{2,1,0:T(8,128)(2,1)S(1)}) custom-call(bf16[256,2048]{1,0:T(8,128)(2,1)S(1)} %constant_dynamic-update-slice_fusion.4.x.refs_0_, bf16[4,2048,768]{2,1,0:T(8,128)(2,1)S(1)} %get-tuple-element.46.gate, bf16[4,2048,768]{2,1,0:T(8,128)(2,1)} %w_up.1), custom_call_target="tpu_custom_call" | custom-call | flops 3221225472 | bytes 12582912 | tf_op jit(solution)/shard_map/gate/pallas_call | solution.py:374
  30.8 0.0 copy-done.1
  30.8 3.4 %up.2 = (bf16[4,256,768]{2,1,0:T(8,128)(2,1)S(1)}, bf16[4,256,768]{2,1,0:T(8,128)(2,1)S(1)}, bf16[4,256,768]{2,1,0:T(8,128)(2,1)S(1)}, bf16[2,768,2048]{2,1,0:T(...) custom-call(bf16[256,2048]{1,0:T(8,128)(2,1)S(1)} %constant_dynamic-update-slice_fusion.4.x.refs_0_, ...), custom_call_target="tpu_custom_call" | custom-call | flops 1610612736 | bytes 6291456 | tf_op jit(solution)/shard_map/up/pallas_call | solution.py:393
  34.2 0.0 collective-permute-done.8
  34.3 0.1 constant_dynamic-update-slice_fusion.11
  34.3 0.2 collective-permute-start.9
  34.5 0.1 turn.1.x_part
  34.6 4.1 %up.3 = (bf16[4,256,768]{2,1,0:T(8,128)(2,1)S(1)}, bf16[4,256,768]{2,1,0:T(8,128)(2,1)S(1)}, bf16[4,256,768]{2,1,0:T(8,128)(2,1)S(1)}, bf16[2,768,2048]{2,1,0:T(...) custom-call(bf16[256,2048]{1,0:T(8,128)(2,1)S(1)} %constant_dynamic-, ...), custom_call_target="tpu_custom_call", output_to_operand_aliasing={{0}: (6, {}), {1}: (7, {}), {2}: (8, {})} | custom-call | flops 1610612736 | bytes 6291456 | tf_op jit(solution)/shard_map/up/pallas_call | solution.py:393
  38.7 0.0 collective-permute-done.9
  38.7 0.1 constant_dynamic-update-slice_fusion.13.refs_0_.packet
  38.8 7.3 %hidden.1 = (bf16[4,256,768]{2,1,0:T(8,128)(2,1)S(1)}, bf16[4,256,768]{2,1,0:T(8,128)(2,1)S(1)}, bf16[4,256,768]{2,1,0:T(8,128)(2,1)S(1)}, bf16[64,1152]{1,0:T(8...) custom-call(bf16[256,2176]{1,0:T(8,128)(2,1)S(1)} %constant_dynamic-update-, ...), custom_call_target="tpu_custom_call" | custom-call | flops 6442450944 | bytes 25165824 | tf_op jit(solution)/shard_map/hidden/pallas_call | solution.py:431
  46.1 1.6 %collective-permute-start.10 = (bf16[64,1152]{1,0:T(8,128)(2,1)S(1)}, bf16[64,1152]{1,0:T(8,128)(2,1)S(1)}, u32[]{:S(2)}, u32[]{:S(2)}) collective-permute-start(bf16[64,1152]{1,0:T(8,128)(2,1)S(1)} %get-tuple-element.63), channel_id=1, source_target_pairs={{0,8},{4,12},{8,0},{12,4},{1,9},{5,13},{9,1},{13,5},{2,10},{6,14},... | collective-permute-start | bytes 442376 | tf_op jit(solution)/shard_map/ppermute | solution.py:294
  47.7 0.1 collective-permute-start.11
  47.7 0.6 collective-permute-start.12
  48.3 6.2 %grad_in.1 = (f32[4,512,768]{2,1,0:T(8,128)}, f32[4,512,768]{2,1,0:T(8,128)}, f32[8,128]{1,0:T(8,128)S(1)}) custom-call(bf16[512,256]{1,0:T(8,128)(2,1)S(1)} %turn.1.x_part, bf16[4,256,768]{2,1,0:T(8,128)(2,1)S(1)} %get-tuple-element.66.d_gate, bf16[4,256,768]{2,1,0:T(8,128)(2,1)S(1)} %get-tuple-element.67.d_up), custom_call_target="tpu_custom_call" | custom-call | flops 1610612736 | bytes 12582912 | tf_op jit(solution)/shard_map/grad_in/pallas_call | solution.py:451
  54.6 0.0 collective-permute-done.10.refs_1_
  54.6 0.0 collective-permute-done.11.refs_2_
  54.6 0.3 collective-permute-done.12.refs_3_
  54.9 0.0 copy-done
  54.9 0.8 %reduce.1 = (f32[8,16]{1,0:T(8,128)}, bf16[16,1024]{1,0:T(8,128)(2,1)S(1)}, bf16[16,1024]{1,0:T(8,128)(2,1)S(1)}, bf16[16,1024]{1,0:T(8,128)(2,1)S(1)}, bf16[16,...) custom-call(bf16[64,1152]{1,0:T(8,128)(2,1)S(1)} %get-tuple-element.62.refs_0_, ...), custom_call_target="tpu_custom_call" | custom-call | tf_op jit(solution)/shard_map/reduce/pallas_call | solution.py:466
  55.7 0.0 collective-permute-start.13
  55.7 2.0 %collective-permute-start.14 = (bf16[16,1024]{1,0:T(8,128)(2,1)S(1)}, bf16[16,1024]{1,0:T(8,128)(2,1)S(1)}, u32[]{:S(2)}, u32[]{:S(2)}) collective-permute-start(bf16[16,1024]{1,0:T(8,128)(2,1)S(1)} %get-tuple-element.71), channel_id=1, source_target_pairs={{0,2},{1,3},{2,0},{3,1},{4,6},{5,7},{6,4},{7,5},{8,10},{9,11},{10,... | collective-permute-start | bytes 98312 | tf_op jit(solution)/shard_map/ppermute | solution.py:294
  57.7 2.4 %collective-permute-start.15 = (bf16[16,1024]{1,0:T(8,128)(2,1)S(1)}, bf16[16,1024]{1,0:T(8,128)(2,1)S(1)}, u32[]{:S(2)}, u32[]{:S(2)}) collective-permute-start(bf16[16,1024]{1,0:T(8,128)(2,1)S(1)} %get-tuple-element.72), channel_id=1, source_target_pairs={{0,3},{1,2},{2,1},{3,0},{4,7},{5,6},{6,5},{7,4},{8,11},{9,10},{10,... | collective-permute-start | bytes 98312 | tf_op jit(solution)/shard_map/ppermute | solution.py:294
  60.1 3.6 %grad_out.1 = (f32[4,768,512]{2,1,0:T(8,128)}, f32[8,128]{1,0:T(8,128)S(1)}) custom-call(bf16[256,2176]{1,0:T(8,128)(2,1)S(1)} %constant_dynamic-update-slice_fusion.13.refs_0_.packet, bf16[4,256,768]{2,1,0:T(8,128)(2,1)S(1)} %get-tuple-element.73.hidden, f32[8,128]{1,0:T(8,128)S(1)} %get-tuple-element.74.after), custom_call_target="tpu_custom_call" | custom-call | flops 805306368 | bytes 6291456 | tf_op jit(solution)/shard_map/grad_out/pallas_call | solution.py:478
  63.7 0.0 collective-permute-done.13.refs_1_
  63.7 0.0 collective-permute-done.14.refs_2_
  63.7 0.0 collective-permute-done.15.refs_3_
  63.7 0.7 %join.1 = (bf16[16,2048]{1,0:T(8,128)(2,1)}, bf16[16,2048]{1,0:T(8,128)(2,1)}) custom-call(bf16[16,1024]{1,0:T(8,128)(2,1)S(1)} %get-tuple-element.69.refs_0_, bf16[16,1024]{1,0:T(8,128)(2,1)S(1)} %collective-permute-done.13.refs_1_, bf16[16,1024]{1,0:T(8,128)(2,1)S(1)} %collective-permute-done.14.refs_2_, ...), custom_call_target="tpu_custom_call" | custom-call | tf_op jit(solution)/shard_map/join/pallas_call | solution.py:493
  (14 shorter events, 0.2 us)
Async XLA Ops:
  0.6 10.1 %collective-permute-start = (bf16[16,2048]{1,0:T(8,128)(2,1)}, bf16[16,2048]{1,0:T(8,128)(2,1)S(1)}, u32[]{:S(2)}, u32[]{:S(2)}) collective-permute-start(bf16[16,2048]{1,0:T(8,128)(2,1)} %tokens.1), channel_id=1, source_target_pairs={{0,1},{1,0},{2,3},{3,2},{4,5},{5,4},{6,7},{7,6},{8,9},{9,8},{10,11... | collective-permute-start | bytes 196616 | tf_op jit(solution)/shard_map/ppermute | solution.py:294
  3.7 12.3 %collective-permute-start.2 = (bf16[16,2048]{1,0:T(8,128)(2,1)}, bf16[16,2048]{1,0:T(8,128)(2,1)S(1)}, u32[]{:S(2)}, u32[]{:S(2)}) collective-permute-start(bf16[16,2048]{1,0:T(8,128)(2,1)} %tokens.1), channel_id=1, source_target_pairs={{0,3},{1,2},{2,1},{3,0},{4,7},{5,6},{6,5},{7,4},{8,11},{9,10},{10,... | collective-permute-start | bytes 196616 | tf_op jit(solution)/shard_map/ppermute | solution.py:294
  6.2 9.8 %collective-permute-start.1 = (bf16[16,2048]{1,0:T(8,128)(2,1)}, bf16[16,2048]{1,0:T(8,128)(2,1)S(1)}, u32[]{:S(2)}, u32[]{:S(2)}) collective-permute-start(bf16[16,2048]{1,0:T(8,128)(2,1)} %tokens.1), channel_id=1, source_target_pairs={{0,2},{1,3},{2,0},{3,1},{4,6},{5,7},{6,4},{7,5},{8,10},{9,11},{10,... | collective-permute-start | bytes 196616 | tf_op jit(solution)/shard_map/ppermute | solution.py:294
  7.4 16.9 %collective-permute-start.7 = (bf16[16,2176]{1,0:T(8,128)(2,1)S(1)}, bf16[16,2176]{1,0:T(8,128)(2,1)S(1)}, u32[]{:S(2)}, u32[]{:S(2)}) collective-permute-start(bf16[16,2176]{1,0:T(8,128)(2,1)S(1)} %get-tuple-element.49), channel_id=1, source_target_pairs={{0,3},{1,2},{2,1},{3,0},{4,7},{5,6},{6,5},{7,4},{8,11},{9,10},{10,... | collective-permute-start | bytes 208904 | tf_op jit(solution)/shard_map/ppermute | solution.py:294
  10.3 11.9 %collective-permute-start.6 = (bf16[16,2176]{1,0:T(8,128)(2,1)S(1)}, bf16[16,2176]{1,0:T(8,128)(2,1)S(1)}, u32[]{:S(2)}, u32[]{:S(2)}) collective-permute-start(bf16[16,2176]{1,0:T(8,128)(2,1)S(1)} %get-tuple-element.49), channel_id=1, source_target_pairs={{0,2},{1,3},{2,0},{3,1},{4,6},{5,7},{6,4},{7,5},{8,10},{9,11},{10,... | collective-permute-start | bytes 208904 | tf_op jit(solution)/shard_map/ppermute | solution.py:294
  10.7 11.5 %collective-permute-start.5 = (bf16[16,2176]{1,0:T(8,128)(2,1)S(1)}, bf16[16,2176]{1,0:T(8,128)(2,1)S(1)}, u32[]{:S(2)}, u32[]{:S(2)}) collective-permute-start(bf16[16,2176]{1,0:T(8,128)(2,1)S(1)} %get-tuple-element.49), channel_id=1, source_target_pairs={{0,1},{1,0},{2,3},{3,2},{4,5},{5,4},{6,7},{7,6},{8,9},{9,8},{10,11... | collective-permute-start | bytes 208904 | tf_op jit(solution)/shard_map/ppermute | solution.py:294
  16.0 8.1 %collective-permute-start.3 = (bf16[64,2048]{1,0:T(8,128)(2,1)S(1)}, bf16[64,2048]{1,0:T(8,128)(2,1)S(1)}, u32[]{:S(2)}, u32[]{:S(2)}) collective-permute-start(bf16[64,2048]{1,0:T(8,128)(2,1)S(1)} %constant_dynamic-update-slice_fusion.value), channel_id=1, source_target_pairs={{0,8},{4,12},{8,0},{12,4},{1,9},{5,13},{9,1},{13,5},{2,10},{6,14},... | collective-permute-start | bytes 786440 | tf_op jit(solution)/shard_map/ppermute | solution.py:294
  24.2 2.0 %collective-permute-start.4 = (bf16[128,2048]{1,0:T(8,128)(2,1)S(1)}, bf16[128,2048]{1,0:T(8,128)(2,1)S(1)}, u32[]{:S(2)}, u32[]{:S(2)}) collective-permute-start(bf16[128,2048]{1,0:T(8,128)(2,1)S(1)} %pad_maximum_fusion), channel_id=1, source_target_pairs={{0,4},{4,0},{8,12},{12,8},{1,5},{5,1},{9,13},{13,9},{2,6},{6,2},{1... | collective-permute-start | bytes 1572872 | tf_op jit(solution)/shard_map/ppermute | solution.py:294
  24.3 10.0 %collective-permute-start.8 = (bf16[64,2176]{1,0:T(8,128)(2,1)S(1)}, bf16[64,2176]{1,0:T(8,128)(2,1)S(1)}, u32[]{:S(2)}, u32[]{:S(2)}) collective-permute-start(bf16[64,2176]{1,0:T(8,128)(2,1)S(1)} %constant_dynamic-update-slice_fusion.7.refs_5_), channel_id=1, source_target_pairs={{0,8},{4,12},{8,0},{12,4},{1,9},{5,13},{9,1},{13,5},{2,10},{6,14},... | collective-permute-start | bytes 835592 | tf_op jit(solution)/shard_map/ppermute | solution.py:294
  26.2 4.6 %copy-start.1 = (s32[4,6]{1,0:T(4,128)S(1)}, s32[4,6]{1,0:T(4,128)}, u32[]{:S(2)}) copy-start(s32[4,6]{1,0:T(4,128)} %refs_1_.3) | copy-start | bytes 292
  34.3 4.4 %collective-permute-start.9 = (bf16[128,2176]{1,0:T(8,128)(2,1)S(1)}, bf16[128,2176]{1,0:T(8,128)(2,1)S(1)}, u32[]{:S(2)}, u32[]{:S(2)}) collective-permute-start(bf16[128,2176]{1,0:T(8,128)(2,1)S(1)} %get-tuple-element.82.after), channel_id=1, source_target_pairs={{0,4},{4,0},{8,12},{12,8},{1,5},{5,1},{9,13},{13,9},{2,6},{6,2},{1... | collective-permute-start | bytes 1671176 | tf_op jit(solution)/shard_map/ppermute | solution.py:294
  46.1 8.5 %collective-permute-start.10 = (bf16[64,1152]{1,0:T(8,128)(2,1)S(1)}, bf16[64,1152]{1,0:T(8,128)(2,1)S(1)}, u32[]{:S(2)}, u32[]{:S(2)}) collective-permute-start(bf16[64,1152]{1,0:T(8,128)(2,1)S(1)} %get-tuple-element.63), channel_id=1, source_target_pairs={{0,8},{4,12},{8,0},{12,4},{1,9},{5,13},{9,1},{13,5},{2,10},{6,14},... | collective-permute-start | bytes 442376 | tf_op jit(solution)/shard_map/ppermute | solution.py:294
  47.7 6.9 %collective-permute-start.11 = (bf16[64,1152]{1,0:T(8,128)(2,1)S(1)}, bf16[64,1152]{1,0:T(8,128)(2,1)S(1)}, u32[]{:S(2)}, u32[]{:S(2)}) collective-permute-start(bf16[64,1152]{1,0:T(8,128)(2,1)S(1)} %get-tuple-element.64), channel_id=1, source_target_pairs={{0,4},{4,0},{8,12},{12,8},{1,5},{5,1},{9,13},{13,9},{2,6},{6,2},{1... | collective-permute-start | bytes 442376 | tf_op jit(solution)/shard_map/ppermute | solution.py:294
  47.7 7.2 %collective-permute-start.12 = (bf16[64,1152]{1,0:T(8,128)(2,1)S(1)}, bf16[64,1152]{1,0:T(8,128)(2,1)S(1)}, u32[]{:S(2)}, u32[]{:S(2)}) collective-permute-start(bf16[64,1152]{1,0:T(8,128)(2,1)S(1)} %get-tuple-element.65), channel_id=1, source_target_pairs={{0,12},{4,8},{8,4},{12,0},{1,13},{5,9},{9,5},{13,1},{2,14},{6,10},... | collective-permute-start | bytes 442376 | tf_op jit(solution)/shard_map/ppermute | solution.py:294
  48.3 6.6 %copy-start = (s32[16,8]{0,1:T(8,128)S(1)}, s32[16,8]{0,1:T(8,128)}, u32[]{:S(2)}) copy-start(s32[16,8]{0,1:T(8,128)} %param.10) | copy-start | bytes 1540
  55.7 8.0 %collective-permute-start.13 = (bf16[16,1024]{1,0:T(8,128)(2,1)S(1)}, bf16[16,1024]{1,0:T(8,128)(2,1)S(1)}, u32[]{:S(2)}, u32[]{:S(2)}) collective-permute-start(bf16[16,1024]{1,0:T(8,128)(2,1)S(1)} %get-tuple-element.70), channel_id=1, source_target_pairs={{0,1},{1,0},{2,3},{3,2},{4,5},{5,4},{6,7},{7,6},{8,9},{9,8},{10,11... | collective-permute-start | bytes 98312 | tf_op jit(solution)/shard_map/ppermute | solution.py:294
  55.7 8.0 %collective-permute-start.14 = (bf16[16,1024]{1,0:T(8,128)(2,1)S(1)}, bf16[16,1024]{1,0:T(8,128)(2,1)S(1)}, u32[]{:S(2)}, u32[]{:S(2)}) collective-permute-start(bf16[16,1024]{1,0:T(8,128)(2,1)S(1)} %get-tuple-element.71), channel_id=1, source_target_pairs={{0,2},{1,3},{2,0},{3,1},{4,6},{5,7},{6,4},{7,5},{8,10},{9,11},{10,... | collective-permute-start | bytes 98312 | tf_op jit(solution)/shard_map/ppermute | solution.py:294
  57.7 6.1 %collective-permute-start.15 = (bf16[16,1024]{1,0:T(8,128)(2,1)S(1)}, bf16[16,1024]{1,0:T(8,128)(2,1)S(1)}, u32[]{:S(2)}, u32[]{:S(2)}) collective-permute-start(bf16[16,1024]{1,0:T(8,128)(2,1)S(1)} %get-tuple-element.72), channel_id=1, source_target_pairs={{0,3},{1,2},{2,1},{3,0},{4,7},{5,6},{6,5},{7,4},{8,11},{9,10},{10,... | collective-permute-start | bytes 98312 | tf_op jit(solution)/shard_map/ppermute | solution.py:294

commit v10 on v8

--- a/solution.py
+++ b/solution.py
@@ -33,17 +33,19 @@
     return pl.ds(pl.multiple_of(index * size, size), size)
 
 
-def route_kernel(cotangent, expert_ids, route_weights, value, packet, same, ids, values, sems):
-    rows, width = cotangent.shape
+def route_kernel(
+    tokens, cotangent, expert_ids, route_weights, own_tokens, packet, ids, values, sems
+):
+    rows, width = tokens.shape
     lanes = packet.shape[1] - width
     copies = [
         pltpu.make_async_copy(expert_ids, ids, sems.at[0]),
         pltpu.make_async_copy(route_weights, values, sems.at[1]),
-        pltpu.make_async_copy(cotangent, packet.at[:, :width], sems.at[2]),
+        pltpu.make_async_copy(tokens, own_tokens, sems.at[2]),
+        pltpu.make_async_copy(cotangent, packet.at[:, :width], sems.at[3]),
     ]
     for copy in copies:
         copy.start()
-    same[...] = value[...]
     for copy in copies:
         copy.wait()
     at = ids_along((lanes, rows), 0)
@@ -54,13 +56,14 @@
     packet[:, width:] = dense.T.astype(packet.dtype)
 
 
-def load_kernel(weight, tokens, target, own_tokens, sems):
+def load_kernel(weight, value, same, *refs):
+    targets, sems = refs[:-1], refs[-1]
     copies = [
-        pltpu.make_async_copy(tokens, own_tokens, sems.at[0]),
-        pltpu.make_async_copy(weight, target, sems.at[1]),
+        pltpu.make_async_copy(weight.at[i], target, sems.at[i]) for i, target in enumerate(targets)
     ]
     for copy in copies:
         copy.start()
+    same[...] = value[...]
     for copy in copies:
         copy.wait()
 
@@ -82,91 +85,93 @@
 
 
 def gate_up_kernel(first, last, *refs):
-    x, masks, gate, w_up, value = refs[:5]
-    hidden, slope_up, slope_gate, same, up_buf, sems = refs[-6:]
-    hidden_units = gate.shape[2]
+    count = last - first
+    gates, refs = refs[:count], refs[count:]
+    x, masks, w_up, w_down, value = refs[:5]
+    known, (same, up, sems) = refs[5:-3], refs[-3:]
+    hidden_units = gates[0].shape[1]
     bf16 = jnp.bfloat16
+    hiddens, slope_ups, slope_gates, gate_parts, up_parts, downs = [known[k::6] for k in range(6)]
+    mine = aligned(lax.axis_index("dp"), gate_parts[0].shape[0])
+    ups = [
+        pltpu.make_async_copy(w_up.at[first + i], up.at[i % 2], sems.at[i]) for i in range(count)
+    ]
+    keeps = [
+        pltpu.make_async_copy(up.at[i % 2, mine, :], up_parts[i], sems.at[3 * count + i])
+        for i in range(count)
+    ]
     loads = [
-        pltpu.make_async_copy(w_up.at[e], up_buf.at[(e - first) % 2], sems.at[(e - first) % 2])
-        for e in range(first, last)
-    ]
-    for load in loads[:2]:
+        pltpu.make_async_copy(gates[i].at[mine, :], gate_parts[i], sems.at[count + i])
+        for i in range(count)
+    ] + [
+        pltpu.make_async_copy(w_down.at[first + i], downs[i], sems.at[2 * count + i])
+        for i in range(count)
+    ]
+    for load in ups[:2] + loads:
         load.start()
     same[...] = value[...]
-
-    for expert in range(first, last):
-        up = up_buf.at[(expert - first) % 2]
-        loads[expert - first].wait()
-
-        def tile(rows, expert=expert, up=up):
-            for start in range(0, hidden_units, CHUNK):
-                cols = slice(start, start + CHUNK)
-                gate_pre = dot(x[rows, :], gate[expert, :, cols], NN)
-                up_proj = dot(x[rows, :], up[:, cols], NN)
-                at = ids_along((1, CHUNK), 1)
-                keep = jnp.zeros((1, CHUNK), jnp.float32)
-                for j in range(CHUNK // BLK):
-                    kept = masks[expert, start // BLK + j].astype(jnp.float32)
-                    keep = jnp.where(at // BLK == j, kept, keep)
-                sigma = 0.5 + 0.5 * jnp.tanh(0.5 * gate_pre)
-                silu = gate_pre * sigma
-                up_kept = up_proj * keep
-                hidden[expert, rows, cols] = (silu * up_kept).astype(bf16)
-                slope_up[expert, rows, cols] = (silu * keep).astype(bf16)
-                slope = up_kept * (sigma + silu * (1.0 - sigma))
-                slope_gate[expert, rows, cols] = slope.astype(bf16)
-
-        over_tiles(x.shape[0], tile)
-        if expert + 2 < last:
-            loads[expert + 2 - first].start()
-
-
-def hidden_kernel(count, *refs):
-    packet, units, slope_up, slope_gate, w_gate, w_up, w_down, hidden, d_gate, d_up = refs[:10]
-    outs, refs = refs[10 : 10 + count], refs[10 + count :]
-    inner, mixed, token_grad, down_buf, gate_buf, up_buf, sems = refs
-    local_experts, hidden_units, width = w_down.shape
+    chunks = [slice(start, start + CHUNK) for start in range(0, hidden_units, CHUNK)]
+
+    def products(rows, weights):
+        return [dot(x[rows, :], weights[:, cols], NN) for cols in chunks]
+
+    def finish(i, rows, cols, gate_pre, up_proj):
+        at = ids_along((1, CHUNK), 1)
+        keep = jnp.zeros((1, CHUNK), jnp.float32)
+        for j in range(CHUNK // BLK):
+            kept = masks[first + i, cols.start // BLK + j].astype(jnp.float32)
+            keep = jnp.where(at // BLK == j, kept, keep)
+        sigma = 0.5 + 0.5 * jnp.tanh(0.5 * gate_pre)
+        silu = gate_pre * sigma
+        up_kept = up_proj * keep
+        hiddens[i][rows, cols] = (silu * up_kept).astype(bf16)
+        slope_ups[i][rows, cols] = (silu * keep).astype(bf16)
+        slope = up_kept * (sigma + silu * (1.0 - sigma))
+        slope_gates[i][rows, cols] = slope.astype(bf16)
+
+    for i in range(count):
+
+        def tile(rows, i=i, early=None):
+            gate_pres = early or products(rows, gates[i])
+            for cols, gate_pre, up_proj in zip(chunks, gate_pres, products(rows, up.at[i % 2])):
+                finish(i, rows, cols, gate_pre, up_proj)
+
+        if x.shape[0] == TILE:
+            early = products(slice(0, TILE), gates[i])
+            ups[i].wait()
+            tile(slice(0, TILE), early=early)
+        else:
+            ups[i].wait()
+            over_tiles(x.shape[0], tile)
+        keeps[i].start()
+        if i + 2 < count:
+            keeps[i].wait()
+            ups[i + 2].start()
+    for load in loads + keeps[max(count - 2, 0) :]:
+        load.wait()
+
+
+def hidden_kernel(local_experts, count, *refs):
+    packet, refs = refs[0], refs[1:]
+    known = [refs[i * 6 : i * 6 + 6] for i in range(local_experts)]
+    refs = refs[6 * local_experts :]
+    hidden, d_gate, d_up = refs[:3]
+    outs, (inner, mixed, token_grad) = refs[3 : 3 + count], refs[3 + count :]
+    hidden_units, width = known[0][5].shape
     tokens, part = mixed.shape
     lanes = packet.shape[1] - width
     half = lanes // 2
     base = lax.axis_index("expert") * local_experts
     mine = aligned(lax.axis_index("dp"), part)
     bf16, f32 = jnp.bfloat16, jnp.float32
-
-    def copies(expert):
-        slot = lax.rem(expert, 2)
-        return [
-            pltpu.make_async_copy(
-                w_down.at[expert, slice(i * CHUNK, (i + 1) * CHUNK), :],
-                down_buf.at[slot, slice(i * CHUNK, (i + 1) * CHUNK), :],
-                sems.at[slot, 2 + i],
-            )
-            for i in range(hidden_units // CHUNK)
-        ] + [
-            pltpu.make_async_copy(w_gate.at[expert, mine, :], gate_buf.at[slot], sems.at[slot, 0]),
-            pltpu.make_async_copy(w_up.at[expert, mine, :], up_buf.at[slot], sems.at[slot, 1]),
-        ]
-
-    for copy in copies(0):
-        copy.start()
     inner[...] = jnp.zeros(inner.shape, inner.dtype)
     mixed[...] = jnp.zeros(mixed.shape, mixed.dtype)
     token_grad[...] = jnp.zeros(token_grad.shape, token_grad.dtype)
 
-    def one_expert(expert, carry):
-        @pl.when(expert + 1 < local_experts)
-        def _():
-            for copy in copies(expert + 1):
-                copy.start()
-
-        slot = lax.rem(expert, 2)
-        down, gate, up = down_buf.at[slot], gate_buf.at[slot], up_buf.at[slot]
-        arriving = copies(expert)
-        if tokens != TILE:
-            for copy in arriving:
-                copy.wait()
-
-        def tile(rows):
+    for expert in range(local_experts):
+
+        def tile(rows, expert=expert):
+            units, slope_up, slope_gate, gate, up, down = known[expert]
             dense = packet[rows, width:].astype(f32)
             at = ids_along((TILE, lanes), 1)
             hit = at == base + expert
@@ -174,14 +179,12 @@
             total = jnp.zeros((TILE, 1), f32)
             for start in range(0, hidden_units, CHUNK):
                 cols = slice(start, start + CHUNK)
-                if tokens == TILE:
-                    arriving[start // CHUNK].wait()
                 back = dot(packet[rows, :width], down[cols, :], NT)
-                part_units = units[expert, rows, cols].astype(f32)
+                part_units = units[rows, cols].astype(f32)
                 total += jnp.sum(part_units * back, axis=1, keepdims=True)
                 back = back * weights
-                new_gate = back * slope_gate[expert, rows, cols].astype(f32)
-                new_up = back * slope_up[expert, rows, cols].astype(f32)
+                new_gate = back * slope_gate[rows, cols].astype(f32)
+                new_up = back * slope_up[rows, cols].astype(f32)
                 hidden[expert, rows, cols] = (part_units * weights).astype(bf16)
                 d_gate[expert, rows, cols] = new_gate.astype(bf16)
                 d_up[expert, rows, cols] = new_up.astype(bf16)
@@ -189,18 +192,13 @@
             inner[rows, :] += jnp.where(
                 hit, high, jnp.where(at == base + expert + half, total - high, 0.0)
             )
-            if tokens == TILE:
-                for copy in arriving[-2:]:
-                    copy.wait()
             mixed[rows, :] += dot(hidden[expert, rows, :], down[:, mine], NN)
             token_grad[rows, :] += dot(d_gate[expert, rows, :], gate[...], NT) + dot(
                 d_up[expert, rows, :], up[...], NT
             )
 
         over_tiles(tokens, tile)
-        return carry
-
-    lax.fori_loop(0, local_experts, one_expert, 0)
+
     rows = outs[0].shape[0]
     for i, out in enumerate(outs):
         block = slice(i * rows, (i + 1) * rows)
@@ -341,68 +339,71 @@
     bf16, f32 = jnp.bfloat16, jnp.float32
     struct = jax.ShapeDtypeStruct
     one = 2 * local_experts * width * hidden_units
-    room = 16 + (everyone - TILE) * (2 * part + lanes) * 14 // MIB
+    room = 11 + (everyone - TILE) * (2 * part + lanes) * 10 // MIB
     dummy = struct((8, LANES), f32)
     ids_t = expert_ids.T
     w_gate, w_up, w_down = [in_hbm(w) for w in (w_gate, w_up, w_down)]
 
-    tokens_near = exchange(tokens, "dp", range(1, columns))
-    gate, own_tokens = pl.pallas_call(
-        load_kernel,
-        out_shape=[pltpu.VMEM(w_gate.shape, bf16), struct(tokens.shape, bf16)],
-        in_specs=[HBM] * 2,
-        out_specs=[VMEM] * 2,
-        scratch_shapes=[pltpu.SemaphoreType.DMA((2,))],
-        cost_estimate=cost(0, one),
-        compiler_params=params(room),
-        name="load_gate",
-    )(w_gate, in_hbm(tokens))
-    gate = in_vmem(gate)
-    x_column = jnp.concatenate([own_tokens] + tokens_near)
-    x_across = exchange(x_column, "expert", chips)
-
-    packet, x_column = pl.pallas_call(
+    own_tokens, packet = pl.pallas_call(
         route_kernel,
-        out_shape=[struct((rows, width + lanes), bf16), struct(x_column.shape, bf16)],
-        in_specs=[HBM] * 3 + [VMEM],
+        out_shape=[struct(tokens.shape, bf16), struct((rows, width + lanes), bf16)],
+        in_specs=[HBM] * 4,
         out_specs=[VMEM] * 2,
         scratch_shapes=[
             pltpu.VMEM(ids_t.shape, jnp.int32),
             pltpu.VMEM(ids_t.shape, bf16),
-            pltpu.SemaphoreType.DMA((3,)),
+            pltpu.SemaphoreType.DMA((4,)),
         ],
         compiler_params=params(room),
         name="route",
-    )(*[in_hbm(a) for a in (cotangent, ids_t, route_weights.T)], x_column)
+    )(*[in_hbm(a) for a in (tokens, cotangent, ids_t, route_weights.T)])
+
+    x_column = jnp.concatenate([own_tokens] + exchange(tokens, "dp", range(1, columns)))
     c_column = jnp.concatenate([packet] + exchange(packet, "dp", range(1, columns)))
+    x_across = exchange(x_column, "expert", chips)
+    c_across = exchange(c_column, "expert", chips)
+    x_column, *gates = pl.pallas_call(
+        load_kernel,
+        out_shape=[struct(x_column.shape, bf16)]
+        + [pltpu.VMEM(w_gate.shape[1:], bf16)] * local_experts,
+        in_specs=[HBM, VMEM],
+        out_specs=[VMEM] * (1 + local_experts),
+        scratch_shapes=[pltpu.SemaphoreType.DMA((local_experts,))],
+        cost_estimate=cost(0, one),
+        compiler_params=params(room),
+        name="load_gate",
+    )(w_gate, x_column)
+    gates = [in_vmem(gate) for gate in gates]
     x = jnp.concatenate([x_column] + x_across)
     x = jnp.concatenate([x, swap(x, "expert", 1)])
 
-    units = struct((local_experts, everyone, hidden_units), bf16)
-    def gate_up(first, last, value, known):
-        return pl.pallas_call(
+    def gate_up(first, last, value):
+        count = last - first
+        one_expert = [struct((everyone, hidden_units), bf16)] * 3
+        one_expert += [pltpu.VMEM((part, hidden_units), bf16)] * 2
+        one_expert += [pltpu.VMEM(w_down.shape[1:], bf16)]
+        *known, same = pl.pallas_call(
             functools.partial(gate_up_kernel, first, last),
-            out_shape=[units] * 3
-            + [struct(value.shape, value.dtype)],
-            in_specs=[VMEM, SMEM, VMEM, HBM] + [VMEM] * (1 + len(known)),
-            out_specs=[VMEM] * 4,
+            out_shape=one_expert * count + [struct(value.shape, value.dtype)],
+            in_specs=[VMEM] * (count + 1) + [SMEM, HBM, HBM, VMEM],
+            out_specs=[VMEM] * (6 * count + 1),
             scratch_shapes=[
-                pltpu.VMEM((min(2, last - first), width, hidden_units), bf16),
-                pltpu.SemaphoreType.DMA((2,)),
+                pltpu.VMEM((min(2, count), width, hidden_units), bf16),
+                pltpu.SemaphoreType.DMA((4 * count,)),
             ],
-            input_output_aliases={5 + i: i for i in range(len(known))},
             cost_estimate=cost(
-                2 * everyone * one * (last - first) // local_experts,
-                2 * one * (last - first) // local_experts,
+                2 * everyone * one * count // local_experts, 2 * one * count // local_experts
             ),
             compiler_params=params(room),
             name="gate_up",
-        )(x, block_masks, gate, w_up, value, *known)
-
-    *factors, c_column = gate_up(0, 1, c_column, [])
-    c_across = exchange(c_column, "expert", chips)
-    if local_experts > 1:
-        *factors, c_column = gate_up(1, local_experts, c_column, factors)
+        )(*gates[first:last], x, block_masks, w_up, w_down, value)
+        return [in_vmem(a) if i % 6 >= 3 else a for i, a in enumerate(known)], same
+
+    middle = local_experts // 2
+    known, c_column = gate_up(0, middle or local_experts, c_column)
+    if middle:
+        more, _ = gate_up(middle, local_experts, c_column)
+        known = known + more
     c_half = jnp.concatenate([c_column] + c_across)
     packets = jnp.concatenate([c_half, swap(c_half, "expert", 1)])
     x_part = pl.pallas_call(
@@ -414,25 +415,22 @@
         name="turn",
     )(x, c_half)
 
+    units = struct((local_experts, everyone, hidden_units), bf16)
     hidden, d_gate, d_up, *partials = pl.pallas_call(
-        functools.partial(hidden_kernel, sources),
+        functools.partial(hidden_kernel, local_experts, sources),
         out_shape=[units] * 3
         + [struct((columns * rows, 2 * part + lanes), bf16)] * sources,
-        in_specs=[VMEM] * 4 + [HBM] * 3,
+        in_specs=[VMEM] * (1 + len(known)),
         out_specs=[VMEM] * (3 + sources),
         scratch_shapes=[
             pltpu.VMEM((everyone, lanes), f32),
             pltpu.VMEM((everyone, part), f32),
             pltpu.VMEM((everyone, part), f32),
-            pltpu.VMEM((min(2, local_experts), hidden_units, width), bf16),
-            pltpu.VMEM((min(2, local_experts), part, hidden_units), bf16),
-            pltpu.VMEM((min(2, local_experts), part, hidden_units), bf16),
-            pltpu.SemaphoreType.DMA((2, 2 + hidden_units // CHUNK)),
         ],
         cost_estimate=cost(2 * everyone * one, 2 * one),
         compiler_params=params(room),
         name="hidden",
-    )(packets, *factors, w_gate, w_up, w_down)
+    )(packets, *known)
     arrived = [
         swap(partial, "expert", other) if other else partial
         for other, partial in zip(expert_order, partials)

time: 73.9 us -> 66.8 us (0.904)
  Pallas kernels: 45.4 us -> 37.9 us
  starting transfers between devices: 19 us -> 20 us
    pallas_call x3, Pallas kernels: 20.7 us -> 12.7 us  [the longest x1 7.01 us: per_device(): pl.pallas_call(functools.partial(hidden_kernel, local_experts, sources),...]
    ppermute x16, starting transfers between devices: 19 us -> 20 us  [swap(): return lax.ppermute(value, axis, [(i, i ^ mask) for i in range(size)])]
  transfers between devices with their start and end apart: 16 -> 16, of which waited for: 6 -> 5; matrix products, arithmetic and copies ran while one was open for 0% -> 0% of each run, Pallas kernels for 33% -> 44%
where the time goes in v10:
time: 66.8 us; the launch traced here: 66.6 us
  Pallas kernels  37.9 us (57%)
  starting transfers between devices  20 us (30%)
  waiting for transfers between devices  7.45 us (11%)
  between operations  0.89 us (1%)
    ppermute x16, starting transfers between devices, swap(): return lax.ppermute(value, axis, [(i, i ^ mask) for i in range(size)])  20 us
    pallas_call x2, Pallas kernels, gate_up(): pl.pallas_call(functools.partial(gate_up_kernel, first, last), out_shape=...  13.7 us
    ppermute x16, waiting for transfers between devices, swap(): return lax.ppermute(value, axis, [(i, i ^ mask) for i in range(size)])  7.45 us
    pallas_call x1, Pallas kernels, per_device(): pl.pallas_call(functools.partial(hidden_kernel, local_experts, sources),...  7.01 us
    pallas_call x1, Pallas kernels, per_device(): pl.pallas_call(grad_in_kernel, out_shape=[struct((local_experts, part, hi...  6.26 us
    pallas_call x1, Pallas kernels, per_device(): pl.pallas_call(load_kernel, out_shape=[struct(x_column.shape, bf16)] + [p...  4.69 us
    pallas_call x1, Pallas kernels, per_device(): pl.pallas_call(grad_out_kernel, out_shape=[struct((local_experts, hidden_...  3.62 us
  transfers between devices with their start and end apart: 16, of which 5 were waited for; matrix products, arithmetic and copies ran while one was open for 0% of the time, Pallas kernels for 44%

profile of v10, /device:TPU:0, one launch (start us, length us, event | category | flops | bytes accessed | tf_op | source)
XLA Modules:
  0.0 66.6 jit_solution(3778545906022363700)
XLA Ops:
  0.6 3.1 %collective-permute-start = (bf16[16,2048]{1,0:T(8,128)(2,1)}, bf16[16,2048]{1,0:T(8,128)(2,1)S(1)}, u32[]{:S(2)}, u32[]{:S(2)}) collective-permute-start(bf16[16,2048]{1,0:T(8,128)(2,1)} %tokens.1), channel_id=1, source_target_pairs={{0,1},{1,0},{2,3},{3,2},{4,5},{5,4},{6,7},{7,6},{8,9},{9,8},{10,11... | collective-permute-start | bytes 196616 | tf_op jit(solution)/shard_map/ppermute | solution.py:305
  3.7 2.5 %collective-permute-start.2 = (bf16[16,2048]{1,0:T(8,128)(2,1)}, bf16[16,2048]{1,0:T(8,128)(2,1)S(1)}, u32[]{:S(2)}, u32[]{:S(2)}) collective-permute-start(bf16[16,2048]{1,0:T(8,128)(2,1)} %tokens.1), channel_id=1, source_target_pairs={{0,3},{1,2},{2,1},{3,0},{4,7},{5,6},{6,5},{7,4},{8,11},{9,10},{10,... | collective-permute-start | bytes 196616 | tf_op jit(solution)/shard_map/ppermute | solution.py:305
  6.2 0.1 collective-permute-start.1
  6.3 1.0 %route.1 = (bf16[16,2048]{1,0:T(8,128)(2,1)S(1)}, bf16[16,2176]{1,0:T(8,128)(2,1)S(1)}) custom-call(bf16[16,2048]{1,0:T(8,128)(2,1)} %tokens.1, bf16[16,2048]{1,0:T(8,128)(2,1)} %cotangent.1, s32[8,16]{1,0:T(8,128)} %bitcast.3, bf16[8,16]{1,0:T(8,128)(2,1)} %bitcast.5), custom_call_target="tpu_custom_call" | custom-call | tf_op jit(solution)/shard_map/route/pallas_call | solution.py:347
  7.4 3.0 %collective-permute-start.7 = (bf16[16,2176]{1,0:T(8,128)(2,1)S(1)}, bf16[16,2176]{1,0:T(8,128)(2,1)S(1)}, u32[]{:S(2)}, u32[]{:S(2)}) collective-permute-start(bf16[16,2176]{1,0:T(8,128)(2,1)S(1)} %get-tuple-element.62), channel_id=1, source_target_pairs={{0,3},{1,2},{2,1},{3,0},{4,7},{5,6},{6,5},{7,4},{8,11},{9,10},{10,... | collective-permute-start | bytes 208904 | tf_op jit(solution)/shard_map/ppermute | solution.py:305
  10.3 0.3 collective-permute-start.6
  10.7 0.0 collective-permute-done
  10.7 1.2 %collective-permute-start.5 = (bf16[16,2176]{1,0:T(8,128)(2,1)S(1)}, bf16[16,2176]{1,0:T(8,128)(2,1)S(1)}, u32[]{:S(2)}, u32[]{:S(2)}) collective-permute-start(bf16[16,2176]{1,0:T(8,128)(2,1)S(1)} %get-tuple-element.62), channel_id=1, source_target_pairs={{0,1},{1,0},{2,3},{3,2},{4,5},{5,4},{6,7},{7,6},{8,9},{9,8},{10,11... | collective-permute-start | bytes 208904 | tf_op jit(solution)/shard_map/ppermute | solution.py:305
  11.9 4.1 %collective-permute-done.1 = bf16[16,2048]{1,0:T(8,128)(2,1)S(1)} collective-permute-done((bf16[16,2048]{1,0:T(8,128)(2,1)}, bf16[16,2048]{1,0:T(8,128)(2,1)S(1)}, u32[]{:S(2)}, u32[]{:S(2)}) %collective-permute-start.1) | collective-permute-done | bytes 65568 | tf_op jit(solution)/shard_map/ppermute | solution.py:305
  16.0 0.0 collective-permute-done.2
  16.0 1.6 %collective-permute-start.3 = (bf16[64,2048]{1,0:T(8,128)(2,1)S(1)}, bf16[64,2048]{1,0:T(8,128)(2,1)S(1)}, u32[]{:S(2)}, u32[]{:S(2)}) collective-permute-start(bf16[64,2048]{1,0:T(8,128)(2,1)S(1)} %constant_dynamic-update-slice_fusion.value), channel_id=1, source_target_pairs={{0,8},{4,12},{8,0},{12,4},{1,9},{5,13},{9,1},{13,5},{2,10},{6,14},... | collective-permute-start | bytes 786440 | tf_op jit(solution)/shard_map/ppermute | solution.py:305
  17.6 4.7 %load_gate.1 = (bf16[64,2048]{1,0:T(8,128)(2,1)S(1)}, bf16[2048,768]{1,0:T(8,128)(2,1)S(1)}, bf16[2048,768]{1,0:T(8,128)(2,1)S(1)}, bf16[2048,768]{1,0:T(8,128)(2,1)S(1)}, bf16[2048,768]{1,0:T(8,128)(2,1)S(1)}) custom-call(bf16[4,2048,768]{2,1,0:T(8,128)(2,1)} %weight.1, bf16[64,2048]{1,0:T(8,128)(2,1)S(1)} %constant_dynamic-update-slice_fusion.value), custom_call_target="tpu_custom_call" | custom-call | bytes 12582912 | tf_op jit(solution)/shard_map/load_gate/pallas_call | solution.py:365
  22.3 0.0 copy-start.1
  22.3 0.0 collective-permute-done.5
  22.3 0.0 collective-permute-done.6
  22.4 1.7 %collective-permute-done.3 = bf16[64,2048]{1,0:T(8,128)(2,1)S(1)} collective-permute-done((bf16[64,2048]{1,0:T(8,128)(2,1)S(1)}, bf16[64,2048]{1,0:T(8,128)(2,1)S(1)}, u32[]{:S(2)}, u32[]{:S(2)}) %collective-permute-start.3) | collective-permute-done | bytes 262176 | tf_op jit(solution)/shard_map/ppermute | solution.py:305
  24.2 0.1 collective-permute-start.4
  24.2 0.0 collective-permute-done.7
  24.3 1.6 %collective-permute-start.8 = (bf16[64,2176]{1,0:T(8,128)(2,1)S(1)}, bf16[64,2176]{1,0:T(8,128)(2,1)S(1)}, u32[]{:S(2)}, u32[]{:S(2)}) collective-permute-start(bf16[64,2176]{1,0:T(8,128)(2,1)S(1)} %constant_dynamic-update-slice_fusion.7.refs_6_), channel_id=1, source_target_pairs={{0,8},{4,12},{8,0},{12,4},{1,9},{5,13},{9,1},{13,5},{2,10},{6,14},... | collective-permute-start | bytes 835592 | tf_op jit(solution)/shard_map/ppermute | solution.py:305
  25.9 0.3 collective-permute-done.4
  26.2 0.0 copy-done.1
  26.2 6.4 %gate_up.2 = (bf16[256,768]{1,0:T(8,128)(2,1)S(1)}, bf16[256,768]{1,0:T(8,128)(2,1)S(1)}, bf16[256,768]{1,0:T(8,128)(2,1)S(1)}, bf16[512,768]{1,0:T(8,128)(2,1)S...) custom-call(bf16[2048,768]{1,0:T(8,128)(2,1)S(1)} %get-tuple-element, ...), custom_call_target="tpu_custom_call" | custom-call | flops 3221225472 | bytes 12582912 | tf_op jit(solution)/shard_map/gate_up/pallas_call | solution.py:385
  32.7 0.7 %collective-permute-done.8 = bf16[64,2176]{1,0:T(8,128)(2,1)S(1)} collective-permute-done((bf16[64,2176]{1,0:T(8,128)(2,1)S(1)}, bf16[64,2176]{1,0:T(8,128)(2,1)S(1)}, u32[]{:S(2)}, u32[]{:S(2)}) %collective-permute-start.8) | collective-permute-done | bytes 278560 | tf_op jit(solution)/shard_map/ppermute | solution.py:305
  33.4 0.1 collective-permute-start.9
  33.5 0.1 turn.1.x_part
  33.6 7.3 %gate_up.3 = (bf16[256,768]{1,0:T(8,128)(2,1)S(1)}, bf16[256,768]{1,0:T(8,128)(2,1)S(1)}, bf16[256,768]{1,0:T(8,128)(2,1)S(1)}, bf16[512,768]{1,0:T(8,128)(2,1)S...) custom-call(bf16[2048,768]{1,0:T(8,128)(2,1)S(1)} %get-tuple-element, ...), custom_call_target="tpu_custom_call" | custom-call | flops 3221225472 | bytes 12582912 | tf_op jit(solution)/shard_map/gate_up/pallas_call | solution.py:385
  40.9 0.0 collective-permute-done.9
  40.9 0.1 constant_dynamic-update-slice_fusion.13.refs_0_.packet
  41.0 7.0 %hidden.1 = (bf16[4,256,768]{2,1,0:T(8,128)(2,1)S(1)}, bf16[4,256,768]{2,1,0:T(8,128)(2,1)S(1)}, bf16[4,256,768]{2,1,0:T(8,128)(2,1)S(1)}, bf16[64,1152]{1,0:T(8...) custom-call(bf16[256,2176]{1,0:T(8,128)(2,1)S(1)} %constant_dynamic-update-, ...), custom_call_target="tpu_custom_call" | custom-call | flops 6442450944 | bytes 25165824 | tf_op jit(solution)/shard_map/hidden/pallas_call | solution.py:419
  48.0 0.0 copy-start
  48.0 1.6 %collective-permute-start.10 = (bf16[64,1152]{1,0:T(8,128)(2,1)S(1)}, bf16[64,1152]{1,0:T(8,128)(2,1)S(1)}, u32[]{:S(2)}, u32[]{:S(2)}) collective-permute-start(bf16[64,1152]{1,0:T(8,128)(2,1)S(1)} %get-tuple-element.91), channel_id=1, source_target_pairs={{0,8},{4,12},{8,0},{12,4},{1,9},{5,13},{9,1},{13,5},{2,10},{6,14},... | collective-permute-start | bytes 442376 | tf_op jit(solution)/shard_map/ppermute | solution.py:305
  49.6 0.2 collective-permute-start.11
  49.8 0.4 collective-permute-start.12
  50.3 6.3 %grad_in.1 = (f32[4,512,768]{2,1,0:T(8,128)}, f32[4,512,768]{2,1,0:T(8,128)}, f32[8,128]{1,0:T(8,128)S(1)}) custom-call(bf16[512,256]{1,0:T(8,128)(2,1)S(1)} %turn.1.x_part, bf16[4,256,768]{2,1,0:T(8,128)(2,1)S(1)} %get-tuple-element.94.d_gate, bf16[4,256,768]{2,1,0:T(8,128)(2,1)S(1)} %get-tuple-element.95.d_up), custom_call_target="tpu_custom_call" | custom-call | flops 1610612736 | bytes 12582912 | tf_op jit(solution)/shard_map/grad_in/pallas_call | solution.py:439
  56.5 0.0 collective-permute-done.10.refs_1_
  56.5 0.0 collective-permute-done.11.refs_2_
  56.5 0.6 collective-permute-done.12.refs_3_
  57.1 0.0 copy-done
  57.1 0.8 %reduce.1 = (f32[8,16]{1,0:T(8,128)}, bf16[16,1024]{1,0:T(8,128)(2,1)S(1)}, bf16[16,1024]{1,0:T(8,128)(2,1)S(1)}, bf16[16,1024]{1,0:T(8,128)(2,1)S(1)}, bf16[16,...) custom-call(bf16[64,1152]{1,0:T(8,128)(2,1)S(1)} %get-tuple-element.90.refs_0_, ...), custom_call_target="tpu_custom_call" | custom-call | tf_op jit(solution)/shard_map/reduce/pallas_call | solution.py:454
  57.9 0.0 collective-permute-start.13
  57.9 1.9 %collective-permute-start.14 = (bf16[16,1024]{1,0:T(8,128)(2,1)S(1)}, bf16[16,1024]{1,0:T(8,128)(2,1)S(1)}, u32[]{:S(2)}, u32[]{:S(2)}) collective-permute-start(bf16[16,1024]{1,0:T(8,128)(2,1)S(1)} %get-tuple-element.99), channel_id=1, source_target_pairs={{0,2},{1,3},{2,0},{3,1},{4,6},{5,7},{6,4},{7,5},{8,10},{9,11},{10,... | collective-permute-start | bytes 98312 | tf_op jit(solution)/shard_map/ppermute | solution.py:305
  59.8 2.5 %collective-permute-start.15 = (bf16[16,1024]{1,0:T(8,128)(2,1)S(1)}, bf16[16,1024]{1,0:T(8,128)(2,1)S(1)}, u32[]{:S(2)}, u32[]{:S(2)}) collective-permute-start(bf16[16,1024]{1,0:T(8,128)(2,1)S(1)} %get-tuple-element.100), channel_id=1, source_target_pairs={{0,3},{1,2},{2,1},{3,0},{4,7},{5,6},{6,5},{7,4},{8,11},{9,10},{10,... | collective-permute-start | bytes 98312 | tf_op jit(solution)/shard_map/ppermute | solution.py:305
  62.3 3.6 %grad_out.1 = (f32[4,768,512]{2,1,0:T(8,128)}, f32[8,128]{1,0:T(8,128)S(1)}) custom-call(bf16[256,2176]{1,0:T(8,128)(2,1)S(1)} %constant_dynamic-update-slice_fusion.13.refs_0_.packet, bf16[4,256,768]{2,1,0:T(8,128)(2,1)S(1)} %get-tuple-element.101.hidden, f32[8,128]{1,0:T(8,128)S(1)} %get-tuple-element.102.after), custom_call_target="tpu_custom_call" | custom-call | flops 805306368 | bytes 6291456 | tf_op jit(solution)/shard_map/grad_out/pallas_call | solution.py:466
  65.9 0.0 collective-permute-done.13.refs_1_
  65.9 0.0 collective-permute-done.14.refs_2_
  65.9 0.0 collective-permute-done.15.refs_3_
  65.9 0.7 %join.1 = (bf16[16,2048]{1,0:T(8,128)(2,1)}, bf16[16,2048]{1,0:T(8,128)(2,1)}) custom-call(bf16[16,1024]{1,0:T(8,128)(2,1)S(1)} %get-tuple-element.97.refs_0_, bf16[16,1024]{1,0:T(8,128)(2,1)S(1)} %collective-permute-done.13.refs_1_, bf16[16,1024]{1,0:T(8,128)(2,1)S(1)} %collective-permute-done.14.refs_2_, ...), custom_call_target="tpu_custom_call" | custom-call | tf_op jit(solution)/shard_map/join/pallas_call | solution.py:481
  (14 shorter events, 0.3 us)
Async XLA Ops:
  0.6 10.1 %collective-permute-start = (bf16[16,2048]{1,0:T(8,128)(2,1)}, bf16[16,2048]{1,0:T(8,128)(2,1)S(1)}, u32[]{:S(2)}, u32[]{:S(2)}) collective-permute-start(bf16[16,2048]{1,0:T(8,128)(2,1)} %tokens.1), channel_id=1, source_target_pairs={{0,1},{1,0},{2,3},{3,2},{4,5},{5,4},{6,7},{7,6},{8,9},{9,8},{10,11... | collective-permute-start | bytes 196616 | tf_op jit(solution)/shard_map/ppermute | solution.py:305
  3.7 12.3 %collective-permute-start.2 = (bf16[16,2048]{1,0:T(8,128)(2,1)}, bf16[16,2048]{1,0:T(8,128)(2,1)S(1)}, u32[]{:S(2)}, u32[]{:S(2)}) collective-permute-start(bf16[16,2048]{1,0:T(8,128)(2,1)} %tokens.1), channel_id=1, source_target_pairs={{0,3},{1,2},{2,1},{3,0},{4,7},{5,6},{6,5},{7,4},{8,11},{9,10},{10,... | collective-permute-start | bytes 196616 | tf_op jit(solution)/shard_map/ppermute | solution.py:305
  6.2 9.8 %collective-permute-start.1 = (bf16[16,2048]{1,0:T(8,128)(2,1)}, bf16[16,2048]{1,0:T(8,128)(2,1)S(1)}, u32[]{:S(2)}, u32[]{:S(2)}) collective-permute-start(bf16[16,2048]{1,0:T(8,128)(2,1)} %tokens.1), channel_id=1, source_target_pairs={{0,2},{1,3},{2,0},{3,1},{4,6},{5,7},{6,4},{7,5},{8,10},{9,11},{10,... | collective-permute-start | bytes 196616 | tf_op jit(solution)/shard_map/ppermute | solution.py:305
  7.4 16.9 %collective-permute-start.7 = (bf16[16,2176]{1,0:T(8,128)(2,1)S(1)}, bf16[16,2176]{1,0:T(8,128)(2,1)S(1)}, u32[]{:S(2)}, u32[]{:S(2)}) collective-permute-start(bf16[16,2176]{1,0:T(8,128)(2,1)S(1)} %get-tuple-element.62), channel_id=1, source_target_pairs={{0,3},{1,2},{2,1},{3,0},{4,7},{5,6},{6,5},{7,4},{8,11},{9,10},{10,... | collective-permute-start | bytes 208904 | tf_op jit(solution)/shard_map/ppermute | solution.py:305
  10.3 12.0 %collective-permute-start.6 = (bf16[16,2176]{1,0:T(8,128)(2,1)S(1)}, bf16[16,2176]{1,0:T(8,128)(2,1)S(1)}, u32[]{:S(2)}, u32[]{:S(2)}) collective-permute-start(bf16[16,2176]{1,0:T(8,128)(2,1)S(1)} %get-tuple-element.62), channel_id=1, source_target_pairs={{0,2},{1,3},{2,0},{3,1},{4,6},{5,7},{6,4},{7,5},{8,10},{9,11},{10,... | collective-permute-start | bytes 208904 | tf_op jit(solution)/shard_map/ppermute | solution.py:305
  10.7 11.6 %collective-permute-start.5 = (bf16[16,2176]{1,0:T(8,128)(2,1)S(1)}, bf16[16,2176]{1,0:T(8,128)(2,1)S(1)}, u32[]{:S(2)}, u32[]{:S(2)}) collective-permute-start(bf16[16,2176]{1,0:T(8,128)(2,1)S(1)} %get-tuple-element.62), channel_id=1, source_target_pairs={{0,1},{1,0},{2,3},{3,2},{4,5},{5,4},{6,7},{7,6},{8,9},{9,8},{10,11... | collective-permute-start | bytes 208904 | tf_op jit(solution)/shard_map/ppermute | solution.py:305
  16.0 8.1 %collective-permute-start.3 = (bf16[64,2048]{1,0:T(8,128)(2,1)S(1)}, bf16[64,2048]{1,0:T(8,128)(2,1)S(1)}, u32[]{:S(2)}, u32[]{:S(2)}) collective-permute-start(bf16[64,2048]{1,0:T(8,128)(2,1)S(1)} %constant_dynamic-update-slice_fusion.value), channel_id=1, source_target_pairs={{0,8},{4,12},{8,0},{12,4},{1,9},{5,13},{9,1},{13,5},{2,10},{6,14},... | collective-permute-start | bytes 786440 | tf_op jit(solution)/shard_map/ppermute | solution.py:305
  22.3 3.9 %copy-start.1 = (s32[4,6]{1,0:T(4,128)S(1)}, s32[4,6]{1,0:T(4,128)}, u32[]{:S(2)}) copy-start(s32[4,6]{1,0:T(4,128)} %refs_3_.3) | copy-start | bytes 292
  24.2 2.0 %collective-permute-start.4 = (bf16[128,2048]{1,0:T(8,128)(2,1)S(1)}, bf16[128,2048]{1,0:T(8,128)(2,1)S(1)}, u32[]{:S(2)}, u32[]{:S(2)}) collective-permute-start(bf16[128,2048]{1,0:T(8,128)(2,1)S(1)} %pad_maximum_fusion), channel_id=1, source_target_pairs={{0,4},{4,0},{8,12},{12,8},{1,5},{5,1},{9,13},{13,9},{2,6},{6,2},{1... | collective-permute-start | bytes 1572872 | tf_op jit(solution)/shard_map/ppermute | solution.py:305
  24.3 9.1 %collective-permute-start.8 = (bf16[64,2176]{1,0:T(8,128)(2,1)S(1)}, bf16[64,2176]{1,0:T(8,128)(2,1)S(1)}, u32[]{:S(2)}, u32[]{:S(2)}) collective-permute-start(bf16[64,2176]{1,0:T(8,128)(2,1)S(1)} %constant_dynamic-update-slice_fusion.7.refs_6_), channel_id=1, source_target_pairs={{0,8},{4,12},{8,0},{12,4},{1,9},{5,13},{9,1},{13,5},{2,10},{6,14},... | collective-permute-start | bytes 835592 | tf_op jit(solution)/shard_map/ppermute | solution.py:305
  33.4 7.5 %collective-permute-start.9 = (bf16[128,2176]{1,0:T(8,128)(2,1)S(1)}, bf16[128,2176]{1,0:T(8,128)(2,1)S(1)}, u32[]{:S(2)}, u32[]{:S(2)}) collective-permute-start(bf16[128,2176]{1,0:T(8,128)(2,1)S(1)} %get-tuple-element.110.after), channel_id=1, source_target_pairs={{0,4},{4,0},{8,12},{12,8},{1,5},{5,1},{9,13},{13,9},{2,6},{6,2},{1... | collective-permute-start | bytes 1671176 | tf_op jit(solution)/shard_map/ppermute | solution.py:305
  48.0 9.1 %copy-start = (s32[16,8]{0,1:T(8,128)S(1)}, s32[16,8]{0,1:T(8,128)}, u32[]{:S(2)}) copy-start(s32[16,8]{0,1:T(8,128)} %param.10) | copy-start | bytes 1540
  48.0 8.5 %collective-permute-start.10 = (bf16[64,1152]{1,0:T(8,128)(2,1)S(1)}, bf16[64,1152]{1,0:T(8,128)(2,1)S(1)}, u32[]{:S(2)}, u32[]{:S(2)}) collective-permute-start(bf16[64,1152]{1,0:T(8,128)(2,1)S(1)} %get-tuple-element.91), channel_id=1, source_target_pairs={{0,8},{4,12},{8,0},{12,4},{1,9},{5,13},{9,1},{13,5},{2,10},{6,14},... | collective-permute-start | bytes 442376 | tf_op jit(solution)/shard_map/ppermute | solution.py:305
  49.6 6.9 %collective-permute-start.11 = (bf16[64,1152]{1,0:T(8,128)(2,1)S(1)}, bf16[64,1152]{1,0:T(8,128)(2,1)S(1)}, u32[]{:S(2)}, u32[]{:S(2)}) collective-permute-start(bf16[64,1152]{1,0:T(8,128)(2,1)S(1)} %get-tuple-element.92), channel_id=1, source_target_pairs={{0,4},{4,0},{8,12},{12,8},{1,5},{5,1},{9,13},{13,9},{2,6},{6,2},{1... | collective-permute-start | bytes 442376 | tf_op jit(solution)/shard_map/ppermute | solution.py:305
  49.8 7.3 %collective-permute-start.12 = (bf16[64,1152]{1,0:T(8,128)(2,1)S(1)}, bf16[64,1152]{1,0:T(8,128)(2,1)S(1)}, u32[]{:S(2)}, u32[]{:S(2)}) collective-permute-start(bf16[64,1152]{1,0:T(8,128)(2,1)S(1)} %get-tuple-element.93), channel_id=1, source_target_pairs={{0,12},{4,8},{8,4},{12,0},{1,13},{5,9},{9,5},{13,1},{2,14},{6,10},... | collective-permute-start | bytes 442376 | tf_op jit(solution)/shard_map/ppermute | solution.py:305
  57.9 8.0 %collective-permute-start.13 = (bf16[16,1024]{1,0:T(8,128)(2,1)S(1)}, bf16[16,1024]{1,0:T(8,128)(2,1)S(1)}, u32[]{:S(2)}, u32[]{:S(2)}) collective-permute-start(bf16[16,1024]{1,0:T(8,128)(2,1)S(1)} %get-tuple-element.98), channel_id=1, source_target_pairs={{0,1},{1,0},{2,3},{3,2},{4,5},{5,4},{6,7},{7,6},{8,9},{9,8},{10,11... | collective-permute-start | bytes 98312 | tf_op jit(solution)/shard_map/ppermute | solution.py:305
  57.9 8.0 %collective-permute-start.14 = (bf16[16,1024]{1,0:T(8,128)(2,1)S(1)}, bf16[16,1024]{1,0:T(8,128)(2,1)S(1)}, u32[]{:S(2)}, u32[]{:S(2)}) collective-permute-start(bf16[16,1024]{1,0:T(8,128)(2,1)S(1)} %get-tuple-element.99), channel_id=1, source_target_pairs={{0,2},{1,3},{2,0},{3,1},{4,6},{5,7},{6,4},{7,5},{8,10},{9,11},{10,... | collective-permute-start | bytes 98312 | tf_op jit(solution)/shard_map/ppermute | solution.py:305
  59.8 6.1 %collective-permute-start.15 = (bf16[16,1024]{1,0:T(8,128)(2,1)S(1)}, bf16[16,1024]{1,0:T(8,128)(2,1)S(1)}, u32[]{:S(2)}, u32[]{:S(2)}) collective-permute-start(bf16[16,1024]{1,0:T(8,128)(2,1)S(1)} %get-tuple-element.100), channel_id=1, source_target_pairs={{0,3},{1,2},{2,1},{3,0},{4,7},{5,6},{6,5},{7,4},{8,11},{9,10},{10,... | collective-permute-start | bytes 98312 | tf_op jit(solution)/shard_map/ppermute | solution.py:305

commit v11 on v10

--- a/solution.py
+++ b/solution.py
@@ -86,68 +86,45 @@
 
 def gate_up_kernel(first, last, *refs):
     count = last - first
-    gates, refs = refs[:count], refs[count:]
-    x, masks, w_up, w_down, value = refs[:5]
-    known, (same, up, sems) = refs[5:-3], refs[-3:]
+    gates, ups, refs = refs[:count], refs[count : 2 * count], refs[2 * count :]
+    x, masks, w_down, value = refs[:4]
+    known, (same, sems) = refs[4:-2], refs[-2:]
     hidden_units = gates[0].shape[1]
     bf16 = jnp.bfloat16
     hiddens, slope_ups, slope_gates, gate_parts, up_parts, downs = [known[k::6] for k in range(6)]
     mine = aligned(lax.axis_index("dp"), gate_parts[0].shape[0])
-    ups = [
-        pltpu.make_async_copy(w_up.at[first + i], up.at[i % 2], sems.at[i]) for i in range(count)
-    ]
-    keeps = [
-        pltpu.make_async_copy(up.at[i % 2, mine, :], up_parts[i], sems.at[3 * count + i])
-        for i in range(count)
-    ]
-    loads = [
-        pltpu.make_async_copy(gates[i].at[mine, :], gate_parts[i], sems.at[count + i])
-        for i in range(count)
-    ] + [
-        pltpu.make_async_copy(w_down.at[first + i], downs[i], sems.at[2 * count + i])
-        for i in range(count)
-    ]
-    for load in ups[:2] + loads:
+    loads = []
+    for i in range(count):
+        loads += [
+            pltpu.make_async_copy(w_down.at[first + i], downs[i], sems.at[3 * i]),
+            pltpu.make_async_copy(gates[i].at[mine, :], gate_parts[i], sems.at[3 * i + 1]),
+            pltpu.make_async_copy(ups[i].at[mine, :], up_parts[i], sems.at[3 * i + 2]),
+        ]
+    for load in loads:
         load.start()
     same[...] = value[...]
-    chunks = [slice(start, start + CHUNK) for start in range(0, hidden_units, CHUNK)]
-
-    def products(rows, weights):
-        return [dot(x[rows, :], weights[:, cols], NN) for cols in chunks]
-
-    def finish(i, rows, cols, gate_pre, up_proj):
-        at = ids_along((1, CHUNK), 1)
-        keep = jnp.zeros((1, CHUNK), jnp.float32)
-        for j in range(CHUNK // BLK):
-            kept = masks[first + i, cols.start // BLK + j].astype(jnp.float32)
-            keep = jnp.where(at // BLK == j, kept, keep)
-        sigma = 0.5 + 0.5 * jnp.tanh(0.5 * gate_pre)
-        silu = gate_pre * sigma
-        up_kept = up_proj * keep
-        hiddens[i][rows, cols] = (silu * up_kept).astype(bf16)
-        slope_ups[i][rows, cols] = (silu * keep).astype(bf16)
-        slope = up_kept * (sigma + silu * (1.0 - sigma))
-        slope_gates[i][rows, cols] = slope.astype(bf16)
-
-    for i in range(count):
-
-        def tile(rows, i=i, early=None):
-            gate_pres = early or products(rows, gates[i])
-            for cols, gate_pre, up_proj in zip(chunks, gate_pres, products(rows, up.at[i % 2])):
-                finish(i, rows, cols, gate_pre, up_proj)
-
-        if x.shape[0] == TILE:
-            early = products(slice(0, TILE), gates[i])
-            ups[i].wait()
-            tile(slice(0, TILE), early=early)
-        else:
-            ups[i].wait()
-            over_tiles(x.shape[0], tile)
-        keeps[i].start()
-        if i + 2 < count:
-            keeps[i].wait()
-            ups[i + 2].start()
-    for load in loads + keeps[max(count - 2, 0) :]:
+
+    def tile(rows):
+        for i in range(count):
+            for start in range(0, hidden_units, CHUNK):
+                cols = slice(start, start + CHUNK)
+                gate_pre = dot(x[rows, :], gates[i][:, cols], NN)
+                up_proj = dot(x[rows, :], ups[i][:, cols], NN)
+                at = ids_along((1, CHUNK), 1)
+                keep = jnp.zeros((1, CHUNK), jnp.float32)
+                for j in range(CHUNK // BLK):
+                    kept = masks[first + i, start // BLK + j].astype(jnp.float32)
+                    keep = jnp.where(at // BLK == j, kept, keep)
+                sigma = 0.5 + 0.5 * jnp.tanh(0.5 * gate_pre)
+                silu = gate_pre * sigma
+                up_kept = up_proj * keep
+                hiddens[i][rows, cols] = (silu * up_kept).astype(bf16)
+                slope_ups[i][rows, cols] = (silu * keep).astype(bf16)
+                slope = up_kept * (sigma + silu * (1.0 - sigma))
+                slope_gates[i][rows, cols] = slope.astype(bf16)
+
+    over_tiles(x.shape[0], tile)
+    for load in loads:
         load.wait()
 
 
@@ -339,7 +316,7 @@
     bf16, f32 = jnp.bfloat16, jnp.float32
     struct = jax.ShapeDtypeStruct
     one = 2 * local_experts * width * hidden_units
-    room = 11 + (everyone - TILE) * (2 * part + lanes) * 10 // MIB
+    room = 8 + (everyone - TILE) * (2 * part + lanes) * 10 // MIB
     dummy = struct((8, LANES), f32)
     ids_t = expert_ids.T
     w_gate, w_up, w_down = [in_hbm(w) for w in (w_gate, w_up, w_down)]
@@ -358,22 +335,27 @@
         name="route",
     )(*[in_hbm(a) for a in (tokens, cotangent, ids_t, route_weights.T)])
 
-    x_column = jnp.concatenate([own_tokens] + exchange(tokens, "dp", range(1, columns)))
+    def load(weight, value, name):
+        same, *loaded = pl.pallas_call(
+            load_kernel,
+            out_shape=[struct(value.shape, bf16)]
+            + [pltpu.VMEM(weight.shape[1:], bf16)] * local_experts,
+            in_specs=[HBM, VMEM],
+            out_specs=[VMEM] * (1 + local_experts),
+            scratch_shapes=[pltpu.SemaphoreType.DMA((local_experts,))],
+            cost_estimate=cost(0, one),
+            compiler_params=params(room),
+            name=name,
+        )(weight, value)
+        return [in_vmem(array) for array in loaded], same
+
+    tokens_near = exchange(tokens, "dp", range(1, columns))
     c_column = jnp.concatenate([packet] + exchange(packet, "dp", range(1, columns)))
+    ups, own_tokens = load(w_up, own_tokens, "load_up")
+    x_column = jnp.concatenate([own_tokens] + tokens_near)
     x_across = exchange(x_column, "expert", chips)
     c_across = exchange(c_column, "expert", chips)
-    x_column, *gates = pl.pallas_call(
-        load_kernel,
-        out_shape=[struct(x_column.shape, bf16)]
-        + [pltpu.VMEM(w_gate.shape[1:], bf16)] * local_experts,
-        in_specs=[HBM, VMEM],
-        out_specs=[VMEM] * (1 + local_experts),
-        scratch_shapes=[pltpu.SemaphoreType.DMA((local_experts,))],
-        cost_estimate=cost(0, one),
-        compiler_params=params(room),
-        name="load_gate",
-    )(w_gate, x_column)
-    gates = [in_vmem(gate) for gate in gates]
+    gates, x_column = load(w_gate, x_column, "load_gate")
     x = jnp.concatenate([x_column] + x_across)
     x = jnp.concatenate([x, swap(x, "expert", 1)])
 
@@ -385,18 +367,15 @@
         *known, same = pl.pallas_call(
             functools.partial(gate_up_kernel, first, last),
             out_shape=one_expert * count + [struct(value.shape, value.dtype)],
-            in_specs=[VMEM] * (count + 1) + [SMEM, HBM, HBM, VMEM],
+            in_specs=[VMEM] * (2 * count + 1) + [SMEM, HBM, VMEM],
             out_specs=[VMEM] * (6 * count + 1),
-            scratch_shapes=[
-                pltpu.VMEM((min(2, count), width, hidden_units), bf16),
-                pltpu.SemaphoreType.DMA((4 * count,)),
-            ],
+            scratch_shapes=[pltpu.SemaphoreType.DMA((3 * count,))],
             cost_estimate=cost(
                 2 * everyone * one * count // local_experts, 2 * one * count // local_experts
             ),
             compiler_params=params(room),
             name="gate_up",
-        )(*gates[first:last], x, block_masks, w_up, w_down, value)
+        )(*gates[first:last], *ups[first:last], x, block_masks, w_down, value)
         return [in_vmem(a) if i % 6 >= 3 else a for i, a in enumerate(known)], same
 
     middle = local_experts // 2

time: 66.8 us -> 65.1 us (0.975)
  waiting for transfers between devices: 7.45 us -> 4.59 us
  Pallas kernels: 37.9 us -> 39 us
    pallas_call x1 -> x2, Pallas kernels: 4.69 us -> 9.37 us  [load(): pl.pallas_call(load_kernel, out_shape=[struct(value.shape, bf16)] + [pltp...]
    pallas_call x2, Pallas kernels: 13.7 us -> 10.2 us  [gate_up(): pl.pallas_call(functools.partial(gate_up_kernel, first, last), out_shape=...]
    ppermute x16, waiting for transfers between devices: 7.45 us -> 4.59 us  [swap(): return lax.ppermute(value, axis, [(i, i ^ mask) for i in range(size)])]
  transfers between devices with their start and end apart: 16 -> 16, of which waited for: 5 -> 5; matrix products, arithmetic and copies ran while one was open for 0% -> 0% of each run, Pallas kernels for 44% -> 47%
where the time goes in v11:
time: 65.1 us; the launch traced here: 64.9 us
  Pallas kernels  39 us (60%)
  starting transfers between devices  20 us (31%)
  waiting for transfers between devices  4.59 us (7%)
  between operations  0.91 us (1%)
    ppermute x16, starting transfers between devices, swap(): return lax.ppermute(value, axis, [(i, i ^ mask) for i in range(size)])  20 us
    pallas_call x2, Pallas kernels, gate_up(): pl.pallas_call(functools.partial(gate_up_kernel, first, last), out_shape=...  10.2 us
    pallas_call x2, Pallas kernels, load(): pl.pallas_call(load_kernel, out_shape=[struct(value.shape, bf16)] + [pltp...  9.37 us
    pallas_call x1, Pallas kernels, per_device(): pl.pallas_call(functools.partial(hidden_kernel, local_experts, sources),...  6.97 us
    pallas_call x1, Pallas kernels, per_device(): pl.pallas_call(grad_in_kernel, out_shape=[struct((local_experts, part, hi...  6.24 us
    ppermute x16, waiting for transfers between devices, swap(): return lax.ppermute(value, axis, [(i, i ^ mask) for i in range(size)])  4.59 us
    pallas_call x1, Pallas kernels, per_device(): pl.pallas_call(grad_out_kernel, out_shape=[struct((local_experts, hidden_...  3.62 us
  transfers between devices with their start and end apart: 16, of which 5 were waited for; matrix products, arithmetic and copies ran while one was open for 0% of the time, Pallas kernels for 47%

profile of v11, /device:TPU:0, one launch (start us, length us, event | category | flops | bytes accessed | tf_op | source)
XLA Modules:
  0.0 64.9 jit_solution(9073158504411830324)
XLA Ops:
  0.6 3.1 %collective-permute-start = (bf16[16,2048]{1,0:T(8,128)(2,1)}, bf16[16,2048]{1,0:T(8,128)(2,1)S(1)}, u32[]{:S(2)}, u32[]{:S(2)}) collective-permute-start(bf16[16,2048]{1,0:T(8,128)(2,1)} %tokens.1), channel_id=1, source_target_pairs={{0,1},{1,0},{2,3},{3,2},{4,5},{5,4},{6,7},{7,6},{8,9},{9,8},{10,11... | collective-permute-start | bytes 196616 | tf_op jit(solution)/shard_map/ppermute | solution.py:282
  3.7 2.5 %collective-permute-start.2 = (bf16[16,2048]{1,0:T(8,128)(2,1)}, bf16[16,2048]{1,0:T(8,128)(2,1)S(1)}, u32[]{:S(2)}, u32[]{:S(2)}) collective-permute-start(bf16[16,2048]{1,0:T(8,128)(2,1)} %tokens.1), channel_id=1, source_target_pairs={{0,3},{1,2},{2,1},{3,0},{4,7},{5,6},{6,5},{7,4},{8,11},{9,10},{10,... | collective-permute-start | bytes 196616 | tf_op jit(solution)/shard_map/ppermute | solution.py:282
  6.2 0.1 collective-permute-start.1
  6.3 1.0 %route.1 = (bf16[16,2048]{1,0:T(8,128)(2,1)S(1)}, bf16[16,2176]{1,0:T(8,128)(2,1)S(1)}) custom-call(bf16[16,2048]{1,0:T(8,128)(2,1)} %tokens.1, bf16[16,2048]{1,0:T(8,128)(2,1)} %cotangent.1, s32[8,16]{1,0:T(8,128)} %bitcast.3, bf16[8,16]{1,0:T(8,128)(2,1)} %bitcast.5), custom_call_target="tpu_custom_call" | custom-call | tf_op jit(solution)/shard_map/route/pallas_call | solution.py:324
  7.4 3.0 %collective-permute-start.7 = (bf16[16,2176]{1,0:T(8,128)(2,1)S(1)}, bf16[16,2176]{1,0:T(8,128)(2,1)S(1)}, u32[]{:S(2)}, u32[]{:S(2)}) collective-permute-start(bf16[16,2176]{1,0:T(8,128)(2,1)S(1)} %get-tuple-element.70), channel_id=1, source_target_pairs={{0,3},{1,2},{2,1},{3,0},{4,7},{5,6},{6,5},{7,4},{8,11},{9,10},{10,... | collective-permute-start | bytes 208904 | tf_op jit(solution)/shard_map/ppermute | solution.py:282
  10.3 0.3 collective-permute-start.6
  10.7 4.7 %load_up.1 = (bf16[16,2048]{1,0:T(8,128)(2,1)S(1)}, bf16[2048,768]{1,0:T(8,128)(2,1)S(1)}, bf16[2048,768]{1,0:T(8,128)(2,1)S(1)}, bf16[2048,768]{1,0:T(8,128)(2,1)S(1)}, bf16[2048,768]{1,0:T(8,128)(2,1)S(1)}) custom-call(bf16[4,2048,768]{2,1,0:T(8,128)(2,1)} %weight.2, bf16[16,2048]{1,0:T(8,128)(2,1)S(1)} %get-tuple-element.63.value), custom_call_target="tpu_custom_call" | custom-call | bytes 12582912 | tf_op jit(solution)/shard_map/load_up/pallas_call | solution.py:339
  15.4 0.0 collective-permute-done
  15.4 1.2 %collective-permute-start.5 = (bf16[16,2176]{1,0:T(8,128)(2,1)S(1)}, bf16[16,2176]{1,0:T(8,128)(2,1)S(1)}, u32[]{:S(2)}, u32[]{:S(2)}) collective-permute-start(bf16[16,2176]{1,0:T(8,128)(2,1)S(1)} %get-tuple-element.70), channel_id=1, source_target_pairs={{0,1},{1,0},{2,3},{3,2},{4,5},{5,4},{6,7},{7,6},{8,9},{9,8},{10,11... | collective-permute-start | bytes 208904 | tf_op jit(solution)/shard_map/ppermute | solution.py:282
  16.6 0.0 collective-permute-done.1
  16.6 0.0 collective-permute-done.2
  16.6 1.6 %collective-permute-start.3 = (bf16[64,2048]{1,0:T(8,128)(2,1)S(1)}, bf16[64,2048]{1,0:T(8,128)(2,1)S(1)}, u32[]{:S(2)}, u32[]{:S(2)}) collective-permute-start(bf16[64,2048]{1,0:T(8,128)(2,1)S(1)} %constant_dynamic-update-slice_fusion.value), channel_id=1, source_target_pairs={{0,8},{4,12},{8,0},{12,4},{1,9},{5,13},{9,1},{13,5},{2,10},{6,14},... | collective-permute-start | bytes 786440 | tf_op jit(solution)/shard_map/ppermute | solution.py:282
  18.2 4.7 %load_gate.1 = (bf16[64,2048]{1,0:T(8,128)(2,1)S(1)}, bf16[2048,768]{1,0:T(8,128)(2,1)S(1)}, bf16[2048,768]{1,0:T(8,128)(2,1)S(1)}, bf16[2048,768]{1,0:T(8,128)(2,1)S(1)}, bf16[2048,768]{1,0:T(8,128)(2,1)S(1)}) custom-call(bf16[4,2048,768]{2,1,0:T(8,128)(2,1)} %weight.3, bf16[64,2048]{1,0:T(8,128)(2,1)S(1)} %constant_dynamic-update-slice_fusion.value), custom_call_target="tpu_custom_call" | custom-call | bytes 12582912 | tf_op jit(solution)/shard_map/load_gate/pallas_call | solution.py:339
  22.9 0.0 copy-start.1
  22.9 0.0 collective-permute-done.5
  23.0 0.0 collective-permute-done.6
  23.0 1.1 %collective-permute-done.3 = bf16[64,2048]{1,0:T(8,128)(2,1)S(1)} collective-permute-done((bf16[64,2048]{1,0:T(8,128)(2,1)S(1)}, bf16[64,2048]{1,0:T(8,128)(2,1)S(1)}, u32[]{:S(2)}, u32[]{:S(2)}) %collective-permute-start.3) | collective-permute-done | bytes 262176 | tf_op jit(solution)/shard_map/ppermute | solution.py:282
  24.2 0.1 collective-permute-start.4
  24.3 0.0 collective-permute-done.7
  24.3 1.6 %collective-permute-start.8 = (bf16[64,2176]{1,0:T(8,128)(2,1)S(1)}, bf16[64,2176]{1,0:T(8,128)(2,1)S(1)}, u32[]{:S(2)}, u32[]{:S(2)}) collective-permute-start(bf16[64,2176]{1,0:T(8,128)(2,1)S(1)} %constant_dynamic-update-slice_fusion.7.refs_7_), channel_id=1, source_target_pairs={{0,8},{4,12},{8,0},{12,4},{1,9},{5,13},{9,1},{13,5},{2,10},{6,14},... | collective-permute-start | bytes 835592 | tf_op jit(solution)/shard_map/ppermute | solution.py:282
  25.9 0.3 collective-permute-done.4
  26.2 0.0 copy-done.1
  26.2 4.8 %gate_up.2 = (bf16[256,768]{1,0:T(8,128)(2,1)S(1)}, bf16[256,768]{1,0:T(8,128)(2,1)S(1)}, bf16[256,768]{1,0:T(8,128)(2,1)S(1)}, bf16[512,768]{1,0:T(8,128)(2,1)S...) custom-call(bf16[2048,768]{1,0:T(8,128)(2,1)S(1)} %get-tuple-element, ...), custom_call_target="tpu_custom_call" | custom-call | flops 3221225472 | bytes 12582912 | tf_op jit(solution)/shard_map/gate_up/pallas_call | solution.py:367
  31.0 2.4 %collective-permute-done.8 = bf16[64,2176]{1,0:T(8,128)(2,1)S(1)} collective-permute-done((bf16[64,2176]{1,0:T(8,128)(2,1)S(1)}, bf16[64,2176]{1,0:T(8,128)(2,1)S(1)}, u32[]{:S(2)}, u32[]{:S(2)}) %collective-permute-start.8) | collective-permute-done | bytes 278560 | tf_op jit(solution)/shard_map/ppermute | solution.py:282
  33.4 0.1 collective-permute-start.9
  33.5 0.1 turn.1.x_part
  33.7 5.5 %gate_up.3 = (bf16[256,768]{1,0:T(8,128)(2,1)S(1)}, bf16[256,768]{1,0:T(8,128)(2,1)S(1)}, bf16[256,768]{1,0:T(8,128)(2,1)S(1)}, bf16[512,768]{1,0:T(8,128)(2,1)S...) custom-call(bf16[2048,768]{1,0:T(8,128)(2,1)S(1)} %get-tuple-element, ...), custom_call_target="tpu_custom_call" | custom-call | flops 3221225472 | bytes 12582912 | tf_op jit(solution)/shard_map/gate_up/pallas_call | solution.py:367
  39.1 0.0 collective-permute-done.9
  39.1 0.1 constant_dynamic-update-slice_fusion.13.refs_0_.packet
  39.2 7.0 %hidden.1 = (bf16[4,256,768]{2,1,0:T(8,128)(2,1)S(1)}, bf16[4,256,768]{2,1,0:T(8,128)(2,1)S(1)}, bf16[4,256,768]{2,1,0:T(8,128)(2,1)S(1)}, bf16[64,1152]{1,0:T(8...) custom-call(bf16[256,2176]{1,0:T(8,128)(2,1)S(1)} %constant_dynamic-update-, ...), custom_call_target="tpu_custom_call" | custom-call | flops 6442450944 | bytes 25165824 | tf_op jit(solution)/shard_map/hidden/pallas_call | solution.py:398
  46.2 0.0 copy-start
  46.2 1.6 %collective-permute-start.10 = (bf16[64,1152]{1,0:T(8,128)(2,1)S(1)}, bf16[64,1152]{1,0:T(8,128)(2,1)S(1)}, u32[]{:S(2)}, u32[]{:S(2)}) collective-permute-start(bf16[64,1152]{1,0:T(8,128)(2,1)S(1)} %get-tuple-element.101), channel_id=1, source_target_pairs={{0,8},{4,12},{8,0},{12,4},{1,9},{5,13},{9,1},{13,5},{2,10},{6,14},... | collective-permute-start | bytes 442376 | tf_op jit(solution)/shard_map/ppermute | solution.py:282
  47.8 0.2 collective-permute-start.11
  48.0 0.4 collective-permute-start.12
  48.4 6.2 %grad_in.1 = (f32[4,512,768]{2,1,0:T(8,128)}, f32[4,512,768]{2,1,0:T(8,128)}, f32[8,128]{1,0:T(8,128)S(1)}) custom-call(bf16[512,256]{1,0:T(8,128)(2,1)S(1)} %turn.1.x_part, bf16[4,256,768]{2,1,0:T(8,128)(2,1)S(1)} %get-tuple-element.104.d_gate, bf16[4,256,768]{2,1,0:T(8,128)(2,1)S(1)} %get-tuple-element.105.d_up), custom_call_target="tpu_custom_call" | custom-call | flops 1610612736 | bytes 12582912 | tf_op jit(solution)/shard_map/grad_in/pallas_call | solution.py:418
  54.7 0.0 collective-permute-done.10.refs_1_
  54.7 0.0 collective-permute-done.11.refs_2_
  54.7 0.6 collective-permute-done.12.refs_3_
  55.3 0.0 copy-done
  55.3 0.8 %reduce.1 = (f32[8,16]{1,0:T(8,128)}, bf16[16,1024]{1,0:T(8,128)(2,1)S(1)}, bf16[16,1024]{1,0:T(8,128)(2,1)S(1)}, bf16[16,1024]{1,0:T(8,128)(2,1)S(1)}, bf16[16,...) custom-call(bf16[64,1152]{1,0:T(8,128)(2,1)S(1)} %get-tuple-element.100.refs_0_, ...), custom_call_target="tpu_custom_call" | custom-call | tf_op jit(solution)/shard_map/reduce/pallas_call | solution.py:433
  56.0 0.0 collective-permute-start.13
  56.0 2.5 %collective-permute-start.14 = (bf16[16,1024]{1,0:T(8,128)(2,1)S(1)}, bf16[16,1024]{1,0:T(8,128)(2,1)S(1)}, u32[]{:S(2)}, u32[]{:S(2)}) collective-permute-start(bf16[16,1024]{1,0:T(8,128)(2,1)S(1)} %get-tuple-element.109), channel_id=1, source_target_pairs={{0,2},{1,3},{2,0},{3,1},{4,6},{5,7},{6,4},{7,5},{8,10},{9,11},{10,... | collective-permute-start | bytes 98312 | tf_op jit(solution)/shard_map/ppermute | solution.py:282
  58.5 1.9 %collective-permute-start.15 = (bf16[16,1024]{1,0:T(8,128)(2,1)S(1)}, bf16[16,1024]{1,0:T(8,128)(2,1)S(1)}, u32[]{:S(2)}, u32[]{:S(2)}) collective-permute-start(bf16[16,1024]{1,0:T(8,128)(2,1)S(1)} %get-tuple-element.110), channel_id=1, source_target_pairs={{0,3},{1,2},{2,1},{3,0},{4,7},{5,6},{6,5},{7,4},{8,11},{9,10},{10,... | collective-permute-start | bytes 98312 | tf_op jit(solution)/shard_map/ppermute | solution.py:282
  60.4 3.6 %grad_out.1 = (f32[4,768,512]{2,1,0:T(8,128)}, f32[8,128]{1,0:T(8,128)S(1)}) custom-call(bf16[256,2176]{1,0:T(8,128)(2,1)S(1)} %constant_dynamic-update-slice_fusion.13.refs_0_.packet, bf16[4,256,768]{2,1,0:T(8,128)(2,1)S(1)} %get-tuple-element.111.hidden, f32[8,128]{1,0:T(8,128)S(1)} %get-tuple-element.112.after), custom_call_target="tpu_custom_call" | custom-call | flops 805306368 | bytes 6291456 | tf_op jit(solution)/shard_map/grad_out/pallas_call | solution.py:445
  64.0 0.0 collective-permute-done.13.refs_1_
  64.1 0.0 collective-permute-done.14.refs_2_
  64.1 0.2 collective-permute-done.15.refs_3_
  64.3 0.7 %join.1 = (bf16[16,2048]{1,0:T(8,128)(2,1)}, bf16[16,2048]{1,0:T(8,128)(2,1)}) custom-call(bf16[16,1024]{1,0:T(8,128)(2,1)S(1)} %get-tuple-element.107.refs_0_, bf16[16,1024]{1,0:T(8,128)(2,1)S(1)} %collective-permute-done.13.refs_1_, bf16[16,1024]{1,0:T(8,128)(2,1)S(1)} %collective-permute-done.14.refs_2_, ...), custom_call_target="tpu_custom_call" | custom-call | tf_op jit(solution)/shard_map/join/pallas_call | solution.py:460
  (14 shorter events, 0.3 us)
Async XLA Ops:
  0.6 14.8 %collective-permute-start = (bf16[16,2048]{1,0:T(8,128)(2,1)}, bf16[16,2048]{1,0:T(8,128)(2,1)S(1)}, u32[]{:S(2)}, u32[]{:S(2)}) collective-permute-start(bf16[16,2048]{1,0:T(8,128)(2,1)} %tokens.1), channel_id=1, source_target_pairs={{0,1},{1,0},{2,3},{3,2},{4,5},{5,4},{6,7},{7,6},{8,9},{9,8},{10,11... | collective-permute-start | bytes 196616 | tf_op jit(solution)/shard_map/ppermute | solution.py:282
  3.7 12.9 %collective-permute-start.2 = (bf16[16,2048]{1,0:T(8,128)(2,1)}, bf16[16,2048]{1,0:T(8,128)(2,1)S(1)}, u32[]{:S(2)}, u32[]{:S(2)}) collective-permute-start(bf16[16,2048]{1,0:T(8,128)(2,1)} %tokens.1), channel_id=1, source_target_pairs={{0,3},{1,2},{2,1},{3,0},{4,7},{5,6},{6,5},{7,4},{8,11},{9,10},{10,... | collective-permute-start | bytes 196616 | tf_op jit(solution)/shard_map/ppermute | solution.py:282
  6.2 10.4 %collective-permute-start.1 = (bf16[16,2048]{1,0:T(8,128)(2,1)}, bf16[16,2048]{1,0:T(8,128)(2,1)S(1)}, u32[]{:S(2)}, u32[]{:S(2)}) collective-permute-start(bf16[16,2048]{1,0:T(8,128)(2,1)} %tokens.1), channel_id=1, source_target_pairs={{0,2},{1,3},{2,0},{3,1},{4,6},{5,7},{6,4},{7,5},{8,10},{9,11},{10,... | collective-permute-start | bytes 196616 | tf_op jit(solution)/shard_map/ppermute | solution.py:282
  7.4 16.9 %collective-permute-start.7 = (bf16[16,2176]{1,0:T(8,128)(2,1)S(1)}, bf16[16,2176]{1,0:T(8,128)(2,1)S(1)}, u32[]{:S(2)}, u32[]{:S(2)}) collective-permute-start(bf16[16,2176]{1,0:T(8,128)(2,1)S(1)} %get-tuple-element.70), channel_id=1, source_target_pairs={{0,3},{1,2},{2,1},{3,0},{4,7},{5,6},{6,5},{7,4},{8,11},{9,10},{10,... | collective-permute-start | bytes 208904 | tf_op jit(solution)/shard_map/ppermute | solution.py:282
  10.3 12.6 %collective-permute-start.6 = (bf16[16,2176]{1,0:T(8,128)(2,1)S(1)}, bf16[16,2176]{1,0:T(8,128)(2,1)S(1)}, u32[]{:S(2)}, u32[]{:S(2)}) collective-permute-start(bf16[16,2176]{1,0:T(8,128)(2,1)S(1)} %get-tuple-element.70), channel_id=1, source_target_pairs={{0,2},{1,3},{2,0},{3,1},{4,6},{5,7},{6,4},{7,5},{8,10},{9,11},{10,... | collective-permute-start | bytes 208904 | tf_op jit(solution)/shard_map/ppermute | solution.py:282
  15.4 7.5 %collective-permute-start.5 = (bf16[16,2176]{1,0:T(8,128)(2,1)S(1)}, bf16[16,2176]{1,0:T(8,128)(2,1)S(1)}, u32[]{:S(2)}, u32[]{:S(2)}) collective-permute-start(bf16[16,2176]{1,0:T(8,128)(2,1)S(1)} %get-tuple-element.70), channel_id=1, source_target_pairs={{0,1},{1,0},{2,3},{3,2},{4,5},{5,4},{6,7},{7,6},{8,9},{9,8},{10,11... | collective-permute-start | bytes 208904 | tf_op jit(solution)/shard_map/ppermute | solution.py:282
  16.6 7.5 %collective-permute-start.3 = (bf16[64,2048]{1,0:T(8,128)(2,1)S(1)}, bf16[64,2048]{1,0:T(8,128)(2,1)S(1)}, u32[]{:S(2)}, u32[]{:S(2)}) collective-permute-start(bf16[64,2048]{1,0:T(8,128)(2,1)S(1)} %constant_dynamic-update-slice_fusion.value), channel_id=1, source_target_pairs={{0,8},{4,12},{8,0},{12,4},{1,9},{5,13},{9,1},{13,5},{2,10},{6,14},... | collective-permute-start | bytes 786440 | tf_op jit(solution)/shard_map/ppermute | solution.py:282
  22.9 3.3 %copy-start.1 = (s32[4,6]{1,0:T(4,128)S(1)}, s32[4,6]{1,0:T(4,128)}, u32[]{:S(2)}) copy-start(s32[4,6]{1,0:T(4,128)} %refs_5_.3) | copy-start | bytes 292
  24.2 2.0 %collective-permute-start.4 = (bf16[128,2048]{1,0:T(8,128)(2,1)S(1)}, bf16[128,2048]{1,0:T(8,128)(2,1)S(1)}, u32[]{:S(2)}, u32[]{:S(2)}) collective-permute-start(bf16[128,2048]{1,0:T(8,128)(2,1)S(1)} %pad_maximum_fusion), channel_id=1, source_target_pairs={{0,4},{4,0},{8,12},{12,8},{1,5},{5,1},{9,13},{13,9},{2,6},{6,2},{1... | collective-permute-start | bytes 1572872 | tf_op jit(solution)/shard_map/ppermute | solution.py:282
  24.3 9.1 %collective-permute-start.8 = (bf16[64,2176]{1,0:T(8,128)(2,1)S(1)}, bf16[64,2176]{1,0:T(8,128)(2,1)S(1)}, u32[]{:S(2)}, u32[]{:S(2)}) collective-permute-start(bf16[64,2176]{1,0:T(8,128)(2,1)S(1)} %constant_dynamic-update-slice_fusion.7.refs_7_), channel_id=1, source_target_pairs={{0,8},{4,12},{8,0},{12,4},{1,9},{5,13},{9,1},{13,5},{2,10},{6,14},... | collective-permute-start | bytes 835592 | tf_op jit(solution)/shard_map/ppermute | solution.py:282
  33.4 5.7 %collective-permute-start.9 = (bf16[128,2176]{1,0:T(8,128)(2,1)S(1)}, bf16[128,2176]{1,0:T(8,128)(2,1)S(1)}, u32[]{:S(2)}, u32[]{:S(2)}) collective-permute-start(bf16[128,2176]{1,0:T(8,128)(2,1)S(1)} %get-tuple-element.120.after), channel_id=1, source_target_pairs={{0,4},{4,0},{8,12},{12,8},{1,5},{5,1},{9,13},{13,9},{2,6},{6,2},{1... | collective-permute-start | bytes 1671176 | tf_op jit(solution)/shard_map/ppermute | solution.py:282
  46.2 9.1 %copy-start = (s32[16,8]{0,1:T(8,128)S(1)}, s32[16,8]{0,1:T(8,128)}, u32[]{:S(2)}) copy-start(s32[16,8]{0,1:T(8,128)} %param.10) | copy-start | bytes 1540
  46.2 8.5 %collective-permute-start.10 = (bf16[64,1152]{1,0:T(8,128)(2,1)S(1)}, bf16[64,1152]{1,0:T(8,128)(2,1)S(1)}, u32[]{:S(2)}, u32[]{:S(2)}) collective-permute-start(bf16[64,1152]{1,0:T(8,128)(2,1)S(1)} %get-tuple-element.101), channel_id=1, source_target_pairs={{0,8},{4,12},{8,0},{12,4},{1,9},{5,13},{9,1},{13,5},{2,10},{6,14},... | collective-permute-start | bytes 442376 | tf_op jit(solution)/shard_map/ppermute | solution.py:282
  47.8 6.9 %collective-permute-start.11 = (bf16[64,1152]{1,0:T(8,128)(2,1)S(1)}, bf16[64,1152]{1,0:T(8,128)(2,1)S(1)}, u32[]{:S(2)}, u32[]{:S(2)}) collective-permute-start(bf16[64,1152]{1,0:T(8,128)(2,1)S(1)} %get-tuple-element.102), channel_id=1, source_target_pairs={{0,4},{4,0},{8,12},{12,8},{1,5},{5,1},{9,13},{13,9},{2,6},{6,2},{1... | collective-permute-start | bytes 442376 | tf_op jit(solution)/shard_map/ppermute | solution.py:282
  48.0 7.3 %collective-permute-start.12 = (bf16[64,1152]{1,0:T(8,128)(2,1)S(1)}, bf16[64,1152]{1,0:T(8,128)(2,1)S(1)}, u32[]{:S(2)}, u32[]{:S(2)}) collective-permute-start(bf16[64,1152]{1,0:T(8,128)(2,1)S(1)} %get-tuple-element.103), channel_id=1, source_target_pairs={{0,12},{4,8},{8,4},{12,0},{1,13},{5,9},{9,5},{13,1},{2,14},{6,10},... | collective-permute-start | bytes 442376 | tf_op jit(solution)/shard_map/ppermute | solution.py:282
  56.0 8.0 %collective-permute-start.13 = (bf16[16,1024]{1,0:T(8,128)(2,1)S(1)}, bf16[16,1024]{1,0:T(8,128)(2,1)S(1)}, u32[]{:S(2)}, u32[]{:S(2)}) collective-permute-start(bf16[16,1024]{1,0:T(8,128)(2,1)S(1)} %get-tuple-element.108), channel_id=1, source_target_pairs={{0,1},{1,0},{2,3},{3,2},{4,5},{5,4},{6,7},{7,6},{8,9},{9,8},{10,11... | collective-permute-start | bytes 98312 | tf_op jit(solution)/shard_map/ppermute | solution.py:282
  56.0 8.0 %collective-permute-start.14 = (bf16[16,1024]{1,0:T(8,128)(2,1)S(1)}, bf16[16,1024]{1,0:T(8,128)(2,1)S(1)}, u32[]{:S(2)}, u32[]{:S(2)}) collective-permute-start(bf16[16,1024]{1,0:T(8,128)(2,1)S(1)} %get-tuple-element.109), channel_id=1, source_target_pairs={{0,2},{1,3},{2,0},{3,1},{4,6},{5,7},{6,4},{7,5},{8,10},{9,11},{10,... | collective-permute-start | bytes 98312 | tf_op jit(solution)/shard_map/ppermute | solution.py:282
  58.5 5.7 %collective-permute-start.15 = (bf16[16,1024]{1,0:T(8,128)(2,1)S(1)}, bf16[16,1024]{1,0:T(8,128)(2,1)S(1)}, u32[]{:S(2)}, u32[]{:S(2)}) collective-permute-start(bf16[16,1024]{1,0:T(8,128)(2,1)S(1)} %get-tuple-element.110), channel_id=1, source_target_pairs={{0,3},{1,2},{2,1},{3,0},{4,7},{5,6},{6,5},{7,4},{8,11},{9,10},{10,... | collective-permute-start | bytes 98312 | tf_op jit(solution)/shard_map/ppermute | solution.py:282

commit v12 on v11

--- a/solution.py
+++ b/solution.py
@@ -68,8 +68,17 @@
         copy.wait()
 
 
-def turn_kernel(x, after, x_part):
-    x_part[...] = x[:, aligned(lax.axis_index("dp"), x_part.shape[0])].T
+def turn_kernel(x, after, w_gate, w_up, x_part, gate_part, up_part, sems):
+    mine = aligned(lax.axis_index("dp"), x_part.shape[0])
+    loads = [
+        pltpu.make_async_copy(w_gate.at[:, mine, :], gate_part, sems.at[0]),
+        pltpu.make_async_copy(w_up.at[:, mine, :], up_part, sems.at[1]),
+    ]
+    for load in loads:
+        load.start()
+    x_part[...] = x[:, mine].T
+    for load in loads:
+        load.wait()
 
 
 def over_tiles(tokens, body):
@@ -84,22 +93,16 @@
         lax.fori_loop(0, tokens // TILE, turn, 0)
 
 
-def gate_up_kernel(first, last, *refs):
-    count = last - first
+def gate_up_kernel(count, *refs):
     gates, ups, refs = refs[:count], refs[count : 2 * count], refs[2 * count :]
     x, masks, w_down, value = refs[:4]
-    known, (same, sems) = refs[4:-2], refs[-2:]
+    known, downs, (same, sems) = refs[4 : 4 + 3 * count], refs[4 + 3 * count : -2], refs[-2:]
     hidden_units = gates[0].shape[1]
     bf16 = jnp.bfloat16
-    hiddens, slope_ups, slope_gates, gate_parts, up_parts, downs = [known[k::6] for k in range(6)]
-    mine = aligned(lax.axis_index("dp"), gate_parts[0].shape[0])
-    loads = []
-    for i in range(count):
-        loads += [
-            pltpu.make_async_copy(w_down.at[first + i], downs[i], sems.at[3 * i]),
-            pltpu.make_async_copy(gates[i].at[mine, :], gate_parts[i], sems.at[3 * i + 1]),
-            pltpu.make_async_copy(ups[i].at[mine, :], up_parts[i], sems.at[3 * i + 2]),
-        ]
+    hiddens, slope_ups, slope_gates = [known[k::3] for k in range(3)]
+    loads = [
+        pltpu.make_async_copy(w_down.at[i], down, sems.at[i]) for i, down in enumerate(downs)
+    ]
     for load in loads:
         load.start()
     same[...] = value[...]
@@ -113,7 +116,7 @@
                 at = ids_along((1, CHUNK), 1)
                 keep = jnp.zeros((1, CHUNK), jnp.float32)
                 for j in range(CHUNK // BLK):
-                    kept = masks[first + i, start // BLK + j].astype(jnp.float32)
+                    kept = masks[i, start // BLK + j].astype(jnp.float32)
                     keep = jnp.where(at // BLK == j, kept, keep)
                 sigma = 0.5 + 0.5 * jnp.tanh(0.5 * gate_pre)
                 silu = gate_pre * sigma
@@ -128,13 +131,21 @@
         load.wait()
 
 
-def hidden_kernel(local_experts, count, *refs):
+def hidden_kernel(local_experts, middle, count, *refs):
     packet, refs = refs[0], refs[1:]
-    known = [refs[i * 6 : i * 6 + 6] for i in range(local_experts)]
-    refs = refs[6 * local_experts :]
+    gate, up, refs = refs[0], refs[1], refs[2:]
+    known = [refs[i * 3 : i * 3 + 3] for i in range(local_experts)]
+    refs = refs[3 * local_experts :]
+    downs, w_down, refs = refs[:middle], refs[middle], refs[middle + 1 :]
     hidden, d_gate, d_up = refs[:3]
-    outs, (inner, mixed, token_grad) = refs[3 : 3 + count], refs[3 + count :]
-    hidden_units, width = known[0][5].shape
+    outs, (inner, mixed, token_grad, down_buf, sems) = refs[3 : 3 + count], refs[3 + count :]
+    hidden_units, width = downs[0].shape
+    loads = [
+        pltpu.make_async_copy(w_down.at[i], down_buf.at[i - middle], sems.at[i - middle])
+        for i in range(middle, local_experts)
+    ]
+    for load in loads:
+        load.start()
     tokens, part = mixed.shape
     lanes = packet.shape[1] - width
     half = lanes // 2
@@ -146,9 +157,13 @@
     token_grad[...] = jnp.zeros(token_grad.shape, token_grad.dtype)
 
     for expert in range(local_experts):
+        if expert == middle:
+            for load in loads:
+                load.wait()
 
         def tile(rows, expert=expert):
-            units, slope_up, slope_gate, gate, up, down = known[expert]
+            units, slope_up, slope_gate = known[expert]
+            down = downs[expert] if expert < middle else down_buf.at[expert - middle]
             dense = packet[rows, width:].astype(f32)
             at = ids_along((TILE, lanes), 1)
             hit = at == base + expert
@@ -170,8 +185,8 @@
                 hit, high, jnp.where(at == base + expert + half, total - high, 0.0)
             )
             mixed[rows, :] += dot(hidden[expert, rows, :], down[:, mine], NN)
-            token_grad[rows, :] += dot(d_gate[expert, rows, :], gate[...], NT) + dot(
-                d_up[expert, rows, :], up[...], NT
+            token_grad[rows, :] += dot(d_gate[expert, rows, :], gate[expert], NT) + dot(
+                d_up[expert, rows, :], up[expert], NT
             )
 
         over_tiles(tokens, tile)
@@ -229,19 +244,20 @@
     )
 
 
-def grad_out_kernel(packet, hidden, after, grad_down, done, cot_part, out_down, sems):
-    local_experts = hidden.shape[0]
+def grad_out_kernel(first, last, packet, hidden, after, value, *refs):
+    grad_down, done, same, cot_part, out_down, sems = refs[-6:]
+    same[...] = value[...]
     part = cot_part.shape[1]
     cot_part[...] = packet[:, aligned(lax.axis_index("dp"), part)]
     done[...] = jnp.zeros(done.shape, done.dtype)
 
     def place(step):
-        return (step,)
+        return (first + step,)
 
     def body(step, slot):
-        out_down[slot] = dot(hidden[step].T, cot_part[...], NN)
-
-    write_out(local_experts, place, (grad_down,), (out_down,), sems, body)
+        out_down[slot] = dot(hidden[first + step].T, cot_part[...], NN)
+
+    write_out(last - first, place, (grad_down,), (out_down,), sems, body)
 
 
 def reduce_kernel(count, *refs):
@@ -294,6 +310,24 @@
     return pltpu.with_memory_space_constraint(array, pltpu.VMEM)
 
 
+def doubling(size):
+    masks = [1 << bit for bit in reversed(range(size.bit_length() - 1))]
+    order = [0]
+    for mask in masks:
+        order = order + [other ^ mask for other in order]
+    return masks, order
+
+
+def pass_on(held, axis, masks):
+    for mask in masks:
+        names = sorted(name for name in held if name[0] & mask)
+        rows = held[names[0]].shape[0]
+        sent = swap(jnp.concatenate([held.pop(name) for name in names]), axis, mask)
+        for i, (to, source) in enumerate(names):
+            held[to ^ mask, source ^ mask] = sent[i * rows : (i + 1) * rows]
+    return held
+
+
 def cost(flops, moved):
     return pl.CostEstimate(flops=flops, bytes_accessed=moved, transcendentals=0)
 
@@ -316,7 +350,7 @@
     bf16, f32 = jnp.bfloat16, jnp.float32
     struct = jax.ShapeDtypeStruct
     one = 2 * local_experts * width * hidden_units
-    room = 8 + (everyone - TILE) * (2 * part + lanes) * 10 // MIB
+    room = 12 + (everyone - TILE) * (2 * part + lanes) * 10 // MIB
     dummy = struct((8, LANES), f32)
     ids_t = expert_ids.T
     w_gate, w_up, w_down = [in_hbm(w) for w in (w_gate, w_up, w_down)]
@@ -349,8 +383,11 @@
         )(weight, value)
         return [in_vmem(array) for array in loaded], same
 
-    tokens_near = exchange(tokens, "dp", range(1, columns))
-    c_column = jnp.concatenate([packet] + exchange(packet, "dp", range(1, columns)))
+    masks, order = doubling(columns)
+    tokens_near = exchange(tokens, "dp", order[1:])
+    c_column = packet
+    for mask in masks:
+        c_column = jnp.concatenate([c_column, swap(c_column, "dp", mask)])
     ups, own_tokens = load(w_up, own_tokens, "load_up")
     x_column = jnp.concatenate([own_tokens] + tokens_near)
     x_across = exchange(x_column, "expert", chips)
@@ -359,57 +396,53 @@
     x = jnp.concatenate([x_column] + x_across)
     x = jnp.concatenate([x, swap(x, "expert", 1)])
 
-    def gate_up(first, last, value):
-        count = last - first
-        one_expert = [struct((everyone, hidden_units), bf16)] * 3
-        one_expert += [pltpu.VMEM((part, hidden_units), bf16)] * 2
-        one_expert += [pltpu.VMEM(w_down.shape[1:], bf16)]
-        *known, same = pl.pallas_call(
-            functools.partial(gate_up_kernel, first, last),
-            out_shape=one_expert * count + [struct(value.shape, value.dtype)],
-            in_specs=[VMEM] * (2 * count + 1) + [SMEM, HBM, VMEM],
-            out_specs=[VMEM] * (6 * count + 1),
-            scratch_shapes=[pltpu.SemaphoreType.DMA((3 * count,))],
-            cost_estimate=cost(
-                2 * everyone * one * count // local_experts, 2 * one * count // local_experts
-            ),
-            compiler_params=params(room),
-            name="gate_up",
-        )(*gates[first:last], *ups[first:last], x, block_masks, w_down, value)
-        return [in_vmem(a) if i % 6 >= 3 else a for i, a in enumerate(known)], same
-
-    middle = local_experts // 2
-    known, c_column = gate_up(0, middle or local_experts, c_column)
-    if middle:
-        more, _ = gate_up(middle, local_experts, c_column)
-        known = known + more
+    middle = max(local_experts // 2, 1)
+    *known, c_column = pl.pallas_call(
+        functools.partial(gate_up_kernel, local_experts),
+        out_shape=[struct((everyone, hidden_units), bf16)] * (3 * local_experts)
+        + [pltpu.VMEM(w_down.shape[1:], bf16)] * middle
+        + [struct(c_column.shape, bf16)],
+        in_specs=[VMEM] * (2 * local_experts + 1) + [SMEM, HBM, VMEM],
+        out_specs=[VMEM] * (3 * local_experts + middle + 1),
+        scratch_shapes=[pltpu.SemaphoreType.DMA((middle,))],
+        cost_estimate=cost(2 * everyone * one, 2 * one),
+        compiler_params=params(room),
+        name="gate_up",
+    )(*gates, *ups, x, block_masks, w_down, c_column)
+    known, downs = known[: 3 * local_experts], known[3 * local_experts :]
+    downs = [in_vmem(down) for down in downs]
     c_half = jnp.concatenate([c_column] + c_across)
     packets = jnp.concatenate([c_half, swap(c_half, "expert", 1)])
-    x_part = pl.pallas_call(
+    x_part, *parts = pl.pallas_call(
         turn_kernel,
-        out_shape=struct((part, everyone), bf16),
-        in_specs=[VMEM] * 2,
-        out_specs=VMEM,
+        out_shape=[struct((part, everyone), bf16)]
+        + [pltpu.VMEM((local_experts, part, hidden_units), bf16)] * 2,
+        in_specs=[VMEM] * 2 + [HBM] * 2,
+        out_specs=[VMEM] * 3,
+        scratch_shapes=[pltpu.SemaphoreType.DMA((2,))],
         compiler_params=params(room),
         name="turn",
-    )(x, c_half)
+    )(x, c_half, w_gate, w_up)
+    parts = [in_vmem(array) for array in parts]
 
     units = struct((local_experts, everyone, hidden_units), bf16)
     hidden, d_gate, d_up, *partials = pl.pallas_call(
-        functools.partial(hidden_kernel, local_experts, sources),
+        functools.partial(hidden_kernel, local_experts, middle, sources),
         out_shape=[units] * 3
         + [struct((columns * rows, 2 * part + lanes), bf16)] * sources,
-        in_specs=[VMEM] * (1 + len(known)),
+        in_specs=[VMEM] * (3 + len(known) + middle) + [HBM],
         out_specs=[VMEM] * (3 + sources),
         scratch_shapes=[
             pltpu.VMEM((everyone, lanes), f32),
             pltpu.VMEM((everyone, part), f32),
             pltpu.VMEM((everyone, part), f32),
+            pltpu.VMEM((max(local_experts - middle, 1),) + w_down.shape[1:], bf16),
+            pltpu.SemaphoreType.DMA((max(local_experts - middle, 1),)),
         ],
         cost_estimate=cost(2 * everyone * one, 2 * one),
         compiler_params=params(room),
         name="hidden",
-    )(packets, *known)
+    )(packets, *parts, *known, *downs, w_down)
     arrived = [
         swap(partial, "expert", other) if other else partial
         for other, partial in zip(expert_order, partials)
@@ -438,24 +471,38 @@
         compiler_params=params(room),
         name="reduce",
     )(*arrived, ids_t, done_in)
-    blocks = [
-        swap(block, "dp", other) if other else block for other, block in enumerate(blocks)
-    ]
-
-    grad_down, done_out = pl.pallas_call(
-        grad_out_kernel,
-        out_shape=[struct((local_experts, hidden_units, part), f32), dummy],
-        in_specs=[VMEM] * 3,
-        out_specs=[HBM, VMEM],
-        scratch_shapes=[
-            pltpu.VMEM((everyone, part), bf16),
-            pltpu.VMEM((2, hidden_units, part), f32),
-            pltpu.SemaphoreType.DMA((2, 1)),
-        ],
-        cost_estimate=cost(everyone * one // columns, 2 * one // columns),
-        compiler_params=params(room),
-        name="grad_out",
-    )(packets, hidden, done_sum)
+    held = pass_on({(to, 0): block for to, block in zip(order, blocks)}, "dp", masks[:1])
+
+    def grad_out(first, last, value, after, known):
+        return pl.pallas_call(
+            functools.partial(grad_out_kernel, first, last),
+            out_shape=[
+                struct((local_experts, hidden_units, part), f32),
+                dummy,
+                struct(value.shape, value.dtype),
+            ],
+            in_specs=[VMEM] * 4 + [HBM] * len(known),
+            out_specs=[HBM, VMEM, VMEM],
+            scratch_shapes=[
+                pltpu.VMEM((everyone, part), bf16),
+                pltpu.VMEM((2, hidden_units, part), f32),
+                pltpu.SemaphoreType.DMA((2, 1)),
+            ],
+            input_output_aliases={4: 0} if known else {},
+            cost_estimate=cost(
+                everyone * one // columns * (last - first) // local_experts,
+                2 * one // columns * (last - first) // local_experts,
+            ),
+            compiler_params=params(room),
+            name="grad_out",
+        )(packets, hidden, after, value, *known)
+
+    later = (masks[-1], 0)
+    grad_down, done_out, held[later] = grad_out(0, middle, held[later], done_sum, [])
+    held = pass_on(held, "dp", masks[1:])
+    if middle < local_experts:
+        grad_down, done_out, _ = grad_out(middle, local_experts, done_out, done_out, [grad_down])
+    blocks = [held[0, other] for other in range(columns)]
 
     mixed, token_grad = pl.pallas_call(
         functools.partial(join_kernel, columns),

time: 65.1 us -> 72.9 us (1.12)
  Pallas kernels: 39 us -> 45.3 us
  starting transfers between devices: 20 us -> 17.4 us
  waiting for transfers between devices: 4.59 us -> 7.02 us
  local copies, waits for them, and re-layouts: 0.3 us -> 1.97 us
    pallas_call x5, Pallas kernels: 21 us -> 27.3 us  [the longest x1 10.2 us: per_device(): pl.pallas_call(functools.partial(gate_up_kernel, local_experts), out_shap...]
    ppermute x16 -> x14, starting transfers between devices: 20 us -> 17.4 us  [swap(): return lax.ppermute(value, axis, [(i, i ^ mask) for i in range(size)])]
    ppermute x16 -> x14, waiting for transfers between devices: 4.59 us -> 7.02 us  [swap(): return lax.ppermute(value, axis, [(i, i ^ mask) for i in range(size)])]
    unnamed x13 -> x16, local copies, waits for them, and re-layouts: 0.14 us -> 1.79 us
  transfers between devices with their start and end apart: 16 -> 14, of which waited for: 5 -> 4; matrix products, arithmetic and copies ran while one was open for 0% -> 0% of each run, Pallas kernels for 47% -> 47%
where the time goes in v12:
time: 72.9 us; the launch traced here: 72.7 us
  Pallas kernels  45.3 us (62%)
  starting transfers between devices  17.4 us (24%)
  waiting for transfers between devices  7.02 us (10%)
  local copies, waits for them, and re-layouts  1.97 us (3%)
  between operations  0.92 us (1%)
    ppermute x14, starting transfers between devices, swap(): return lax.ppermute(value, axis, [(i, i ^ mask) for i in range(size)])  17.4 us
    pallas_call x1, Pallas kernels, per_device(): pl.pallas_call(functools.partial(gate_up_kernel, local_experts), out_shap...  10.2 us
    pallas_call x1, Pallas kernels, per_device(): pl.pallas_call(functools.partial(hidden_kernel, local_experts, middle, so...  9.39 us
    pallas_call x2, Pallas kernels, load(): pl.pallas_call(load_kernel, out_shape=[struct(value.shape, bf16)] + [pltp...  9.37 us
    ppermute x14, waiting for transfers between devices, swap(): return lax.ppermute(value, axis, [(i, i ^ mask) for i in range(size)])  7.02 us
    pallas_call x1, Pallas kernels, per_device(): pl.pallas_call(grad_in_kernel, out_shape=[struct((local_experts, part, hi...  6.25 us
    pallas_call x2, Pallas kernels, grad_out(): pl.pallas_call(functools.partial(grad_out_kernel, first, last), out_shape...  4.77 us
    pallas_call x1, Pallas kernels, per_device(): pl.pallas_call(turn_kernel, out_shape=[struct((part, everyone), bf16)] +...  2.89 us
  transfers between devices with their start and end apart: 14, of which 4 were waited for; matrix products, arithmetic and copies ran while one was open for 0% of the time, Pallas kernels for 47%

profile of v12, /device:TPU:0, one launch (start us, length us, event | category | flops | bytes accessed | tf_op | source)
XLA Modules:
  0.0 72.7 jit_solution(5765737096077385036)
XLA Ops:
  0.6 4.1 %collective-permute-start = (bf16[16,2048]{1,0:T(8,128)(2,1)}, bf16[16,2048]{1,0:T(8,128)(2,1)S(1)}, u32[]{:S(2)}, u32[]{:S(2)}) collective-permute-start(bf16[16,2048]{1,0:T(8,128)(2,1)} %tokens.1), channel_id=1, source_target_pairs={{0,2},{1,3},{2,0},{3,1},{4,6},{5,7},{6,4},{7,5},{8,10},{9,11},{10,... | collective-permute-start | bytes 196616 | tf_op jit(solution)/shard_map/ppermute | solution.py:298
  4.7 1.6 %collective-permute-start.1 = (bf16[16,2048]{1,0:T(8,128)(2,1)}, bf16[16,2048]{1,0:T(8,128)(2,1)S(1)}, u32[]{:S(2)}, u32[]{:S(2)}) collective-permute-start(bf16[16,2048]{1,0:T(8,128)(2,1)} %tokens.1), channel_id=1, source_target_pairs={{0,1},{1,0},{2,3},{3,2},{4,5},{5,4},{6,7},{7,6},{8,9},{9,8},{10,11... | collective-permute-start | bytes 196616 | tf_op jit(solution)/shard_map/ppermute | solution.py:298
  6.3 0.0 collective-permute-start.2
  6.3 1.0 %route.1 = (bf16[16,2048]{1,0:T(8,128)(2,1)S(1)}, bf16[16,2176]{1,0:T(8,128)(2,1)S(1)}) custom-call(bf16[16,2048]{1,0:T(8,128)(2,1)} %tokens.1, bf16[16,2048]{1,0:T(8,128)(2,1)} %cotangent.1, s32[8,16]{1,0:T(8,128)} %bitcast.3, bf16[8,16]{1,0:T(8,128)(2,1)} %bitcast.5), custom_call_target="tpu_custom_call" | custom-call | tf_op jit(solution)/shard_map/route/pallas_call | solution.py:358
  7.4 2.0 %collective-permute-start.5 = (bf16[16,2176]{1,0:T(8,128)(2,1)S(1)}, bf16[16,2176]{1,0:T(8,128)(2,1)S(1)}, u32[]{:S(2)}, u32[]{:S(2)}) collective-permute-start(bf16[16,2176]{1,0:T(8,128)(2,1)S(1)} %get-tuple-element.70), channel_id=1, source_target_pairs={{0,2},{1,3},{2,0},{3,1},{4,6},{5,7},{6,4},{7,5},{8,10},{9,11},{10,... | collective-permute-start | bytes 208904 | tf_op jit(solution)/shard_map/ppermute | solution.py:298
  9.3 4.7 %load_up.1 = (bf16[16,2048]{1,0:T(8,128)(2,1)S(1)}, bf16[2048,768]{1,0:T(8,128)(2,1)S(1)}, bf16[2048,768]{1,0:T(8,128)(2,1)S(1)}, bf16[2048,768]{1,0:T(8,128)(2,1)S(1)}, bf16[2048,768]{1,0:T(8,128)(2,1)S(1)}) custom-call(bf16[4,2048,768]{2,1,0:T(8,128)(2,1)} %w_up.1, bf16[16,2048]{1,0:T(8,128)(2,1)S(1)} %get-tuple-element.59.value), custom_call_target="tpu_custom_call" | custom-call | bytes 12582912 | tf_op jit(solution)/shard_map/load_up/pallas_call | solution.py:373
  14.0 0.0 collective-permute-done
  14.1 0.0 collective-permute-done.1
  14.1 0.0 collective-permute-done.2
  14.1 1.6 %collective-permute-start.3 = (bf16[64,2048]{1,0:T(8,128)(2,1)S(1)}, bf16[64,2048]{1,0:T(8,128)(2,1)S(1)}, u32[]{:S(2)}, u32[]{:S(2)}) collective-permute-start(bf16[64,2048]{1,0:T(8,128)(2,1)S(1)} %constant_dynamic-update-slice_fusion.value), channel_id=1, source_target_pairs={{0,8},{4,12},{8,0},{12,4},{1,9},{5,13},{9,1},{13,5},{2,10},{6,14},... | collective-permute-start | bytes 786440 | tf_op jit(solution)/shard_map/ppermute | solution.py:298
  15.7 4.7 %load_gate.1 = (bf16[64,2048]{1,0:T(8,128)(2,1)S(1)}, bf16[2048,768]{1,0:T(8,128)(2,1)S(1)}, bf16[2048,768]{1,0:T(8,128)(2,1)S(1)}, bf16[2048,768]{1,0:T(8,128)(2,1)S(1)}, bf16[2048,768]{1,0:T(8,128)(2,1)S(1)}) custom-call(bf16[4,2048,768]{2,1,0:T(8,128)(2,1)} %w_gate.1, bf16[64,2048]{1,0:T(8,128)(2,1)S(1)} %constant_dynamic-update-slice_fusion.value), custom_call_target="tpu_custom_call" | custom-call | bytes 12582912 | tf_op jit(solution)/shard_map/load_gate/pallas_call | solution.py:373
  20.4 0.0 copy-start
  20.4 1.7 %copy-done = bf16[2048,768]{1,0:T(8,128)(2,1)} copy-done((bf16[2048,768]{1,0:T(8,128)(2,1)}, bf16[2048,768]{1,0:T(8,128)(2,1)S(1)}, u32[]{:S(2)}) %copy-start) | copy-done | bytes 3145752
  22.0 0.0 copy-start.3
  22.1 0.0 collective-permute-done.5
  22.1 2.5 %collective-permute-start.6 = (bf16[32,2176]{1,0:T(8,128)(2,1)S(1)}, bf16[32,2176]{1,0:T(8,128)(2,1)S(1)}, u32[]{:S(2)}, u32[]{:S(2)}) collective-permute-start(bf16[32,2176]{1,0:T(8,128)(2,1)S(1)} %pad_maximum_fusion.1), channel_id=1, source_target_pairs={{0,1},{1,0},{2,3},{3,2},{4,5},{5,4},{6,7},{7,6},{8,9},{9,8},{10,11... | collective-permute-start | bytes 417800 | tf_op jit(solution)/shard_map/ppermute | solution.py:298
  24.6 0.0 collective-permute-done.3
  24.7 0.1 collective-permute-start.4
  24.8 2.9 %collective-permute-done.6 = bf16[32,2176]{1,0:T(8,128)(2,1)S(1)} collective-permute-done((bf16[32,2176]{1,0:T(8,128)(2,1)S(1)}, bf16[32,2176]{1,0:T(8,128)(2,1)S(1)}, u32[]{:S(2)}, u32[]{:S(2)}) %collective-permute-start.6) | collective-permute-done | bytes 139296 | tf_op jit(solution)/shard_map/ppermute | solution.py:298
  27.7 0.6 collective-permute-start.7
  28.3 0.0 collective-permute-done.4
  28.4 0.0 copy-done.3
  28.4 0.0 copy-done.1
  28.4 10.2 %gate_up.1 = (bf16[256,768]{1,0:T(8,128)(2,1)S(1)}, bf16[256,768]{1,0:T(8,128)(2,1)S(1)}, bf16[256,768]{1,0:T(8,128)(2,1)S(1)}, bf16[256,768]{1,0:T(8,128)(2,1)S...) custom-call(bf16[2048,768]{1,0:T(8,128)(2,1)S(1)} %copy-done.1, ...), custom_call_target="tpu_custom_call" | custom-call | flops 6442450944 | bytes 25165824 | tf_op jit(solution)/shard_map/gate_up/pallas_call | solution.py:400
  38.7 0.0 collective-permute-done.7
  38.7 0.1 constant_dynamic-update-slice_fusion.10
  38.7 0.1 collective-permute-start.8
  38.8 2.9 %turn.1 = (bf16[512,256]{1,0:T(8,128)(2,1)S(1)}, bf16[4,512,768]{2,1,0:T(8,128)(2,1)S(1)}, bf16[4,512,768]{2,1,0:T(8,128)(2,1)S(1)}) custom-call(bf16[256,2048]{1,0:T(8,128)(2,1)S(1)} %constant_dynamic-update-slice_fusion.4.refs_8_.x, bf16[128,2176]{1,0:T(8,128)(2,1)S(1)} %get-tuple-element.112.after, bf16[4,2048,768]{2,1,0:T(8,128)(2,1)} %w_gate.1, ...), custom_call_target="tpu_custom_call" | custom-call | tf_op jit(solution)/shard_map/turn/pallas_call | solution.py:416
  41.7 0.0 collective-permute-done.8
  41.7 0.1 constant_dynamic-update-slice_fusion.12.refs_0_.packet
  41.8 9.4 %hidden.1 = (bf16[4,256,768]{2,1,0:T(8,128)(2,1)S(1)}, bf16[4,256,768]{2,1,0:T(8,128)(2,1)S(1)}, bf16[4,256,768]{2,1,0:T(8,128)(2,1)S(1)}, bf16[64,1152]{1,0:T(8...) custom-call(bf16[256,2176]{1,0:T(8,128)(2,1)S(1)} %constant_dynamic-update-, ...), custom_call_target="tpu_custom_call" | custom-call | flops 6442450944 | bytes 25165824 | tf_op jit(solution)/shard_map/hidden/pallas_call | solution.py:429
  51.2 0.0 copy-start.2
  51.2 0.6 collective-permute-start.10
  51.7 1.2 %collective-permute-start.11 = (bf16[64,1152]{1,0:T(8,128)(2,1)S(1)}, bf16[64,1152]{1,0:T(8,128)(2,1)S(1)}, u32[]{:S(2)}, u32[]{:S(2)}) collective-permute-start(bf16[64,1152]{1,0:T(8,128)(2,1)S(1)} %get-tuple-element.91), channel_id=1, source_target_pairs={{0,12},{4,8},{8,4},{12,0},{1,13},{5,9},{9,5},{13,1},{2,14},{6,10},... | collective-permute-start | bytes 442376 | tf_op jit(solution)/shard_map/ppermute | solution.py:298
  52.9 0.5 collective-permute-start.9
  53.4 6.2 %grad_in.1 = (f32[4,512,768]{2,1,0:T(8,128)}, f32[4,512,768]{2,1,0:T(8,128)}, f32[8,128]{1,0:T(8,128)S(1)}) custom-call(bf16[512,256]{1,0:T(8,128)(2,1)S(1)} %get-tuple-element.92.x_part, bf16[4,256,768]{2,1,0:T(8,128)(2,1)S(1)} %get-tuple-element.93.d_gate, bf16[4,256,768]{2,1,0:T(8,128)(2,1)S(1)} %get-tuple-element.94.d_up), custom_call_target="tpu_custom_call" | custom-call | flops 1610612736 | bytes 12582912 | tf_op jit(solution)/shard_map/grad_in/pallas_call | solution.py:451
  59.7 0.0 collective-permute-done.10.refs_2_
  59.7 0.0 collective-permute-done.11.refs_3_
  59.7 1.3 %collective-permute-done.9.refs_1_ = bf16[64,1152]{1,0:T(8,128)(2,1)S(1)} collective-permute-done((bf16[64,1152]{1,0:T(8,128)(2,1)S(1)}, bf16[64,1152]{1,0:T(8,128)(2,1)S(1)}, u32[]{:S(2)}, u32[]{:S(2)}) %collective-permute-start.9) | collective-permute-done | bytes 147488 | tf_op jit(solution)/shard_map/ppermute | solution.py:298
  61.0 0.0 copy-done.2
  61.0 0.8 %reduce.1 = (f32[8,16]{1,0:T(8,128)}, bf16[16,1024]{1,0:T(8,128)(2,1)S(1)}, bf16[16,1024]{1,0:T(8,128)(2,1)S(1)}, bf16[16,1024]{1,0:T(8,128)(2,1)S(1)}, bf16[16,...) custom-call(bf16[64,1152]{1,0:T(8,128)(2,1)S(1)} %get-tuple-element.88.refs_0_, ...), custom_call_target="tpu_custom_call" | custom-call | tf_op jit(solution)/shard_map/reduce/pallas_call | solution.py:466
  61.8 1.2 %collective-permute-start.12 = (bf16[32,1024]{1,0:T(8,128)(2,1)S(1)}, bf16[32,1024]{1,0:T(8,128)(2,1)S(1)}, u32[]{:S(2)}, u32[]{:S(2)}) collective-permute-start(bf16[32,1024]{1,0:T(8,128)(2,1)S(1)} %pad_maximum_fusion.2), channel_id=1, source_target_pairs={{0,2},{1,3},{2,0},{3,1},{4,6},{5,7},{6,4},{7,5},{8,10},{9,11},{10,... | collective-permute-start | bytes 196616 | tf_op jit(solution)/shard_map/ppermute | solution.py:298
  63.0 2.1 %grad_out.2 = (f32[4,768,512]{2,1,0:T(8,128)}, f32[8,128]{1,0:T(8,128)S(1)}, bf16[16,1024]{1,0:T(8,128)(2,1)S(1)}) custom-call(bf16[256,2176]{1,0:T(8,128)(2,1)S(1)} %constant_dynamic-update-slice_fusion.12.refs_0_.packet, bf16[4,256,768]{2,1,0:T(8,128)(2,1)S(1)} %get-tuple-element.97.hidden, f32[8,128]{1,0:T(8,128)S(1)} %get-tuple-element.98.after, ...), custom_call_target="tpu_custom_call" | custom-call | flops 402653184 | bytes 3145728 | tf_op jit(solution)/shard_map/grad_out/pallas_call | solution.py:477
  65.1 2.6 %collective-permute-done.12 = bf16[32,1024]{1,0:T(8,128)(2,1)S(1)} collective-permute-done((bf16[32,1024]{1,0:T(8,128)(2,1)S(1)}, bf16[32,1024]{1,0:T(8,128)(2,1)S(1)}, u32[]{:S(2)}, u32[]{:S(2)}) %collective-permute-start.12) | collective-permute-done | bytes 65568 | tf_op jit(solution)/shard_map/ppermute | solution.py:298
  67.7 1.4 %collective-permute-start.13 = (bf16[32,1024]{1,0:T(8,128)(2,1)S(1)}, bf16[32,1024]{1,0:T(8,128)(2,1)S(1)}, u32[]{:S(2)}, u32[]{:S(2)}) collective-permute-start(bf16[32,1024]{1,0:T(8,128)(2,1)S(1)} %pad_maximum_fusion.3), channel_id=1, source_target_pairs={{0,1},{1,0},{2,3},{3,2},{4,5},{5,4},{6,7},{7,6},{8,9},{9,8},{10,11... | collective-permute-start | bytes 196616 | tf_op jit(solution)/shard_map/ppermute | solution.py:298
  69.1 2.7 %grad_out.3 = (f32[4,768,512]{2,1,0:T(8,128)}, f32[8,128]{1,0:T(8,128)S(1)}, f32[8,128]{1,0:T(8,128)}) custom-call(bf16[256,2176]{1,0:T(8,128)(2,1)S(1)} %constant_dynamic-update-slice_fusion.12.refs_0_.packet, bf16[4,256,768]{2,1,0:T(8,128)(2,1)S(1)} %get-tuple-element.97.hidden, ...), custom_call_target="tpu_custom_call", output_to_operand_aliasing={{0}: (4, {})} | custom-call | flops 402653184 | bytes 3145728 | tf_op jit(solution)/shard_map/grad_out/pallas_call | solution.py:477
  71.8 0.2 collective-permute-done.13
  72.0 0.7 join.1
  (18 shorter events, 0.2 us)
Async XLA Ops:
  0.6 13.4 %collective-permute-start = (bf16[16,2048]{1,0:T(8,128)(2,1)}, bf16[16,2048]{1,0:T(8,128)(2,1)S(1)}, u32[]{:S(2)}, u32[]{:S(2)}) collective-permute-start(bf16[16,2048]{1,0:T(8,128)(2,1)} %tokens.1), channel_id=1, source_target_pairs={{0,2},{1,3},{2,0},{3,1},{4,6},{5,7},{6,4},{7,5},{8,10},{9,11},{10,... | collective-permute-start | bytes 196616 | tf_op jit(solution)/shard_map/ppermute | solution.py:298
  4.7 9.3 %collective-permute-start.1 = (bf16[16,2048]{1,0:T(8,128)(2,1)}, bf16[16,2048]{1,0:T(8,128)(2,1)S(1)}, u32[]{:S(2)}, u32[]{:S(2)}) collective-permute-start(bf16[16,2048]{1,0:T(8,128)(2,1)} %tokens.1), channel_id=1, source_target_pairs={{0,1},{1,0},{2,3},{3,2},{4,5},{5,4},{6,7},{7,6},{8,9},{9,8},{10,11... | collective-permute-start | bytes 196616 | tf_op jit(solution)/shard_map/ppermute | solution.py:298
  6.3 7.8 %collective-permute-start.2 = (bf16[16,2048]{1,0:T(8,128)(2,1)}, bf16[16,2048]{1,0:T(8,128)(2,1)S(1)}, u32[]{:S(2)}, u32[]{:S(2)}) collective-permute-start(bf16[16,2048]{1,0:T(8,128)(2,1)} %tokens.1), channel_id=1, source_target_pairs={{0,3},{1,2},{2,1},{3,0},{4,7},{5,6},{6,5},{7,4},{8,11},{9,10},{10,... | collective-permute-start | bytes 196616 | tf_op jit(solution)/shard_map/ppermute | solution.py:298
  7.4 14.7 %collective-permute-start.5 = (bf16[16,2176]{1,0:T(8,128)(2,1)S(1)}, bf16[16,2176]{1,0:T(8,128)(2,1)S(1)}, u32[]{:S(2)}, u32[]{:S(2)}) collective-permute-start(bf16[16,2176]{1,0:T(8,128)(2,1)S(1)} %get-tuple-element.70), channel_id=1, source_target_pairs={{0,2},{1,3},{2,0},{3,1},{4,6},{5,7},{6,4},{7,5},{8,10},{9,11},{10,... | collective-permute-start | bytes 208904 | tf_op jit(solution)/shard_map/ppermute | solution.py:298
  14.1 10.5 %collective-permute-start.3 = (bf16[64,2048]{1,0:T(8,128)(2,1)S(1)}, bf16[64,2048]{1,0:T(8,128)(2,1)S(1)}, u32[]{:S(2)}, u32[]{:S(2)}) collective-permute-start(bf16[64,2048]{1,0:T(8,128)(2,1)S(1)} %constant_dynamic-update-slice_fusion.value), channel_id=1, source_target_pairs={{0,8},{4,12},{8,0},{12,4},{1,9},{5,13},{9,1},{13,5},{2,10},{6,14},... | collective-permute-start | bytes 786440 | tf_op jit(solution)/shard_map/ppermute | solution.py:298
  20.4 1.7 %copy-start = (bf16[2048,768]{1,0:T(8,128)(2,1)}, bf16[2048,768]{1,0:T(8,128)(2,1)S(1)}, u32[]{:S(2)}) copy-start(bf16[2048,768]{1,0:T(8,128)(2,1)S(1)} %get-tuple-element.61.refs_0_) | copy-start | bytes 9437188
  22.0 6.3 %copy-start.3 = (s32[4,6]{1,0:T(4,128)S(1)}, s32[4,6]{1,0:T(4,128)}, u32[]{:S(2)}) copy-start(s32[4,6]{1,0:T(4,128)} %refs_9_.1) | copy-start | bytes 292
  22.0 6.3 %copy-start.1 = (bf16[2048,768]{1,0:T(8,128)(2,1)S(1)}, bf16[2048,768]{1,0:T(8,128)(2,1)}, u32[]{:S(2)}) copy-start(bf16[2048,768]{1,0:T(8,128)(2,1)} %copy-done) | copy-start | bytes 9437188
  22.1 5.6 %collective-permute-start.6 = (bf16[32,2176]{1,0:T(8,128)(2,1)S(1)}, bf16[32,2176]{1,0:T(8,128)(2,1)S(1)}, u32[]{:S(2)}, u32[]{:S(2)}) collective-permute-start(bf16[32,2176]{1,0:T(8,128)(2,1)S(1)} %pad_maximum_fusion.1), channel_id=1, source_target_pairs={{0,1},{1,0},{2,3},{3,2},{4,5},{5,4},{6,7},{7,6},{8,9},{9,8},{10,11... | collective-permute-start | bytes 417800 | tf_op jit(solution)/shard_map/ppermute | solution.py:298
  24.7 3.6 %collective-permute-start.4 = (bf16[128,2048]{1,0:T(8,128)(2,1)S(1)}, bf16[128,2048]{1,0:T(8,128)(2,1)S(1)}, u32[]{:S(2)}, u32[]{:S(2)}) collective-permute-start(bf16[128,2048]{1,0:T(8,128)(2,1)S(1)} %pad_maximum_fusion), channel_id=1, source_target_pairs={{0,4},{4,0},{8,12},{12,8},{1,5},{5,1},{9,13},{13,9},{2,6},{6,2},{1... | collective-permute-start | bytes 1572872 | tf_op jit(solution)/shard_map/ppermute | solution.py:298
  27.7 11.0 %collective-permute-start.7 = (bf16[64,2176]{1,0:T(8,128)(2,1)S(1)}, bf16[64,2176]{1,0:T(8,128)(2,1)S(1)}, u32[]{:S(2)}, u32[]{:S(2)}) collective-permute-start(bf16[64,2176]{1,0:T(8,128)(2,1)S(1)} %constant_dynamic-update-slice_fusion.7.refs_11_), channel_id=1, source_target_pairs={{0,8},{4,12},{8,0},{12,4},{1,9},{5,13},{9,1},{13,5},{2,10},{6,14},... | collective-permute-start | bytes 835592 | tf_op jit(solution)/shard_map/ppermute | solution.py:298
  38.7 3.0 %collective-permute-start.8 = (bf16[128,2176]{1,0:T(8,128)(2,1)S(1)}, bf16[128,2176]{1,0:T(8,128)(2,1)S(1)}, u32[]{:S(2)}, u32[]{:S(2)}) collective-permute-start(bf16[128,2176]{1,0:T(8,128)(2,1)S(1)} %get-tuple-element.112.after), channel_id=1, source_target_pairs={{0,4},{4,0},{8,12},{12,8},{1,5},{5,1},{9,13},{13,9},{2,6},{6,2},{1... | collective-permute-start | bytes 1671176 | tf_op jit(solution)/shard_map/ppermute | solution.py:298
  51.2 9.9 %copy-start.2 = (s32[16,8]{0,1:T(8,128)S(1)}, s32[16,8]{0,1:T(8,128)}, u32[]{:S(2)}) copy-start(s32[16,8]{0,1:T(8,128)} %param.10) | copy-start | bytes 1540
  51.2 8.5 %collective-permute-start.10 = (bf16[64,1152]{1,0:T(8,128)(2,1)S(1)}, bf16[64,1152]{1,0:T(8,128)(2,1)S(1)}, u32[]{:S(2)}, u32[]{:S(2)}) collective-permute-start(bf16[64,1152]{1,0:T(8,128)(2,1)S(1)} %get-tuple-element.90), channel_id=1, source_target_pairs={{0,4},{4,0},{8,12},{12,8},{1,5},{5,1},{9,13},{13,9},{2,6},{6,2},{1... | collective-permute-start | bytes 442376 | tf_op jit(solution)/shard_map/ppermute | solution.py:298
  51.7 8.0 %collective-permute-start.11 = (bf16[64,1152]{1,0:T(8,128)(2,1)S(1)}, bf16[64,1152]{1,0:T(8,128)(2,1)S(1)}, u32[]{:S(2)}, u32[]{:S(2)}) collective-permute-start(bf16[64,1152]{1,0:T(8,128)(2,1)S(1)} %get-tuple-element.91), channel_id=1, source_target_pairs={{0,12},{4,8},{8,4},{12,0},{1,13},{5,9},{9,5},{13,1},{2,14},{6,10},... | collective-permute-start | bytes 442376 | tf_op jit(solution)/shard_map/ppermute | solution.py:298
  52.9 8.1 %collective-permute-start.9 = (bf16[64,1152]{1,0:T(8,128)(2,1)S(1)}, bf16[64,1152]{1,0:T(8,128)(2,1)S(1)}, u32[]{:S(2)}, u32[]{:S(2)}) collective-permute-start(bf16[64,1152]{1,0:T(8,128)(2,1)S(1)} %get-tuple-element.89), channel_id=1, source_target_pairs={{0,8},{4,12},{8,0},{12,4},{1,9},{5,13},{9,1},{13,5},{2,10},{6,14},... | collective-permute-start | bytes 442376 | tf_op jit(solution)/shard_map/ppermute | solution.py:298
  61.8 5.9 %collective-permute-start.12 = (bf16[32,1024]{1,0:T(8,128)(2,1)S(1)}, bf16[32,1024]{1,0:T(8,128)(2,1)S(1)}, u32[]{:S(2)}, u32[]{:S(2)}) collective-permute-start(bf16[32,1024]{1,0:T(8,128)(2,1)S(1)} %pad_maximum_fusion.2), channel_id=1, source_target_pairs={{0,2},{1,3},{2,0},{3,1},{4,6},{5,7},{6,4},{7,5},{8,10},{9,11},{10,... | collective-permute-start | bytes 196616 | tf_op jit(solution)/shard_map/ppermute | solution.py:298
  67.7 4.3 %collective-permute-start.13 = (bf16[32,1024]{1,0:T(8,128)(2,1)S(1)}, bf16[32,1024]{1,0:T(8,128)(2,1)S(1)}, u32[]{:S(2)}, u32[]{:S(2)}) collective-permute-start(bf16[32,1024]{1,0:T(8,128)(2,1)S(1)} %pad_maximum_fusion.3), channel_id=1, source_target_pairs={{0,1},{1,0},{2,3},{3,2},{4,5},{5,4},{6,7},{7,6},{8,9},{9,8},{10,11... | collective-permute-start | bytes 196616 | tf_op jit(solution)/shard_map/ppermute | solution.py:298

commit v13 on v11

--- a/solution.py
+++ b/solution.py
@@ -84,44 +84,73 @@
         lax.fori_loop(0, tokens // TILE, turn, 0)
 
 
-def gate_up_kernel(first, last, *refs):
+def load_slices(weights, targets, sems):
+    mine = aligned(lax.axis_index("dp"), targets[0].shape[0])
+    copies = [
+        pltpu.make_async_copy(weight.at[mine, :], target, sems.at[i])
+        for i, (weight, target) in enumerate(zip(weights, targets))
+    ]
+    for copy in copies:
+        copy.start()
+    return copies
+
+
+def load_downs(w_down, targets, first, sems):
+    copies = [
+        pltpu.make_async_copy(w_down.at[first + i], target, sems.at[i])
+        for i, target in enumerate(targets)
+    ]
+    for copy in copies:
+        copy.start()
+    return copies
+
+
+def gate_kernel(count, *refs):
+    gates, x, w_down, refs = refs[:count], refs[count], refs[count + 1], refs[count + 2 :]
+    products, parts, downs = refs[:count], refs[count : 2 * count], refs[2 * count : -2]
+    loads = load_downs(w_down, downs, 0, refs[-1]) + load_slices(gates, parts, refs[-2])
+
+    def tile(rows):
+        for gate, product in zip(gates, products):
+            for start in range(0, product.shape[1], CHUNK):
+                cols = slice(start, start + CHUNK)
+                product[rows, cols] = dot(x[rows, :], gate[:, cols], NN)
+
+    over_tiles(x.shape[0], tile)
+    for load in loads:
+        load.wait()
+
+
+def up_kernel(first, last, start_down, *refs):
     count = last - first
-    gates, ups, refs = refs[:count], refs[count : 2 * count], refs[2 * count :]
+    products, ups, refs = refs[:count], refs[count : 2 * count], refs[2 * count :]
     x, masks, w_down, value = refs[:4]
-    known, (same, sems) = refs[4:-2], refs[-2:]
-    hidden_units = gates[0].shape[1]
+    known, parts, refs = refs[4 : 4 + 3 * count], refs[4 + 3 * count : 4 + 4 * count], refs[4 + 4 * count :]
+    downs, (same, part_sems, down_sems) = refs[:-3], refs[-3:]
     bf16 = jnp.bfloat16
-    hiddens, slope_ups, slope_gates, gate_parts, up_parts, downs = [known[k::6] for k in range(6)]
-    mine = aligned(lax.axis_index("dp"), gate_parts[0].shape[0])
-    loads = []
-    for i in range(count):
-        loads += [
-            pltpu.make_async_copy(w_down.at[first + i], downs[i], sems.at[3 * i]),
-            pltpu.make_async_copy(gates[i].at[mine, :], gate_parts[i], sems.at[3 * i + 1]),
-            pltpu.make_async_copy(ups[i].at[mine, :], up_parts[i], sems.at[3 * i + 2]),
-        ]
-    for load in loads:
-        load.start()
+    hidden_units = ups[0].shape[1]
+    loads = load_downs(w_down, downs, start_down, down_sems) + load_slices(ups, parts, part_sems)
     same[...] = value[...]
 
     def tile(rows):
         for i in range(count):
+            hidden, slope_up, slope_gate = known[3 * i : 3 * i + 3]
             for start in range(0, hidden_units, CHUNK):
                 cols = slice(start, start + CHUNK)
-                gate_pre = dot(x[rows, :], gates[i][:, cols], NN)
                 up_proj = dot(x[rows, :], ups[i][:, cols], NN)
                 at = ids_along((1, CHUNK), 1)
                 keep = jnp.zeros((1, CHUNK), jnp.float32)
                 for j in range(CHUNK // BLK):
                     kept = masks[first + i, start // BLK + j].astype(jnp.float32)
                     keep = jnp.where(at // BLK == j, kept, keep)
+                gate_pre = products[i][rows, cols]
                 sigma = 0.5 + 0.5 * jnp.tanh(0.5 * gate_pre)
                 silu = gate_pre * sigma
                 up_kept = up_proj * keep
-                hiddens[i][rows, cols] = (silu * up_kept).astype(bf16)
-                slope_ups[i][rows, cols] = (silu * keep).astype(bf16)
+                hidden[rows, cols] = (silu * up_kept).astype(bf16)
+                slope_up[rows, cols] = (silu * keep).astype(bf16)
                 slope = up_kept * (sigma + silu * (1.0 - sigma))
-                slope_gates[i][rows, cols] = slope.astype(bf16)
+                slope_gate[rows, cols] = slope.astype(bf16)
 
     over_tiles(x.shape[0], tile)
     for load in loads:
@@ -359,30 +388,61 @@
     x = jnp.concatenate([x_column] + x_across)
     x = jnp.concatenate([x, swap(x, "expert", 1)])
 
-    def gate_up(first, last, value):
-        count = last - first
-        one_expert = [struct((everyone, hidden_units), bf16)] * 3
-        one_expert += [pltpu.VMEM((part, hidden_units), bf16)] * 2
-        one_expert += [pltpu.VMEM(w_down.shape[1:], bf16)]
-        *known, same = pl.pallas_call(
-            functools.partial(gate_up_kernel, first, last),
-            out_shape=one_expert * count + [struct(value.shape, value.dtype)],
+    middle = max(local_experts // 2, 1)
+    weight_part = pltpu.VMEM((part, hidden_units), bf16)
+    weight_down = pltpu.VMEM(w_down.shape[1:], bf16)
+    found = pl.pallas_call(
+        functools.partial(gate_kernel, local_experts),
+        out_shape=[struct((everyone, hidden_units), f32)] * local_experts
+        + [weight_part] * local_experts
+        + [weight_down] * middle,
+        in_specs=[VMEM] * (local_experts + 1) + [HBM],
+        out_specs=[VMEM] * (2 * local_experts + middle),
+        scratch_shapes=[
+            pltpu.SemaphoreType.DMA((local_experts,)),
+            pltpu.SemaphoreType.DMA((middle,)),
+        ],
+        cost_estimate=cost(everyone * one, one),
+        compiler_params=params(room),
+        name="gate",
+    )(*gates, x, w_down)
+    found = list(found)
+    products = found[:local_experts]
+    gate_parts = [in_vmem(array) for array in found[local_experts : 2 * local_experts]]
+    downs = [in_vmem(array) for array in found[2 * local_experts :]]
+
+    def up_call(first, last, start_down, value):
+        count, more = last - first, local_experts - start_down
+        found = pl.pallas_call(
+            functools.partial(up_kernel, first, last, start_down),
+            out_shape=[struct((everyone, hidden_units), bf16)] * (3 * count)
+            + [weight_part] * count
+            + [weight_down] * more
+            + [struct(value.shape, value.dtype)],
             in_specs=[VMEM] * (2 * count + 1) + [SMEM, HBM, VMEM],
-            out_specs=[VMEM] * (6 * count + 1),
-            scratch_shapes=[pltpu.SemaphoreType.DMA((3 * count,))],
+            out_specs=[VMEM] * (4 * count + more + 1),
+            scratch_shapes=[
+                pltpu.SemaphoreType.DMA((count,)),
+                pltpu.SemaphoreType.DMA((max(more, 1),)),
+            ],
             cost_estimate=cost(
-                2 * everyone * one * count // local_experts, 2 * one * count // local_experts
+                everyone * one * count // local_experts, one * count // local_experts
             ),
             compiler_params=params(room),
-            name="gate_up",
-        )(*gates[first:last], *ups[first:last], x, block_masks, w_down, value)
-        return [in_vmem(a) if i % 6 >= 3 else a for i, a in enumerate(known)], same
-
-    middle = local_experts // 2
-    known, c_column = gate_up(0, middle or local_experts, c_column)
-    if middle:
-        more, _ = gate_up(middle, local_experts, c_column)
-        known = known + more
+            name="up",
+        )(*products[first:last], *ups[first:last], x, block_masks, w_down, value)
+        found = list(found)
+        arrays = [in_vmem(array) for array in found[3 * count : -1]]
+        return found[: 3 * count], arrays[:count], arrays[count:], found[-1]
+
+    factors, up_parts, more_downs, c_column = up_call(0, middle, middle, c_column)
+    downs = downs + more_downs
+    if middle < local_experts:
+        more, more_parts, _, _ = up_call(middle, local_experts, local_experts, c_column)
+        factors, up_parts = factors + more, up_parts + more_parts
+    known = []
+    for i in range(local_experts):
+        known += factors[3 * i : 3 * i + 3] + [gate_parts[i], up_parts[i], downs[i]]
     c_half = jnp.concatenate([c_column] + c_across)
     packets = jnp.concatenate([c_half, swap(c_half, "expert", 1)])
     x_part = pl.pallas_call(

time: 65.1 us -> 64.1 us (0.985)
  waiting for transfers between devices: 4.59 us -> 2.63 us
    ppermute x16, waiting for transfers between devices: 4.59 us -> 2.63 us  [swap(): return lax.ppermute(value, axis, [(i, i ^ mask) for i in range(size)])]
    pallas_call x2 -> x3, Pallas kernels: 10.2 us -> 11 us  [the longest x2 7.29 us: up_call(): pl.pallas_call(functools.partial(up_kernel, first, last, start_down), out...]
  transfers between devices with their start and end apart: 16 -> 16, of which waited for: 5 -> 4; matrix products, arithmetic and copies ran while one was open for 0% -> 0% of each run, Pallas kernels for 47% -> 49%
where the time goes in v13:
time: 64.1 us; the launch traced here: 64 us
  Pallas kernels  39.6 us (62%)
  starting transfers between devices  20.4 us (32%)
  waiting for transfers between devices  2.63 us (4%)
  between operations  0.94 us (1%)
    ppermute x16, starting transfers between devices, swap(): return lax.ppermute(value, axis, [(i, i ^ mask) for i in range(size)])  20.4 us
    pallas_call x2, Pallas kernels, load(): pl.pallas_call(load_kernel, out_shape=[struct(value.shape, bf16)] + [pltp...  9.37 us
    pallas_call x2, Pallas kernels, up_call(): pl.pallas_call(functools.partial(up_kernel, first, last, start_down), out...  7.29 us
    pallas_call x1, Pallas kernels, per_device(): pl.pallas_call(functools.partial(hidden_kernel, local_experts, sources),...  6.81 us
    pallas_call x1, Pallas kernels, per_device(): pl.pallas_call(grad_in_kernel, out_shape=[struct((local_experts, part, hi...  6.25 us
    pallas_call x1, Pallas kernels, per_device(): pl.pallas_call(functools.partial(gate_kernel, local_experts), out_shape=[...  3.7 us
    pallas_call x1, Pallas kernels, per_device(): pl.pallas_call(grad_out_kernel, out_shape=[struct((local_experts, hidden_...  3.62 us
    ppermute x16, waiting for transfers between devices, swap(): return lax.ppermute(value, axis, [(i, i ^ mask) for i in range(size)])  2.63 us
  transfers between devices with their start and end apart: 16, of which 4 were waited for; matrix products, arithmetic and copies ran while one was open for 0% of the time, Pallas kernels for 49%

profile of v13, /device:TPU:0, one launch (start us, length us, event | category | flops | bytes accessed | tf_op | source)
XLA Modules:
  0.0 64.0 jit_solution(13706632588250821138)
XLA Ops:
  0.6 3.1 %collective-permute-start = (bf16[16,2048]{1,0:T(8,128)(2,1)}, bf16[16,2048]{1,0:T(8,128)(2,1)S(1)}, u32[]{:S(2)}, u32[]{:S(2)}) collective-permute-start(bf16[16,2048]{1,0:T(8,128)(2,1)} %tokens.1), channel_id=1, source_target_pairs={{0,1},{1,0},{2,3},{3,2},{4,5},{5,4},{6,7},{7,6},{8,9},{9,8},{10,11... | collective-permute-start | bytes 196616 | tf_op jit(solution)/shard_map/ppermute | solution.py:311
  3.7 2.6 %collective-permute-start.1 = (bf16[16,2048]{1,0:T(8,128)(2,1)}, bf16[16,2048]{1,0:T(8,128)(2,1)S(1)}, u32[]{:S(2)}, u32[]{:S(2)}) collective-permute-start(bf16[16,2048]{1,0:T(8,128)(2,1)} %tokens.1), channel_id=1, source_target_pairs={{0,2},{1,3},{2,0},{3,1},{4,6},{5,7},{6,4},{7,5},{8,10},{9,11},{10,... | collective-permute-start | bytes 196616 | tf_op jit(solution)/shard_map/ppermute | solution.py:311
  6.3 0.0 collective-permute-start.2
  6.3 1.0 %route.1 = (bf16[16,2048]{1,0:T(8,128)(2,1)S(1)}, bf16[16,2176]{1,0:T(8,128)(2,1)S(1)}) custom-call(bf16[16,2048]{1,0:T(8,128)(2,1)} %tokens.1, bf16[16,2048]{1,0:T(8,128)(2,1)} %cotangent.1, s32[8,16]{1,0:T(8,128)} %bitcast.3, bf16[8,16]{1,0:T(8,128)(2,1)} %bitcast.5), custom_call_target="tpu_custom_call" | custom-call | tf_op jit(solution)/shard_map/route/pallas_call | solution.py:353
  7.4 1.0 %collective-permute-start.5 = (bf16[16,2176]{1,0:T(8,128)(2,1)S(1)}, bf16[16,2176]{1,0:T(8,128)(2,1)S(1)}, u32[]{:S(2)}, u32[]{:S(2)}) collective-permute-start(bf16[16,2176]{1,0:T(8,128)(2,1)S(1)} %get-tuple-element.78), channel_id=1, source_target_pairs={{0,1},{1,0},{2,3},{3,2},{4,5},{5,4},{6,7},{7,6},{8,9},{9,8},{10,11... | collective-permute-start | bytes 208904 | tf_op jit(solution)/shard_map/ppermute | solution.py:311
  8.3 3.5 %collective-permute-start.6 = (bf16[16,2176]{1,0:T(8,128)(2,1)S(1)}, bf16[16,2176]{1,0:T(8,128)(2,1)S(1)}, u32[]{:S(2)}, u32[]{:S(2)}) collective-permute-start(bf16[16,2176]{1,0:T(8,128)(2,1)S(1)} %get-tuple-element.78), channel_id=1, source_target_pairs={{0,2},{1,3},{2,0},{3,1},{4,6},{5,7},{6,4},{7,5},{8,10},{9,11},{10,... | collective-permute-start | bytes 208904 | tf_op jit(solution)/shard_map/ppermute | solution.py:311
  11.8 4.7 %load_up.1 = (bf16[16,2048]{1,0:T(8,128)(2,1)S(1)}, bf16[2048,768]{1,0:T(8,128)(2,1)S(1)}, bf16[2048,768]{1,0:T(8,128)(2,1)S(1)}, bf16[2048,768]{1,0:T(8,128)(2,1)S(1)}, bf16[2048,768]{1,0:T(8,128)(2,1)S(1)}) custom-call(bf16[4,2048,768]{2,1,0:T(8,128)(2,1)} %weight.2, bf16[16,2048]{1,0:T(8,128)(2,1)S(1)} %get-tuple-element.67.value), custom_call_target="tpu_custom_call" | custom-call | bytes 12582912 | tf_op jit(solution)/shard_map/load_up/pallas_call | solution.py:368
  16.5 0.0 collective-permute-done
  16.5 0.1 collective-permute-start.7
  16.6 0.0 collective-permute-done.1
  16.6 0.0 collective-permute-done.2
  16.7 1.8 %collective-permute-start.3 = (bf16[64,2048]{1,0:T(8,128)(2,1)S(1)}, bf16[64,2048]{1,0:T(8,128)(2,1)S(1)}, u32[]{:S(2)}, u32[]{:S(2)}) collective-permute-start(bf16[64,2048]{1,0:T(8,128)(2,1)S(1)} %constant_dynamic-update-slice_fusion.value), channel_id=1, source_target_pairs={{0,8},{4,12},{8,0},{12,4},{1,9},{5,13},{9,1},{13,5},{2,10},{6,14},... | collective-permute-start | bytes 786440 | tf_op jit(solution)/shard_map/ppermute | solution.py:311
  18.4 4.7 %load_gate.1 = (bf16[64,2048]{1,0:T(8,128)(2,1)S(1)}, bf16[2048,768]{1,0:T(8,128)(2,1)S(1)}, bf16[2048,768]{1,0:T(8,128)(2,1)S(1)}, bf16[2048,768]{1,0:T(8,128)(2,1)S(1)}, bf16[2048,768]{1,0:T(8,128)(2,1)S(1)}) custom-call(bf16[4,2048,768]{2,1,0:T(8,128)(2,1)} %weight.3, bf16[64,2048]{1,0:T(8,128)(2,1)S(1)} %constant_dynamic-update-slice_fusion.value), custom_call_target="tpu_custom_call" | custom-call | bytes 12582912 | tf_op jit(solution)/shard_map/load_gate/pallas_call | solution.py:368
  23.1 0.0 collective-permute-done.5
  23.2 0.0 collective-permute-done.6
  23.2 0.2 collective-permute-done.3
  23.4 0.1 collective-permute-start.4
  23.5 0.0 collective-permute-done.7
  23.5 1.6 %collective-permute-start.8 = (bf16[64,2176]{1,0:T(8,128)(2,1)S(1)}, bf16[64,2176]{1,0:T(8,128)(2,1)S(1)}, u32[]{:S(2)}, u32[]{:S(2)}) collective-permute-start(bf16[64,2176]{1,0:T(8,128)(2,1)S(1)} %constant_dynamic-update-slice_fusion.7.refs_7_), channel_id=1, source_target_pairs={{0,8},{4,12},{8,0},{12,4},{1,9},{5,13},{9,1},{13,5},{2,10},{6,14},... | collective-permute-start | bytes 835592 | tf_op jit(solution)/shard_map/ppermute | solution.py:311
  25.1 0.3 collective-permute-done.4
  25.5 0.0 copy-start.1
  25.5 3.7 %gate.1 = (f32[256,768]{1,0:T(8,128)S(1)}, f32[256,768]{1,0:T(8,128)S(1)}, f32[256,768]{1,0:T(8,128)S(1)}, f32[256,768]{1,0:T(8,128)S(1)}, bf16[512,768]{1,0:T(8...) custom-call(bf16[2048,768]{1,0:T(8,128)(2,1)S(1)} %get-tuple-element, ...), custom_call_target="tpu_custom_call" | custom-call | flops 3221225472 | bytes 12582912 | tf_op jit(solution)/shard_map/gate/pallas_call | solution.py:394
  29.2 3.5 %up.2 = (bf16[256,768]{1,0:T(8,128)(2,1)S(1)}, bf16[256,768]{1,0:T(8,128)(2,1)S(1)}, bf16[256,768]{1,0:T(8,128)(2,1)S(1)}, bf16[256,768]{1,0:T(8,128)(2,1)S(1)},...) custom-call(f32[256,768]{1,0:T(8,128)S(1)} %get-tuple-element.74.ref, ...), custom_call_target="tpu_custom_call" | custom-call | flops 1610612736 | bytes 6291456 | tf_op jit(solution)/shard_map/up/pallas_call | solution.py:416
  32.7 0.0 collective-permute-done.8
  32.7 0.1 constant_dynamic-update-slice_fusion.11
  32.8 0.2 collective-permute-start.9
  33.0 0.1 turn.1.x_part
  33.1 3.8 %up.3 = (bf16[256,768]{1,0:T(8,128)(2,1)S(1)}, bf16[256,768]{1,0:T(8,128)(2,1)S(1)}, bf16[256,768]{1,0:T(8,128)(2,1)S(1)}, bf16[256,768]{1,0:T(8,128)(2,1)S(1)},...) custom-call(f32[256,768]{1,0:T(8,128)S(1)} %get-tuple-element.92.ref, ...), custom_call_target="tpu_custom_call" | custom-call | flops 1610612736 | bytes 6291456 | tf_op jit(solution)/shard_map/up/pallas_call | solution.py:416
  36.9 0.0 collective-permute-done.9
  36.9 0.1 constant_dynamic-update-slice_fusion.13.refs_0_.packet
  37.0 6.8 %hidden.1 = (bf16[4,256,768]{2,1,0:T(8,128)(2,1)S(1)}, bf16[4,256,768]{2,1,0:T(8,128)(2,1)S(1)}, bf16[4,256,768]{2,1,0:T(8,128)(2,1)S(1)}, bf16[64,1152]{1,0:T(8...) custom-call(bf16[256,2176]{1,0:T(8,128)(2,1)S(1)} %constant_dynamic-update-, ...), custom_call_target="tpu_custom_call" | custom-call | flops 6442450944 | bytes 25165824 | tf_op jit(solution)/shard_map/hidden/pallas_call | solution.py:458
  43.8 0.0 copy-start
  43.8 1.6 %collective-permute-start.10 = (bf16[64,1152]{1,0:T(8,128)(2,1)S(1)}, bf16[64,1152]{1,0:T(8,128)(2,1)S(1)}, u32[]{:S(2)}, u32[]{:S(2)}) collective-permute-start(bf16[64,1152]{1,0:T(8,128)(2,1)S(1)} %get-tuple-element.109), channel_id=1, source_target_pairs={{0,8},{4,12},{8,0},{12,4},{1,9},{5,13},{9,1},{13,5},{2,10},{6,14},... | collective-permute-start | bytes 442376 | tf_op jit(solution)/shard_map/ppermute | solution.py:311
  45.4 0.1 collective-permute-start.11
  45.5 0.6 collective-permute-start.12
  46.1 6.2 %grad_in.1 = (f32[4,512,768]{2,1,0:T(8,128)}, f32[4,512,768]{2,1,0:T(8,128)}, f32[8,128]{1,0:T(8,128)S(1)}) custom-call(bf16[512,256]{1,0:T(8,128)(2,1)S(1)} %turn.1.x_part, bf16[4,256,768]{2,1,0:T(8,128)(2,1)S(1)} %get-tuple-element.112.d_gate, bf16[4,256,768]{2,1,0:T(8,128)(2,1)S(1)} %get-tuple-element.113.d_up), custom_call_target="tpu_custom_call" | custom-call | flops 1610612736 | bytes 12582912 | tf_op jit(solution)/shard_map/grad_in/pallas_call | solution.py:478
  52.3 0.0 collective-permute-done.10.refs_1_
  52.3 0.0 collective-permute-done.11.refs_2_
  52.4 0.3 collective-permute-done.12.refs_3_
  52.6 0.8 %reduce.1 = (f32[8,16]{1,0:T(8,128)}, bf16[16,1024]{1,0:T(8,128)(2,1)S(1)}, bf16[16,1024]{1,0:T(8,128)(2,1)S(1)}, bf16[16,1024]{1,0:T(8,128)(2,1)S(1)}, bf16[16,...) custom-call(bf16[64,1152]{1,0:T(8,128)(2,1)S(1)} %get-tuple-element.108.refs_0_, ...), custom_call_target="tpu_custom_call" | custom-call | tf_op jit(solution)/shard_map/reduce/pallas_call | solution.py:493
  53.4 0.6 collective-permute-start.13
  54.0 3.6 %collective-permute-start.14 = (bf16[16,1024]{1,0:T(8,128)(2,1)S(1)}, bf16[16,1024]{1,0:T(8,128)(2,1)S(1)}, u32[]{:S(2)}, u32[]{:S(2)}) collective-permute-start(bf16[16,1024]{1,0:T(8,128)(2,1)S(1)} %get-tuple-element.117), channel_id=1, source_target_pairs={{0,2},{1,3},{2,0},{3,1},{4,6},{5,7},{6,4},{7,5},{8,10},{9,11},{10,... | collective-permute-start | bytes 98312 | tf_op jit(solution)/shard_map/ppermute | solution.py:311
  57.6 0.2 collective-permute-start.15
  57.8 3.6 %grad_out.1 = (f32[4,768,512]{2,1,0:T(8,128)}, f32[8,128]{1,0:T(8,128)S(1)}) custom-call(bf16[256,2176]{1,0:T(8,128)(2,1)S(1)} %constant_dynamic-update-slice_fusion.13.refs_0_.packet, bf16[4,256,768]{2,1,0:T(8,128)(2,1)S(1)} %get-tuple-element.119.hidden, f32[8,128]{1,0:T(8,128)S(1)} %get-tuple-element.120.after), custom_call_target="tpu_custom_call" | custom-call | flops 805306368 | bytes 6291456 | tf_op jit(solution)/shard_map/grad_out/pallas_call | solution.py:505
  61.4 0.0 collective-permute-done.13.refs_1_
  61.4 0.0 collective-permute-done.14.refs_2_
  61.5 1.8 %collective-permute-done.15.refs_3_ = bf16[16,1024]{1,0:T(8,128)(2,1)S(1)} collective-permute-done((bf16[16,1024]{1,0:T(8,128)(2,1)S(1)}, bf16[16,1024]{1,0:T(8,128)(2,1)S(1)}, u32[]{:S(2)}, u32[]{:S(2)}) %collective-permute-start.15) | collective-permute-done | bytes 32800 | tf_op jit(solution)/shard_map/ppermute | solution.py:311
  63.3 0.7 %join.1 = (bf16[16,2048]{1,0:T(8,128)(2,1)}, bf16[16,2048]{1,0:T(8,128)(2,1)}) custom-call(bf16[16,1024]{1,0:T(8,128)(2,1)S(1)} %get-tuple-element.115.refs_0_, bf16[16,1024]{1,0:T(8,128)(2,1)S(1)} %collective-permute-done.13.refs_1_, bf16[16,1024]{1,0:T(8,128)(2,1)S(1)} %collective-permute-done.14.refs_2_, ...), custom_call_target="tpu_custom_call" | custom-call | tf_op jit(solution)/shard_map/join/pallas_call | solution.py:520
  (15 shorter events, 0.2 us)
Async XLA Ops:
  0.6 15.9 %collective-permute-start = (bf16[16,2048]{1,0:T(8,128)(2,1)}, bf16[16,2048]{1,0:T(8,128)(2,1)S(1)}, u32[]{:S(2)}, u32[]{:S(2)}) collective-permute-start(bf16[16,2048]{1,0:T(8,128)(2,1)} %tokens.1), channel_id=1, source_target_pairs={{0,1},{1,0},{2,3},{3,2},{4,5},{5,4},{6,7},{7,6},{8,9},{9,8},{10,11... | collective-permute-start | bytes 196616 | tf_op jit(solution)/shard_map/ppermute | solution.py:311
  3.7 12.9 %collective-permute-start.1 = (bf16[16,2048]{1,0:T(8,128)(2,1)}, bf16[16,2048]{1,0:T(8,128)(2,1)S(1)}, u32[]{:S(2)}, u32[]{:S(2)}) collective-permute-start(bf16[16,2048]{1,0:T(8,128)(2,1)} %tokens.1), channel_id=1, source_target_pairs={{0,2},{1,3},{2,0},{3,1},{4,6},{5,7},{6,4},{7,5},{8,10},{9,11},{10,... | collective-permute-start | bytes 196616 | tf_op jit(solution)/shard_map/ppermute | solution.py:311
  6.3 10.3 %collective-permute-start.2 = (bf16[16,2048]{1,0:T(8,128)(2,1)}, bf16[16,2048]{1,0:T(8,128)(2,1)S(1)}, u32[]{:S(2)}, u32[]{:S(2)}) collective-permute-start(bf16[16,2048]{1,0:T(8,128)(2,1)} %tokens.1), channel_id=1, source_target_pairs={{0,3},{1,2},{2,1},{3,0},{4,7},{5,6},{6,5},{7,4},{8,11},{9,10},{10,... | collective-permute-start | bytes 196616 | tf_op jit(solution)/shard_map/ppermute | solution.py:311
  7.4 15.8 %collective-permute-start.5 = (bf16[16,2176]{1,0:T(8,128)(2,1)S(1)}, bf16[16,2176]{1,0:T(8,128)(2,1)S(1)}, u32[]{:S(2)}, u32[]{:S(2)}) collective-permute-start(bf16[16,2176]{1,0:T(8,128)(2,1)S(1)} %get-tuple-element.78), channel_id=1, source_target_pairs={{0,1},{1,0},{2,3},{3,2},{4,5},{5,4},{6,7},{7,6},{8,9},{9,8},{10,11... | collective-permute-start | bytes 208904 | tf_op jit(solution)/shard_map/ppermute | solution.py:311
  8.3 14.9 %collective-permute-start.6 = (bf16[16,2176]{1,0:T(8,128)(2,1)S(1)}, bf16[16,2176]{1,0:T(8,128)(2,1)S(1)}, u32[]{:S(2)}, u32[]{:S(2)}) collective-permute-start(bf16[16,2176]{1,0:T(8,128)(2,1)S(1)} %get-tuple-element.78), channel_id=1, source_target_pairs={{0,2},{1,3},{2,0},{3,1},{4,6},{5,7},{6,4},{7,5},{8,10},{9,11},{10,... | collective-permute-start | bytes 208904 | tf_op jit(solution)/shard_map/ppermute | solution.py:311
  16.5 7.0 %collective-permute-start.7 = (bf16[16,2176]{1,0:T(8,128)(2,1)S(1)}, bf16[16,2176]{1,0:T(8,128)(2,1)S(1)}, u32[]{:S(2)}, u32[]{:S(2)}) collective-permute-start(bf16[16,2176]{1,0:T(8,128)(2,1)S(1)} %get-tuple-element.78), channel_id=1, source_target_pairs={{0,3},{1,2},{2,1},{3,0},{4,7},{5,6},{6,5},{7,4},{8,11},{9,10},{10,... | collective-permute-start | bytes 208904 | tf_op jit(solution)/shard_map/ppermute | solution.py:311
  16.7 6.7 %collective-permute-start.3 = (bf16[64,2048]{1,0:T(8,128)(2,1)S(1)}, bf16[64,2048]{1,0:T(8,128)(2,1)S(1)}, u32[]{:S(2)}, u32[]{:S(2)}) collective-permute-start(bf16[64,2048]{1,0:T(8,128)(2,1)S(1)} %constant_dynamic-update-slice_fusion.value), channel_id=1, source_target_pairs={{0,8},{4,12},{8,0},{12,4},{1,9},{5,13},{9,1},{13,5},{2,10},{6,14},... | collective-permute-start | bytes 786440 | tf_op jit(solution)/shard_map/ppermute | solution.py:311
  23.4 2.0 %collective-permute-start.4 = (bf16[128,2048]{1,0:T(8,128)(2,1)S(1)}, bf16[128,2048]{1,0:T(8,128)(2,1)S(1)}, u32[]{:S(2)}, u32[]{:S(2)}) collective-permute-start(bf16[128,2048]{1,0:T(8,128)(2,1)S(1)} %pad_maximum_fusion), channel_id=1, source_target_pairs={{0,4},{4,0},{8,12},{12,8},{1,5},{5,1},{9,13},{13,9},{2,6},{6,2},{1... | collective-permute-start | bytes 1572872 | tf_op jit(solution)/shard_map/ppermute | solution.py:311
  23.5 9.2 %collective-permute-start.8 = (bf16[64,2176]{1,0:T(8,128)(2,1)S(1)}, bf16[64,2176]{1,0:T(8,128)(2,1)S(1)}, u32[]{:S(2)}, u32[]{:S(2)}) collective-permute-start(bf16[64,2176]{1,0:T(8,128)(2,1)S(1)} %constant_dynamic-update-slice_fusion.7.refs_7_), channel_id=1, source_target_pairs={{0,8},{4,12},{8,0},{12,4},{1,9},{5,13},{9,1},{13,5},{2,10},{6,14},... | collective-permute-start | bytes 835592 | tf_op jit(solution)/shard_map/ppermute | solution.py:311
  25.5 3.7 %copy-start.1 = (s32[4,6]{1,0:T(4,128)S(1)}, s32[4,6]{1,0:T(4,128)}, u32[]{:S(2)}) copy-start(s32[4,6]{1,0:T(4,128)} %refs_5_.5) | copy-start | bytes 292
  32.8 4.2 %collective-permute-start.9 = (bf16[128,2176]{1,0:T(8,128)(2,1)S(1)}, bf16[128,2176]{1,0:T(8,128)(2,1)S(1)}, u32[]{:S(2)}, u32[]{:S(2)}) collective-permute-start(bf16[128,2176]{1,0:T(8,128)(2,1)S(1)} %get-tuple-element.128.after), channel_id=1, source_target_pairs={{0,4},{4,0},{8,12},{12,8},{1,5},{5,1},{9,13},{13,9},{2,6},{6,2},{1... | collective-permute-start | bytes 1671176 | tf_op jit(solution)/shard_map/ppermute | solution.py:311
  43.8 8.8 %copy-start = (s32[16,8]{0,1:T(8,128)S(1)}, s32[16,8]{0,1:T(8,128)}, u32[]{:S(2)}) copy-start(s32[16,8]{0,1:T(8,128)} %param.10) | copy-start | bytes 1540
  43.8 8.5 %collective-permute-start.10 = (bf16[64,1152]{1,0:T(8,128)(2,1)S(1)}, bf16[64,1152]{1,0:T(8,128)(2,1)S(1)}, u32[]{:S(2)}, u32[]{:S(2)}) collective-permute-start(bf16[64,1152]{1,0:T(8,128)(2,1)S(1)} %get-tuple-element.109), channel_id=1, source_target_pairs={{0,8},{4,12},{8,0},{12,4},{1,9},{5,13},{9,1},{13,5},{2,10},{6,14},... | collective-permute-start | bytes 442376 | tf_op jit(solution)/shard_map/ppermute | solution.py:311
  45.4 6.9 %collective-permute-start.11 = (bf16[64,1152]{1,0:T(8,128)(2,1)S(1)}, bf16[64,1152]{1,0:T(8,128)(2,1)S(1)}, u32[]{:S(2)}, u32[]{:S(2)}) collective-permute-start(bf16[64,1152]{1,0:T(8,128)(2,1)S(1)} %get-tuple-element.110), channel_id=1, source_target_pairs={{0,4},{4,0},{8,12},{12,8},{1,5},{5,1},{9,13},{13,9},{2,6},{6,2},{1... | collective-permute-start | bytes 442376 | tf_op jit(solution)/shard_map/ppermute | solution.py:311
  45.5 7.1 %collective-permute-start.12 = (bf16[64,1152]{1,0:T(8,128)(2,1)S(1)}, bf16[64,1152]{1,0:T(8,128)(2,1)S(1)}, u32[]{:S(2)}, u32[]{:S(2)}) collective-permute-start(bf16[64,1152]{1,0:T(8,128)(2,1)S(1)} %get-tuple-element.111), channel_id=1, source_target_pairs={{0,12},{4,8},{8,4},{12,0},{1,13},{5,9},{9,5},{13,1},{2,14},{6,10},... | collective-permute-start | bytes 442376 | tf_op jit(solution)/shard_map/ppermute | solution.py:311
  53.4 8.0 %collective-permute-start.13 = (bf16[16,1024]{1,0:T(8,128)(2,1)S(1)}, bf16[16,1024]{1,0:T(8,128)(2,1)S(1)}, u32[]{:S(2)}, u32[]{:S(2)}) collective-permute-start(bf16[16,1024]{1,0:T(8,128)(2,1)S(1)} %get-tuple-element.116), channel_id=1, source_target_pairs={{0,1},{1,0},{2,3},{3,2},{4,5},{5,4},{6,7},{7,6},{8,9},{9,8},{10,11... | collective-permute-start | bytes 98312 | tf_op jit(solution)/shard_map/ppermute | solution.py:311
  54.0 7.5 %collective-permute-start.14 = (bf16[16,1024]{1,0:T(8,128)(2,1)S(1)}, bf16[16,1024]{1,0:T(8,128)(2,1)S(1)}, u32[]{:S(2)}, u32[]{:S(2)}) collective-permute-start(bf16[16,1024]{1,0:T(8,128)(2,1)S(1)} %get-tuple-element.117), channel_id=1, source_target_pairs={{0,2},{1,3},{2,0},{3,1},{4,6},{5,7},{6,4},{7,5},{8,10},{9,11},{10,... | collective-permute-start | bytes 98312 | tf_op jit(solution)/shard_map/ppermute | solution.py:311
  57.6 5.7 %collective-permute-start.15 = (bf16[16,1024]{1,0:T(8,128)(2,1)S(1)}, bf16[16,1024]{1,0:T(8,128)(2,1)S(1)}, u32[]{:S(2)}, u32[]{:S(2)}) collective-permute-start(bf16[16,1024]{1,0:T(8,128)(2,1)S(1)} %get-tuple-element.118), channel_id=1, source_target_pairs={{0,3},{1,2},{2,1},{3,0},{4,7},{5,6},{6,5},{7,4},{8,11},{9,10},{10,... | collective-permute-start | bytes 98312 | tf_op jit(solution)/shard_map/ppermute | solution.py:311

commit v14 on v13

--- a/solution.py
+++ b/solution.py
@@ -264,13 +264,17 @@
     cot_part[...] = packet[:, aligned(lax.axis_index("dp"), part)]
     done[...] = jnp.zeros(done.shape, done.dtype)
 
+    size = out_down.shape[1]
+    blocks = hidden.shape[2] // size
+
     def place(step):
-        return (step,)
+        return step // blocks, aligned(lax.rem(step, blocks), size), slice(None)
 
     def body(step, slot):
-        out_down[slot] = dot(hidden[step].T, cot_part[...], NN)
-
-    write_out(local_experts, place, (grad_down,), (out_down,), sems, body)
+        units = hidden[step // blocks, :, aligned(lax.rem(step, blocks), size)]
+        out_down[slot] = dot(units.T, cot_part[...], NN)
+
+    write_out(local_experts * blocks, place, (grad_down,), (out_down,), sems, body)
 
 
 def reduce_kernel(count, *refs):
@@ -481,8 +485,8 @@
         in_specs=[VMEM] * 3,
         out_specs=[HBM] * 2 + [VMEM],
         scratch_shapes=[
-            pltpu.VMEM((2, min(part, CHUNK), hidden_units), f32),
-            pltpu.VMEM((2, min(part, CHUNK), hidden_units), f32),
+            pltpu.VMEM((2, BLK, hidden_units), f32),
+            pltpu.VMEM((2, BLK, hidden_units), f32),
             pltpu.SemaphoreType.DMA((2, 2)),
         ],
         cost_estimate=cost(2 * everyone * one // columns, 4 * one // columns),
@@ -509,7 +513,7 @@
         out_specs=[HBM, VMEM],
         scratch_shapes=[
             pltpu.VMEM((everyone, part), bf16),
-            pltpu.VMEM((2, hidden_units, part), f32),
+            pltpu.VMEM((2, hidden_units // 2, part), f32),
             pltpu.SemaphoreType.DMA((2, 1)),
         ],
         cost_estimate=cost(everyone * one // columns, 2 * one // columns),

time: 64.1 us -> 66.8 us (1.042)
  Pallas kernels: 39.6 us -> 44 us
  waiting for transfers between devices: 2.63 us -> 0.92 us
    pallas_call x1, Pallas kernels: 6.25 us -> 9.16 us  [per_device(): pl.pallas_call(grad_in_kernel, out_shape=[struct((local_experts, part, hi...]
    ppermute x16, waiting for transfers between devices: 2.63 us -> 0.92 us  [swap(): return lax.ppermute(value, axis, [(i, i ^ mask) for i in range(size)])]
    pallas_call x1, Pallas kernels: 3.62 us -> 5.04 us  [per_device(): pl.pallas_call(grad_out_kernel, out_shape=[struct((local_experts, hidden_...]
  transfers between devices with their start and end apart: 16 -> 16, of which waited for: 4 -> 3; matrix products, arithmetic and copies ran while one was open for 0% -> 0% of each run, Pallas kernels for 49% -> 54%
where the time goes in v14:
time: 66.8 us; the launch traced here: 66.6 us
  Pallas kernels  44 us (66%)
  starting transfers between devices  20.4 us (31%)
  between operations  0.96 us (1%)
  waiting for transfers between devices  0.92 us (1%)
    ppermute x16, starting transfers between devices, swap(): return lax.ppermute(value, axis, [(i, i ^ mask) for i in range(size)])  20.4 us
    pallas_call x2, Pallas kernels, load(): pl.pallas_call(load_kernel, out_shape=[struct(value.shape, bf16)] + [pltp...  9.37 us
    pallas_call x1, Pallas kernels, per_device(): pl.pallas_call(grad_in_kernel, out_shape=[struct((local_experts, part, hi...  9.16 us
    pallas_call x2, Pallas kernels, up_call(): pl.pallas_call(functools.partial(up_kernel, first, last, start_down), out...  7.29 us
    pallas_call x1, Pallas kernels, per_device(): pl.pallas_call(functools.partial(hidden_kernel, local_experts, sources),...  6.81 us
    pallas_call x1, Pallas kernels, per_device(): pl.pallas_call(grad_out_kernel, out_shape=[struct((local_experts, hidden_...  5.04 us
    pallas_call x1, Pallas kernels, per_device(): pl.pallas_call(functools.partial(gate_kernel, local_experts), out_shape=[...  3.7 us
  transfers between devices with their start and end apart: 16, of which 3 were waited for; matrix products, arithmetic and copies ran while one was open for 0% of the time, Pallas kernels for 54%

profile of v14, /device:TPU:0, one launch (start us, length us, event | category | flops | bytes accessed | tf_op | source)
XLA Modules:
  0.0 66.6 jit_solution(16907684335989630684)
XLA Ops:
  0.6 3.1 %collective-permute-start = (bf16[16,2048]{1,0:T(8,128)(2,1)}, bf16[16,2048]{1,0:T(8,128)(2,1)S(1)}, u32[]{:S(2)}, u32[]{:S(2)}) collective-permute-start(bf16[16,2048]{1,0:T(8,128)(2,1)} %tokens.1), channel_id=1, source_target_pairs={{0,1},{1,0},{2,3},{3,2},{4,5},{5,4},{6,7},{7,6},{8,9},{9,8},{10,11... | collective-permute-start | bytes 196616 | tf_op jit(solution)/shard_map/ppermute | solution.py:315
  3.7 2.6 %collective-permute-start.1 = (bf16[16,2048]{1,0:T(8,128)(2,1)}, bf16[16,2048]{1,0:T(8,128)(2,1)S(1)}, u32[]{:S(2)}, u32[]{:S(2)}) collective-permute-start(bf16[16,2048]{1,0:T(8,128)(2,1)} %tokens.1), channel_id=1, source_target_pairs={{0,2},{1,3},{2,0},{3,1},{4,6},{5,7},{6,4},{7,5},{8,10},{9,11},{10,... | collective-permute-start | bytes 196616 | tf_op jit(solution)/shard_map/ppermute | solution.py:315
  6.3 0.0 collective-permute-start.2
  6.3 1.0 %route.1 = (bf16[16,2048]{1,0:T(8,128)(2,1)S(1)}, bf16[16,2176]{1,0:T(8,128)(2,1)S(1)}) custom-call(bf16[16,2048]{1,0:T(8,128)(2,1)} %tokens.1, bf16[16,2048]{1,0:T(8,128)(2,1)} %cotangent.1, s32[8,16]{1,0:T(8,128)} %bitcast.3, bf16[8,16]{1,0:T(8,128)(2,1)} %bitcast.5), custom_call_target="tpu_custom_call" | custom-call | tf_op jit(solution)/shard_map/route/pallas_call | solution.py:357
  7.4 1.0 %collective-permute-start.5 = (bf16[16,2176]{1,0:T(8,128)(2,1)S(1)}, bf16[16,2176]{1,0:T(8,128)(2,1)S(1)}, u32[]{:S(2)}, u32[]{:S(2)}) collective-permute-start(bf16[16,2176]{1,0:T(8,128)(2,1)S(1)} %get-tuple-element.78), channel_id=1, source_target_pairs={{0,1},{1,0},{2,3},{3,2},{4,5},{5,4},{6,7},{7,6},{8,9},{9,8},{10,11... | collective-permute-start | bytes 208904 | tf_op jit(solution)/shard_map/ppermute | solution.py:315
  8.3 3.5 %collective-permute-start.6 = (bf16[16,2176]{1,0:T(8,128)(2,1)S(1)}, bf16[16,2176]{1,0:T(8,128)(2,1)S(1)}, u32[]{:S(2)}, u32[]{:S(2)}) collective-permute-start(bf16[16,2176]{1,0:T(8,128)(2,1)S(1)} %get-tuple-element.78), channel_id=1, source_target_pairs={{0,2},{1,3},{2,0},{3,1},{4,6},{5,7},{6,4},{7,5},{8,10},{9,11},{10,... | collective-permute-start | bytes 208904 | tf_op jit(solution)/shard_map/ppermute | solution.py:315
  11.8 4.7 %load_up.1 = (bf16[16,2048]{1,0:T(8,128)(2,1)S(1)}, bf16[2048,768]{1,0:T(8,128)(2,1)S(1)}, bf16[2048,768]{1,0:T(8,128)(2,1)S(1)}, bf16[2048,768]{1,0:T(8,128)(2,1)S(1)}, bf16[2048,768]{1,0:T(8,128)(2,1)S(1)}) custom-call(bf16[4,2048,768]{2,1,0:T(8,128)(2,1)} %weight.2, bf16[16,2048]{1,0:T(8,128)(2,1)S(1)} %get-tuple-element.67.value), custom_call_target="tpu_custom_call" | custom-call | bytes 12582912 | tf_op jit(solution)/shard_map/load_up/pallas_call | solution.py:372
  16.5 0.0 collective-permute-done
  16.5 0.1 collective-permute-start.7
  16.6 0.0 collective-permute-done.1
  16.6 0.0 collective-permute-done.2
  16.7 1.8 %collective-permute-start.3 = (bf16[64,2048]{1,0:T(8,128)(2,1)S(1)}, bf16[64,2048]{1,0:T(8,128)(2,1)S(1)}, u32[]{:S(2)}, u32[]{:S(2)}) collective-permute-start(bf16[64,2048]{1,0:T(8,128)(2,1)S(1)} %constant_dynamic-update-slice_fusion.value), channel_id=1, source_target_pairs={{0,8},{4,12},{8,0},{12,4},{1,9},{5,13},{9,1},{13,5},{2,10},{6,14},... | collective-permute-start | bytes 786440 | tf_op jit(solution)/shard_map/ppermute | solution.py:315
  18.4 4.7 %load_gate.1 = (bf16[64,2048]{1,0:T(8,128)(2,1)S(1)}, bf16[2048,768]{1,0:T(8,128)(2,1)S(1)}, bf16[2048,768]{1,0:T(8,128)(2,1)S(1)}, bf16[2048,768]{1,0:T(8,128)(2,1)S(1)}, bf16[2048,768]{1,0:T(8,128)(2,1)S(1)}) custom-call(bf16[4,2048,768]{2,1,0:T(8,128)(2,1)} %weight.3, bf16[64,2048]{1,0:T(8,128)(2,1)S(1)} %constant_dynamic-update-slice_fusion.value), custom_call_target="tpu_custom_call" | custom-call | bytes 12582912 | tf_op jit(solution)/shard_map/load_gate/pallas_call | solution.py:372
  23.1 0.0 collective-permute-done.5
  23.2 0.0 collective-permute-done.6
  23.2 0.2 collective-permute-done.3
  23.4 0.1 collective-permute-start.4
  23.5 0.0 collective-permute-done.7
  23.5 1.6 %collective-permute-start.8 = (bf16[64,2176]{1,0:T(8,128)(2,1)S(1)}, bf16[64,2176]{1,0:T(8,128)(2,1)S(1)}, u32[]{:S(2)}, u32[]{:S(2)}) collective-permute-start(bf16[64,2176]{1,0:T(8,128)(2,1)S(1)} %constant_dynamic-update-slice_fusion.7.refs_7_), channel_id=1, source_target_pairs={{0,8},{4,12},{8,0},{12,4},{1,9},{5,13},{9,1},{13,5},{2,10},{6,14},... | collective-permute-start | bytes 835592 | tf_op jit(solution)/shard_map/ppermute | solution.py:315
  25.1 0.3 collective-permute-done.4
  25.5 0.0 copy-start.1
  25.5 3.7 %gate.1 = (f32[256,768]{1,0:T(8,128)S(1)}, f32[256,768]{1,0:T(8,128)S(1)}, f32[256,768]{1,0:T(8,128)S(1)}, f32[256,768]{1,0:T(8,128)S(1)}, bf16[512,768]{1,0:T(8...) custom-call(bf16[2048,768]{1,0:T(8,128)(2,1)S(1)} %get-tuple-element, ...), custom_call_target="tpu_custom_call" | custom-call | flops 3221225472 | bytes 12582912 | tf_op jit(solution)/shard_map/gate/pallas_call | solution.py:398
  29.2 3.5 %up.2 = (bf16[256,768]{1,0:T(8,128)(2,1)S(1)}, bf16[256,768]{1,0:T(8,128)(2,1)S(1)}, bf16[256,768]{1,0:T(8,128)(2,1)S(1)}, bf16[256,768]{1,0:T(8,128)(2,1)S(1)},...) custom-call(f32[256,768]{1,0:T(8,128)S(1)} %get-tuple-element.74.ref, ...), custom_call_target="tpu_custom_call" | custom-call | flops 1610612736 | bytes 6291456 | tf_op jit(solution)/shard_map/up/pallas_call | solution.py:420
  32.7 0.0 collective-permute-done.8
  32.7 0.1 constant_dynamic-update-slice_fusion.11
  32.8 0.2 collective-permute-start.9
  33.0 0.1 turn.1.x_part
  33.1 3.8 %up.3 = (bf16[256,768]{1,0:T(8,128)(2,1)S(1)}, bf16[256,768]{1,0:T(8,128)(2,1)S(1)}, bf16[256,768]{1,0:T(8,128)(2,1)S(1)}, bf16[256,768]{1,0:T(8,128)(2,1)S(1)},...) custom-call(f32[256,768]{1,0:T(8,128)S(1)} %get-tuple-element.92.ref, ...), custom_call_target="tpu_custom_call" | custom-call | flops 1610612736 | bytes 6291456 | tf_op jit(solution)/shard_map/up/pallas_call | solution.py:420
  36.9 0.0 collective-permute-done.9
  36.9 0.1 constant_dynamic-update-slice_fusion.13.refs_0_.packet
  37.0 6.8 %hidden.1 = (bf16[4,256,768]{2,1,0:T(8,128)(2,1)S(1)}, bf16[4,256,768]{2,1,0:T(8,128)(2,1)S(1)}, bf16[4,256,768]{2,1,0:T(8,128)(2,1)S(1)}, bf16[64,1152]{1,0:T(8...) custom-call(bf16[256,2176]{1,0:T(8,128)(2,1)S(1)} %constant_dynamic-update-, ...), custom_call_target="tpu_custom_call" | custom-call | flops 6442450944 | bytes 25165824 | tf_op jit(solution)/shard_map/hidden/pallas_call | solution.py:462
  43.8 0.0 copy-start
  43.8 1.6 %collective-permute-start.10 = (bf16[64,1152]{1,0:T(8,128)(2,1)S(1)}, bf16[64,1152]{1,0:T(8,128)(2,1)S(1)}, u32[]{:S(2)}, u32[]{:S(2)}) collective-permute-start(bf16[64,1152]{1,0:T(8,128)(2,1)S(1)} %get-tuple-element.109), channel_id=1, source_target_pairs={{0,8},{4,12},{8,0},{12,4},{1,9},{5,13},{9,1},{13,5},{2,10},{6,14},... | collective-permute-start | bytes 442376 | tf_op jit(solution)/shard_map/ppermute | solution.py:315
  45.4 0.1 collective-permute-start.11
  45.5 0.6 collective-permute-start.12
  46.1 9.2 %grad_in.1 = (f32[4,512,768]{2,1,0:T(8,128)}, f32[4,512,768]{2,1,0:T(8,128)}, f32[8,128]{1,0:T(8,128)S(1)}) custom-call(bf16[512,256]{1,0:T(8,128)(2,1)S(1)} %turn.1.x_part, bf16[4,256,768]{2,1,0:T(8,128)(2,1)S(1)} %get-tuple-element.112.d_gate, bf16[4,256,768]{2,1,0:T(8,128)(2,1)S(1)} %get-tuple-element.113.d_up), custom_call_target="tpu_custom_call" | custom-call | flops 1610612736 | bytes 12582912 | tf_op jit(solution)/shard_map/grad_in/pallas_call | solution.py:482
  55.2 0.0 collective-permute-done.10.refs_1_
  55.3 0.0 collective-permute-done.11.refs_2_
  55.3 0.0 collective-permute-done.12.refs_3_
  55.3 0.8 %reduce.1 = (f32[8,16]{1,0:T(8,128)}, bf16[16,1024]{1,0:T(8,128)(2,1)S(1)}, bf16[16,1024]{1,0:T(8,128)(2,1)S(1)}, bf16[16,1024]{1,0:T(8,128)(2,1)S(1)}, bf16[16,...) custom-call(bf16[64,1152]{1,0:T(8,128)(2,1)S(1)} %get-tuple-element.108.refs_0_, ...), custom_call_target="tpu_custom_call" | custom-call | tf_op jit(solution)/shard_map/reduce/pallas_call | solution.py:497
  56.1 0.6 collective-permute-start.13
  56.7 3.5 %collective-permute-start.14 = (bf16[16,1024]{1,0:T(8,128)(2,1)S(1)}, bf16[16,1024]{1,0:T(8,128)(2,1)S(1)}, u32[]{:S(2)}, u32[]{:S(2)}) collective-permute-start(bf16[16,1024]{1,0:T(8,128)(2,1)S(1)} %get-tuple-element.117), channel_id=1, source_target_pairs={{0,2},{1,3},{2,0},{3,1},{4,6},{5,7},{6,4},{7,5},{8,10},{9,11},{10,... | collective-permute-start | bytes 98312 | tf_op jit(solution)/shard_map/ppermute | solution.py:315
  60.2 0.2 collective-permute-start.15
  60.4 5.0 %grad_out.1 = (f32[4,768,512]{2,1,0:T(8,128)}, f32[8,128]{1,0:T(8,128)S(1)}) custom-call(bf16[256,2176]{1,0:T(8,128)(2,1)S(1)} %constant_dynamic-update-slice_fusion.13.refs_0_.packet, bf16[4,256,768]{2,1,0:T(8,128)(2,1)S(1)} %get-tuple-element.119.hidden, f32[8,128]{1,0:T(8,128)S(1)} %get-tuple-element.120.after), custom_call_target="tpu_custom_call" | custom-call | flops 805306368 | bytes 6291456 | tf_op jit(solution)/shard_map/grad_out/pallas_call | solution.py:509
  65.5 0.0 collective-permute-done.13.refs_1_
  65.5 0.0 collective-permute-done.14.refs_2_
  65.5 0.4 collective-permute-done.15.refs_3_
  65.9 0.7 join.1
  (15 shorter events, 0.2 us)
Async XLA Ops:
  0.6 15.9 %collective-permute-start = (bf16[16,2048]{1,0:T(8,128)(2,1)}, bf16[16,2048]{1,0:T(8,128)(2,1)S(1)}, u32[]{:S(2)}, u32[]{:S(2)}) collective-permute-start(bf16[16,2048]{1,0:T(8,128)(2,1)} %tokens.1), channel_id=1, source_target_pairs={{0,1},{1,0},{2,3},{3,2},{4,5},{5,4},{6,7},{7,6},{8,9},{9,8},{10,11... | collective-permute-start | bytes 196616 | tf_op jit(solution)/shard_map/ppermute | solution.py:315
  3.7 12.9 %collective-permute-start.1 = (bf16[16,2048]{1,0:T(8,128)(2,1)}, bf16[16,2048]{1,0:T(8,128)(2,1)S(1)}, u32[]{:S(2)}, u32[]{:S(2)}) collective-permute-start(bf16[16,2048]{1,0:T(8,128)(2,1)} %tokens.1), channel_id=1, source_target_pairs={{0,2},{1,3},{2,0},{3,1},{4,6},{5,7},{6,4},{7,5},{8,10},{9,11},{10,... | collective-permute-start | bytes 196616 | tf_op jit(solution)/shard_map/ppermute | solution.py:315
  6.3 10.3 %collective-permute-start.2 = (bf16[16,2048]{1,0:T(8,128)(2,1)}, bf16[16,2048]{1,0:T(8,128)(2,1)S(1)}, u32[]{:S(2)}, u32[]{:S(2)}) collective-permute-start(bf16[16,2048]{1,0:T(8,128)(2,1)} %tokens.1), channel_id=1, source_target_pairs={{0,3},{1,2},{2,1},{3,0},{4,7},{5,6},{6,5},{7,4},{8,11},{9,10},{10,... | collective-permute-start | bytes 196616 | tf_op jit(solution)/shard_map/ppermute | solution.py:315
  7.4 15.8 %collective-permute-start.5 = (bf16[16,2176]{1,0:T(8,128)(2,1)S(1)}, bf16[16,2176]{1,0:T(8,128)(2,1)S(1)}, u32[]{:S(2)}, u32[]{:S(2)}) collective-permute-start(bf16[16,2176]{1,0:T(8,128)(2,1)S(1)} %get-tuple-element.78), channel_id=1, source_target_pairs={{0,1},{1,0},{2,3},{3,2},{4,5},{5,4},{6,7},{7,6},{8,9},{9,8},{10,11... | collective-permute-start | bytes 208904 | tf_op jit(solution)/shard_map/ppermute | solution.py:315
  8.3 14.9 %collective-permute-start.6 = (bf16[16,2176]{1,0:T(8,128)(2,1)S(1)}, bf16[16,2176]{1,0:T(8,128)(2,1)S(1)}, u32[]{:S(2)}, u32[]{:S(2)}) collective-permute-start(bf16[16,2176]{1,0:T(8,128)(2,1)S(1)} %get-tuple-element.78), channel_id=1, source_target_pairs={{0,2},{1,3},{2,0},{3,1},{4,6},{5,7},{6,4},{7,5},{8,10},{9,11},{10,... | collective-permute-start | bytes 208904 | tf_op jit(solution)/shard_map/ppermute | solution.py:315
  16.5 7.0 %collective-permute-start.7 = (bf16[16,2176]{1,0:T(8,128)(2,1)S(1)}, bf16[16,2176]{1,0:T(8,128)(2,1)S(1)}, u32[]{:S(2)}, u32[]{:S(2)}) collective-permute-start(bf16[16,2176]{1,0:T(8,128)(2,1)S(1)} %get-tuple-element.78), channel_id=1, source_target_pairs={{0,3},{1,2},{2,1},{3,0},{4,7},{5,6},{6,5},{7,4},{8,11},{9,10},{10,... | collective-permute-start | bytes 208904 | tf_op jit(solution)/shard_map/ppermute | solution.py:315
  16.7 6.7 %collective-permute-start.3 = (bf16[64,2048]{1,0:T(8,128)(2,1)S(1)}, bf16[64,2048]{1,0:T(8,128)(2,1)S(1)}, u32[]{:S(2)}, u32[]{:S(2)}) collective-permute-start(bf16[64,2048]{1,0:T(8,128)(2,1)S(1)} %constant_dynamic-update-slice_fusion.value), channel_id=1, source_target_pairs={{0,8},{4,12},{8,0},{12,4},{1,9},{5,13},{9,1},{13,5},{2,10},{6,14},... | collective-permute-start | bytes 786440 | tf_op jit(solution)/shard_map/ppermute | solution.py:315
  23.4 2.0 %collective-permute-start.4 = (bf16[128,2048]{1,0:T(8,128)(2,1)S(1)}, bf16[128,2048]{1,0:T(8,128)(2,1)S(1)}, u32[]{:S(2)}, u32[]{:S(2)}) collective-permute-start(bf16[128,2048]{1,0:T(8,128)(2,1)S(1)} %pad_maximum_fusion), channel_id=1, source_target_pairs={{0,4},{4,0},{8,12},{12,8},{1,5},{5,1},{9,13},{13,9},{2,6},{6,2},{1... | collective-permute-start | bytes 1572872 | tf_op jit(solution)/shard_map/ppermute | solution.py:315
  23.5 9.2 %collective-permute-start.8 = (bf16[64,2176]{1,0:T(8,128)(2,1)S(1)}, bf16[64,2176]{1,0:T(8,128)(2,1)S(1)}, u32[]{:S(2)}, u32[]{:S(2)}) collective-permute-start(bf16[64,2176]{1,0:T(8,128)(2,1)S(1)} %constant_dynamic-update-slice_fusion.7.refs_7_), channel_id=1, source_target_pairs={{0,8},{4,12},{8,0},{12,4},{1,9},{5,13},{9,1},{13,5},{2,10},{6,14},... | collective-permute-start | bytes 835592 | tf_op jit(solution)/shard_map/ppermute | solution.py:315
  25.5 3.7 %copy-start.1 = (s32[4,6]{1,0:T(4,128)S(1)}, s32[4,6]{1,0:T(4,128)}, u32[]{:S(2)}) copy-start(s32[4,6]{1,0:T(4,128)} %refs_5_.5) | copy-start | bytes 292
  32.8 4.2 %collective-permute-start.9 = (bf16[128,2176]{1,0:T(8,128)(2,1)S(1)}, bf16[128,2176]{1,0:T(8,128)(2,1)S(1)}, u32[]{:S(2)}, u32[]{:S(2)}) collective-permute-start(bf16[128,2176]{1,0:T(8,128)(2,1)S(1)} %get-tuple-element.128.after), channel_id=1, source_target_pairs={{0,4},{4,0},{8,12},{12,8},{1,5},{5,1},{9,13},{13,9},{2,6},{6,2},{1... | collective-permute-start | bytes 1671176 | tf_op jit(solution)/shard_map/ppermute | solution.py:315
  43.8 11.5 %copy-start = (s32[16,8]{0,1:T(8,128)S(1)}, s32[16,8]{0,1:T(8,128)}, u32[]{:S(2)}) copy-start(s32[16,8]{0,1:T(8,128)} %param.10) | copy-start | bytes 1540
  43.8 11.4 %collective-permute-start.10 = (bf16[64,1152]{1,0:T(8,128)(2,1)S(1)}, bf16[64,1152]{1,0:T(8,128)(2,1)S(1)}, u32[]{:S(2)}, u32[]{:S(2)}) collective-permute-start(bf16[64,1152]{1,0:T(8,128)(2,1)S(1)} %get-tuple-element.109), channel_id=1, source_target_pairs={{0,8},{4,12},{8,0},{12,4},{1,9},{5,13},{9,1},{13,5},{2,10},{6,14},... | collective-permute-start | bytes 442376 | tf_op jit(solution)/shard_map/ppermute | solution.py:315
  45.4 9.9 %collective-permute-start.11 = (bf16[64,1152]{1,0:T(8,128)(2,1)S(1)}, bf16[64,1152]{1,0:T(8,128)(2,1)S(1)}, u32[]{:S(2)}, u32[]{:S(2)}) collective-permute-start(bf16[64,1152]{1,0:T(8,128)(2,1)S(1)} %get-tuple-element.110), channel_id=1, source_target_pairs={{0,4},{4,0},{8,12},{12,8},{1,5},{5,1},{9,13},{13,9},{2,6},{6,2},{1... | collective-permute-start | bytes 442376 | tf_op jit(solution)/shard_map/ppermute | solution.py:315
  45.5 9.8 %collective-permute-start.12 = (bf16[64,1152]{1,0:T(8,128)(2,1)S(1)}, bf16[64,1152]{1,0:T(8,128)(2,1)S(1)}, u32[]{:S(2)}, u32[]{:S(2)}) collective-permute-start(bf16[64,1152]{1,0:T(8,128)(2,1)S(1)} %get-tuple-element.111), channel_id=1, source_target_pairs={{0,12},{4,8},{8,4},{12,0},{1,13},{5,9},{9,5},{13,1},{2,14},{6,10},... | collective-permute-start | bytes 442376 | tf_op jit(solution)/shard_map/ppermute | solution.py:315
  56.1 9.4 %collective-permute-start.13 = (bf16[16,1024]{1,0:T(8,128)(2,1)S(1)}, bf16[16,1024]{1,0:T(8,128)(2,1)S(1)}, u32[]{:S(2)}, u32[]{:S(2)}) collective-permute-start(bf16[16,1024]{1,0:T(8,128)(2,1)S(1)} %get-tuple-element.116), channel_id=1, source_target_pairs={{0,1},{1,0},{2,3},{3,2},{4,5},{5,4},{6,7},{7,6},{8,9},{9,8},{10,11... | collective-permute-start | bytes 98312 | tf_op jit(solution)/shard_map/ppermute | solution.py:315
  56.7 8.8 %collective-permute-start.14 = (bf16[16,1024]{1,0:T(8,128)(2,1)S(1)}, bf16[16,1024]{1,0:T(8,128)(2,1)S(1)}, u32[]{:S(2)}, u32[]{:S(2)}) collective-permute-start(bf16[16,1024]{1,0:T(8,128)(2,1)S(1)} %get-tuple-element.117), channel_id=1, source_target_pairs={{0,2},{1,3},{2,0},{3,1},{4,6},{5,7},{6,4},{7,5},{8,10},{9,11},{10,... | collective-permute-start | bytes 98312 | tf_op jit(solution)/shard_map/ppermute | solution.py:315
  60.2 5.7 %collective-permute-start.15 = (bf16[16,1024]{1,0:T(8,128)(2,1)S(1)}, bf16[16,1024]{1,0:T(8,128)(2,1)S(1)}, u32[]{:S(2)}, u32[]{:S(2)}) collective-permute-start(bf16[16,1024]{1,0:T(8,128)(2,1)S(1)} %get-tuple-element.118), channel_id=1, source_target_pairs={{0,3},{1,2},{2,1},{3,0},{4,7},{5,6},{6,5},{7,4},{8,11},{9,10},{10,... | collective-permute-start | bytes 98312 | tf_op jit(solution)/shard_map/ppermute | solution.py:315

commit v15 on v13

--- a/solution.py
+++ b/solution.py
@@ -481,12 +481,12 @@
         in_specs=[VMEM] * 3,
         out_specs=[HBM] * 2 + [VMEM],
         scratch_shapes=[
-            pltpu.VMEM((2, min(part, CHUNK), hidden_units), f32),
-            pltpu.VMEM((2, min(part, CHUNK), hidden_units), f32),
+            pltpu.VMEM((2, part, hidden_units), f32),
+            pltpu.VMEM((2, part, hidden_units), f32),
             pltpu.SemaphoreType.DMA((2, 2)),
         ],
         cost_estimate=cost(2 * everyone * one // columns, 4 * one // columns),
-        compiler_params=params(room),
+        compiler_params=params(room + 6),
         name="grad_in",
     )(x_part, d_gate, d_up)
 

time: 64.1 us -> 64.3 us (level)
  waiting for transfers between devices: 2.63 us -> 3.62 us
  Pallas kernels: 39.6 us -> 38.8 us
    pallas_call x1, Pallas kernels: 6.25 us -> 5.22 us  [per_device(): pl.pallas_call(grad_in_kernel, out_shape=[struct((local_experts, part, hi...]
    ppermute x16, waiting for transfers between devices: 2.63 us -> 3.62 us  [swap(): return lax.ppermute(value, axis, [(i, i ^ mask) for i in range(size)])]
  transfers between devices with their start and end apart: 16 -> 16, of which waited for: 4 -> 4; matrix products, arithmetic and copies ran while one was open for 0% -> 0% of each run, Pallas kernels for 49% -> 47%
where the time goes in v15:
time: 64.3 us; the launch traced here: 64.1 us
  Pallas kernels  38.8 us (60%)
  starting transfers between devices  20.4 us (32%)
  waiting for transfers between devices  3.62 us (6%)
  between operations  0.94 us (1%)
    ppermute x16, starting transfers between devices, swap(): return lax.ppermute(value, axis, [(i, i ^ mask) for i in range(size)])  20.4 us
    pallas_call x2, Pallas kernels, load(): pl.pallas_call(load_kernel, out_shape=[struct(value.shape, bf16)] + [pltp...  9.37 us
    pallas_call x2, Pallas kernels, up_call(): pl.pallas_call(functools.partial(up_kernel, first, last, start_down), out...  7.27 us
    pallas_call x1, Pallas kernels, per_device(): pl.pallas_call(functools.partial(hidden_kernel, local_experts, sources),...  7 us
    pallas_call x1, Pallas kernels, per_device(): pl.pallas_call(grad_in_kernel, out_shape=[struct((local_experts, part, hi...  5.22 us
    pallas_call x1, Pallas kernels, per_device(): pl.pallas_call(functools.partial(gate_kernel, local_experts), out_shape=[...  3.7 us
    ppermute x16, waiting for transfers between devices, swap(): return lax.ppermute(value, axis, [(i, i ^ mask) for i in range(size)])  3.62 us
    pallas_call x1, Pallas kernels, per_device(): pl.pallas_call(grad_out_kernel, out_shape=[struct((local_experts, hidden_...  3.62 us
  transfers between devices with their start and end apart: 16, of which 4 were waited for; matrix products, arithmetic and copies ran while one was open for 0% of the time, Pallas kernels for 47%

profile of v15, /device:TPU:0, one launch (start us, length us, event | category | flops | bytes accessed | tf_op | source)
XLA Modules:
  0.0 64.1 jit_solution(6730969677631335821)
XLA Ops:
  0.6 3.1 %collective-permute-start = (bf16[16,2048]{1,0:T(8,128)(2,1)}, bf16[16,2048]{1,0:T(8,128)(2,1)S(1)}, u32[]{:S(2)}, u32[]{:S(2)}) collective-permute-start(bf16[16,2048]{1,0:T(8,128)(2,1)} %tokens.1), channel_id=1, source_target_pairs={{0,1},{1,0},{2,3},{3,2},{4,5},{5,4},{6,7},{7,6},{8,9},{9,8},{10,11... | collective-permute-start | bytes 196616 | tf_op jit(solution)/shard_map/ppermute | solution.py:311
  3.7 2.6 %collective-permute-start.1 = (bf16[16,2048]{1,0:T(8,128)(2,1)}, bf16[16,2048]{1,0:T(8,128)(2,1)S(1)}, u32[]{:S(2)}, u32[]{:S(2)}) collective-permute-start(bf16[16,2048]{1,0:T(8,128)(2,1)} %tokens.1), channel_id=1, source_target_pairs={{0,2},{1,3},{2,0},{3,1},{4,6},{5,7},{6,4},{7,5},{8,10},{9,11},{10,... | collective-permute-start | bytes 196616 | tf_op jit(solution)/shard_map/ppermute | solution.py:311
  6.3 0.0 collective-permute-start.2
  6.3 1.0 %route.1 = (bf16[16,2048]{1,0:T(8,128)(2,1)S(1)}, bf16[16,2176]{1,0:T(8,128)(2,1)S(1)}) custom-call(bf16[16,2048]{1,0:T(8,128)(2,1)} %tokens.1, bf16[16,2048]{1,0:T(8,128)(2,1)} %cotangent.1, s32[8,16]{1,0:T(8,128)} %bitcast.3, bf16[8,16]{1,0:T(8,128)(2,1)} %bitcast.5), custom_call_target="tpu_custom_call" | custom-call | tf_op jit(solution)/shard_map/route/pallas_call | solution.py:353
  7.4 1.0 %collective-permute-start.5 = (bf16[16,2176]{1,0:T(8,128)(2,1)S(1)}, bf16[16,2176]{1,0:T(8,128)(2,1)S(1)}, u32[]{:S(2)}, u32[]{:S(2)}) collective-permute-start(bf16[16,2176]{1,0:T(8,128)(2,1)S(1)} %get-tuple-element.78), channel_id=1, source_target_pairs={{0,1},{1,0},{2,3},{3,2},{4,5},{5,4},{6,7},{7,6},{8,9},{9,8},{10,11... | collective-permute-start | bytes 208904 | tf_op jit(solution)/shard_map/ppermute | solution.py:311
  8.3 3.5 %collective-permute-start.6 = (bf16[16,2176]{1,0:T(8,128)(2,1)S(1)}, bf16[16,2176]{1,0:T(8,128)(2,1)S(1)}, u32[]{:S(2)}, u32[]{:S(2)}) collective-permute-start(bf16[16,2176]{1,0:T(8,128)(2,1)S(1)} %get-tuple-element.78), channel_id=1, source_target_pairs={{0,2},{1,3},{2,0},{3,1},{4,6},{5,7},{6,4},{7,5},{8,10},{9,11},{10,... | collective-permute-start | bytes 208904 | tf_op jit(solution)/shard_map/ppermute | solution.py:311
  11.8 4.7 %load_up.1 = (bf16[16,2048]{1,0:T(8,128)(2,1)S(1)}, bf16[2048,768]{1,0:T(8,128)(2,1)S(1)}, bf16[2048,768]{1,0:T(8,128)(2,1)S(1)}, bf16[2048,768]{1,0:T(8,128)(2,1)S(1)}, bf16[2048,768]{1,0:T(8,128)(2,1)S(1)}) custom-call(bf16[4,2048,768]{2,1,0:T(8,128)(2,1)} %weight.2, bf16[16,2048]{1,0:T(8,128)(2,1)S(1)} %get-tuple-element.67.value), custom_call_target="tpu_custom_call" | custom-call | bytes 12582912 | tf_op jit(solution)/shard_map/load_up/pallas_call | solution.py:368
  16.5 0.0 collective-permute-done
  16.5 0.1 collective-permute-start.7
  16.6 0.0 collective-permute-done.1
  16.6 0.0 collective-permute-done.2
  16.7 1.8 %collective-permute-start.3 = (bf16[64,2048]{1,0:T(8,128)(2,1)S(1)}, bf16[64,2048]{1,0:T(8,128)(2,1)S(1)}, u32[]{:S(2)}, u32[]{:S(2)}) collective-permute-start(bf16[64,2048]{1,0:T(8,128)(2,1)S(1)} %constant_dynamic-update-slice_fusion.value), channel_id=1, source_target_pairs={{0,8},{4,12},{8,0},{12,4},{1,9},{5,13},{9,1},{13,5},{2,10},{6,14},... | collective-permute-start | bytes 786440 | tf_op jit(solution)/shard_map/ppermute | solution.py:311
  18.4 4.7 %load_gate.1 = (bf16[64,2048]{1,0:T(8,128)(2,1)S(1)}, bf16[2048,768]{1,0:T(8,128)(2,1)S(1)}, bf16[2048,768]{1,0:T(8,128)(2,1)S(1)}, bf16[2048,768]{1,0:T(8,128)(2,1)S(1)}, bf16[2048,768]{1,0:T(8,128)(2,1)S(1)}) custom-call(bf16[4,2048,768]{2,1,0:T(8,128)(2,1)} %weight.3, bf16[64,2048]{1,0:T(8,128)(2,1)S(1)} %constant_dynamic-update-slice_fusion.value), custom_call_target="tpu_custom_call" | custom-call | bytes 12582912 | tf_op jit(solution)/shard_map/load_gate/pallas_call | solution.py:368
  23.1 0.0 collective-permute-done.5
  23.2 0.0 collective-permute-done.6
  23.2 0.2 collective-permute-done.3
  23.4 0.1 collective-permute-start.4
  23.5 0.0 collective-permute-done.7
  23.5 1.6 %collective-permute-start.8 = (bf16[64,2176]{1,0:T(8,128)(2,1)S(1)}, bf16[64,2176]{1,0:T(8,128)(2,1)S(1)}, u32[]{:S(2)}, u32[]{:S(2)}) collective-permute-start(bf16[64,2176]{1,0:T(8,128)(2,1)S(1)} %constant_dynamic-update-slice_fusion.7.refs_7_), channel_id=1, source_target_pairs={{0,8},{4,12},{8,0},{12,4},{1,9},{5,13},{9,1},{13,5},{2,10},{6,14},... | collective-permute-start | bytes 835592 | tf_op jit(solution)/shard_map/ppermute | solution.py:311
  25.1 0.3 collective-permute-done.4
  25.5 0.0 copy-start.1
  25.5 3.7 %gate.1 = (f32[256,768]{1,0:T(8,128)S(1)}, f32[256,768]{1,0:T(8,128)S(1)}, f32[256,768]{1,0:T(8,128)S(1)}, f32[256,768]{1,0:T(8,128)S(1)}, bf16[512,768]{1,0:T(8...) custom-call(bf16[2048,768]{1,0:T(8,128)(2,1)S(1)} %get-tuple-element, ...), custom_call_target="tpu_custom_call" | custom-call | flops 3221225472 | bytes 12582912 | tf_op jit(solution)/shard_map/gate/pallas_call | solution.py:394
  29.2 3.5 %up.2 = (bf16[256,768]{1,0:T(8,128)(2,1)S(1)}, bf16[256,768]{1,0:T(8,128)(2,1)S(1)}, bf16[256,768]{1,0:T(8,128)(2,1)S(1)}, bf16[256,768]{1,0:T(8,128)(2,1)S(1)},...) custom-call(f32[256,768]{1,0:T(8,128)S(1)} %get-tuple-element.74.ref, ...), custom_call_target="tpu_custom_call" | custom-call | flops 1610612736 | bytes 6291456 | tf_op jit(solution)/shard_map/up/pallas_call | solution.py:416
  32.7 0.0 collective-permute-done.8
  32.7 0.1 constant_dynamic-update-slice_fusion.11
  32.8 0.2 collective-permute-start.9
  33.0 0.1 turn.1.x_part
  33.1 3.8 %up.3 = (bf16[256,768]{1,0:T(8,128)(2,1)S(1)}, bf16[256,768]{1,0:T(8,128)(2,1)S(1)}, bf16[256,768]{1,0:T(8,128)(2,1)S(1)}, bf16[256,768]{1,0:T(8,128)(2,1)S(1)},...) custom-call(f32[256,768]{1,0:T(8,128)S(1)} %get-tuple-element.92.ref, ...), custom_call_target="tpu_custom_call" | custom-call | flops 1610612736 | bytes 6291456 | tf_op jit(solution)/shard_map/up/pallas_call | solution.py:416
  36.9 0.0 collective-permute-done.9
  36.9 0.1 constant_dynamic-update-slice_fusion.13.refs_0_.packet
  37.0 7.0 %hidden.1 = (bf16[4,256,768]{2,1,0:T(8,128)(2,1)S(1)}, bf16[4,256,768]{2,1,0:T(8,128)(2,1)S(1)}, bf16[4,256,768]{2,1,0:T(8,128)(2,1)S(1)}, bf16[64,1152]{1,0:T(8...) custom-call(bf16[256,2176]{1,0:T(8,128)(2,1)S(1)} %constant_dynamic-update-, ...), custom_call_target="tpu_custom_call" | custom-call | flops 6442450944 | bytes 25165824 | tf_op jit(solution)/shard_map/hidden/pallas_call | solution.py:458
  44.0 0.0 copy-start
  44.0 1.6 %collective-permute-start.10 = (bf16[64,1152]{1,0:T(8,128)(2,1)S(1)}, bf16[64,1152]{1,0:T(8,128)(2,1)S(1)}, u32[]{:S(2)}, u32[]{:S(2)}) collective-permute-start(bf16[64,1152]{1,0:T(8,128)(2,1)S(1)} %get-tuple-element.109), channel_id=1, source_target_pairs={{0,8},{4,12},{8,0},{12,4},{1,9},{5,13},{9,1},{13,5},{2,10},{6,14},... | collective-permute-start | bytes 442376 | tf_op jit(solution)/shard_map/ppermute | solution.py:311
  45.6 0.1 collective-permute-start.11
  45.7 0.6 collective-permute-start.12
  46.2 5.2 %grad_in.1 = (f32[4,512,768]{2,1,0:T(8,128)}, f32[4,512,768]{2,1,0:T(8,128)}, f32[8,128]{1,0:T(8,128)S(1)}) custom-call(bf16[512,256]{1,0:T(8,128)(2,1)S(1)} %turn.1.x_part, bf16[4,256,768]{2,1,0:T(8,128)(2,1)S(1)} %get-tuple-element.112.d_gate, bf16[4,256,768]{2,1,0:T(8,128)(2,1)S(1)} %get-tuple-element.113.d_up), custom_call_target="tpu_custom_call" | custom-call | flops 1610612736 | bytes 12582912 | tf_op jit(solution)/shard_map/grad_in/pallas_call | solution.py:478
  51.5 0.0 collective-permute-done.10.refs_1_
  51.5 0.0 collective-permute-done.11.refs_2_
  51.5 1.3 %collective-permute-done.12.refs_3_ = bf16[64,1152]{1,0:T(8,128)(2,1)S(1)} collective-permute-done((bf16[64,1152]{1,0:T(8,128)(2,1)S(1)}, bf16[64,1152]{1,0:T(8,128)(2,1)S(1)}, u32[]{:S(2)}, u32[]{:S(2)}) %collective-permute-start.12) | collective-permute-done | bytes 147488 | tf_op jit(solution)/shard_map/ppermute | solution.py:311
  52.8 0.8 %reduce.1 = (f32[8,16]{1,0:T(8,128)}, bf16[16,1024]{1,0:T(8,128)(2,1)S(1)}, bf16[16,1024]{1,0:T(8,128)(2,1)S(1)}, bf16[16,1024]{1,0:T(8,128)(2,1)S(1)}, bf16[16,...) custom-call(bf16[64,1152]{1,0:T(8,128)(2,1)S(1)} %get-tuple-element.108.refs_0_, ...), custom_call_target="tpu_custom_call" | custom-call | tf_op jit(solution)/shard_map/reduce/pallas_call | solution.py:493
  53.6 0.6 collective-permute-start.13
  54.2 3.5 %collective-permute-start.14 = (bf16[16,1024]{1,0:T(8,128)(2,1)S(1)}, bf16[16,1024]{1,0:T(8,128)(2,1)S(1)}, u32[]{:S(2)}, u32[]{:S(2)}) collective-permute-start(bf16[16,1024]{1,0:T(8,128)(2,1)S(1)} %get-tuple-element.117), channel_id=1, source_target_pairs={{0,2},{1,3},{2,0},{3,1},{4,6},{5,7},{6,4},{7,5},{8,10},{9,11},{10,... | collective-permute-start | bytes 98312 | tf_op jit(solution)/shard_map/ppermute | solution.py:311
  57.7 0.3 collective-permute-start.15
  58.0 3.6 %grad_out.1 = (f32[4,768,512]{2,1,0:T(8,128)}, f32[8,128]{1,0:T(8,128)S(1)}) custom-call(bf16[256,2176]{1,0:T(8,128)(2,1)S(1)} %constant_dynamic-update-slice_fusion.13.refs_0_.packet, bf16[4,256,768]{2,1,0:T(8,128)(2,1)S(1)} %get-tuple-element.119.hidden, f32[8,128]{1,0:T(8,128)S(1)} %get-tuple-element.120.after), custom_call_target="tpu_custom_call" | custom-call | flops 805306368 | bytes 6291456 | tf_op jit(solution)/shard_map/grad_out/pallas_call | solution.py:505
  61.6 0.0 collective-permute-done.13.refs_1_
  61.6 0.0 collective-permute-done.14.refs_2_
  61.6 1.8 %collective-permute-done.15.refs_3_ = bf16[16,1024]{1,0:T(8,128)(2,1)S(1)} collective-permute-done((bf16[16,1024]{1,0:T(8,128)(2,1)S(1)}, bf16[16,1024]{1,0:T(8,128)(2,1)S(1)}, u32[]{:S(2)}, u32[]{:S(2)}) %collective-permute-start.15) | collective-permute-done | bytes 32800 | tf_op jit(solution)/shard_map/ppermute | solution.py:311
  63.4 0.7 %join.1 = (bf16[16,2048]{1,0:T(8,128)(2,1)}, bf16[16,2048]{1,0:T(8,128)(2,1)}) custom-call(bf16[16,1024]{1,0:T(8,128)(2,1)S(1)} %get-tuple-element.115.refs_0_, bf16[16,1024]{1,0:T(8,128)(2,1)S(1)} %collective-permute-done.13.refs_1_, bf16[16,1024]{1,0:T(8,128)(2,1)S(1)} %collective-permute-done.14.refs_2_, ...), custom_call_target="tpu_custom_call" | custom-call | tf_op jit(solution)/shard_map/join/pallas_call | solution.py:520
  (15 shorter events, 0.2 us)
Async XLA Ops:
  0.6 15.9 %collective-permute-start = (bf16[16,2048]{1,0:T(8,128)(2,1)}, bf16[16,2048]{1,0:T(8,128)(2,1)S(1)}, u32[]{:S(2)}, u32[]{:S(2)}) collective-permute-start(bf16[16,2048]{1,0:T(8,128)(2,1)} %tokens.1), channel_id=1, source_target_pairs={{0,1},{1,0},{2,3},{3,2},{4,5},{5,4},{6,7},{7,6},{8,9},{9,8},{10,11... | collective-permute-start | bytes 196616 | tf_op jit(solution)/shard_map/ppermute | solution.py:311
  3.7 12.9 %collective-permute-start.1 = (bf16[16,2048]{1,0:T(8,128)(2,1)}, bf16[16,2048]{1,0:T(8,128)(2,1)S(1)}, u32[]{:S(2)}, u32[]{:S(2)}) collective-permute-start(bf16[16,2048]{1,0:T(8,128)(2,1)} %tokens.1), channel_id=1, source_target_pairs={{0,2},{1,3},{2,0},{3,1},{4,6},{5,7},{6,4},{7,5},{8,10},{9,11},{10,... | collective-permute-start | bytes 196616 | tf_op jit(solution)/shard_map/ppermute | solution.py:311
  6.3 10.3 %collective-permute-start.2 = (bf16[16,2048]{1,0:T(8,128)(2,1)}, bf16[16,2048]{1,0:T(8,128)(2,1)S(1)}, u32[]{:S(2)}, u32[]{:S(2)}) collective-permute-start(bf16[16,2048]{1,0:T(8,128)(2,1)} %tokens.1), channel_id=1, source_target_pairs={{0,3},{1,2},{2,1},{3,0},{4,7},{5,6},{6,5},{7,4},{8,11},{9,10},{10,... | collective-permute-start | bytes 196616 | tf_op jit(solution)/shard_map/ppermute | solution.py:311
  7.4 15.8 %collective-permute-start.5 = (bf16[16,2176]{1,0:T(8,128)(2,1)S(1)}, bf16[16,2176]{1,0:T(8,128)(2,1)S(1)}, u32[]{:S(2)}, u32[]{:S(2)}) collective-permute-start(bf16[16,2176]{1,0:T(8,128)(2,1)S(1)} %get-tuple-element.78), channel_id=1, source_target_pairs={{0,1},{1,0},{2,3},{3,2},{4,5},{5,4},{6,7},{7,6},{8,9},{9,8},{10,11... | collective-permute-start | bytes 208904 | tf_op jit(solution)/shard_map/ppermute | solution.py:311
  8.3 14.9 %collective-permute-start.6 = (bf16[16,2176]{1,0:T(8,128)(2,1)S(1)}, bf16[16,2176]{1,0:T(8,128)(2,1)S(1)}, u32[]{:S(2)}, u32[]{:S(2)}) collective-permute-start(bf16[16,2176]{1,0:T(8,128)(2,1)S(1)} %get-tuple-element.78), channel_id=1, source_target_pairs={{0,2},{1,3},{2,0},{3,1},{4,6},{5,7},{6,4},{7,5},{8,10},{9,11},{10,... | collective-permute-start | bytes 208904 | tf_op jit(solution)/shard_map/ppermute | solution.py:311
  16.5 7.0 %collective-permute-start.7 = (bf16[16,2176]{1,0:T(8,128)(2,1)S(1)}, bf16[16,2176]{1,0:T(8,128)(2,1)S(1)}, u32[]{:S(2)}, u32[]{:S(2)}) collective-permute-start(bf16[16,2176]{1,0:T(8,128)(2,1)S(1)} %get-tuple-element.78), channel_id=1, source_target_pairs={{0,3},{1,2},{2,1},{3,0},{4,7},{5,6},{6,5},{7,4},{8,11},{9,10},{10,... | collective-permute-start | bytes 208904 | tf_op jit(solution)/shard_map/ppermute | solution.py:311
  16.7 6.7 %collective-permute-start.3 = (bf16[64,2048]{1,0:T(8,128)(2,1)S(1)}, bf16[64,2048]{1,0:T(8,128)(2,1)S(1)}, u32[]{:S(2)}, u32[]{:S(2)}) collective-permute-start(bf16[64,2048]{1,0:T(8,128)(2,1)S(1)} %constant_dynamic-update-slice_fusion.value), channel_id=1, source_target_pairs={{0,8},{4,12},{8,0},{12,4},{1,9},{5,13},{9,1},{13,5},{2,10},{6,14},... | collective-permute-start | bytes 786440 | tf_op jit(solution)/shard_map/ppermute | solution.py:311
  23.4 2.0 %collective-permute-start.4 = (bf16[128,2048]{1,0:T(8,128)(2,1)S(1)}, bf16[128,2048]{1,0:T(8,128)(2,1)S(1)}, u32[]{:S(2)}, u32[]{:S(2)}) collective-permute-start(bf16[128,2048]{1,0:T(8,128)(2,1)S(1)} %pad_maximum_fusion), channel_id=1, source_target_pairs={{0,4},{4,0},{8,12},{12,8},{1,5},{5,1},{9,13},{13,9},{2,6},{6,2},{1... | collective-permute-start | bytes 1572872 | tf_op jit(solution)/shard_map/ppermute | solution.py:311
  23.5 9.2 %collective-permute-start.8 = (bf16[64,2176]{1,0:T(8,128)(2,1)S(1)}, bf16[64,2176]{1,0:T(8,128)(2,1)S(1)}, u32[]{:S(2)}, u32[]{:S(2)}) collective-permute-start(bf16[64,2176]{1,0:T(8,128)(2,1)S(1)} %constant_dynamic-update-slice_fusion.7.refs_7_), channel_id=1, source_target_pairs={{0,8},{4,12},{8,0},{12,4},{1,9},{5,13},{9,1},{13,5},{2,10},{6,14},... | collective-permute-start | bytes 835592 | tf_op jit(solution)/shard_map/ppermute | solution.py:311
  25.5 3.7 %copy-start.1 = (s32[4,6]{1,0:T(4,128)S(1)}, s32[4,6]{1,0:T(4,128)}, u32[]{:S(2)}) copy-start(s32[4,6]{1,0:T(4,128)} %refs_5_.5) | copy-start | bytes 292
  32.8 4.1 %collective-permute-start.9 = (bf16[128,2176]{1,0:T(8,128)(2,1)S(1)}, bf16[128,2176]{1,0:T(8,128)(2,1)S(1)}, u32[]{:S(2)}, u32[]{:S(2)}) collective-permute-start(bf16[128,2176]{1,0:T(8,128)(2,1)S(1)} %get-tuple-element.128.after), channel_id=1, source_target_pairs={{0,4},{4,0},{8,12},{12,8},{1,5},{5,1},{9,13},{13,9},{2,6},{6,2},{1... | collective-permute-start | bytes 1671176 | tf_op jit(solution)/shard_map/ppermute | solution.py:311
  44.0 8.8 %copy-start = (s32[16,8]{0,1:T(8,128)S(1)}, s32[16,8]{0,1:T(8,128)}, u32[]{:S(2)}) copy-start(s32[16,8]{0,1:T(8,128)} %param.10) | copy-start | bytes 1540
  44.0 7.5 %collective-permute-start.10 = (bf16[64,1152]{1,0:T(8,128)(2,1)S(1)}, bf16[64,1152]{1,0:T(8,128)(2,1)S(1)}, u32[]{:S(2)}, u32[]{:S(2)}) collective-permute-start(bf16[64,1152]{1,0:T(8,128)(2,1)S(1)} %get-tuple-element.109), channel_id=1, source_target_pairs={{0,8},{4,12},{8,0},{12,4},{1,9},{5,13},{9,1},{13,5},{2,10},{6,14},... | collective-permute-start | bytes 442376 | tf_op jit(solution)/shard_map/ppermute | solution.py:311
  45.6 5.9 %collective-permute-start.11 = (bf16[64,1152]{1,0:T(8,128)(2,1)S(1)}, bf16[64,1152]{1,0:T(8,128)(2,1)S(1)}, u32[]{:S(2)}, u32[]{:S(2)}) collective-permute-start(bf16[64,1152]{1,0:T(8,128)(2,1)S(1)} %get-tuple-element.110), channel_id=1, source_target_pairs={{0,4},{4,0},{8,12},{12,8},{1,5},{5,1},{9,13},{13,9},{2,6},{6,2},{1... | collective-permute-start | bytes 442376 | tf_op jit(solution)/shard_map/ppermute | solution.py:311
  45.7 7.1 %collective-permute-start.12 = (bf16[64,1152]{1,0:T(8,128)(2,1)S(1)}, bf16[64,1152]{1,0:T(8,128)(2,1)S(1)}, u32[]{:S(2)}, u32[]{:S(2)}) collective-permute-start(bf16[64,1152]{1,0:T(8,128)(2,1)S(1)} %get-tuple-element.111), channel_id=1, source_target_pairs={{0,12},{4,8},{8,4},{12,0},{1,13},{5,9},{9,5},{13,1},{2,14},{6,10},... | collective-permute-start | bytes 442376 | tf_op jit(solution)/shard_map/ppermute | solution.py:311
  53.6 8.0 %collective-permute-start.13 = (bf16[16,1024]{1,0:T(8,128)(2,1)S(1)}, bf16[16,1024]{1,0:T(8,128)(2,1)S(1)}, u32[]{:S(2)}, u32[]{:S(2)}) collective-permute-start(bf16[16,1024]{1,0:T(8,128)(2,1)S(1)} %get-tuple-element.116), channel_id=1, source_target_pairs={{0,1},{1,0},{2,3},{3,2},{4,5},{5,4},{6,7},{7,6},{8,9},{9,8},{10,11... | collective-permute-start | bytes 98312 | tf_op jit(solution)/shard_map/ppermute | solution.py:311
  54.2 7.5 %collective-permute-start.14 = (bf16[16,1024]{1,0:T(8,128)(2,1)S(1)}, bf16[16,1024]{1,0:T(8,128)(2,1)S(1)}, u32[]{:S(2)}, u32[]{:S(2)}) collective-permute-start(bf16[16,1024]{1,0:T(8,128)(2,1)S(1)} %get-tuple-element.117), channel_id=1, source_target_pairs={{0,2},{1,3},{2,0},{3,1},{4,6},{5,7},{6,4},{7,5},{8,10},{9,11},{10,... | collective-permute-start | bytes 98312 | tf_op jit(solution)/shard_map/ppermute | solution.py:311
  57.7 5.7 %collective-permute-start.15 = (bf16[16,1024]{1,0:T(8,128)(2,1)S(1)}, bf16[16,1024]{1,0:T(8,128)(2,1)S(1)}, u32[]{:S(2)}, u32[]{:S(2)}) collective-permute-start(bf16[16,1024]{1,0:T(8,128)(2,1)S(1)} %get-tuple-element.118), channel_id=1, source_target_pairs={{0,3},{1,2},{2,1},{3,0},{4,7},{5,6},{6,5},{7,4},{8,11},{9,10},{10,... | collective-permute-start | bytes 98312 | tf_op jit(solution)/shard_map/ppermute | solution.py:311

commit v16 on v15

--- a/solution.py
+++ b/solution.py
@@ -9,7 +9,7 @@
 
 BLK = 128
 LANES = 128
-CHUNK = 256
+CHUNK = 768
 TILE = 256
 MIB = 1 << 20
 

time: 64.3 us -> 64.1 us (level)
  no operation moved by 1% of the time
where the time goes in v16:
time: 64.1 us; the launch traced here: 64 us
  Pallas kernels  38.6 us (60%)
  starting transfers between devices  20.4 us (32%)
  waiting for transfers between devices  3.64 us (6%)
  between operations  0.94 us (1%)
    ppermute x16, starting transfers between devices, swap(): return lax.ppermute(value, axis, [(i, i ^ mask) for i in range(size)])  20.4 us
    pallas_call x2, Pallas kernels, load(): pl.pallas_call(load_kernel, out_shape=[struct(value.shape, bf16)] + [pltp...  9.37 us
    pallas_call x2, Pallas kernels, up_call(): pl.pallas_call(functools.partial(up_kernel, first, last, start_down), out...  7.15 us
    pallas_call x1, Pallas kernels, per_device(): pl.pallas_call(functools.partial(hidden_kernel, local_experts, sources),...  6.97 us
    pallas_call x1, Pallas kernels, per_device(): pl.pallas_call(grad_in_kernel, out_shape=[struct((local_experts, part, hi...  5.22 us
    pallas_call x1, Pallas kernels, per_device(): pl.pallas_call(functools.partial(gate_kernel, local_experts), out_shape=[...  3.7 us
    ppermute x16, waiting for transfers between devices, swap(): return lax.ppermute(value, axis, [(i, i ^ mask) for i in range(size)])  3.64 us
    pallas_call x1, Pallas kernels, per_device(): pl.pallas_call(grad_out_kernel, out_shape=[struct((local_experts, hidden_...  3.63 us
  transfers between devices with their start and end apart: 16, of which 4 were waited for; matrix products, arithmetic and copies ran while one was open for 0% of the time, Pallas kernels for 47%

profile of v16, /device:TPU:0, one launch (start us, length us, event | category | flops | bytes accessed | tf_op | source)
XLA Modules:
  0.0 64.0 jit_solution(3047435145258568660)
XLA Ops:
  0.6 3.1 %collective-permute-start = (bf16[16,2048]{1,0:T(8,128)(2,1)}, bf16[16,2048]{1,0:T(8,128)(2,1)S(1)}, u32[]{:S(2)}, u32[]{:S(2)}) collective-permute-start(bf16[16,2048]{1,0:T(8,128)(2,1)} %tokens.1), channel_id=1, source_target_pairs={{0,1},{1,0},{2,3},{3,2},{4,5},{5,4},{6,7},{7,6},{8,9},{9,8},{10,11... | collective-permute-start | bytes 196616 | tf_op jit(solution)/shard_map/ppermute | solution.py:311
  3.7 2.6 %collective-permute-start.1 = (bf16[16,2048]{1,0:T(8,128)(2,1)}, bf16[16,2048]{1,0:T(8,128)(2,1)S(1)}, u32[]{:S(2)}, u32[]{:S(2)}) collective-permute-start(bf16[16,2048]{1,0:T(8,128)(2,1)} %tokens.1), channel_id=1, source_target_pairs={{0,2},{1,3},{2,0},{3,1},{4,6},{5,7},{6,4},{7,5},{8,10},{9,11},{10,... | collective-permute-start | bytes 196616 | tf_op jit(solution)/shard_map/ppermute | solution.py:311
  6.3 0.0 collective-permute-start.2
  6.3 1.0 %route.1 = (bf16[16,2048]{1,0:T(8,128)(2,1)S(1)}, bf16[16,2176]{1,0:T(8,128)(2,1)S(1)}) custom-call(bf16[16,2048]{1,0:T(8,128)(2,1)} %tokens.1, bf16[16,2048]{1,0:T(8,128)(2,1)} %cotangent.1, s32[8,16]{1,0:T(8,128)} %bitcast.3, bf16[8,16]{1,0:T(8,128)(2,1)} %bitcast.5), custom_call_target="tpu_custom_call" | custom-call | tf_op jit(solution)/shard_map/route/pallas_call | solution.py:353
  7.4 1.0 %collective-permute-start.5 = (bf16[16,2176]{1,0:T(8,128)(2,1)S(1)}, bf16[16,2176]{1,0:T(8,128)(2,1)S(1)}, u32[]{:S(2)}, u32[]{:S(2)}) collective-permute-start(bf16[16,2176]{1,0:T(8,128)(2,1)S(1)} %get-tuple-element.78), channel_id=1, source_target_pairs={{0,1},{1,0},{2,3},{3,2},{4,5},{5,4},{6,7},{7,6},{8,9},{9,8},{10,11... | collective-permute-start | bytes 208904 | tf_op jit(solution)/shard_map/ppermute | solution.py:311
  8.3 3.5 %collective-permute-start.6 = (bf16[16,2176]{1,0:T(8,128)(2,1)S(1)}, bf16[16,2176]{1,0:T(8,128)(2,1)S(1)}, u32[]{:S(2)}, u32[]{:S(2)}) collective-permute-start(bf16[16,2176]{1,0:T(8,128)(2,1)S(1)} %get-tuple-element.78), channel_id=1, source_target_pairs={{0,2},{1,3},{2,0},{3,1},{4,6},{5,7},{6,4},{7,5},{8,10},{9,11},{10,... | collective-permute-start | bytes 208904 | tf_op jit(solution)/shard_map/ppermute | solution.py:311
  11.8 4.7 %load_up.1 = (bf16[16,2048]{1,0:T(8,128)(2,1)S(1)}, bf16[2048,768]{1,0:T(8,128)(2,1)S(1)}, bf16[2048,768]{1,0:T(8,128)(2,1)S(1)}, bf16[2048,768]{1,0:T(8,128)(2,1)S(1)}, bf16[2048,768]{1,0:T(8,128)(2,1)S(1)}) custom-call(bf16[4,2048,768]{2,1,0:T(8,128)(2,1)} %weight.2, bf16[16,2048]{1,0:T(8,128)(2,1)S(1)} %get-tuple-element.67.value), custom_call_target="tpu_custom_call" | custom-call | bytes 12582912 | tf_op jit(solution)/shard_map/load_up/pallas_call | solution.py:368
  16.5 0.0 collective-permute-done
  16.5 0.1 collective-permute-start.7
  16.6 0.0 collective-permute-done.1
  16.6 0.0 collective-permute-done.2
  16.7 1.8 %collective-permute-start.3 = (bf16[64,2048]{1,0:T(8,128)(2,1)S(1)}, bf16[64,2048]{1,0:T(8,128)(2,1)S(1)}, u32[]{:S(2)}, u32[]{:S(2)}) collective-permute-start(bf16[64,2048]{1,0:T(8,128)(2,1)S(1)} %constant_dynamic-update-slice_fusion.value), channel_id=1, source_target_pairs={{0,8},{4,12},{8,0},{12,4},{1,9},{5,13},{9,1},{13,5},{2,10},{6,14},... | collective-permute-start | bytes 786440 | tf_op jit(solution)/shard_map/ppermute | solution.py:311
  18.4 4.7 %load_gate.1 = (bf16[64,2048]{1,0:T(8,128)(2,1)S(1)}, bf16[2048,768]{1,0:T(8,128)(2,1)S(1)}, bf16[2048,768]{1,0:T(8,128)(2,1)S(1)}, bf16[2048,768]{1,0:T(8,128)(2,1)S(1)}, bf16[2048,768]{1,0:T(8,128)(2,1)S(1)}) custom-call(bf16[4,2048,768]{2,1,0:T(8,128)(2,1)} %weight.3, bf16[64,2048]{1,0:T(8,128)(2,1)S(1)} %constant_dynamic-update-slice_fusion.value), custom_call_target="tpu_custom_call" | custom-call | bytes 12582912 | tf_op jit(solution)/shard_map/load_gate/pallas_call | solution.py:368
  23.1 0.0 collective-permute-done.5
  23.2 0.0 collective-permute-done.6
  23.2 0.2 collective-permute-done.3
  23.4 0.1 collective-permute-start.4
  23.5 0.0 collective-permute-done.7
  23.5 1.6 %collective-permute-start.8 = (bf16[64,2176]{1,0:T(8,128)(2,1)S(1)}, bf16[64,2176]{1,0:T(8,128)(2,1)S(1)}, u32[]{:S(2)}, u32[]{:S(2)}) collective-permute-start(bf16[64,2176]{1,0:T(8,128)(2,1)S(1)} %constant_dynamic-update-slice_fusion.7.refs_7_), channel_id=1, source_target_pairs={{0,8},{4,12},{8,0},{12,4},{1,9},{5,13},{9,1},{13,5},{2,10},{6,14},... | collective-permute-start | bytes 835592 | tf_op jit(solution)/shard_map/ppermute | solution.py:311
  25.1 0.3 collective-permute-done.4
  25.5 0.0 copy-start.1
  25.5 3.7 %gate.1 = (f32[256,768]{1,0:T(8,128)S(1)}, f32[256,768]{1,0:T(8,128)S(1)}, f32[256,768]{1,0:T(8,128)S(1)}, f32[256,768]{1,0:T(8,128)S(1)}, bf16[512,768]{1,0:T(8...) custom-call(bf16[2048,768]{1,0:T(8,128)(2,1)S(1)} %get-tuple-element, ...), custom_call_target="tpu_custom_call" | custom-call | flops 3221225472 | bytes 12582912 | tf_op jit(solution)/shard_map/gate/pallas_call | solution.py:394
  29.2 3.5 %up.2 = (bf16[256,768]{1,0:T(8,128)(2,1)S(1)}, bf16[256,768]{1,0:T(8,128)(2,1)S(1)}, bf16[256,768]{1,0:T(8,128)(2,1)S(1)}, bf16[256,768]{1,0:T(8,128)(2,1)S(1)},...) custom-call(f32[256,768]{1,0:T(8,128)S(1)} %get-tuple-element.74.ref, ...), custom_call_target="tpu_custom_call" | custom-call | flops 1610612736 | bytes 6291456 | tf_op jit(solution)/shard_map/up/pallas_call | solution.py:416
  32.7 0.0 collective-permute-done.8
  32.7 0.1 constant_dynamic-update-slice_fusion.11
  32.8 0.2 collective-permute-start.9
  33.0 0.1 turn.1.x_part
  33.1 3.7 %up.3 = (bf16[256,768]{1,0:T(8,128)(2,1)S(1)}, bf16[256,768]{1,0:T(8,128)(2,1)S(1)}, bf16[256,768]{1,0:T(8,128)(2,1)S(1)}, bf16[256,768]{1,0:T(8,128)(2,1)S(1)},...) custom-call(f32[256,768]{1,0:T(8,128)S(1)} %get-tuple-element.92.ref, ...), custom_call_target="tpu_custom_call" | custom-call | flops 1610612736 | bytes 6291456 | tf_op jit(solution)/shard_map/up/pallas_call | solution.py:416
  36.8 0.0 collective-permute-done.9
  36.8 0.1 constant_dynamic-update-slice_fusion.13.refs_0_.packet
  36.9 7.0 %hidden.1 = (bf16[4,256,768]{2,1,0:T(8,128)(2,1)S(1)}, bf16[4,256,768]{2,1,0:T(8,128)(2,1)S(1)}, bf16[4,256,768]{2,1,0:T(8,128)(2,1)S(1)}, bf16[64,1152]{1,0:T(8...) custom-call(bf16[256,2176]{1,0:T(8,128)(2,1)S(1)} %constant_dynamic-update-, ...), custom_call_target="tpu_custom_call" | custom-call | flops 6442450944 | bytes 25165824 | tf_op jit(solution)/shard_map/hidden/pallas_call | solution.py:458
  43.9 0.0 copy-start
  43.9 1.6 %collective-permute-start.10 = (bf16[64,1152]{1,0:T(8,128)(2,1)S(1)}, bf16[64,1152]{1,0:T(8,128)(2,1)S(1)}, u32[]{:S(2)}, u32[]{:S(2)}) collective-permute-start(bf16[64,1152]{1,0:T(8,128)(2,1)S(1)} %get-tuple-element.109), channel_id=1, source_target_pairs={{0,8},{4,12},{8,0},{12,4},{1,9},{5,13},{9,1},{13,5},{2,10},{6,14},... | collective-permute-start | bytes 442376 | tf_op jit(solution)/shard_map/ppermute | solution.py:311
  45.4 0.1 collective-permute-start.11
  45.5 0.6 collective-permute-start.12
  46.1 5.2 %grad_in.1 = (f32[4,512,768]{2,1,0:T(8,128)}, f32[4,512,768]{2,1,0:T(8,128)}, f32[8,128]{1,0:T(8,128)S(1)}) custom-call(bf16[512,256]{1,0:T(8,128)(2,1)S(1)} %turn.1.x_part, bf16[4,256,768]{2,1,0:T(8,128)(2,1)S(1)} %get-tuple-element.112.d_gate, bf16[4,256,768]{2,1,0:T(8,128)(2,1)S(1)} %get-tuple-element.113.d_up), custom_call_target="tpu_custom_call" | custom-call | flops 1610612736 | bytes 12582912 | tf_op jit(solution)/shard_map/grad_in/pallas_call | solution.py:478
  51.3 0.0 collective-permute-done.10.refs_1_
  51.3 0.0 collective-permute-done.11.refs_2_
  51.4 1.3 %collective-permute-done.12.refs_3_ = bf16[64,1152]{1,0:T(8,128)(2,1)S(1)} collective-permute-done((bf16[64,1152]{1,0:T(8,128)(2,1)S(1)}, bf16[64,1152]{1,0:T(8,128)(2,1)S(1)}, u32[]{:S(2)}, u32[]{:S(2)}) %collective-permute-start.12) | collective-permute-done | bytes 147488 | tf_op jit(solution)/shard_map/ppermute | solution.py:311
  52.7 0.8 %reduce.1 = (f32[8,16]{1,0:T(8,128)}, bf16[16,1024]{1,0:T(8,128)(2,1)S(1)}, bf16[16,1024]{1,0:T(8,128)(2,1)S(1)}, bf16[16,1024]{1,0:T(8,128)(2,1)S(1)}, bf16[16,...) custom-call(bf16[64,1152]{1,0:T(8,128)(2,1)S(1)} %get-tuple-element.108.refs_0_, ...), custom_call_target="tpu_custom_call" | custom-call | tf_op jit(solution)/shard_map/reduce/pallas_call | solution.py:493
  53.4 0.6 collective-permute-start.13
  54.1 3.5 %collective-permute-start.14 = (bf16[16,1024]{1,0:T(8,128)(2,1)S(1)}, bf16[16,1024]{1,0:T(8,128)(2,1)S(1)}, u32[]{:S(2)}, u32[]{:S(2)}) collective-permute-start(bf16[16,1024]{1,0:T(8,128)(2,1)S(1)} %get-tuple-element.117), channel_id=1, source_target_pairs={{0,2},{1,3},{2,0},{3,1},{4,6},{5,7},{6,4},{7,5},{8,10},{9,11},{10,... | collective-permute-start | bytes 98312 | tf_op jit(solution)/shard_map/ppermute | solution.py:311
  57.6 0.2 collective-permute-start.15
  57.8 3.6 %grad_out.1 = (f32[4,768,512]{2,1,0:T(8,128)}, f32[8,128]{1,0:T(8,128)S(1)}) custom-call(bf16[256,2176]{1,0:T(8,128)(2,1)S(1)} %constant_dynamic-update-slice_fusion.13.refs_0_.packet, bf16[4,256,768]{2,1,0:T(8,128)(2,1)S(1)} %get-tuple-element.119.hidden, f32[8,128]{1,0:T(8,128)S(1)} %get-tuple-element.120.after), custom_call_target="tpu_custom_call" | custom-call | flops 805306368 | bytes 6291456 | tf_op jit(solution)/shard_map/grad_out/pallas_call | solution.py:505
  61.5 0.0 collective-permute-done.13.refs_1_
  61.5 0.0 collective-permute-done.14.refs_2_
  61.5 1.8 %collective-permute-done.15.refs_3_ = bf16[16,1024]{1,0:T(8,128)(2,1)S(1)} collective-permute-done((bf16[16,1024]{1,0:T(8,128)(2,1)S(1)}, bf16[16,1024]{1,0:T(8,128)(2,1)S(1)}, u32[]{:S(2)}, u32[]{:S(2)}) %collective-permute-start.15) | collective-permute-done | bytes 32800 | tf_op jit(solution)/shard_map/ppermute | solution.py:311
  63.3 0.7 %join.1 = (bf16[16,2048]{1,0:T(8,128)(2,1)}, bf16[16,2048]{1,0:T(8,128)(2,1)}) custom-call(bf16[16,1024]{1,0:T(8,128)(2,1)S(1)} %get-tuple-element.115.refs_0_, bf16[16,1024]{1,0:T(8,128)(2,1)S(1)} %collective-permute-done.13.refs_1_, bf16[16,1024]{1,0:T(8,128)(2,1)S(1)} %collective-permute-done.14.refs_2_, ...), custom_call_target="tpu_custom_call" | custom-call | tf_op jit(solution)/shard_map/join/pallas_call | solution.py:520
  (15 shorter events, 0.2 us)
Async XLA Ops:
  0.6 15.9 %collective-permute-start = (bf16[16,2048]{1,0:T(8,128)(2,1)}, bf16[16,2048]{1,0:T(8,128)(2,1)S(1)}, u32[]{:S(2)}, u32[]{:S(2)}) collective-permute-start(bf16[16,2048]{1,0:T(8,128)(2,1)} %tokens.1), channel_id=1, source_target_pairs={{0,1},{1,0},{2,3},{3,2},{4,5},{5,4},{6,7},{7,6},{8,9},{9,8},{10,11... | collective-permute-start | bytes 196616 | tf_op jit(solution)/shard_map/ppermute | solution.py:311
  3.7 12.9 %collective-permute-start.1 = (bf16[16,2048]{1,0:T(8,128)(2,1)}, bf16[16,2048]{1,0:T(8,128)(2,1)S(1)}, u32[]{:S(2)}, u32[]{:S(2)}) collective-permute-start(bf16[16,2048]{1,0:T(8,128)(2,1)} %tokens.1), channel_id=1, source_target_pairs={{0,2},{1,3},{2,0},{3,1},{4,6},{5,7},{6,4},{7,5},{8,10},{9,11},{10,... | collective-permute-start | bytes 196616 | tf_op jit(solution)/shard_map/ppermute | solution.py:311
  6.3 10.3 %collective-permute-start.2 = (bf16[16,2048]{1,0:T(8,128)(2,1)}, bf16[16,2048]{1,0:T(8,128)(2,1)S(1)}, u32[]{:S(2)}, u32[]{:S(2)}) collective-permute-start(bf16[16,2048]{1,0:T(8,128)(2,1)} %tokens.1), channel_id=1, source_target_pairs={{0,3},{1,2},{2,1},{3,0},{4,7},{5,6},{6,5},{7,4},{8,11},{9,10},{10,... | collective-permute-start | bytes 196616 | tf_op jit(solution)/shard_map/ppermute | solution.py:311
  7.4 15.8 %collective-permute-start.5 = (bf16[16,2176]{1,0:T(8,128)(2,1)S(1)}, bf16[16,2176]{1,0:T(8,128)(2,1)S(1)}, u32[]{:S(2)}, u32[]{:S(2)}) collective-permute-start(bf16[16,2176]{1,0:T(8,128)(2,1)S(1)} %get-tuple-element.78), channel_id=1, source_target_pairs={{0,1},{1,0},{2,3},{3,2},{4,5},{5,4},{6,7},{7,6},{8,9},{9,8},{10,11... | collective-permute-start | bytes 208904 | tf_op jit(solution)/shard_map/ppermute | solution.py:311
  8.3 14.9 %collective-permute-start.6 = (bf16[16,2176]{1,0:T(8,128)(2,1)S(1)}, bf16[16,2176]{1,0:T(8,128)(2,1)S(1)}, u32[]{:S(2)}, u32[]{:S(2)}) collective-permute-start(bf16[16,2176]{1,0:T(8,128)(2,1)S(1)} %get-tuple-element.78), channel_id=1, source_target_pairs={{0,2},{1,3},{2,0},{3,1},{4,6},{5,7},{6,4},{7,5},{8,10},{9,11},{10,... | collective-permute-start | bytes 208904 | tf_op jit(solution)/shard_map/ppermute | solution.py:311
  16.5 7.0 %collective-permute-start.7 = (bf16[16,2176]{1,0:T(8,128)(2,1)S(1)}, bf16[16,2176]{1,0:T(8,128)(2,1)S(1)}, u32[]{:S(2)}, u32[]{:S(2)}) collective-permute-start(bf16[16,2176]{1,0:T(8,128)(2,1)S(1)} %get-tuple-element.78), channel_id=1, source_target_pairs={{0,3},{1,2},{2,1},{3,0},{4,7},{5,6},{6,5},{7,4},{8,11},{9,10},{10,... | collective-permute-start | bytes 208904 | tf_op jit(solution)/shard_map/ppermute | solution.py:311
  16.7 6.7 %collective-permute-start.3 = (bf16[64,2048]{1,0:T(8,128)(2,1)S(1)}, bf16[64,2048]{1,0:T(8,128)(2,1)S(1)}, u32[]{:S(2)}, u32[]{:S(2)}) collective-permute-start(bf16[64,2048]{1,0:T(8,128)(2,1)S(1)} %constant_dynamic-update-slice_fusion.value), channel_id=1, source_target_pairs={{0,8},{4,12},{8,0},{12,4},{1,9},{5,13},{9,1},{13,5},{2,10},{6,14},... | collective-permute-start | bytes 786440 | tf_op jit(solution)/shard_map/ppermute | solution.py:311
  23.4 2.0 %collective-permute-start.4 = (bf16[128,2048]{1,0:T(8,128)(2,1)S(1)}, bf16[128,2048]{1,0:T(8,128)(2,1)S(1)}, u32[]{:S(2)}, u32[]{:S(2)}) collective-permute-start(bf16[128,2048]{1,0:T(8,128)(2,1)S(1)} %pad_maximum_fusion), channel_id=1, source_target_pairs={{0,4},{4,0},{8,12},{12,8},{1,5},{5,1},{9,13},{13,9},{2,6},{6,2},{1... | collective-permute-start | bytes 1572872 | tf_op jit(solution)/shard_map/ppermute | solution.py:311
  23.5 9.2 %collective-permute-start.8 = (bf16[64,2176]{1,0:T(8,128)(2,1)S(1)}, bf16[64,2176]{1,0:T(8,128)(2,1)S(1)}, u32[]{:S(2)}, u32[]{:S(2)}) collective-permute-start(bf16[64,2176]{1,0:T(8,128)(2,1)S(1)} %constant_dynamic-update-slice_fusion.7.refs_7_), channel_id=1, source_target_pairs={{0,8},{4,12},{8,0},{12,4},{1,9},{5,13},{9,1},{13,5},{2,10},{6,14},... | collective-permute-start | bytes 835592 | tf_op jit(solution)/shard_map/ppermute | solution.py:311
  25.5 3.7 %copy-start.1 = (s32[4,6]{1,0:T(4,128)S(1)}, s32[4,6]{1,0:T(4,128)}, u32[]{:S(2)}) copy-start(s32[4,6]{1,0:T(4,128)} %refs_5_.5) | copy-start | bytes 292
  32.8 4.0 %collective-permute-start.9 = (bf16[128,2176]{1,0:T(8,128)(2,1)S(1)}, bf16[128,2176]{1,0:T(8,128)(2,1)S(1)}, u32[]{:S(2)}, u32[]{:S(2)}) collective-permute-start(bf16[128,2176]{1,0:T(8,128)(2,1)S(1)} %get-tuple-element.128.after), channel_id=1, source_target_pairs={{0,4},{4,0},{8,12},{12,8},{1,5},{5,1},{9,13},{13,9},{2,6},{6,2},{1... | collective-permute-start | bytes 1671176 | tf_op jit(solution)/shard_map/ppermute | solution.py:311
  43.9 8.8 %copy-start = (s32[16,8]{0,1:T(8,128)S(1)}, s32[16,8]{0,1:T(8,128)}, u32[]{:S(2)}) copy-start(s32[16,8]{0,1:T(8,128)} %param.10) | copy-start | bytes 1540
  43.9 7.5 %collective-permute-start.10 = (bf16[64,1152]{1,0:T(8,128)(2,1)S(1)}, bf16[64,1152]{1,0:T(8,128)(2,1)S(1)}, u32[]{:S(2)}, u32[]{:S(2)}) collective-permute-start(bf16[64,1152]{1,0:T(8,128)(2,1)S(1)} %get-tuple-element.109), channel_id=1, source_target_pairs={{0,8},{4,12},{8,0},{12,4},{1,9},{5,13},{9,1},{13,5},{2,10},{6,14},... | collective-permute-start | bytes 442376 | tf_op jit(solution)/shard_map/ppermute | solution.py:311
  45.4 5.9 %collective-permute-start.11 = (bf16[64,1152]{1,0:T(8,128)(2,1)S(1)}, bf16[64,1152]{1,0:T(8,128)(2,1)S(1)}, u32[]{:S(2)}, u32[]{:S(2)}) collective-permute-start(bf16[64,1152]{1,0:T(8,128)(2,1)S(1)} %get-tuple-element.110), channel_id=1, source_target_pairs={{0,4},{4,0},{8,12},{12,8},{1,5},{5,1},{9,13},{13,9},{2,6},{6,2},{1... | collective-permute-start | bytes 442376 | tf_op jit(solution)/shard_map/ppermute | solution.py:311
  45.5 7.1 %collective-permute-start.12 = (bf16[64,1152]{1,0:T(8,128)(2,1)S(1)}, bf16[64,1152]{1,0:T(8,128)(2,1)S(1)}, u32[]{:S(2)}, u32[]{:S(2)}) collective-permute-start(bf16[64,1152]{1,0:T(8,128)(2,1)S(1)} %get-tuple-element.111), channel_id=1, source_target_pairs={{0,12},{4,8},{8,4},{12,0},{1,13},{5,9},{9,5},{13,1},{2,14},{6,10},... | collective-permute-start | bytes 442376 | tf_op jit(solution)/shard_map/ppermute | solution.py:311
  53.4 8.0 %collective-permute-start.13 = (bf16[16,1024]{1,0:T(8,128)(2,1)S(1)}, bf16[16,1024]{1,0:T(8,128)(2,1)S(1)}, u32[]{:S(2)}, u32[]{:S(2)}) collective-permute-start(bf16[16,1024]{1,0:T(8,128)(2,1)S(1)} %get-tuple-element.116), channel_id=1, source_target_pairs={{0,1},{1,0},{2,3},{3,2},{4,5},{5,4},{6,7},{7,6},{8,9},{9,8},{10,11... | collective-permute-start | bytes 98312 | tf_op jit(solution)/shard_map/ppermute | solution.py:311
  54.1 7.4 %collective-permute-start.14 = (bf16[16,1024]{1,0:T(8,128)(2,1)S(1)}, bf16[16,1024]{1,0:T(8,128)(2,1)S(1)}, u32[]{:S(2)}, u32[]{:S(2)}) collective-permute-start(bf16[16,1024]{1,0:T(8,128)(2,1)S(1)} %get-tuple-element.117), channel_id=1, source_target_pairs={{0,2},{1,3},{2,0},{3,1},{4,6},{5,7},{6,4},{7,5},{8,10},{9,11},{10,... | collective-permute-start | bytes 98312 | tf_op jit(solution)/shard_map/ppermute | solution.py:311
  57.6 5.7 %collective-permute-start.15 = (bf16[16,1024]{1,0:T(8,128)(2,1)S(1)}, bf16[16,1024]{1,0:T(8,128)(2,1)S(1)}, u32[]{:S(2)}, u32[]{:S(2)}) collective-permute-start(bf16[16,1024]{1,0:T(8,128)(2,1)S(1)} %get-tuple-element.118), channel_id=1, source_target_pairs={{0,3},{1,2},{2,1},{3,0},{4,7},{5,6},{6,5},{7,4},{8,11},{9,10},{10,... | collective-permute-start | bytes 98312 | tf_op jit(solution)/shard_map/ppermute | solution.py:311
